TPU v7x, 32 devices: a whole 2x2x4 slice. The times are simulated.
32 devices in a mesh: seq: 16 (over z, y, x), ffn: 2 (over core).
Axes of the slice: x: 2, y: 2, z: 4, core: 2. Of those that a mesh axis runs over, the one named last changes fastest.
Arguments:
- tokens: bfloat16 [8192, 2048], P(('seq', 'ffn')), may hold values from -6 to 6
- ln1_gain: float32 [2048], replicated, may hold values from 0.5 to 1.5
- ln1_bias: float32 [2048], replicated, may hold values from -1.5 to 1.5
- w_query: bfloat16 [2048, 2048], P('seq', 'ffn'), may hold values from -0.125 to 0.125
- w_key: bfloat16 [2048, 2048], P('seq', 'ffn'), may hold values from -0.125 to 0.125
- w_value: bfloat16 [2048, 4096], P('seq', 'ffn'), may hold values from -0.125 to 0.125
- w_gate: bfloat16 [2048, 4096], P('seq', 'ffn'), may hold values from -0.125 to 0.125
- w_out: bfloat16 [4096, 2048], P('ffn', 'seq'), may hold values from -0.125 to 0.125
- decay_log: float32 [8192, 8], P('seq', 'ffn'), may hold values from -1 to 0
- ln2_gain: float32 [2048], replicated, may hold values from 0.5 to 1.5
- ln2_bias: float32 [2048], replicated, may hold values from -1.5 to 1.5
- w_up: bfloat16 [2048, 4096], P(None, 'ffn'), may hold values from -0.125 to 0.125
- w_down: bfloat16 [4096, 2048], P('ffn'), may hold values from -0.125 to 0.125
- cotangent: bfloat16 [8192, 2048], P('seq'), may hold values from -6 to 6
Outputs:
- block_out: bfloat16 [8192, 2048], P(('seq', 'ffn'))
- grad_tokens: bfloat16 [8192, 2048], P(('seq', 'ffn'))
- grad_ln1_gain: float32 [2048], replicated
- grad_ln1_bias: float32 [2048], replicated
- grad_w_query: float32 [2048, 2048], P('seq', 'ffn')
- grad_w_key: float32 [2048, 2048], P('seq', 'ffn')
- grad_w_value: float32 [2048, 4096], P('seq', 'ffn')
- grad_w_gate: float32 [2048, 4096], P('seq', 'ffn')
- grad_w_out: float32 [4096, 2048], P('ffn', 'seq')
- grad_ln2_gain: float32 [2048], replicated
- grad_ln2_bias: float32 [2048], replicated
- grad_w_up: float32 [2048, 4096], P('seq', 'ffn')
- grad_w_down: float32 [4096, 2048], P('ffn', 'seq')
All inputs are finite; a program needn't handle non-finite values.
Results may differ from a plain program's by a relative error of at most 0.02.
Values may be sent and summed in bfloat16 or wider, within the bound.
A program may use at most 512 MiB of HBM per device.

v0:
```python
import jax
import jax.numpy as jnp
from jax import lax
from jax.sharding import PartitionSpec as P

STRETCH = 512
SEQUENCE_LENGTH = 8192


def carried_in(value, axis, join, neutral, backward):
    count = lax.axis_size(axis)
    place = lax.axis_index(axis)
    ahead = count - 1 - place if backward else place
    gathered = jax.tree.map(
        lambda a, kind: lax.all_gather(a.astype(kind), axis), value, (jnp.bfloat16, jnp.bfloat16)
    )
    state = jax.tree.map(lambda a, e: jnp.zeros_like(a) + jnp.asarray(e, a.dtype), value, neutral)

    def one(step, state):
        source = count - 1 - step if backward else step
        return join(
            state,
            jax.tree.map(
                lambda a, own: lax.dynamic_index_in_dim(a, source, 0, False).astype(own.dtype),
                gathered,
                value,
            ),
        )

    return lax.fori_loop(0, ahead, one, state)


def layer_norm(values_in, gain_vec, bias_vec):
    average = jnp.mean(values_in, axis=-1, keepdims=True)
    centered = values_in - average
    variance = jnp.mean(centered * centered, axis=-1, keepdims=True)
    return centered * lax.rsqrt(variance + 1e-05) * gain_vec + bias_vec


def group_norm(values_in):
    average = jnp.mean(values_in, axis=-1, keepdims=True)
    centered = values_in - average
    variance = jnp.mean(centered * centered, axis=-1, keepdims=True)
    return centered * lax.rsqrt(variance + 1e-05)


def exact_gelu(values_in):
    return jax.nn.gelu(values_in, approximate=False)


def swish_gate(gate_proj, grouped):
    return jax.nn.silu(gate_proj) * grouped


def rotate(values_in, positions, direction):
    half_width = values_in.shape[-1] // 2
    frequency = 10000.0 ** (-jnp.linspace(0.0, 1.0, half_width, dtype=jnp.float32))
    angles = positions.astype(jnp.float32)[:, None] * frequency[None, :] * direction
    cosine = jnp.cos(angles)[:, None, :]
    sine_part = jnp.sin(angles)[:, None, :]
    first_half = values_in[..., :half_width]
    second_half = values_in[..., half_width:]
    return jnp.concatenate(
        [
            first_half * cosine - second_half * sine_part,
            second_half * cosine + first_half * sine_part,
        ],
        axis=-1,
    )


def decay_mask(cumulative):
    across = cumulative.T
    gaps = across[:, :, None] - across[:, None, :]
    indices = jnp.arange(cumulative.shape[0])
    lower = indices[:, None] >= indices[None, :]
    return jnp.where(lower[None], jnp.exp(jnp.minimum(gaps, 0.0)), 0.0)


def carry_forward(earlier_part, later_part):
    return (
        earlier_part[0] * later_part[0],
        later_part[0][:, None, None] * earlier_part[1] + later_part[1],
    )


def carry_backward(earlier_part, later_part):
    return (
        earlier_part[0] * later_part[0],
        later_part[1] + later_part[0][:, None, None] * earlier_part[1],
    )


def local_step(state_in, inputs):
    q_block, k_block, v_block, cumulative = inputs
    raw_scores = jnp.einsum("thk,shk->hts", q_block, k_block, preferred_element_type=jnp.float32)
    weighted = (raw_scores * decay_mask(cumulative)).astype(jnp.bfloat16)
    inside = jnp.einsum("hts,shd->thd", weighted, v_block, preferred_element_type=jnp.float32)
    tail_values = (
        v_block.astype(jnp.float32) * jnp.exp(cumulative[-1:] - cumulative)[:, :, None]
    ).astype(jnp.bfloat16)
    key_values = jnp.einsum(
        "shk,shd->hkd", k_block, tail_values, preferred_element_type=jnp.float32
    )
    next_state = jnp.exp(cumulative[-1])[:, None, None] * state_in + key_values
    return (next_state, (state_in, inside))


def back_step(grad_state, inputs):
    q_block, k_block, v_block, cumulative, q_decayed, prev_state, query_out, grad_out = inputs
    weights_mask = decay_mask(cumulative)
    grad_kv = grad_state.astype(jnp.bfloat16)
    tail_scale = jnp.exp(cumulative[-1:] - cumulative)
    tail_values = (v_block.astype(jnp.float32) * tail_scale[:, :, None]).astype(jnp.bfloat16)
    grad_tail = jnp.einsum("shk,hkd->shd", k_block, grad_kv, preferred_element_type=jnp.float32)
    grad_keys = jnp.einsum("shd,hkd->shk", tail_values, grad_kv, preferred_element_type=jnp.float32)
    grad_decayed = jnp.einsum(
        "thd,hkd->thk",
        grad_out,
        prev_state.astype(jnp.bfloat16),
        preferred_element_type=jnp.float32,
    )
    grad_query = grad_decayed * jnp.exp(cumulative)[:, :, None]
    raw_scores = jnp.einsum("thk,shk->hts", q_block, k_block, preferred_element_type=jnp.float32)
    weighted = (raw_scores * weights_mask).astype(jnp.bfloat16)
    grad_weighted = jnp.einsum(
        "thd,shd->hts", grad_out, v_block, preferred_element_type=jnp.float32
    )
    grad_scores = (grad_weighted * weights_mask).astype(jnp.bfloat16)
    grad_query = grad_query + jnp.einsum(
        "hts,shk->thk", grad_scores, k_block, preferred_element_type=jnp.float32
    )
    grad_keys = grad_keys + jnp.einsum(
        "hts,thk->shk", grad_scores, q_block, preferred_element_type=jnp.float32
    )
    grad_values = grad_tail * tail_scale[:, :, None] + jnp.einsum(
        "hts,thd->shd", weighted, grad_out, preferred_element_type=jnp.float32
    )
    grad_prev = jnp.exp(cumulative[-1])[:, None, None] * grad_state + query_out
    return (grad_prev, (grad_query, grad_keys, grad_values))


def shards(
    tokens,
    ln1_gain,
    ln1_bias,
    w_query,
    w_key,
    w_value,
    w_gate,
    w_out,
    decay_log,
    ln2_gain,
    ln2_bias,
    w_up,
    w_down,
    cotangent,
):
    row_count = tokens.shape[0]
    span_rows = cotangent.shape[0]
    head_count = decay_log.shape[1]
    inputs32 = tokens.astype(jnp.float32)
    xn_first, norm1_back = jax.vjp(layer_norm, inputs32, ln1_gain, ln1_bias)
    normed_span = lax.all_gather(xn_first.astype(jnp.bfloat16), "ffn", axis=0, tiled=True)
    query_w, key_w, value_w, gate_w, out_w = (
        lax.all_gather(w_query, "seq", axis=0, tiled=True),
        lax.all_gather(w_key, "seq", axis=0, tiled=True),
        lax.all_gather(w_value, "seq", axis=0, tiled=True),
        lax.all_gather(w_gate, "seq", axis=0, tiled=True),
        lax.all_gather(w_out, "seq", axis=1, tiled=True),
    )
    key_width = query_w.shape[1] // head_count
    value_width = value_w.shape[1] // head_count
    query_proj = jnp.dot(normed_span, query_w, preferred_element_type=jnp.float32)
    key_proj = jnp.dot(normed_span, key_w, preferred_element_type=jnp.float32)
    value_proj = jnp.dot(normed_span, value_w, preferred_element_type=jnp.float32).astype(
        jnp.bfloat16
    )
    gate_proj = jnp.dot(normed_span, gate_w, preferred_element_type=jnp.float32)
    span_start = lax.axis_index("seq") * span_rows
    positions = (span_start + jnp.arange(span_rows)) % SEQUENCE_LENGTH
    carries_in = (span_start % SEQUENCE_LENGTH != 0).astype(jnp.float32)
    q_rot = rotate(query_proj.reshape(span_rows, head_count, key_width), positions, 1.0).astype(
        jnp.bfloat16
    )
    k_rot = rotate(key_proj.reshape(span_rows, head_count, key_width), positions, 1.0).astype(
        jnp.bfloat16
    )
    block_count = span_rows // STRETCH
    q_blocks = q_rot.reshape(block_count, STRETCH, head_count, key_width)
    k_blocks = k_rot.reshape(block_count, STRETCH, head_count, key_width)
    v_blocks = value_proj.reshape(block_count, STRETCH, head_count, value_width)
    cumulative = jnp.cumsum(decay_log.reshape(block_count, STRETCH, head_count), axis=1)
    block_decay = cumulative[:, -1, :]
    zero_state = jnp.zeros((head_count, key_width, value_width), jnp.float32)
    unit_decay = jnp.ones((head_count,), jnp.float32)
    local_end, (local_prev, inside) = lax.scan(
        local_step, zero_state, (q_blocks, k_blocks, v_blocks, cumulative)
    )
    through = jnp.exp(jnp.sum(block_decay, axis=0)) * carries_in
    decay_in, incoming = carried_in(
        (through, local_end), "seq", carry_forward, (unit_decay, zero_state), False
    )
    incoming = incoming * carries_in
    before_block = jnp.exp(jnp.cumsum(block_decay, axis=0) - block_decay)
    prev_states = local_prev + before_block[:, :, None, None] * incoming[None]
    q_decayed = (q_blocks.astype(jnp.float32) * jnp.exp(cumulative)[..., None]).astype(jnp.bfloat16)
    carried = jnp.einsum(
        "cthk,chkd->cthd",
        q_decayed,
        prev_states.astype(jnp.bfloat16),
        preferred_element_type=jnp.float32,
    )
    retained = (inside + carried).reshape(span_rows, head_count, value_width)
    grouped, group_back = jax.vjp(group_norm, retained)
    grouped = grouped.reshape(span_rows, head_count * value_width)
    gated, gate_back = jax.vjp(swish_gate, gate_proj, grouped)
    gated_low = gated.astype(jnp.bfloat16)
    attn_share = jnp.dot(gated_low, out_w, preferred_element_type=jnp.float32)
    attn_rows = lax.psum_scatter(
        attn_share.astype(jnp.bfloat16), "ffn", scatter_dimension=0, tiled=True
    ).astype(jnp.float32)
    residual = inputs32 + attn_rows
    xn_second, norm2_back = jax.vjp(layer_norm, residual, ln2_gain, ln2_bias)
    ffn_span = lax.all_gather(xn_second.astype(jnp.bfloat16), "ffn", axis=0, tiled=True)
    upper = jnp.dot(ffn_span, w_up, preferred_element_type=jnp.float32)
    active, gelu_back = jax.vjp(exact_gelu, upper)
    active_low = active.astype(jnp.bfloat16)
    ffn_share = jnp.dot(active_low, w_down, preferred_element_type=jnp.float32)
    ffn_rows_out = lax.psum_scatter(
        ffn_share.astype(jnp.bfloat16), "ffn", scatter_dimension=0, tiled=True
    ).astype(jnp.float32)
    block_out = (residual + ffn_rows_out).astype(jnp.bfloat16)
    own_start = lax.axis_index("ffn") * row_count
    cot_own = lax.dynamic_slice_in_dim(cotangent, own_start, row_count, 0).astype(jnp.float32)
    grad_active = jnp.einsum("td,fd->tf", cotangent, w_down, preferred_element_type=jnp.float32)
    grad_upper = gelu_back(grad_active)[0].astype(jnp.bfloat16)
    grad_down = jnp.einsum("tf,td->fd", active_low, cotangent, preferred_element_type=jnp.float32)
    grad_up = jnp.einsum("td,tf->df", ffn_span, grad_upper, preferred_element_type=jnp.float32)
    grad_xn2_share = jnp.einsum("tf,df->td", grad_upper, w_up, preferred_element_type=jnp.float32)
    grad_xn2 = lax.psum_scatter(
        grad_xn2_share.astype(jnp.bfloat16), "ffn", scatter_dimension=0, tiled=True
    ).astype(jnp.float32)
    grad_resid, grad_gain2, grad_bias2 = norm2_back(grad_xn2)
    grad_resid = grad_resid + cot_own
    grad_attn = lax.all_gather(grad_resid.astype(jnp.bfloat16), "ffn", axis=0, tiled=True)
    grad_gated = jnp.einsum("td,vd->tv", grad_attn, out_w, preferred_element_type=jnp.float32)
    grad_out_w = jnp.einsum("tv,td->vd", gated_low, grad_attn, preferred_element_type=jnp.float32)
    grad_gate, grad_grouped = gate_back(grad_gated)
    grad_retained = group_back(grad_grouped.reshape(span_rows, head_count, value_width))[0]
    grad_ret_blocks = grad_retained.astype(jnp.bfloat16).reshape(
        block_count, STRETCH, head_count, value_width
    )
    query_out = jnp.einsum(
        "cthk,cthd->chkd", q_decayed, grad_ret_blocks, preferred_element_type=jnp.float32
    )
    local_grad = jnp.sum(before_block[:, :, None, None] * query_out, axis=0) * carries_in
    decay_out, outgoing = carried_in(
        (through, local_grad), "seq", carry_backward, (unit_decay, zero_state), True
    )
    grad_first, (grad_q_blocks, grad_k_blocks, grad_v_blocks) = lax.scan(
        back_step,
        outgoing,
        (
            q_blocks,
            k_blocks,
            v_blocks,
            cumulative,
            q_decayed,
            prev_states,
            query_out,
            grad_ret_blocks,
        ),
        reverse=True,
    )
    grad_query = rotate(grad_q_blocks.reshape(span_rows, head_count, key_width), positions, -1.0)
    grad_query = grad_query.reshape(span_rows, head_count * key_width).astype(jnp.bfloat16)
    grad_keys = rotate(grad_k_blocks.reshape(span_rows, head_count, key_width), positions, -1.0)
    grad_keys = grad_keys.reshape(span_rows, head_count * key_width).astype(jnp.bfloat16)
    grad_values = grad_v_blocks.reshape(span_rows, head_count * value_width).astype(jnp.bfloat16)
    grad_gate_low = grad_gate.astype(jnp.bfloat16)
    grad_query_w = jnp.einsum(
        "td,tq->dq", normed_span, grad_query, preferred_element_type=jnp.float32
    )
    grad_key_w = jnp.einsum("td,tq->dq", normed_span, grad_keys, preferred_element_type=jnp.float32)
    grad_value_w = jnp.einsum(
        "td,tv->dv", normed_span, grad_values, preferred_element_type=jnp.float32
    )
    grad_gate_w = jnp.einsum(
        "td,tv->dv", normed_span, grad_gate_low, preferred_element_type=jnp.float32
    )
    grad_xn1_share = jnp.einsum(
        "tq,dq->td", grad_query, query_w, preferred_element_type=jnp.float32
    )
    grad_xn1_share = grad_xn1_share + jnp.einsum(
        "tq,dq->td", grad_keys, key_w, preferred_element_type=jnp.float32
    )
    grad_xn1_share = grad_xn1_share + jnp.einsum(
        "tv,dv->td", grad_values, value_w, preferred_element_type=jnp.float32
    )
    grad_xn1_share = grad_xn1_share + jnp.einsum(
        "tv,dv->td", grad_gate_low, gate_w, preferred_element_type=jnp.float32
    )
    grad_xn1 = lax.psum_scatter(
        grad_xn1_share.astype(jnp.bfloat16), "ffn", scatter_dimension=0, tiled=True
    ).astype(jnp.float32)
    grad_inputs, grad_gain1, grad_bias1 = norm1_back(grad_xn1)
    grad_tokens = (grad_resid + grad_inputs).astype(jnp.bfloat16)
    gain_one, bias_one, gain_two, bias_two = lax.psum(
        (grad_gain1, grad_bias1, grad_gain2, grad_bias2), ("seq", "ffn")
    )
    sum_query, sum_key, sum_value, sum_gate, sum_out, sum_up, sum_down = (
        lax.psum_scatter(grad_query_w, "seq", scatter_dimension=0, tiled=True),
        lax.psum_scatter(grad_key_w, "seq", scatter_dimension=0, tiled=True),
        lax.psum_scatter(grad_value_w, "seq", scatter_dimension=0, tiled=True),
        lax.psum_scatter(grad_gate_w, "seq", scatter_dimension=0, tiled=True),
        lax.psum_scatter(grad_out_w, "seq", scatter_dimension=1, tiled=True),
        lax.psum_scatter(grad_up, "seq", scatter_dimension=0, tiled=True),
        lax.psum_scatter(grad_down, "seq", scatter_dimension=1, tiled=True),
    )
    return (
        block_out,
        grad_tokens,
        gain_one,
        bias_one,
        sum_query,
        sum_key,
        sum_value,
        sum_gate,
        sum_out,
        gain_two,
        bias_two,
        sum_up,
        sum_down,
    )


def solution(mesh):
    return jax.shard_map(
        shards,
        mesh=mesh,
        in_specs=(
            P(("seq", "ffn"), None),
            P(),
            P(),
            P("seq", "ffn"),
            P("seq", "ffn"),
            P("seq", "ffn"),
            P("seq", "ffn"),
            P("ffn", "seq"),
            P("seq", "ffn"),
            P(),
            P(),
            P(None, "ffn"),
            P("ffn", None),
            P("seq", None),
        ),
        out_specs=(
            P(("seq", "ffn"), None),
            P(("seq", "ffn"), None),
            P(),
            P(),
            P("seq", "ffn"),
            P("seq", "ffn"),
            P("seq", "ffn"),
            P("seq", "ffn"),
            P("ffn", "seq"),
            P(),
            P(),
            P("seq", "ffn"),
            P("ffn", "seq"),
        ),
        check_vma=False,
    )
```

profile of v0, /device:TPU:16, one launch (start us, length us, event | category | flops | bytes accessed | tf_op | source)
XLA Modules:
  0.0 3324.7 jit_solution(9640181958086577545)
XLA Ops:
  25.1 79.3 %all-gather.20.cloned.1.call-done = bf16[2048,1024]{1,0:T(8,128)(2,1)} async-done(((bf16[128,1024]{1,0:T(8,128)(2,1)}), bf16[2048,1024]{1,0:T(8,128)(2,1)}) %all-gather.20.cloned.1.call-update) | async-done | bytes 4194320 | tf_op jit(solution)/shard_map/all_gather | solution.py:166
  113.1 68.8 %all-gather.22.cloned.1.call-done = bf16[2048,1024]{1,0:T(8,128)(2,1)} async-done(((bf16[128,1024]{1,0:T(8,128)(2,1)}), bf16[2048,1024]{1,0:T(8,128)(2,1)}) %all-gather.22.cloned.1.call-update) | async-done | bytes 4194320 | tf_op jit(solution)/shard_map/all_gather | solution.py:167
  195.5 100.1 %all-gather.18.cloned.1.call-done = bf16[2048,2048]{1,0:T(8,128)(2,1)} async-done(((bf16[128,2048]{1,0:T(8,128)(2,1)}), bf16[2048,2048]{1,0:T(8,128)(2,1)}) %all-gather.18.cloned.1.call-update) | async-done | bytes 8388624 | tf_op jit(solution)/shard_map/all_gather | solution.py:168
  312.9 30.5 all-gather
  351.3 150.1 %all-gather.30.cloned.1.call-done = bf16[64,256,512]{2,1,0:T(8,128)(2,1)} async-done(((bf16[4,256,512]{2,1,0:T(8,128)(2,1)}), bf16[64,256,512]{2,1,0:T(8,128)(2,1)}) %all-gather.30.cloned.1.call-update) | async-done | bytes 16777232 | tf_op jit(solution)/shard_map/all_gather | solution.py:15
  501.7 16.1 while.16
  544.8 70.4 %all-gather.16.cloned.1.call-done = bf16[2048,2048]{1,0:T(8,128)(2,1)} async-done(((bf16[128,2048]{1,0:T(8,128)(2,1)}), bf16[2048,2048]{1,0:T(8,128)(2,1)}) %all-gather.16.cloned.1.call-update) | async-done | bytes 8388624 | tf_op jit(solution)/shard_map/all_gather | solution.py:169
  615.2 15.3 multiply_convert_fusion.2
  630.5 128.0 %all-gather.24.cloned.1.call-done = bf16[2048,2048]{1,0:T(8,128)(2,1)} async-done(((bf16[2048,128]{1,0:T(8,128)(2,1)}), bf16[2048,2048]{1,0:T(8,128)(2,1)}) %all-gather.24.cloned.1.call-update) | async-done | bytes 8388624 | tf_op jit(solution)/shard_map/all_gather | solution.py:170
  781.4 11.7 all-gather.26.cloned.1.call-done
  800.8 18.9 add_convert_fusion.2
  860.5 11.9 all-gather.28.cloned.1.call-done
  872.4 17.5 fusion.5
  920.6 176.4 %all-gather.32.cloned.1.call-done = bf16[64,256,512]{2,1,0:T(8,128)(2,1)} async-done(((bf16[4,256,512]{2,1,0:T(8,128)(2,1)}), bf16[64,256,512]{2,1,0:T(8,128)(2,1)}) %all-gather.32.cloned.1.call-update) | async-done | bytes 16777232 | tf_op jit(solution)/shard_map/all_gather | solution.py:15
  1097.2 18.7 while.17
  1186.7 12.5 fusion.75
  1230.1 71.1 %all-reduce = (f32[2048]{0:T(1024)}, f32[2048]{0:T(1024)}, f32[2048]{0:T(1024)}, f32[2048]{0:T(1024)}) all-reduce(f32[2048]{0:T(1024)S(1)} %get-tuple-element.236, f32[2048]{0:T(1024)S(1)} %get-tuple-element.239, f32[2048]{0:T(1024)S(1)} %copy-done.47, f32[2048]{0:T(1024)S(1)} %copy-done.48), channel_id=1, replica_groups=mesh['seq'=16,'ffn'=2] {'seq','ffn'}, use_global_device_ids=true, to_apply=%region_23.25 | all-reduce | flops 8192 | bytes 65536 | tf_op jit(solution)/shard_map/psum | solution.py:309
  1304.6 227.5 %reduce-scatter.30.cloned.1.call-done = f32[128,2048]{1,0:T(8,128)} async-done(((f32[2048,2048]{1,0:T(8,128)}), f32[128,2048]{1,0:T(8,128)}) %reduce-scatter.30.cloned.1.call-update) | async-done | bytes 1048592 | tf_op jit(solution)/shard_map/reduce_scatter | solution.py:318
  1532.1 354.7 %reduce-scatter.32.cloned.1.call-done = f32[2048,128]{1,0:T(8,128)} async-done(((f32[2048,2048]{1,0:T(8,128)}), f32[2048,128]{1,0:T(8,128)}) %reduce-scatter.32.cloned.1.call-update) | async-done | bytes 1048592 | tf_op jit(solution)/shard_map/reduce_scatter | solution.py:319
  1886.8 354.8 %reduce-scatter.26.cloned.1.call-done = f32[128,2048]{1,0:T(8,128)} async-done(((f32[2048,2048]{1,0:T(8,128)}), f32[128,2048]{1,0:T(8,128)}) %reduce-scatter.26.cloned.1.call-update) | async-done | bytes 1048592 | tf_op jit(solution)/shard_map/reduce_scatter | solution.py:316
  2241.6 354.8 %reduce-scatter.28.cloned.1.call-done = f32[2048,128]{1,0:T(8,128)} async-done(((f32[2048,2048]{1,0:T(8,128)}), f32[2048,128]{1,0:T(8,128)}) %reduce-scatter.28.cloned.1.call-update) | async-done | bytes 1048592 | tf_op jit(solution)/shard_map/reduce_scatter | solution.py:317
  2596.4 186.1 %reduce-scatter.20.cloned.1.call-done = f32[128,1024]{1,0:T(8,128)} async-done(((f32[2048,1024]{1,0:T(8,128)}), f32[128,1024]{1,0:T(8,128)}) %reduce-scatter.20.cloned.1.call-update) | async-done | bytes 524304 | tf_op jit(solution)/shard_map/reduce_scatter | solution.py:313
  2782.5 183.0 %reduce-scatter.22.cloned.1.call-done = f32[128,1024]{1,0:T(8,128)} async-done(((f32[2048,1024]{1,0:T(8,128)}), f32[128,1024]{1,0:T(8,128)}) %reduce-scatter.22.cloned.1.call-update) | async-done | bytes 524304 | tf_op jit(solution)/shard_map/reduce_scatter | solution.py:314
  2965.5 352.0 %reduce-scatter.24.cloned.1.call-done = f32[128,2048]{1,0:T(8,128)} async-done(((f32[2048,2048]{1,0:T(8,128)}), f32[128,2048]{1,0:T(8,128)}) %reduce-scatter.24.cloned.1.call-update) | async-done | bytes 1048592 | tf_op jit(solution)/shard_map/reduce_scatter | solution.py:315
  (321 shorter events, 333.6 us)
Async XLA Ops:
  7.2 17.8 all-gather.14.cloned.1.call-start
  13.0 91.4 %all-gather.20.cloned.1.call-start = ((), (), s32[]{:S(2)}) async-start(), calls=%async_computation.14 | async-start | bytes 4456448 | tf_op jit(solution)/shard_map/all_gather | solution.py:166
  13.7 168.1 %all-gather.22.cloned.1.call-start = ((), (), s32[]{:S(2)}) async-start(), calls=%async_computation.15 | async-start | bytes 4456448 | tf_op jit(solution)/shard_map/all_gather | solution.py:167
  14.5 281.1 %all-gather.18.cloned.1.call-start = ((), (), s32[]{:S(2)}) async-start(), calls=%async_computation.13 | async-start | bytes 8912896 | tf_op jit(solution)/shard_map/all_gather | solution.py:168
  15.1 486.4 %all-gather.30.cloned.1.call-start = ((), (), s32[]{:S(2)}) async-start(), calls=%async_computation.30 | async-start | bytes 17825792 | tf_op jit(solution)/shard_map/all_gather | solution.py:15
  17.5 326.2 %copy-start.40 = (f32[1,4,512]{2,1,0:T(4,128)}, f32[1,4,512]{2,1,0:T(4,128)S(1)}, u32[]{:S(2)}) copy-start(f32[1,4,512]{2,1,0:T(4,128)S(1)} %get-tuple-element.266) | copy-start | bytes 24580
  17.8 289.7 %copy-start.43 = (f32[512,4]{0,1:T(4,128)}, f32[512,4]{0,1:T(4,128)S(1)}, u32[]{:S(2)}) copy-start(f32[512,4]{0,1:T(4,128)S(1)} %fusion.50) | copy-start | bytes 24580
  193.7 101.8 %copy-start.62 = (bf16[512,2048]{1,0:T(8,128)(2,1)S(1)}, bf16[512,2048]{1,0:T(8,128)(2,1)}, u32[]{:S(2)}) copy-start(bf16[512,2048]{1,0:T(8,128)(2,1)} %all-gather.14.cloned.1.call-done) | copy-start | bytes 6291460
  311.5 303.7 %all-gather.16.cloned.1.call-start = ((), (), s32[]{:S(2)}) async-start(), calls=%async_computation.12 | async-start | bytes 8912896 | tf_op jit(solution)/shard_map/all_gather | solution.py:169
  312.0 446.4 %all-gather.24.cloned.1.call-start = ((), (), s32[]{:S(2)}) async-start(), calls=%async_computation.16 | async-start | bytes 8912896 | tf_op jit(solution)/shard_map/all_gather | solution.py:170
  312.8 464.6 %reduce-scatter.12.cloned.1.call-start = ((), (), s32[]{:S(2)}) async-start(), calls=%async_computation.17 | async-start | bytes 3145728 | tf_op jit(solution)/shard_map/reduce_scatter | solution.py:220
  768.3 24.8 all-gather.26.cloned.1.call-start
  781.2 61.8 %reduce-scatter.16.cloned.1.call-start = ((), (), s32[]{:S(2)}) async-start(), calls=%async_computation.20 | async-start | bytes 3145728 | tf_op jit(solution)/shard_map/reduce_scatter | solution.py:241
  826.9 26.9 reduce-scatter.14.cloned.1.call-start
  842.9 29.4 all-gather.28.cloned.1.call-start
  860.5 236.5 %all-gather.32.cloned.1.call-start = ((), (), s32[]{:S(2)}) async-start(), calls=%async_computation.31 | async-start | bytes 17825792 | tf_op jit(solution)/shard_map/all_gather | solution.py:15
  905.2 319.5 %reduce-scatter.18.cloned.1.call-start = ((), (), s32[]{:S(2)}) async-start(), calls=%async_computation.22 | async-start | bytes 3145728 | tf_op jit(solution)/shard_map/reduce_scatter | solution.py:304
  1152.3 379.8 %reduce-scatter.30.cloned.1.call-start = ((), (), s32[]{:S(2)}) async-start(), calls=%async_computation.28 | async-start | bytes 17825792 | tf_op jit(solution)/shard_map/reduce_scatter | solution.py:318
  1163.7 723.1 %reduce-scatter.32.cloned.1.call-start = ((), (), s32[]{:S(2)}) async-start(), calls=%async_computation.29 | async-start | bytes 17825792 | tf_op jit(solution)/shard_map/reduce_scatter | solution.py:319
  1175.2 1066.4 %reduce-scatter.26.cloned.1.call-start = ((), (), s32[]{:S(2)}) async-start(), calls=%async_computation.26 | async-start | bytes 17825792 | tf_op jit(solution)/shard_map/reduce_scatter | solution.py:316
  1186.7 1409.7 %reduce-scatter.28.cloned.1.call-start = ((), (), s32[]{:S(2)}) async-start(), calls=%async_computation.27 | async-start | bytes 17825792 | tf_op jit(solution)/shard_map/reduce_scatter | solution.py:317
  1199.3 1583.2 %reduce-scatter.20.cloned.1.call-start = ((), (), s32[]{:S(2)}) async-start(), calls=%async_computation.23 | async-start | bytes 8912896 | tf_op jit(solution)/shard_map/reduce_scatter | solution.py:313
  1206.3 1759.2 %reduce-scatter.22.cloned.1.call-start = ((), (), s32[]{:S(2)}) async-start(), calls=%async_computation.24 | async-start | bytes 8912896 | tf_op jit(solution)/shard_map/reduce_scatter | solution.py:314
  1213.3 2104.2 %reduce-scatter.24.cloned.1.call-start = ((), (), s32[]{:S(2)}) async-start(), calls=%async_computation.25 | async-start | bytes 17825792 | tf_op jit(solution)/shard_map/reduce_scatter | solution.py:315
  (69 other events, 478.6 us)
Sparse Core Ops, SparseCore 0:
  13.1 11.9 all-gather.13
  27.8 76.5 all-gather.19
  107.1 74.6 all-gather.21
  184.5 111.0 all-gather.17
  311.6 189.8 all-gather.29
  504.1 111.0 all-gather.15
  617.9 140.5 all-gather.23
  768.4 8.9 reduce-scatter.11
  781.3 11.7 all-gather.25
  827.1 10.7 reduce-scatter.15
  843.0 10.7 reduce-scatter.13
  860.6 11.7 all-gather.27
  905.3 191.6 all-gather.31
  1152.4 28.1 reduce-scatter.17
  1183.3 348.7 reduce-scatter.29
  1534.9 351.9 reduce-scatter.31
  1889.5 352.0 reduce-scatter.25
  2244.3 352.0 reduce-scatter.27
  2599.2 183.1 reduce-scatter.19
  2785.2 180.2 reduce-scatter.21
  2968.3 349.0 reduce-scatter.23
where the time goes:
time: 3340 us; the launch traced here: 3320 us
  waiting for transfers between devices  2830 us (85%)
  matrix products  223 us (7%)
  blocking collectives  102 us (3%)
  other arithmetic  82.4 us (2%)
  local copies, waits for them, and re-layouts  65.9 us (2%)
    reduce_scatter x1, waiting for transfers between devices, shards(): lax.psum_scatter(grad_out_w, 'seq', scatter_dimension=1, tiled=True)  355 us
    reduce_scatter x1, waiting for transfers between devices, shards(): lax.psum_scatter(grad_gate_w, 'seq', scatter_dimension=0, tiled=True)  355 us
    reduce_scatter x1, waiting for transfers between devices, shards(): lax.psum_scatter(grad_down, 'seq', scatter_dimension=1, tiled=True)  355 us
    reduce_scatter x1, waiting for transfers between devices, shards(): lax.psum_scatter(grad_value_w, 'seq', scatter_dimension=0, tiled=True)  352 us
    all_gather x2, waiting for transfers between devices, carried_in(): lax.all_gather(a.astype(kind), axis)  327 us
    reduce_scatter x1, waiting for transfers between devices, shards(): lax.psum_scatter(grad_up, 'seq', scatter_dimension=0, tiled=True)  228 us
    reduce_scatter x1, waiting for transfers between devices, shards(): lax.psum_scatter(grad_query_w, 'seq', scatter_dimension=0, tiled=True)  186 us
    reduce_scatter x1, waiting for transfers between devices, shards(): lax.psum_scatter(grad_key_w, 'seq', scatter_dimension=0, tiled=True)  183 us
  transfers between devices with their start and end apart: 21, of which 19 were waited for; matrix products, arithmetic and copies ran while one was open for 6% of the time, Pallas kernels for 0%

commit v1 on v0

v1 whole, which is shorter than its diff:
```python
import functools

import jax
import jax.numpy as jnp
from jax import lax
from jax.experimental import pallas as pl
from jax.experimental.pallas import tpu as pltpu
from jax.sharding import PartitionSpec as P

STRETCH = 512
SEQUENCE_LENGTH = 8192
PLANE = 4
LINE = 4
SPANS = PLANE * LINE
MESH = pl.DeviceIdType.MESH
VMEM_LIMIT = 60 * 1024 * 1024
ANY = pl.BlockSpec(memory_space=pl.ANY)
VM = pl.BlockSpec(memory_space=pltpu.VMEM)
BF16 = jnp.bfloat16
F32 = jnp.float32


class Place:
    def __init__(self):
        s = lax.axis_index("seq")
        self.f = lax.axis_index("ffn")
        lo = s % SPANS
        self.base = s - lo
        self.z = lo // PLANE
        self.p = lo % PLANE

    def plane(self, m):
        return self.at(self.z, self.xor(m), self.f)

    def xor(self, m):
        p = self.p
        low, high = p % 2, p // 2
        if m & 1:
            low = 1 - low
        if m & 2:
            high = 1 - high
        return high * 2 + low

    def at(self, z, p, f):
        return (self.base + z * PLANE + p, f)

    def partner(self):
        return self.at(self.z, self.p, 1 - self.f)

    def up(self):
        return self.at(self.z + 1, self.p, self.f)

    def down(self):
        return self.at(self.z - 1, self.p, self.f)


def greet(peers):
    bar = pltpu.get_barrier_semaphore()
    count = 0
    for device, cond in peers:
        if cond is None:
            pl.semaphore_signal(bar, inc=1, device_id=device, device_id_type=MESH)
            count = count + 1
        else:

            @pl.when(cond)
            def _():
                pl.semaphore_signal(bar, inc=1, device_id=device, device_id_type=MESH)

            count = count + cond.astype(jnp.int32)
    pl.semaphore_wait(bar, count)


def remote(src, dst, send, recv, device):
    return pltpu.make_async_remote_copy(
        src_ref=src, dst_ref=dst, send_sem=send, recv_sem=recv, device_id=device, device_id_type=MESH
    )


def comm_call(kernel, outs, ins, scratch, cid, in_specs=None, out_specs=None):
    return pl.pallas_call(
        kernel,
        out_shape=outs,
        in_specs=in_specs if in_specs is not None else [ANY] * len(ins),
        out_specs=out_specs if out_specs is not None else [ANY] * len(outs),
        scratch_shapes=scratch,
        compiler_params=pltpu.CompilerParams(
            collective_id=cid, has_side_effects=True, vmem_limit_bytes=VMEM_LIMIT
        ),
    )(*ins)


DMA = pltpu.SemaphoreType.DMA


def gather_kernel(widths, rows, *refs):
    count = len(widths)
    xn_ref, dec_ref = refs[:2]
    shards_in = refs[2 : 2 + count]
    xg, decg = refs[2 + count : 4 + count]
    full = refs[4 + count : 4 + 2 * count]
    lsem, psend, precv, usend, dsend, zrecv, xsend, xrecv, csend, crecv, tsend, trecv = refs[4 + 2 * count :]
    me = Place()
    z, p, f = me.z, me.p, me.f
    spot = z * PLANE + p
    chunk = shards_in[0].shape[0]
    deep = chunk * PLANE
    greet(
        [(me.plane(m), None) for m in (1, 2, 3)]
        + [(me.partner(), None), (me.up(), z < LINE - 1), (me.down(), z > 0)]
    )

    def part(i, q):
        w = widths[i]
        if rows[i]:
            return shards_in[i].at[pl.ds(pl.multiple_of(q * w, w), w), :]
        return shards_in[i].at[:, pl.ds(pl.multiple_of(q * w, w), w)]

    def slot(i, ss):
        at = pl.ds(pl.multiple_of(ss * chunk, chunk), chunk)
        return full[i].at[:, at] if rows[i] else full[i].at[at, :]

    def block(i, zz):
        at = pl.ds(pl.multiple_of(zz * deep, deep), deep)
        return full[i].at[:, at] if rows[i] else full[i].at[at, :]

    local, plane = [], []
    for i in range(count):
        own = pltpu.make_async_copy(part(i, p), slot(i, spot), lsem.at[i])
        own.start()
        local.append(own)
        sends = []
        for m in (1, 2, 3):
            c = remote(part(i, me.xor(m)), slot(i, spot), psend.at[i, m], precv.at[i, m], me.plane(m))
            c.start()
            sends.append(c)
        plane.append(sends)
    tiny = []
    for m in (1, 2, 3):
        c = remote(dec_ref, decg.at[p], tsend.at[m], trecv.at[m], me.plane(m))
        c.start()
        tiny.append(c)
    dec_own = pltpu.make_async_copy(dec_ref, decg.at[p], lsem.at[count])
    dec_own.start()

    seat = p * 2 + f
    x_own = pltpu.make_async_copy(xn_ref, xg.at[seat], lsem.at[count + 1])
    x_own.start()
    half = xn_ref.shape[0] // 2
    x1 = remote(xn_ref, xg.at[seat], xsend.at[0], xrecv.at[0], me.plane(1))
    x2 = remote(xn_ref, xg.at[seat], xsend.at[1], xrecv.at[1], me.plane(2))
    xc = remote(xn_ref, xg.at[seat], csend.at[0], crecv.at[0], me.partner())
    x1.start()
    x2.start()
    xc.start()

    def up_copy(i, zz):
        return remote(block(i, zz), block(i, zz), usend.at[i, zz], zrecv.at[i, zz], me.up())

    def down_copy(i, zz):
        return remote(block(i, zz), block(i, zz), dsend.at[i, zz], zrecv.at[i, zz], me.down())

    for i in range(count):
        local[i].wait()
        for c in plane[i]:
            c.wait_recv()

        @pl.when(z < LINE - 1)
        def _():
            up_copy(i, z).start()

        @pl.when(z > 0)
        def _():
            down_copy(i, z).start()

    seat1, seat2, seat3 = (me.xor(m) * 2 + f for m in (1, 2, 3))
    low, high = pl.ds(0, half), pl.ds(half, half)
    x1.wait_recv()
    g1 = remote(xg.at[seat1, low], xg.at[seat1, low], xsend.at[2], xrecv.at[2], me.plane(2))
    g1.start()
    c1 = remote(xg.at[seat1], xg.at[seat1], csend.at[1], crecv.at[1], me.partner())
    c1.start()
    x2.wait_recv()
    g2 = remote(xg.at[seat2, high], xg.at[seat2, high], xsend.at[3], xrecv.at[3], me.plane(1))
    g2.start()
    c2 = remote(xg.at[seat2], xg.at[seat2], csend.at[2], crecv.at[2], me.partner())
    c2.start()
    g1.wait_recv()
    g2.wait_recv()
    c3 = remote(xg.at[seat3], xg.at[seat3], csend.at[3], crecv.at[3], me.partner())
    c3.start()

    for t in range(1, LINE):
        for i in range(count):

            @pl.when(z - t >= 0)
            def _():
                up_copy(i, z - t).wait_recv()

                @pl.when(z < LINE - 1)
                def _():
                    up_copy(i, z - t).start()

            @pl.when(z + t < LINE)
            def _():
                down_copy(i, z + t).wait_recv()

                @pl.when(z > 0)
                def _():
                    down_copy(i, z + t).start()

    for c in (xc, c1, c2, c3):
        c.wait()
    for c in (x1, x2, g1, g2):
        c.wait_send()
    for c in tiny:
        c.wait()
    dec_own.wait()
    x_own.wait()
    for i in range(count):
        for c in plane[i]:
            c.wait_send()
        for zz in range(LINE):

            @pl.when((z < LINE - 1) & (zz <= z))
            def _():
                up_copy(i, zz).wait_send()

            @pl.when((z > 0) & (zz >= z))
            def _():
                down_copy(i, zz).wait_send()


def gather_in(xn, dec, shards_in, rows, cid):
    count = len(shards_in)
    chunk = shards_in[0].shape[0]
    widths, outs = [], []
    for w, r in zip(shards_in, rows):
        if r:
            widths.append(w.shape[0] // PLANE)
            outs.append(jax.ShapeDtypeStruct((w.shape[0] // PLANE, chunk * SPANS), BF16))
        else:
            widths.append(w.shape[1] // PLANE)
            outs.append(jax.ShapeDtypeStruct((chunk * SPANS, w.shape[1] // PLANE), BF16))
    outs = [
        jax.ShapeDtypeStruct((2 * PLANE,) + xn.shape, BF16),
        jax.ShapeDtypeStruct((PLANE,) + dec.shape, F32),
    ] + outs
    scratch = [
        DMA((count + 2,)),
        DMA((count, PLANE)),
        DMA((count, PLANE)),
        DMA((count, LINE)),
        DMA((count, LINE)),
        DMA((count, LINE)),
        DMA((4,)),
        DMA((4,)),
        DMA((4,)),
        DMA((4,)),
        DMA((PLANE,)),
        DMA((PLANE,)),
    ]
    return comm_call(
        functools.partial(gather_kernel, widths, rows), outs, [xn, dec] + shards_in, scratch, cid
    )


def plane_gather_kernel(x_ref, out, lsem, xsend, xrecv, csend, crecv):
    me = Place()
    p, f = me.p, me.f
    greet([(me.plane(1), None), (me.plane(2), None), (me.partner(), None)])
    seat, seat1, seat2, seat3 = (me.xor(m) * 2 + f for m in (0, 1, 2, 3))
    half = x_ref.shape[0] // 2
    low, high = pl.ds(0, half), pl.ds(half, half)
    own = pltpu.make_async_copy(x_ref, out.at[seat], lsem)
    own.start()
    x1 = [
        remote(x_ref.at[h], out.at[seat, h], xsend.at[k], xrecv.at[k], me.plane(1))
        for k, h in ((0, low), (1, high))
    ]
    x2 = [
        remote(x_ref.at[h], out.at[seat, h], xsend.at[k], xrecv.at[k], me.plane(2))
        for k, h in ((2, high), (3, low))
    ]
    for a, b in zip(x1, x2):
        a.start()
        b.start()
    c0 = remote(x_ref, out.at[seat], csend.at[0], crecv.at[0], me.partner())
    c0.start()
    x1[0].wait_recv()
    g1 = remote(out.at[seat1, low], out.at[seat1, low], xsend.at[4], xrecv.at[4], me.plane(2))
    g1.start()
    x2[0].wait_recv()
    g2 = remote(out.at[seat2, high], out.at[seat2, high], xsend.at[5], xrecv.at[5], me.plane(1))
    g2.start()
    x1[1].wait_recv()
    c1 = remote(out.at[seat1], out.at[seat1], csend.at[1], crecv.at[1], me.partner())
    c1.start()
    x2[1].wait_recv()
    c2 = remote(out.at[seat2], out.at[seat2], csend.at[2], crecv.at[2], me.partner())
    c2.start()
    g1.wait_recv()
    c3 = remote(out.at[seat3, low], out.at[seat3, low], csend.at[3], crecv.at[3], me.partner())
    c3.start()
    g2.wait_recv()
    c4 = remote(out.at[seat3, high], out.at[seat3, high], csend.at[4], crecv.at[4], me.partner())
    c4.start()
    for c in (c0, c1, c2, c3, c4):
        c.wait()
    for c in x1 + x2 + [g1, g2]:
        c.wait_send()
    own.wait()


def plane_gather(x, cid):
    return comm_call(
        plane_gather_kernel,
        [jax.ShapeDtypeStruct((2 * PLANE,) + x.shape, x.dtype)],
        [x],
        [DMA, DMA((6,)), DMA((6,)), DMA((5,)), DMA((5,))],
        cid,
    )[0]


def plane_reduce_kernel(x_ref, out, rx0, rx1a, rx1b, rx2a, rx2b, csend, crecv, xsend, xrecv):
    me = Place()
    p, f = me.p, me.f
    greet([(me.plane(1), None), (me.plane(2), None), (me.partner(), None)])
    q = [me.xor(m) for m in range(4)]
    wide = x_ref.shape[-1] // 2
    ca, cb = pl.ds(0, wide), pl.ds(wide, wide)
    order = (3, 1, 2, 0)
    first = []
    for m in order:
        c = remote(x_ref.at[q[m], 1 - f], rx0.at[q[m]], csend.at[m], crecv.at[m], me.partner())
        c.start()
        first.append(c)

    def add(dst, cols, other, others_cols):
        rows = dst.shape[0]

        @pl.loop(0, rows, step=64)
        def _(r):
            at = pl.ds(pl.multiple_of(r, 64), 64)
            dst[at, cols] = (dst[at, cols].astype(F32) + other[at, others_cols].astype(F32)).astype(BF16)

    everything = pl.ds(0, 2 * wide)
    whole = pl.ds(0, wide)
    sends = {}
    for c, m in zip(first, order):
        c.wait_recv()
        add(rx0.at[q[m]], everything, x_ref.at[q[m], f], everything)
        if m & 1:
            k = 0 if m == 3 else 1
            s = remote(rx0.at[q[m], :, ca], rx1a.at[k], xsend.at[k], xrecv.at[k], me.plane(1))
            s.start()
            sends["a", k] = s
        if m & 2:
            k = 0 if m == 3 else 1
            s = remote(rx0.at[q[m], :, cb], rx1b.at[k], xsend.at[2 + k], xrecv.at[2 + k], me.plane(2))
            s.start()
            sends["b", k] = s
    sends["a", 0].wait_recv()
    add(rx1a.at[0], whole, rx0.at[q[2]], ca)
    s2a = remote(rx1a.at[0], rx2a, xsend.at[4], xrecv.at[4], me.plane(2))
    s2a.start()
    sends["b", 0].wait_recv()
    add(rx1b.at[0], whole, rx0.at[q[1]], cb)
    s2b = remote(rx1b.at[0], rx2b, xsend.at[5], xrecv.at[5], me.plane(1))
    s2b.start()
    sends["a", 1].wait_recv()
    sends["b", 1].wait_recv()
    s2a.wait_recv()
    s2b.wait_recv()

    @pl.loop(0, out.shape[0], step=32)
    def _(r):
        at = pl.ds(pl.multiple_of(r, 32), 32)
        out[at, ca] = rx0[q[0], at, ca].astype(F32) + rx1a[1, at, :].astype(F32) + rx2a[at, :].astype(F32)
        out[at, cb] = rx0[q[0], at, cb].astype(F32) + rx1b[1, at, :].astype(F32) + rx2b[at, :].astype(F32)

    for c in first + list(sends.values()) + [s2a, s2b]:
        c.wait_send()


def plane_reduce(x, cid):
    _, _, rows, cols = x.shape
    return comm_call(
        plane_reduce_kernel,
        [jax.ShapeDtypeStruct((rows, cols), F32)],
        [x],
        [
            pltpu.VMEM((PLANE, rows, cols), BF16),
            pltpu.VMEM((2, rows, cols // 2), BF16),
            pltpu.VMEM((2, rows, cols // 2), BF16),
            pltpu.VMEM((rows, cols // 2), BF16),
            pltpu.VMEM((rows, cols // 2), BF16),
            DMA((4,)),
            DMA((4,)),
            DMA((6,)),
            DMA((6,)),
        ],
        cid,
        in_specs=[VM],
        out_specs=[VM],
    )[0]


def pair_gather_kernel(x_ref, out, lsem, csend, crecv):
    me = Place()
    greet([(me.partner(), None)])
    own = pltpu.make_async_copy(x_ref, out.at[me.f], lsem)
    own.start()
    c = remote(x_ref, out.at[me.f], csend, crecv, me.partner())
    c.start()
    own.wait()
    c.wait()


def pair_gather(x, cid):
    return comm_call(
        pair_gather_kernel, [jax.ShapeDtypeStruct((2,) + x.shape, x.dtype)], [x], [DMA, DMA, DMA], cid
    )[0]


def pair_reduce_kernel(x_ref, out, rx, csend, crecv):
    me = Place()
    greet([(me.partner(), None)])
    c = remote(x_ref.at[1 - me.f], rx, csend, crecv, me.partner())
    c.start()
    c.wait_recv()

    @pl.loop(0, out.shape[0], step=32)
    def _(r):
        at = pl.ds(pl.multiple_of(r, 32), 32)
        out[at, :] = x_ref[me.f, at, :].astype(F32) + rx[at, :].astype(F32)

    c.wait_send()


def pair_reduce(x, cid):
    _, rows, cols = x.shape
    return comm_call(
        pair_reduce_kernel,
        [jax.ShapeDtypeStruct((rows, cols), F32)],
        [x],
        [pltpu.VMEM((rows, cols), BF16), DMA, DMA],
        cid,
        in_specs=[VM],
        out_specs=[VM],
    )[0]


def line_states_kernel(backward, x_ref, d_ref, out, dout, lsem, xsend, xrecv, dsend, drecv):
    me = Place()
    z = me.z
    others = [(z + t) % LINE for t in range(1, LINE)]
    greet([(me.at(o, me.p, me.f), None) for o in others])
    own = pltpu.make_async_copy(x_ref, out.at[z], lsem.at[0])
    own.start()
    down = pltpu.make_async_copy(d_ref, dout.at[z], lsem.at[1])
    down.start()

    def pair(step, to, slot):
        sem = step - 1
        device = me.at(to, me.p, me.f)
        return (
            remote(x_ref, out.at[slot], xsend.at[sem], xrecv.at[sem], device),
            remote(d_ref, dout.at[slot], dsend.at[sem], drecv.at[sem], device),
        )

    sign = -1 if backward else 1
    for t in range(1, LINE):
        to, source = z + sign * t, z - sign * t

        @pl.when((to >= 0) & (to < LINE))
        def _():
            for c in pair(t, to, z):
                c.start()

    for t in range(1, LINE):
        to, source = z + sign * t, z - sign * t

        @pl.when((source >= 0) & (source < LINE))
        def _():
            for c in pair(t, source, source):
                c.wait_recv()

        @pl.when((to >= 0) & (to < LINE))
        def _():
            for c in pair(t, to, z):
                c.wait_send()

    own.wait()
    down.wait()


def line_states(x, total, backward, cid):
    sent = jnp.broadcast_to(total, (8, 128))
    got, logs = comm_call(
        functools.partial(line_states_kernel, backward),
        [
            jax.ShapeDtypeStruct((LINE,) + x.shape, x.dtype),
            jax.ShapeDtypeStruct((LINE, 8, 128), F32),
        ],
        [x, sent],
        [DMA((2,)), DMA((3,)), DMA((3,)), DMA((3,)), DMA((3,))],
        cid,
    )
    z = (lax.axis_index("seq") % SPANS) // PLANE
    state = jnp.zeros(x.shape, F32)
    for j in reversed(range(LINE)) if backward else range(LINE):
        used = j > z if backward else j < z
        state = jnp.where(used, jnp.exp(logs[j, 0, 0]) * state + got[j].astype(F32), state)
    return state


def line_scatter_kernel(a_ref, out, up, dn, fin, usend, urecv, dsend, drecv, psend, precv, lsem):
    me = Place()
    z, p = me.z, me.p
    greet(
        [(me.plane(m), None) for m in (1, 2, 3)] + [(me.up(), z < LINE - 1), (me.down(), z > 0)]
    )
    parts = usend.shape[1]
    rows, cols = a_ref.shape[2:]
    wide = cols // parts

    def add(dst, src, at):
        for q in range(PLANE):
            dst[q, :, at] = (dst[q, :, at].astype(F32) + src[q, :, at].astype(F32)).astype(BF16)

    def up_copy(src, zz, c):
        at = pl.ds(c * wide, wide)
        return remote(src.at[zz, :, :, at], up.at[zz, :, :, at], usend.at[zz, c], urecv.at[zz, c], me.up())

    def dn_copy(src, zz, c):
        at = pl.ds(c * wide, wide)
        return remote(src.at[zz, :, :, at], dn.at[zz, :, :, at], dsend.at[zz, c], drecv.at[zz, c], me.down())

    for t in range(LINE - 1):
        zu, zd = LINE - 1 - t, t
        for c in range(parts):
            at = pl.ds(c * wide, wide)

            @pl.when(z == 0)
            def _():
                up_copy(a_ref, zu, c).start()

            @pl.when((z > 0) & (z < zu))
            def _():
                up_copy(up, zu, c).wait_recv()
                add(up.at[zu], a_ref.at[zu], at)
                up_copy(up, zu, c).start()

            @pl.when(z == LINE - 1)
            def _():
                dn_copy(a_ref, zd, c).start()

            @pl.when((z < LINE - 1) & (z > zd))
            def _():
                dn_copy(dn, zd, c).wait_recv()
                add(dn.at[zd], a_ref.at[zd], at)
                dn_copy(dn, zd, c).start()

    plane = []
    for c in range(parts):
        at = pl.ds(c * wide, wide)
        for q in range(PLANE):
            fin[q, :, at] = a_ref[z, q, :, at]

        @pl.when(z > 0)
        def _():
            up_copy(up, z, c).wait_recv()
            add(fin, up.at[z], at)

        @pl.when(z < LINE - 1)
        def _():
            dn_copy(dn, z, c).wait_recv()
            add(fin, dn.at[z], at)

        for m in (1, 2, 3):
            s = remote(fin.at[me.xor(m), :, at], out.at[p, :, at], psend.at[c, m], precv.at[c, m], me.plane(m))
            s.start()
            plane.append(s)
    own = pltpu.make_async_copy(fin.at[p], out.at[p], lsem)
    own.start()
    for s in plane:
        s.wait()
    own.wait()
    for zz in range(LINE):
        for c in range(parts):

            @pl.when((z < LINE - 1) & (zz > z))
            def _():
                up_copy(up, zz, c).wait_send()

            @pl.when((z > 0) & (zz < z))
            def _():
                dn_copy(dn, zz, c).wait_send()


def line_scatter(a, parts, cid):
    _, _, rows, cols = a.shape
    return comm_call(
        line_scatter_kernel,
        [jax.ShapeDtypeStruct((PLANE, rows, cols), BF16)],
        [a],
        [
            pltpu.VMEM((LINE, PLANE, rows, cols), BF16),
            pltpu.VMEM((LINE, PLANE, rows, cols), BF16),
            pltpu.VMEM((PLANE, rows, cols), BF16),
            DMA((LINE, parts)),
            DMA((LINE, parts)),
            DMA((LINE, parts)),
            DMA((LINE, parts)),
            DMA((parts, PLANE)),
            DMA((parts, PLANE)),
            DMA,
        ],
        cid,
        in_specs=[VM],
        out_specs=[VM],
    )[0]


def layer_norm(values_in, gain_vec, bias_vec):
    average = jnp.mean(values_in, axis=-1, keepdims=True)
    centered = values_in - average
    variance = jnp.mean(centered * centered, axis=-1, keepdims=True)
    return centered * lax.rsqrt(variance + 1e-05) * gain_vec + bias_vec


def group_norm(values_in):
    average = jnp.mean(values_in, axis=-1, keepdims=True)
    centered = values_in - average
    variance = jnp.mean(centered * centered, axis=-1, keepdims=True)
    return centered * lax.rsqrt(variance + 1e-05)


def exact_gelu(values_in):
    return jax.nn.gelu(values_in, approximate=False)


def swish_gate(gate_proj, grouped):
    return jax.nn.silu(gate_proj) * grouped


def angles_of(positions, half_width):
    frequency = 10000.0 ** (-jnp.linspace(0.0, 1.0, half_width, dtype=F32))
    angles = positions.astype(F32)[:, None] * frequency[None, :]
    return jnp.cos(angles), jnp.sin(angles)


def rotate(values_in, cosine, sine_part):
    half_width = values_in.shape[-1] // 2
    first_half = values_in[..., :half_width]
    second_half = values_in[..., half_width:]
    return jnp.concatenate(
        [
            first_half * cosine - second_half * sine_part,
            second_half * cosine + first_half * sine_part,
        ],
        axis=-1,
    )


def dot(spec, a, b):
    return jnp.einsum(spec, a, b, preferred_element_type=F32)


def shards(
    tokens,
    ln1_gain,
    ln1_bias,
    w_query,
    w_key,
    w_value,
    w_gate,
    w_out,
    decay_log,
    ln2_gain,
    ln2_bias,
    w_up,
    w_down,
    cotangent,
):
    row_count, width = tokens.shape
    span_rows = cotangent.shape[0]
    heads = decay_log.shape[1]
    repeats = lax.axis_size("seq") // SPANS
    peers = [[lo + SPANS * k for k in range(repeats)] for lo in range(SPANS)]
    narrow = width // (SPANS * repeats)

    def wide_in(w, axis):
        if repeats == 1:
            return w
        return lax.all_gather(w, "seq", axis_index_groups=peers, axis=axis, tiled=True)

    def narrow_out(g, axis):
        if repeats == 1:
            return g
        return lax.psum_scatter(
            g, "seq", scatter_dimension=axis, axis_index_groups=peers, tiled=True
        )

    def features_in(a):
        if repeats == 1:
            return a
        return a.reshape(a.shape[:-1] + (repeats, SPANS, narrow)).swapaxes(-3, -2).reshape(a.shape)

    def features_out(a):
        if repeats == 1:
            return a
        return a.reshape(a.shape[:-1] + (SPANS, repeats, narrow)).swapaxes(-3, -2).reshape(a.shape)

    spot = lax.axis_index("seq") % SPANS
    z, p = spot // PLANE, spot % PLANE
    group_rows = span_rows * PLANE
    blocks = group_rows // STRETCH

    inputs32 = tokens.astype(F32)
    xn_first, norm1_back = jax.vjp(layer_norm, inputs32, ln1_gain, ln1_bias)
    decays = jnp.pad(decay_log.T, ((0, 8 - heads), (0, 0)))
    xg, decay_rows, key_w, value_w, query_w, gate_w, out_w = gather_in(
        features_in(xn_first.astype(BF16)),
        decays,
        [
            wide_in(w_key, 0),
            wide_in(w_value, 0),
            wide_in(w_query, 0),
            wide_in(w_gate, 0),
            wide_in(w_out, 1),
        ],
        (False, False, False, False, True),
        0,
    )
    normed = xg.reshape(group_rows, width)
    key_width, value_width = key_w.shape[1], value_w.shape[1]
    log_decay = lax.dynamic_index_in_dim(decay_rows, p, 1, False).reshape(blocks, STRETCH)
    cumulative = jnp.cumsum(log_decay, axis=1)
    last = cumulative[:, -1]
    total = jnp.sum(last)

    positions = (z * group_rows + jnp.arange(group_rows)) % SEQUENCE_LENGTH
    cosine, sine_part = angles_of(positions, key_width // 2)
    q_rot = rotate(dot("td,dq->tq", normed, query_w), cosine, sine_part).astype(BF16)
    k_rot = rotate(dot("td,dq->tq", normed, key_w), cosine, sine_part).astype(BF16)
    value = dot("td,dv->tv", normed, value_w).astype(BF16)
    gate_proj = dot("td,dv->tv", normed, gate_w)

    q_blocks = q_rot.reshape(blocks, STRETCH, key_width)
    k_blocks = k_rot.reshape(blocks, STRETCH, key_width)
    v_blocks = value.reshape(blocks, STRETCH, value_width)
    tail_scale = jnp.exp(last[:, None] - cumulative)
    tail_values = (v_blocks.astype(F32) * tail_scale[:, :, None]).astype(BF16)
    key_values = dot("csk,csd->ckd", k_blocks, tail_values)
    local = [jnp.zeros((key_width, value_width), F32)]
    for c in range(blocks):
        local.append(jnp.exp(last[c]) * local[-1] + key_values[c])
    incoming = line_states(local[-1].astype(BF16), total, False, 1)
    before = jnp.exp(jnp.cumsum(last) - last)
    prev_states = jnp.stack([local[c] + before[c] * incoming for c in range(blocks)]).astype(BF16)

    gaps = cumulative[:, :, None] - cumulative[:, None, :]
    indices = jnp.arange(STRETCH)
    lower = indices[:, None] >= indices[None, :]
    mask = jnp.where(lower[None], jnp.exp(jnp.minimum(gaps, 0.0)), 0.0)
    weighted = (dot("ctk,csk->cts", q_blocks, k_blocks) * mask).astype(BF16)
    q_decayed = (q_blocks.astype(F32) * jnp.exp(cumulative)[:, :, None]).astype(BF16)
    retained = dot("cts,csd->ctd", weighted, v_blocks) + dot("ctk,ckd->ctd", q_decayed, prev_states)
    retained = retained.reshape(group_rows, value_width)
    grouped, group_back = jax.vjp(group_norm, retained)
    gated, gate_back = jax.vjp(swish_gate, gate_proj, grouped)
    gated_low = gated.astype(BF16)
    attn_share = dot("tv,vd->td", gated_low, out_w).astype(BF16)
    attn_rows = plane_reduce(attn_share.reshape(PLANE, 2, row_count, width), 2)

    residual = inputs32 + features_out(attn_rows)
    xn_second, norm2_back = jax.vjp(layer_norm, residual, ln2_gain, ln2_bias)
    ffn_span = pair_gather(xn_second.astype(BF16), 3).reshape(span_rows, width)
    upper = dot("td,df->tf", ffn_span, w_up)
    active, gelu_back = jax.vjp(exact_gelu, upper)
    active_low = active.astype(BF16)
    grad_down = dot("tf,td->fd", active_low, cotangent).astype(BF16)
    sum_down = lax.psum_scatter(grad_down, "seq", scatter_dimension=1, tiled=True).astype(F32)
    grad_active = dot("td,fd->tf", cotangent, w_down)
    grad_upper = gelu_back(grad_active)[0].astype(BF16)
    grad_up = dot("td,tf->df", ffn_span, grad_upper).astype(BF16)
    sum_up = lax.psum_scatter(grad_up, "seq", scatter_dimension=0, tiled=True).astype(F32)
    ffn_share = dot("tf,fd->td", active_low, w_down).astype(BF16)
    ffn_rows_out = pair_reduce(ffn_share.reshape(2, row_count, width), 4)
    block_out = (residual + ffn_rows_out).astype(BF16)
    own_start = lax.axis_index("ffn") * row_count
    cot_own = lax.dynamic_slice_in_dim(cotangent, own_start, row_count, 0).astype(F32)
    grad_xn2_share = dot("tf,df->td", grad_upper, w_up).astype(BF16)
    grad_xn2 = pair_reduce(grad_xn2_share.reshape(2, row_count, width), 5)
    grad_resid, grad_gain2, grad_bias2 = norm2_back(grad_xn2)
    grad_resid = grad_resid + cot_own

    grad_attn = plane_gather(features_in(grad_resid.astype(BF16)), 6).reshape(group_rows, width)
    grad_gated = dot("td,vd->tv", grad_attn, out_w)
    grad_out_w = dot("td,tv->dv", grad_attn, gated_low).astype(BF16)
    grad_gate, grad_grouped = gate_back(grad_gated)
    grad_gate_low = grad_gate.astype(BF16)
    grad_retained = group_back(grad_grouped)[0].astype(BF16)
    grad_blocks = grad_retained.reshape(blocks, STRETCH, value_width)

    query_out = dot("ctk,ctd->ckd", q_decayed, grad_blocks)
    local_grad = jnp.sum(before[:, None, None] * query_out, axis=0)
    outgoing = line_states(local_grad.astype(BF16), total, True, 7)
    after = [outgoing]
    for c in reversed(range(1, blocks)):
        after.append(jnp.exp(last[c]) * after[-1] + query_out[c])
    grad_kv = jnp.stack(after[::-1]).astype(BF16)

    grad_weighted = dot("ctd,csd->cts", grad_blocks, v_blocks)
    grad_scores = (grad_weighted * mask).astype(BF16)
    grad_q = dot("ctd,ckd->ctk", grad_blocks, prev_states) * jnp.exp(cumulative)[:, :, None]
    grad_q = grad_q + dot("cts,csk->ctk", grad_scores, k_blocks)
    grad_k = dot("csd,ckd->csk", tail_values, grad_kv) + dot("cts,ctk->csk", grad_scores, q_blocks)
    grad_v = dot("csk,ckd->csd", k_blocks, grad_kv) * tail_scale[:, :, None]
    grad_v = grad_v + dot("cts,ctd->csd", weighted, grad_blocks)
    grad_query = rotate(grad_q.reshape(group_rows, key_width), cosine, -sine_part).astype(BF16)
    grad_keys = rotate(grad_k.reshape(group_rows, key_width), cosine, -sine_part).astype(BF16)
    grad_values = grad_v.reshape(group_rows, value_width).astype(BF16)

    grad_heads = jnp.concatenate([grad_query, grad_keys, grad_values, grad_gate_low], axis=1)
    heads_w = jnp.concatenate([query_w, key_w, value_w, gate_w], axis=1)
    grad_xn1_share = dot("tq,dq->td", grad_heads, heads_w).astype(BF16)
    grad_heads_w = dot("td,tq->dq", normed, grad_heads).astype(BF16)
    grad_xn1 = plane_reduce(grad_xn1_share.reshape(PLANE, 2, row_count, width), 8)
    sums = line_scatter(
        jnp.concatenate([grad_heads_w, grad_out_w], axis=1).reshape(
            LINE, PLANE, width // SPANS, 2 * key_width + 3 * value_width
        ),
        4,
        9,
    )
    grad_inputs, grad_gain1, grad_bias1 = norm1_back(features_out(grad_xn1))
    grad_tokens = (grad_resid + grad_inputs).astype(BF16)
    gain_one, bias_one, gain_two, bias_two = lax.psum(
        (grad_gain1, grad_bias1, grad_gain2, grad_bias2), ("seq", "ffn")
    )

    def columns(start, size):
        taken = sums[:, :, start : start + size].astype(F32).swapaxes(0, 1)
        return narrow_out(taken.reshape(taken.shape[0], PLANE * size), 0)

    sum_query = columns(0, key_width)
    sum_key = columns(key_width, key_width)
    sum_value = columns(2 * key_width, value_width)
    sum_gate = columns(2 * key_width + value_width, value_width)
    sum_out = columns(2 * key_width + 2 * value_width, value_width).T
    return (
        block_out,
        grad_tokens,
        gain_one,
        bias_one,
        sum_query,
        sum_key,
        sum_value,
        sum_gate,
        sum_out,
        gain_two,
        bias_two,
        sum_up,
        sum_down,
    )


def solution(mesh):
    return jax.shard_map(
        shards,
        mesh=mesh,
        in_specs=(
            P(("seq", "ffn"), None),
            P(),
            P(),
            P("seq", "ffn"),
            P("seq", "ffn"),
            P("seq", "ffn"),
            P("seq", "ffn"),
            P("ffn", "seq"),
            P("seq", "ffn"),
            P(),
            P(),
            P(None, "ffn"),
            P("ffn", None),
            P("seq", None),
        ),
        out_specs=(
            P(("seq", "ffn"), None),
            P(("seq", "ffn"), None),
            P(),
            P(),
            P("seq", "ffn"),
            P("seq", "ffn"),
            P("seq", "ffn"),
            P("seq", "ffn"),
            P("ffn", "seq"),
            P(),
            P(),
            P("seq", "ffn"),
            P("ffn", "seq"),
        ),
        check_vma=False,
    )
```

time: 3340 us -> 1040 us (0.31)
  waiting for transfers between devices: 2830 us -> 0.04 us
  Pallas kernels: 0 us -> 657 us
  blocking collectives: 102 us -> 39 us
  matrix products: 223 us -> 167 us
    reduce_scatter x10 -> x0, waiting for transfers between devices: 1800 us -> none  [the longest x1 355 us: shards(): lax.psum_scatter(grad_out_w, 'seq', scatter_dimension=1, tiled=True)]
    all_gather x10 -> x0, waiting for transfers between devices: 801 us -> none  [the longest x2 327 us: carried_in(): lax.all_gather(a.astype(kind), axis)]
    pallas_call x0 -> x10, Pallas kernels: none -> 657 us  [comm_call(): pl.pallas_call(kernel, out_shape=outs, in_specs=in_specs if in_specs is n...]
    reduce_scatter x1, waiting for transfers between devices: 228 us -> 0.01 us  [shards(): lax.psum_scatter(grad_up, 'seq', scatter_dimension=0, tiled=True)]
    dot_general x33 -> x27, matrix products: 223 us -> 167 us  [dot(): return jnp.einsum(spec, a, b, preferred_element_type=F32)]
  transfers between devices with their start and end apart: 21 -> 2, of which waited for: 19 -> 0; matrix products, arithmetic and copies ran while one was open for 6% -> 18% of each run, Pallas kernels for 0% -> 39%
where the time goes in v1:
time: 1040 us; the launch traced here: 1030 us
  Pallas kernels  657 us (63%)
  matrix products  167 us (16%)
  other arithmetic  77 us (7%)
  local copies, waits for them, and re-layouts  61.9 us (6%)
  blocking collectives  39 us (4%)
  between operations  23.9 us (2%)
    pallas_call x10, Pallas kernels, comm_call(): pl.pallas_call(kernel, out_shape=outs, in_specs=in_specs if in_specs is n...  657 us
    dot_general x27, matrix products, dot(): return jnp.einsum(spec, a, b, preferred_element_type=F32)  167 us
    psum x1, blocking collectives, shards(): lax.psum((grad_gain1, grad_bias1, grad_gain2, grad_bias2), ('seq', 'ffn'))  39 us
    unnamed x163, local copies, waits for them, and re-layouts  34.3 us
  transfers between devices with their start and end apart: 2, of which 0 were waited for; matrix products, arithmetic and copies ran while one was open for 18% of the time, Pallas kernels for 39%

profile of v1, /device:TPU:16, one launch (start us, length us, event | category | flops | bytes accessed | tf_op | source)
XLA Modules:
  0.0 1025.7 jit_solution(10535397735617185016)
XLA Ops:
  14.6 153.1 %shard_map.237 = (bf16[8,256,2048]{2,1,0:T(8,128)(2,1)}, f32[4,8,512]{2,1,0:T(8,128)}, bf16[2048,256]{1,0:T(8,128)(2,1)}, bf16[2048,512]{1,0:T(8,128)(2,1)}, bf1...) custom-call(bf16[256,2048]{1,0:T(8,128)(2,1)} %fusion.24.refs_0_, ...), custom_call_target="tpu_custom_call" | custom-call | tf_op jit(solution)/shard_map/pallas_call | solution.py:81
  175.4 8.6 convolution_convert_fusion.8
  199.3 23.1 %shard_map.238 = (bf16[4,256,512]{2,1,0:T(8,128)(2,1)}, f32[4,8,128]{2,1,0:T(8,128)}) custom-call(bf16[256,512]{1,0:T(8,128)(2,1)} %get-tuple-element.85.x_ref, f32[8,128]{1,0:T(8,128)} %broadcast_in_dim.27.d_ref), custom_call_target="tpu_custom_call" | custom-call | tf_op jit(solution)/shard_map/pallas_call | solution.py:81
  239.3 6.9 multiply_convert_fusion.2
  253.0 42.0 %shard_map.239 = f32[256,2048]{1,0:T(8,128)} custom-call(bf16[4,2,256,2048]{3,2,1,0:T(8,128)(2,1)} %bitcast.133), custom_call_target="tpu_custom_call" | custom-call | tf_op jit(solution)/shard_map/pallas_call | solution.py:81
  298.8 33.7 %shard_map.240 = bf16[2,256,2048]{2,1,0:T(8,128)(2,1)} custom-call(bf16[256,2048]{1,0:T(8,128)(2,1)} %add_convert_fusion.5.x_ref), custom_call_target="tpu_custom_call" | custom-call | tf_op jit(solution)/shard_map/pallas_call | solution.py:81
  332.5 7.7 fusion.107
  340.2 16.8 %add_convert_fusion.2 = (bf16[512,2048]{1,0:T(8,128)(2,1)}, f32[512,2048]{1,0:T(8,128)S(1)}) fusion(f32[512,2048]{1,0:T(8,128)S(1)} %fusion.107, bf16[512,2048]{1,0:T(8,128)(2,1)S(1)} %copy-done.28, bf16[2048,2048]{1,0:T(8,128)(2,1)} %param.26), kind=kOutput, calls=%fused_computation.25 | convolution fusion | flops 4370464768 | bytes 20971520 | tf_op jit(solution)/shard_map/td,fd->tf/dot_general | solution.py:668
  359.4 6.9 convolution_convert_fusion
  366.3 12.3 %copy.67 = bf16[2048,2048]{0,1:T(8,128)(2,1)} copy(bf16[2048,2048]{1,0:T(8,128)(2,1)} %convolution_convert_fusion) | data formatting | bytes 16777216
  378.9 10.1 convolution_convert_fusion.1
  389.0 10.0 convolution_convert_fusion.7
  399.0 9.4 convolution_convert_fusion.6
  428.6 96.3 %shard_map.243 = bf16[8,256,2048]{2,1,0:T(8,128)(2,1)} custom-call(bf16[256,2048]{1,0:T(8,128)(2,1)} %fusion.48.x_ref), custom_call_target="tpu_custom_call" | custom-call | tf_op jit(solution)/shard_map/pallas_call | solution.py:81
  524.9 14.2 %multiply_reduce_fusion = (f32[2048]{0:T(1024)S(1)}, f32[2048,512]{1,0:T(8,128)S(1)}) fusion(f32[4,512,512]{2,1,0:T(8,128)} %copy-done.2, f32[2048]{0:T(1024)S(1)} %bitcast.176, f32[2048,512]{1,0:T(8,128)} %get-tuple-element.130, bf16[2048,2048]{1,0:T(8,128)(2,1)} %bitcast.134, bf16[512,2048]{1,0:T(8,128)(2,1)S(1)} %copy-done.67), kind=kOutput, calls=%fused_computation.24 | convolution fusion | flops 4303353856 | bytes 23085056 | tf_op jit(solution)/shard_map/td,vd->tv/dot_general | solution.py:668
  552.1 33.9 %shard_map.244 = (bf16[4,256,512]{2,1,0:T(8,128)(2,1)}, f32[4,8,128]{2,1,0:T(8,128)}) custom-call(bf16[256,512]{1,0:T(8,128)(2,1)} %get-tuple-element.133.x_ref, f32[8,128]{1,0:T(8,128)} %broadcast_in_dim.27.d_ref), custom_call_target="tpu_custom_call" | custom-call | tf_op jit(solution)/shard_map/pallas_call | solution.py:81
  621.6 19.4 %convolution_convert_fusion.2 = bf16[2048,2048]{1,0:T(8,128)(2,1)} fusion(bf16[2048,1536]{1,0:T(8,128)(2,1)S(1)} %constant_dynamic-update-slice_fusion, bf16[2048,512]{1,0:T(8,128)(2,1)} %get-tuple-element.25, bf16[2048,512]{1,0:T(8,128)(2,1)} %get-tuple-element.29, bf16[2048,256]{1,0:T(8,128)(2,1)S(1)} %copy-done.69, bf16[2048,256]{1,0:T(8,128)(2,1)S(1)} %copy-done.71), kind=kOutput, calls=%fused_computation.3 | convolution fusion | flops 12914262016 | bytes 20971520 | tf_op jit(solution)/shard_map/tq,dq->td/dot_general | solution.py:668
  641.1 107.1 %shard_map.245 = f32[256,2048]{1,0:T(8,128)} custom-call(bf16[4,2,256,2048]{3,2,1,0:T(8,128)(2,1)} %bitcast.132), custom_call_target="tpu_custom_call" | custom-call | tf_op jit(solution)/shard_map/pallas_call | solution.py:81
  748.2 8.8 convolution_convert_fusion.5
  757.0 18.0 %convolution_convert_fusion.4 = bf16[2048,1536]{0,1:T(8,128)(2,1)} fusion(bf16[2048,2048]{1,0:T(8,128)(2,1)} %bitcast.187, bf16[2048,1536]{1,0:T(8,128)(2,1)S(1)} %copy-done.48), kind=kOutput, calls=%fused_computation.5 | convolution fusion | flops 12888047616 | bytes 20971520 | tf_op jit(solution)/shard_map/td,tq->dq/dot_general | solution.py:668
  775.1 7.7 pad_maximum_fusion
  782.8 12.3 %copy.53 = bf16[2048,2048]{1,0:T(8,128)(2,1)} copy(bf16[2048,2048]{0,1:T(8,128)(2,1)} %pad_maximum_fusion) | data formatting | bytes 16777216 | tf_op jit(solution)/shard_map/concatenate | solution.py:833
  795.1 155.7 %shard_map.246 = bf16[4,128,2048]{2,1,0:T(8,128)(2,1)} custom-call(bf16[4,4,128,2048]{3,2,1,0:T(8,128)(2,1)} %bitcast.128), custom_call_target="tpu_custom_call" | custom-call | tf_op jit(solution)/shard_map/pallas_call | solution.py:81
  971.1 39.0 %all-reduce.1 = (f32[2048]{0:T(1024)}, f32[2048]{0:T(1024)}, f32[2048]{0:T(1024)}, f32[2048]{0:T(1024)}) all-reduce(f32[2048]{0:T(1024)S(1)} %get-tuple-element.63, f32[2048]{0:T(1024)S(1)} %get-tuple-element.66, f32[2048]{0:T(1024)S(1)} %get-tuple-element.61, ...), channel_id=1, replica_groups=mesh['seq'=16,'ffn'=2] {'seq','ffn'}, use_global_device_ids=true, to_apply=%region_18.19 | all-reduce | flops 8192 | bytes 65536 | tf_op jit(solution)/shard_map/psum | solution.py:841
  (254 shorter events, 148.6 us)
Async XLA Ops:
  7.2 1006.7 %reduce-scatter.7.cloned.1.call-start = ((), (), s32[]{:S(2)}) async-start(), calls=%async_computation.3 | async-start | bytes 8912896
  7.4 219.0 %copy-start.41 = (pred[512,512]{1,0:T(8,128)(4,1)}, pred[512,512]{1,0:T(8,128)(4,1)S(1)}, u32[]{:S(2)}) copy-start(pred[512,512]{1,0:T(8,128)(4,1)S(1)} %iota_compare_fusion) | copy-start | bytes 786436
  8.9 161.2 %copy-start.49 = (f32[256]{0:T(256)}, f32[256]{0:T(256)S(1)}, u32[]{:S(2)}) copy-start(f32[256]{0:T(256)S(1)} %broadcast_multiply_fusion.2) | copy-start | bytes 3076
  10.6 158.0 %copy-start.59 = (f32[256]{0:T(256)}, f32[256]{0:T(256)S(1)}, u32[]{:S(2)}) copy-start(f32[256]{0:T(256)S(1)} %fusion.26) | copy-start | bytes 3076
  10.6 159.6 %copy-start.55 = (f32[256]{0:T(256)}, f32[256]{0:T(256)S(1)}, u32[]{:S(2)}) copy-start(f32[256]{0:T(256)S(1)} %fusion.81) | copy-start | bytes 3076
  170.3 56.1 %copy-start.53 = (f32[1,4,4,128]{3,1,2,0:T(4,128)}, f32[1,4,4,128]{3,1,2,0:T(4,128)S(1)}, u32[]{:S(2)}) copy-start(f32[1,4,4,128]{3,1,2,0:T(4,128)S(1)} %copy.79) | copy-start | bytes 24580
  171.6 17.7 %copy-start.39 = (f32[2048]{0:T(1024)}, f32[2048]{0:T(1024)S(1)}, u32[]{:S(2)}) copy-start(f32[2048]{0:T(1024)S(1)} %fusion.77) | copy-start | bytes 24580
  175.3 18.9 %copy-start.51 = (f32[4,512]{1,0:T(4,128)}, f32[4,512]{1,0:T(4,128)S(1)}, u32[]{:S(2)}) copy-start(f32[4,512]{1,0:T(4,128)S(1)} %get-tuple-element.121) | copy-start | bytes 24580
  175.3 59.4 %copy-start.45 = (f32[4,512]{1,0:T(4,128)}, f32[4,512]{1,0:T(4,128)S(1)}, u32[]{:S(2)}) copy-start(f32[4,512]{1,0:T(4,128)S(1)} %get-tuple-element.122) | copy-start | bytes 24580
  184.0 45.1 %copy-start.17 = (bf16[2048,512]{1,0:T(8,128)(2,1)}, bf16[2048,512]{1,0:T(8,128)(2,1)S(1)}, u32[]{:S(2)}) copy-start(bf16[2048,512]{1,0:T(8,128)(2,1)S(1)} %convolution_convert_fusion.8) | copy-start | bytes 6291460
  194.2 32.2 %copy-start.24 = (bf16[2048,128]{1,0:T(8,128)(2,1)}, bf16[2048,128]{1,0:T(8,128)(2,1)S(1)}, u32[]{:S(2)}) copy-start(bf16[2048,128]{1,0:T(8,128)(2,1)S(1)} %get-tuple-element.111) | copy-start | bytes 1572868
  194.2 40.5 %copy-start.13 = (bf16[2048,128]{1,0:T(8,128)(2,1)}, bf16[2048,128]{1,0:T(8,128)(2,1)S(1)}, u32[]{:S(2)}) copy-start(bf16[2048,128]{1,0:T(8,128)(2,1)S(1)} %get-tuple-element.90) | copy-start | bytes 1572868
  194.2 40.5 %copy-start.15 = (bf16[2048,128]{1,0:T(8,128)(2,1)}, bf16[2048,128]{1,0:T(8,128)(2,1)S(1)}, u32[]{:S(2)}) copy-start(bf16[2048,128]{1,0:T(8,128)(2,1)S(1)} %get-tuple-element.91) | copy-start | bytes 1572868
  235.8 10.4 %copy-start.2 = (f32[4,512,512]{2,1,0:T(8,128)}, f32[4,512,512]{2,1,0:T(8,128)S(1)}, u32[]{:S(2)}) copy-start(f32[4,512,512]{2,1,0:T(8,128)S(1)} %get-tuple-element.128) | copy-start | bytes 12582916
  253.0 42.0 %copy-start = (bf16[256,2048]{1,0:T(8,128)(2,1)S(1)}, bf16[256,2048]{1,0:T(8,128)(2,1)}, u32[]{:S(2)}) copy-start(bf16[256,2048]{1,0:T(8,128)(2,1)} %param.14) | copy-start | bytes 3145732
  378.7 637.6 %reduce-scatter.5.cloned.1.call-start = ((), (), s32[]{:S(2)}) async-start(), calls=%async_computation.2 | async-start | bytes 8912896 | tf_op jit(solution)/shard_map/reduce_scatter | solution.py:789
  428.6 96.3 %copy-start.67 = (bf16[512,2048]{1,0:T(8,128)(2,1)S(1)}, bf16[512,2048]{1,0:T(8,128)(2,1)}, u32[]{:S(2)}) copy-start(bf16[512,2048]{1,0:T(8,128)(2,1)} %get-tuple-element.32) | copy-start | bytes 6291460
  524.9 14.2 %copy-start.3 = (f32[4,512,512]{2,1,0:T(8,128)S(1)}, f32[4,512,512]{2,1,0:T(8,128)}, u32[]{:S(2)}) copy-start(f32[4,512,512]{2,1,0:T(8,128)} %copy-done.2) | copy-start | bytes 12582916
  524.9 14.2 %copy-start.22 = (f32[2048,512]{1,0:T(8,128)S(1)}, f32[2048,512]{1,0:T(8,128)}, u32[]{:S(2)}) copy-start(f32[2048,512]{1,0:T(8,128)} %get-tuple-element.130) | copy-start | bytes 12582916
  552.1 41.2 %copy-start.25 = (bf16[2048,128]{1,0:T(8,128)(2,1)S(1)}, bf16[2048,128]{1,0:T(8,128)(2,1)}, u32[]{:S(2)}) copy-start(bf16[2048,128]{1,0:T(8,128)(2,1)} %copy-done.24) | copy-start | bytes 1572868
  604.6 13.9 %copy-start.7 = (bf16[4,512,512]{2,1,0:T(8,128)(2,1)S(1)}, bf16[4,512,512]{2,1,0:T(8,128)(2,1)}, u32[]{:S(2)}) copy-start(bf16[4,512,512]{2,1,0:T(8,128)(2,1)} %copy-done.6) | copy-start | bytes 6291460
  621.6 19.5 %copy-start.47 = (bf16[2048,1536]{1,0:T(8,128)(2,1)}, bf16[2048,1536]{1,0:T(8,128)(2,1)S(1)}, u32[]{:S(2)}) copy-start(bf16[2048,1536]{1,0:T(8,128)(2,1)S(1)} %constant_dynamic-update-slice_fusion) | copy-start | bytes 18874372
  959.3 10.3 %copy-start.43 = (f32[2048]{0:T(1024)S(1)}, f32[2048]{0:T(1024)}, u32[]{:S(2)}) copy-start(f32[2048]{0:T(1024)} %param.15) | copy-start | bytes 24580
  959.3 10.3 %copy-start.50 = (f32[256]{0:T(256)S(1)}, f32[256]{0:T(256)}, u32[]{:S(2)}) copy-start(f32[256]{0:T(256)} %copy-done.49) | copy-start | bytes 3076
  (54 other events, 198.0 us)
Sparse Core Ops, SparseCore 0:
  378.8 215.5 reduce-scatter.6
  596.7 213.3 reduce-scatter.4

commit v2 on v1

--- a/solution.py
+++ b/solution.py
@@ -99,7 +99,8 @@
     shards_in = refs[2 : 2 + count]
     xg, decg = refs[2 + count : 4 + count]
     full = refs[4 + count : 4 + 2 * count]
-    lsem, psend, precv, usend, dsend, zrecv, xsend, xrecv, csend, crecv, tsend, trecv = refs[4 + 2 * count :]
+    hold = refs[4 + 2 * count : 4 + 3 * count]
+    lsem, psend, precv, usend, dsend, zrecv, xsend, xrecv, csend, crecv, tsend, trecv = refs[4 + 3 * count :]
     me = Place()
     z, p, f = me.z, me.p, me.f
     spot = z * PLANE + p
@@ -124,11 +125,12 @@
         at = pl.ds(pl.multiple_of(zz * deep, deep), deep)
         return full[i].at[:, at] if rows[i] else full[i].at[at, :]
 
-    local, plane = [], []
+    local, plane, held = [], [], []
     for i in range(count):
-        own = pltpu.make_async_copy(part(i, p), slot(i, spot), lsem.at[i])
-        own.start()
-        local.append(own)
+        load = pltpu.make_async_copy(part(i, p), hold[i], lsem.at[i])
+        load.start()
+        held.append(load)
+        local.append(pltpu.make_async_copy(hold[i], slot(i, spot), lsem.at[i]))
         sends = []
         for m in (1, 2, 3):
             c = remote(part(i, me.xor(m)), slot(i, spot), psend.at[i, m], precv.at[i, m], me.plane(m))
@@ -160,6 +162,9 @@
     def down_copy(i, zz):
         return remote(block(i, zz), block(i, zz), dsend.at[i, zz], zrecv.at[i, zz], me.down())
 
+    for i in range(count):
+        held[i].wait()
+        local[i].start()
     for i in range(count):
         local[i].wait()
         for c in plane[i]:
@@ -246,7 +251,11 @@
         jax.ShapeDtypeStruct((2 * PLANE,) + xn.shape, BF16),
         jax.ShapeDtypeStruct((PLANE,) + dec.shape, F32),
     ] + outs
-    scratch = [
+    parts = [
+        (w.shape[0] // PLANE, chunk) if r else (chunk, w.shape[1] // PLANE)
+        for w, r in zip(shards_in, rows)
+    ]
+    scratch = [pltpu.VMEM(shape, BF16) for shape in parts] + [
         DMA((count + 2,)),
         DMA((count, PLANE)),
         DMA((count, PLANE)),
@@ -261,65 +270,13 @@
         DMA((PLANE,)),
     ]
     return comm_call(
-        functools.partial(gather_kernel, widths, rows), outs, [xn, dec] + shards_in, scratch, cid
-    )
-
-
-def plane_gather_kernel(x_ref, out, lsem, xsend, xrecv, csend, crecv):
-    me = Place()
-    p, f = me.p, me.f
-    greet([(me.plane(1), None), (me.plane(2), None), (me.partner(), None)])
-    seat, seat1, seat2, seat3 = (me.xor(m) * 2 + f for m in (0, 1, 2, 3))
-    half = x_ref.shape[0] // 2
-    low, high = pl.ds(0, half), pl.ds(half, half)
-    own = pltpu.make_async_copy(x_ref, out.at[seat], lsem)
-    own.start()
-    x1 = [
-        remote(x_ref.at[h], out.at[seat, h], xsend.at[k], xrecv.at[k], me.plane(1))
-        for k, h in ((0, low), (1, high))
-    ]
-    x2 = [
-        remote(x_ref.at[h], out.at[seat, h], xsend.at[k], xrecv.at[k], me.plane(2))
-        for k, h in ((2, high), (3, low))
-    ]
-    for a, b in zip(x1, x2):
-        a.start()
-        b.start()
-    c0 = remote(x_ref, out.at[seat], csend.at[0], crecv.at[0], me.partner())
-    c0.start()
-    x1[0].wait_recv()
-    g1 = remote(out.at[seat1, low], out.at[seat1, low], xsend.at[4], xrecv.at[4], me.plane(2))
-    g1.start()
-    x2[0].wait_recv()
-    g2 = remote(out.at[seat2, high], out.at[seat2, high], xsend.at[5], xrecv.at[5], me.plane(1))
-    g2.start()
-    x1[1].wait_recv()
-    c1 = remote(out.at[seat1], out.at[seat1], csend.at[1], crecv.at[1], me.partner())
-    c1.start()
-    x2[1].wait_recv()
-    c2 = remote(out.at[seat2], out.at[seat2], csend.at[2], crecv.at[2], me.partner())
-    c2.start()
-    g1.wait_recv()
-    c3 = remote(out.at[seat3, low], out.at[seat3, low], csend.at[3], crecv.at[3], me.partner())
-    c3.start()
-    g2.wait_recv()
-    c4 = remote(out.at[seat3, high], out.at[seat3, high], csend.at[4], crecv.at[4], me.partner())
-    c4.start()
-    for c in (c0, c1, c2, c3, c4):
-        c.wait()
-    for c in x1 + x2 + [g1, g2]:
-        c.wait_send()
-    own.wait()
-
-
-def plane_gather(x, cid):
-    return comm_call(
-        plane_gather_kernel,
-        [jax.ShapeDtypeStruct((2 * PLANE,) + x.shape, x.dtype)],
-        [x],
-        [DMA, DMA((6,)), DMA((6,)), DMA((5,)), DMA((5,))],
+        functools.partial(gather_kernel, widths, rows),
+        outs,
+        [xn, dec] + shards_in,
+        scratch,
         cid,
-    )[0]
+        in_specs=[VM] + [ANY] * (count + 1),
+    )
 
 
 def plane_reduce_kernel(x_ref, out, rx0, rx1a, rx1b, rx2a, rx2b, csend, crecv, xsend, xrecv):
@@ -406,49 +363,283 @@
     )[0]
 
 
-def pair_gather_kernel(x_ref, out, lsem, csend, crecv):
+def nn(a, b):
+    return jnp.dot(a, b, preferred_element_type=F32)
+
+
+def nt(a, b):
+    return lax.dot_general(a, b, (((1,), (1,)), ((), ())), preferred_element_type=F32)
+
+
+def tn(a, b):
+    return lax.dot_general(a, b, (((0,), (0,)), ((), ())), preferred_element_type=F32)
+
+
+def rows_at(r, size):
+    return pl.ds(pl.multiple_of(r, size), size)
+
+
+def add_into(dst, cols, other, other_cols):
+    @pl.loop(0, dst.shape[0], step=64)
+    def _(r):
+        at = rows_at(r, 64)
+        dst[at, cols] = (dst[at, cols].astype(F32) + other[at, other_cols].astype(F32)).astype(BF16)
+
+
+def start(copy):
+    copy.start()
+    return copy
+
+
+def ffn_kernel(
+    x_ref, tok_ref, gain_ref, bias_ref, wu_ref, wd_ref, cot_ref,
+    block_out, resid_grad, gains, da, fu, fd,
+    wu, wd, rx0, rx1a, rx1b, rx2a, rx2b, resid, xn, act, dact, du, part, prx, dab, stage,
+    lsem, csend, crecv, xsend, xrecv, psend, precv, gsend, grecv, ssem,
+):
     me = Place()
-    greet([(me.partner(), None)])
-    own = pltpu.make_async_copy(x_ref, out.at[me.f], lsem)
-    own.start()
-    c = remote(x_ref, out.at[me.f], csend, crecv, me.partner())
-    c.start()
+    p, f = me.p, me.f
+    greet([(me.plane(1), None), (me.plane(2), None), (me.partner(), None)])
+    rows, width = tok_ref.shape
+    hidden = wu.shape[1]
+    q = [me.xor(m) for m in range(4)]
+    wide = width // 2
+    ca, cb = pl.ds(0, wide), pl.ds(wide, wide)
+    everything, whole = pl.ds(0, width), pl.ds(0, wide)
+    load_d = start(pltpu.make_async_copy(wd_ref, wd, lsem.at[0]))
+    load_u = start(pltpu.make_async_copy(wu_ref, wu, lsem.at[1]))
+    order = (3, 1, 2, 0)
+    first = [
+        start(remote(x_ref.at[q[m], 1 - f], rx0.at[q[m]], csend.at[m], crecv.at[m], me.partner()))
+        for m in order
+    ]
+    sends = {}
+    for c, m in zip(first, order):
+        c.wait_recv()
+        add_into(rx0.at[q[m]], everything, x_ref.at[q[m], f], everything)
+        k = 0 if m == 3 else 1
+        if m & 1:
+            sends["a", k] = start(
+                remote(rx0.at[q[m], :, ca], rx1a.at[k], xsend.at[k], xrecv.at[k], me.plane(1))
+            )
+        if m & 2:
+            sends["b", k] = start(
+                remote(rx0.at[q[m], :, cb], rx1b.at[k], xsend.at[2 + k], xrecv.at[2 + k], me.plane(2))
+            )
+
+    load_d.wait()
+
+    @pl.loop(0, hidden, step=256)
+    def _(c):
+        at = rows_at(c, 256)
+        dact[:, at] = nt(cot_ref[...], wd[at, :])
+
+    sends["a", 0].wait_recv()
+    add_into(rx1a.at[0], whole, rx0.at[q[2]], ca)
+    s2a = start(remote(rx1a.at[0], rx2a, xsend.at[4], xrecv.at[4], me.plane(2)))
+    sends["b", 0].wait_recv()
+    add_into(rx1b.at[0], whole, rx0.at[q[1]], cb)
+    s2b = start(remote(rx1b.at[0], rx2b, xsend.at[5], xrecv.at[5], me.plane(1)))
+    sends["a", 1].wait_recv()
+    sends["b", 1].wait_recv()
+    load_u.wait()
+    s2a.wait_recv()
+    s2b.wait_recv()
+
+    mine = f * rows
+    theirs = (1 - f) * rows
+    step = 32
+
+    @pl.loop(0, rows, step=step)
+    def _(r):
+        at = rows_at(r, step)
+        left = rx0[q[0], at, ca].astype(F32) + rx1a[1, at, :].astype(F32) + rx2a[at, :].astype(F32)
+        right = rx0[q[0], at, cb].astype(F32) + rx1b[1, at, :].astype(F32) + rx2b[at, :].astype(F32)
+        v = tok_ref[at, :].astype(F32) + jnp.concatenate([left, right], axis=1)
+        resid[at, :] = v
+        average = jnp.mean(v, axis=1, keepdims=True)
+        centered = v - average
+        scale = lax.rsqrt(jnp.mean(centered * centered, axis=1, keepdims=True) + 1e-05)
+        xn[pl.ds(pl.multiple_of(mine + r, step), step), :] = (
+            centered * scale * gain_ref[...] + bias_ref[...]
+        ).astype(BF16)
+
+    own_rows = rows_at(mine, rows)
+    their_rows = rows_at(theirs, rows)
+    swap_x = start(remote(xn.at[own_rows], xn.at[own_rows], psend.at[0], precv.at[0], me.partner()))
+
+    def hidden_part(at_rows):
+        @pl.loop(0, hidden, step=512)
+        def _(c):
+            at = rows_at(c, 512)
+            u = nn(xn[at_rows, :], wu[:, at])
+            e = 0.5 * (1.0 + lax.erf(u * 0.7071067811865476))
+            act[at_rows, at] = (u * e).astype(BF16)
+            slope = e + u * jnp.exp(-0.5 * u * u) * 0.3989422804014327
+            du[at_rows, at] = (dact[at_rows, at] * slope).astype(BF16)
+
+    hidden_part(own_rows)
+    swap_x.wait_recv()
+    hidden_part(their_rows)
+
+    @pl.loop(0, width, step=256)
+    def _(c):
+        at = rows_at(c, 256)
+        part[0, :, at] = nt(du[their_rows, :], wu[at, :]).astype(BF16)
+
+    swap_d = start(remote(part.at[0], prx.at[0], psend.at[1], precv.at[1], me.partner()))
+    @pl.loop(0, width, step=256)
+    def _(c):
+        at = rows_at(c, 256)
+        resid_grad[:, at] = nt(du[own_rows, :], wu[at, :])
+
+    swap_d.wait_recv()
+    gains[...] = jnp.zeros_like(gains)
+
+    @pl.loop(0, rows, step=step)
+    def _(r):
+        at = rows_at(r, step)
+        dx = resid_grad[at, :] + prx[0, at, :].astype(F32)
+        v = resid[at, :]
+        average = jnp.mean(v, axis=1, keepdims=True)
+        centered = v - average
+        scale = lax.rsqrt(jnp.mean(centered * centered, axis=1, keepdims=True) + 1e-05)
+        hat = centered * scale
+        gains[0:1, :] += jnp.sum(dx * hat, axis=0, keepdims=True)
+        gains[1:2, :] += jnp.sum(dx, axis=0, keepdims=True)
+        g = dx * gain_ref[...]
+        back = scale * (
+            g - jnp.mean(g, axis=1, keepdims=True) - hat * jnp.mean(g * hat, axis=1, keepdims=True)
+        )
+        back = back + cot_ref[pl.ds(pl.multiple_of(mine + r, step), step), :].astype(F32)
+        resid_grad[at, :] = back
+        dab[at, :] = back.astype(BF16)
+
+    half = rows // 2
+    low, high = pl.ds(0, half), pl.ds(half, half)
+    seat, seat1, seat2, seat3 = (me.xor(m) * 2 + f for m in (0, 1, 2, 3))
+    own = start(pltpu.make_async_copy(dab, da.at[seat], lsem.at[2]))
+    x1, x2 = [], []
+    for k, (h1, h2) in enumerate(((low, high), (high, low))):
+        x1.append(start(remote(dab.at[h1], da.at[seat, h1], gsend.at[k], grecv.at[k], me.plane(1))))
+        x2.append(
+            start(remote(dab.at[h2], da.at[seat, h2], gsend.at[2 + k], grecv.at[2 + k], me.plane(2)))
+        )
+    to_core = [start(remote(dab, da.at[seat], gsend.at[6], grecv.at[6], me.partner()))]
+
+    @pl.loop(0, width, step=256)
+    def _(c):
+        at = rows_at(c, 256)
+        part[1, :, at] = nn(act[their_rows, :], wd[:, at]).astype(BF16)
+
+    swap_o = start(remote(part.at[1], prx.at[1], psend.at[2], precv.at[2], me.partner()))
+    @pl.loop(0, width, step=256)
+    def _(c):
+        at = rows_at(c, 256)
+        resid[:, at] = resid[:, at] + nn(act[own_rows, :], wd[:, at])
+
+    swap_o.wait_recv()
+
+    @pl.loop(0, rows, step=step)
+    def _(r):
+        at = rows_at(r, step)
+        block_out[at, :] = (resid[at, :] + prx[1, at, :].astype(F32)).astype(BF16)
+
+    x1[0].wait_recv()
+    g1 = start(remote(da.at[seat1, low], da.at[seat1, low], gsend.at[4], grecv.at[4], me.plane(2)))
+    x2[0].wait_recv()
+    g2 = start(remote(da.at[seat2, high], da.at[seat2, high], gsend.at[5], grecv.at[5], me.plane(1)))
+
+    def weights_part(left, right, out, base):
+        def spill(slot, i):
+            return pltpu.make_async_copy(stage.at[slot], out.at[rows_at(i * 256, 256), :], ssem.at[slot])
+
+        @pl.loop(0, width // 256)
+        def _(i):
+            slot = i % 2
+
+            @pl.when(i >= 2)
+            def _():
+                spill(slot, i - 2).wait()
+
+            @pl.loop(0, hidden, step=512)
+            def _(c):
+                at = rows_at(c, 512)
+                stage[slot, :, at] = tn(left[:, rows_at(i * 256, 256)], right[:, at]).astype(BF16)
+
+            spill(slot, i).start()
+
+        for k in (2, 1):
+            i = width // 256 - k
+            spill(i % 2, i).wait()
+
+    weights_part(xn, du, fu, 0)
+    x1[1].wait_recv()
+    to_core.append(start(remote(da.at[seat1], da.at[seat1], gsend.at[7], grecv.at[7], me.partner())))
+    x2[1].wait_recv()
+    to_core.append(start(remote(da.at[seat2], da.at[seat2], gsend.at[8], grecv.at[8], me.partner())))
+    weights_part(cot_ref, act, fd, 0)
+    g1.wait_recv()
+    to_core.append(
+        start(remote(da.at[seat3, low], da.at[seat3, low], gsend.at[9], grecv.at[9], me.partner()))
+    )
+    g2.wait_recv()
+    to_core.append(
+        start(remote(da.at[seat3, high], da.at[seat3, high], gsend.at[10], grecv.at[10], me.partner()))
+    )
+    for c in to_core:
+        c.wait()
+    for c in x1 + x2 + [g1, g2, swap_x, swap_d, swap_o, s2a, s2b] + first + list(sends.values()):
+        c.wait_send()
     own.wait()
-    c.wait()
-
-
-def pair_gather(x, cid):
+
+
+def ffn_part(share, tokens, gain, bias, w_up, w_down, cotangent, cid):
+    _, _, rows, width = share.shape
+    span, hidden = 2 * rows, w_up.shape[1]
     return comm_call(
-        pair_gather_kernel, [jax.ShapeDtypeStruct((2,) + x.shape, x.dtype)], [x], [DMA, DMA, DMA], cid
-    )[0]
-
-
-def pair_reduce_kernel(x_ref, out, rx, csend, crecv):
-    me = Place()
-    greet([(me.partner(), None)])
-    c = remote(x_ref.at[1 - me.f], rx, csend, crecv, me.partner())
-    c.start()
-    c.wait_recv()
-
-    @pl.loop(0, out.shape[0], step=32)
-    def _(r):
-        at = pl.ds(pl.multiple_of(r, 32), 32)
-        out[at, :] = x_ref[me.f, at, :].astype(F32) + rx[at, :].astype(F32)
-
-    c.wait_send()
-
-
-def pair_reduce(x, cid):
-    _, rows, cols = x.shape
-    return comm_call(
-        pair_reduce_kernel,
-        [jax.ShapeDtypeStruct((rows, cols), F32)],
-        [x],
-        [pltpu.VMEM((rows, cols), BF16), DMA, DMA],
+        ffn_kernel,
+        [
+            jax.ShapeDtypeStruct((rows, width), BF16),
+            jax.ShapeDtypeStruct((rows, width), F32),
+            jax.ShapeDtypeStruct((8, width), F32),
+            jax.ShapeDtypeStruct((2 * PLANE, rows, width), BF16),
+            jax.ShapeDtypeStruct((width, hidden), BF16),
+            jax.ShapeDtypeStruct((width, hidden), BF16),
+        ],
+        [share, tokens, gain[None], bias[None], w_up, w_down, cotangent],
+        [
+            pltpu.VMEM(w_up.shape, BF16),
+            pltpu.VMEM(w_down.shape, BF16),
+            pltpu.VMEM((PLANE, rows, width), BF16),
+            pltpu.VMEM((2, rows, width // 2), BF16),
+            pltpu.VMEM((2, rows, width // 2), BF16),
+            pltpu.VMEM((rows, width // 2), BF16),
+            pltpu.VMEM((rows, width // 2), BF16),
+            pltpu.VMEM((rows, width), F32),
+            pltpu.VMEM((span, width), BF16),
+            pltpu.VMEM((span, hidden), BF16),
+            pltpu.VMEM((span, hidden), F32),
+            pltpu.VMEM((span, hidden), BF16),
+            pltpu.VMEM((2, rows, width), BF16),
+            pltpu.VMEM((2, rows, width), BF16),
+            pltpu.VMEM((rows, width), BF16),
+            pltpu.VMEM((2, 256, hidden), BF16),
+            DMA((3,)),
+            DMA((4,)),
+            DMA((4,)),
+            DMA((6,)),
+            DMA((6,)),
+            DMA((3,)),
+            DMA((3,)),
+            DMA((11,)),
+            DMA((11,)),
+            DMA((2,)),
+        ],
         cid,
-        in_specs=[VM],
-        out_specs=[VM],
-    )[0]
+        in_specs=[VM, VM, VM, VM, ANY, ANY, VM],
+        out_specs=[VM, VM, VM, ANY, ANY, ANY],
+    )
 
 
 def line_states_kernel(backward, x_ref, d_ref, out, dout, lsem, xsend, xrecv, dsend, drecv):
@@ -506,6 +697,7 @@
         [x, sent],
         [DMA((2,)), DMA((3,)), DMA((3,)), DMA((3,)), DMA((3,))],
         cid,
+        in_specs=[VM, VM],
     )
     z = (lax.axis_index("seq") % SPANS) // PLANE
     state = jnp.zeros(x.shape, F32)
@@ -515,108 +707,105 @@
     return state
 
 
-def line_scatter_kernel(a_ref, out, up, dn, fin, usend, urecv, dsend, drecv, psend, precv, lsem):
+def everyone(size):
+    return range(0, size, SPANS)
+
+
+def swap(x, mask):
+    n = lax.axis_size("seq")
+    return lax.ppermute(x, "seq", [(s, s ^ mask) for s in range(n)])
+
+
+def take(x, index, axis):
+    return lax.dynamic_index_in_dim(x, index, axis, False)
+
+
+def plus(a, b):
+    return (a.astype(F32) + b.astype(F32)).astype(BF16)
+
+
+def line_sum(x, z):
+    n = lax.axis_size("seq")
+    up = dn = None
+    for t in range(1, LINE):
+        up_at = jnp.clip(LINE - t + z, 0, LINE - 1)
+        dn_at = jnp.clip(z + t - LINE, 0, LINE - 1)
+        ups = [
+            (b + k * PLANE + p, b + (k + 1) * PLANE + p)
+            for b in everyone(n)
+            for k in range(t)
+            for p in range(PLANE)
+        ]
+        dns = [
+            (b + (LINE - 1 - k) * PLANE + p, b + (LINE - 2 - k) * PLANE + p)
+            for b in everyone(n)
+            for k in range(t)
+            for p in range(PLANE)
+        ]
+        send_up, send_dn = take(x, up_at, 0), take(x, dn_at, 0)
+        if t > 1:
+            send_up, send_dn = plus(send_up, up), plus(send_dn, dn)
+        up = lax.ppermute(send_up, "seq", ups)
+        dn = lax.ppermute(send_dn, "seq", dns)
+    return take(x, z, 0).astype(F32) + up.astype(F32) + dn.astype(F32)
+
+
+def plane_sum(x, p, first):
+    here = (p // 2, p % 2)
+    if first == 1:
+        kept, sent = take(x, here[1], 2), take(x, 1 - here[1], 2)
+        x = plus(kept, swap(sent, 1))
+        kept, sent = take(x, here[0], 1), take(x, 1 - here[0], 1)
+        return plus(kept, swap(sent, 2))
+    kept, sent = take(x, here[0], 1), take(x, 1 - here[0], 1)
+    x = plus(kept, swap(sent, 2))
+    kept, sent = take(x, here[1], 1), take(x, 1 - here[1], 1)
+    return plus(kept, swap(sent, 1))
+
+
+def plane_deal(x, p):
+    got = [take(x, p, 0)]
+    for mask in range(1, PLANE):
+        got.append(swap(take(x, p ^ mask, 0), mask))
+    return jnp.stack([sum_of_choice(got, p, q) for q in range(PLANE)])
+
+
+def sum_of_choice(got, p, q):
+    out = got[0]
+    for mask in range(1, PLANE):
+        out = jnp.where((p ^ q) == mask, got[mask], out)
+    return out
+
+
+def gains_kernel(x_ref, out, rx, send, recv):
     me = Place()
-    z, p = me.z, me.p
-    greet(
-        [(me.plane(m), None) for m in (1, 2, 3)] + [(me.up(), z < LINE - 1), (me.down(), z > 0)]
-    )
-    parts = usend.shape[1]
-    rows, cols = a_ref.shape[2:]
-    wide = cols // parts
-
-    def add(dst, src, at):
-        for q in range(PLANE):
-            dst[q, :, at] = (dst[q, :, at].astype(F32) + src[q, :, at].astype(F32)).astype(BF16)
-
-    def up_copy(src, zz, c):
-        at = pl.ds(c * wide, wide)
-        return remote(src.at[zz, :, :, at], up.at[zz, :, :, at], usend.at[zz, c], urecv.at[zz, c], me.up())
-
-    def dn_copy(src, zz, c):
-        at = pl.ds(c * wide, wide)
-        return remote(src.at[zz, :, :, at], dn.at[zz, :, :, at], dsend.at[zz, c], drecv.at[zz, c], me.down())
-
-    for t in range(LINE - 1):
-        zu, zd = LINE - 1 - t, t
-        for c in range(parts):
-            at = pl.ds(c * wide, wide)
-
-            @pl.when(z == 0)
-            def _():
-                up_copy(a_ref, zu, c).start()
-
-            @pl.when((z > 0) & (z < zu))
-            def _():
-                up_copy(up, zu, c).wait_recv()
-                add(up.at[zu], a_ref.at[zu], at)
-                up_copy(up, zu, c).start()
-
-            @pl.when(z == LINE - 1)
-            def _():
-                dn_copy(a_ref, zd, c).start()
-
-            @pl.when((z < LINE - 1) & (z > zd))
-            def _():
-                dn_copy(dn, zd, c).wait_recv()
-                add(dn.at[zd], a_ref.at[zd], at)
-                dn_copy(dn, zd, c).start()
-
-    plane = []
-    for c in range(parts):
-        at = pl.ds(c * wide, wide)
-        for q in range(PLANE):
-            fin[q, :, at] = a_ref[z, q, :, at]
-
-        @pl.when(z > 0)
-        def _():
-            up_copy(up, z, c).wait_recv()
-            add(fin, up.at[z], at)
-
-        @pl.when(z < LINE - 1)
-        def _():
-            dn_copy(dn, z, c).wait_recv()
-            add(fin, dn.at[z], at)
-
-        for m in (1, 2, 3):
-            s = remote(fin.at[me.xor(m), :, at], out.at[p, :, at], psend.at[c, m], precv.at[c, m], me.plane(m))
-            s.start()
-            plane.append(s)
-    own = pltpu.make_async_copy(fin.at[p], out.at[p], lsem)
-    own.start()
-    for s in plane:
-        s.wait()
-    own.wait()
-    for zz in range(LINE):
-        for c in range(parts):
-
-            @pl.when((z < LINE - 1) & (zz > z))
-            def _():
-                up_copy(up, zz, c).wait_send()
-
-            @pl.when((z > 0) & (zz < z))
-            def _():
-                dn_copy(dn, zz, c).wait_send()
-
-
-def line_scatter(a, parts, cid):
-    _, _, rows, cols = a.shape
+    rounds = [
+        [me.partner()],
+        [me.plane(m) for m in (1, 2, 3)],
+        [me.at((me.z + t) % LINE, me.p, me.f) for t in (1, 2, 3)],
+    ]
+    greet([(d, None) for r in rounds for d in r])
+    out[...] = x_ref[...]
+    k = 0
+    for peers in rounds:
+        copies = []
+        for d in peers:
+            c = remote(out, rx.at[k], send.at[k], recv.at[k], d)
+            c.start()
+            copies.append(c)
+            k += 1
+        for c in copies:
+            c.wait()
+        for j in range(k - len(peers), k):
+            out[...] += rx[j]
+
+
+def gains_sum(x, cid):
     return comm_call(
-        line_scatter_kernel,
-        [jax.ShapeDtypeStruct((PLANE, rows, cols), BF16)],
-        [a],
-        [
-            pltpu.VMEM((LINE, PLANE, rows, cols), BF16),
-            pltpu.VMEM((LINE, PLANE, rows, cols), BF16),
-            pltpu.VMEM((PLANE, rows, cols), BF16),
-            DMA((LINE, parts)),
-            DMA((LINE, parts)),
-            DMA((LINE, parts)),
-            DMA((LINE, parts)),
-            DMA((parts, PLANE)),
-            DMA((parts, PLANE)),
-            DMA,
-        ],
+        gains_kernel,
+        [jax.ShapeDtypeStruct(x.shape, F32)],
+        [x],
+        [pltpu.VMEM((7,) + x.shape, F32), DMA((7,)), DMA((7,))],
         cid,
         in_specs=[VM],
         out_specs=[VM],
@@ -718,11 +907,15 @@
     group_rows = span_rows * PLANE
     blocks = group_rows // STRETCH
 
+    tokens, cotangent, w_down = features_in(tokens), features_in(cotangent), features_in(w_down)
+    w_up = features_in(w_up.T).T if repeats > 1 else w_up
+    ln1_gain, ln1_bias = features_in(ln1_gain), features_in(ln1_bias)
+    ln2_gain, ln2_bias = features_in(ln2_gain), features_in(ln2_bias)
     inputs32 = tokens.astype(F32)
     xn_first, norm1_back = jax.vjp(layer_norm, inputs32, ln1_gain, ln1_bias)
     decays = jnp.pad(decay_log.T, ((0, 8 - heads), (0, 0)))
     xg, decay_rows, key_w, value_w, query_w, gate_w, out_w = gather_in(
-        features_in(xn_first.astype(BF16)),
+        xn_first.astype(BF16),
         decays,
         [
             wide_in(w_key, 0),
@@ -773,31 +966,27 @@
     gated, gate_back = jax.vjp(swish_gate, gate_proj, grouped)
     gated_low = gated.astype(BF16)
     attn_share = dot("tv,vd->td", gated_low, out_w).astype(BF16)
-    attn_rows = plane_reduce(attn_share.reshape(PLANE, 2, row_count, width), 2)
-
-    residual = inputs32 + features_out(attn_rows)
-    xn_second, norm2_back = jax.vjp(layer_norm, residual, ln2_gain, ln2_bias)
-    ffn_span = pair_gather(xn_second.astype(BF16), 3).reshape(span_rows, width)
-    upper = dot("td,df->tf", ffn_span, w_up)
-    active, gelu_back = jax.vjp(exact_gelu, upper)
-    active_low = active.astype(BF16)
-    grad_down = dot("tf,td->fd", active_low, cotangent).astype(BF16)
-    sum_down = lax.psum_scatter(grad_down, "seq", scatter_dimension=1, tiled=True).astype(F32)
-    grad_active = dot("td,fd->tf", cotangent, w_down)
-    grad_upper = gelu_back(grad_active)[0].astype(BF16)
-    grad_up = dot("td,tf->df", ffn_span, grad_upper).astype(BF16)
-    sum_up = lax.psum_scatter(grad_up, "seq", scatter_dimension=0, tiled=True).astype(F32)
-    ffn_share = dot("tf,fd->td", active_low, w_down).astype(BF16)
-    ffn_rows_out = pair_reduce(ffn_share.reshape(2, row_count, width), 4)
-    block_out = (residual + ffn_rows_out).astype(BF16)
-    own_start = lax.axis_index("ffn") * row_count
-    cot_own = lax.dynamic_slice_in_dim(cotangent, own_start, row_count, 0).astype(F32)
-    grad_xn2_share = dot("tf,df->td", grad_upper, w_up).astype(BF16)
-    grad_xn2 = pair_reduce(grad_xn2_share.reshape(2, row_count, width), 5)
-    grad_resid, grad_gain2, grad_bias2 = norm2_back(grad_xn2)
-    grad_resid = grad_resid + cot_own
-
-    grad_attn = plane_gather(features_in(grad_resid.astype(BF16)), 6).reshape(group_rows, width)
+    block_out, grad_resid, gains_second, grad_attn, grad_up, grad_down = ffn_part(
+        attn_share.reshape(PLANE, 2, row_count, width),
+        tokens,
+        ln2_gain,
+        ln2_bias,
+        w_up,
+        w_down,
+        cotangent,
+        2,
+    )
+    split = (LINE, 2, 2, width // SPANS, w_up.shape[1])
+    ffn_sum = line_sum(
+        jnp.concatenate(
+            [plane_sum(grad_up.reshape(split), p, 1), plane_sum(grad_down.reshape(split), p, 2)], axis=-1
+        ),
+        z,
+    )
+    sum_up = narrow_out(ffn_sum[:, : w_up.shape[1]], 0)
+    sum_down = narrow_out(ffn_sum[:, w_up.shape[1] :], 0).T
+
+    grad_attn = grad_attn.reshape(group_rows, width)
     grad_gated = dot("td,vd->tv", grad_attn, out_w)
     grad_out_w = dot("td,tv->dv", grad_attn, gated_low).astype(BF16)
     grad_gate, grad_grouped = gate_back(grad_gated)
@@ -825,22 +1014,28 @@
     grad_values = grad_v.reshape(group_rows, value_width).astype(BF16)
 
     grad_heads = jnp.concatenate([grad_query, grad_keys, grad_values, grad_gate_low], axis=1)
+    grad_qkv = jnp.concatenate([grad_query, grad_keys, grad_values], axis=1)
     heads_w = jnp.concatenate([query_w, key_w, value_w, gate_w], axis=1)
     grad_xn1_share = dot("tq,dq->td", grad_heads, heads_w).astype(BF16)
-    grad_heads_w = dot("td,tq->dq", normed, grad_heads).astype(BF16)
+    grad_heads_w = dot("td,tq->dq", normed, grad_qkv).astype(BF16)
+    grad_gate_w = dot("td,tq->dq", normed, grad_gate_low).astype(BF16)
     grad_xn1 = plane_reduce(grad_xn1_share.reshape(PLANE, 2, row_count, width), 8)
-    sums = line_scatter(
-        jnp.concatenate([grad_heads_w, grad_out_w], axis=1).reshape(
-            LINE, PLANE, width // SPANS, 2 * key_width + 3 * value_width
-        ),
-        4,
-        9,
-    )
-    grad_inputs, grad_gain1, grad_bias1 = norm1_back(features_out(grad_xn1))
+    first = jnp.concatenate([grad_gate_w, grad_out_w], axis=1)
+    sums = jnp.concatenate(
+        [
+            plane_deal(line_sum(g.reshape(LINE, PLANE, width // SPANS, -1), z).astype(BF16), p)
+            for g in (grad_heads_w, first)
+        ],
+        axis=-1,
+    )
+    grad_inputs, grad_gain1, grad_bias1 = norm1_back(grad_xn1)
     grad_tokens = (grad_resid + grad_inputs).astype(BF16)
-    gain_one, bias_one, gain_two, bias_two = lax.psum(
-        (grad_gain1, grad_bias1, grad_gain2, grad_bias2), ("seq", "ffn")
-    )
+    gains = jnp.concatenate([grad_gain1[None], grad_bias1[None], gains_second[:6]])
+    gains = gains_sum(gains, 10)
+    if repeats > 1:
+        gains = lax.psum(gains, "seq", axis_index_groups=peers)
+    gains = features_out(gains)
+    gain_one, bias_one, gain_two, bias_two = gains[0], gains[1], gains[2], gains[3]
 
     def columns(start, size):
         taken = sums[:, :, start : start + size].astype(F32).swapaxes(0, 1)
@@ -852,8 +1047,8 @@
     sum_gate = columns(2 * key_width + value_width, value_width)
     sum_out = columns(2 * key_width + 2 * value_width, value_width).T
     return (
-        block_out,
-        grad_tokens,
+        features_out(block_out),
+        features_out(grad_tokens),
         gain_one,
         bias_one,
         sum_query,

time: 1040 us -> 906 us (0.87)
  Pallas kernels: 657 us -> 408 us
  waiting for transfers between devices: 0.04 us -> 88 us
  local copies, waits for them, and re-layouts: 61.9 us -> 130 us
  matrix products: 167 us -> 104 us
  starting transfers between devices: 0.25 us -> 56.3 us
  blocking collectives: 39 us -> 0 us
  other arithmetic: 77 us -> 97.1 us
  between operations: 23.9 us -> 10.8 us
    pallas_call x10 -> x6, Pallas kernels: 657 us -> 408 us  [comm_call(): pl.pallas_call(kernel, out_shape=outs, in_specs=in_specs if in_specs is n...]
    ppermute x0 -> x28, waiting for transfers between devices: none -> 88 us  [the longest x9 80.9 us: line_sum(): dn = lax.ppermute(send_dn, 'seq', dns)]
    dot_general x27 -> x22, matrix products: 167 us -> 104 us  [dot(): return jnp.einsum(spec, a, b, preferred_element_type=F32)]
    ppermute x0 -> x28, starting transfers between devices: none -> 56.3 us  [the longest x9 28.2 us: line_sum(): dn = lax.ppermute(send_dn, 'seq', dns)]
    dynamic_slice x0 -> x7, local copies, waits for them, and re-layouts: none -> 52 us  [take(): return lax.dynamic_index_in_dim(x, index, axis, False)]
    psum x1 -> x0, blocking collectives: 39 us -> none  [shards(): lax.psum((grad_gain1, grad_bias1, grad_gain2, grad_bias2), ('seq', 'ffn'))]
    convert_element_type x5 -> x15, other arithmetic: 8.7 us -> 30 us  [the longest x13 28.8 us: plus(): return (a.astype(F32) + b.astype(F32)).astype(BF16)]
    unnamed x163 -> x179, local copies, waits for them, and re-layouts: 34.3 us -> 48.9 us
  transfers between devices with their start and end apart: 2 -> 28, of which waited for: 0 -> 7; matrix products, arithmetic and copies ran while one was open for 18% -> 26% of each run, Pallas kernels for 39% -> 14%
where the time goes in v2:
time: 906 us; the launch traced here: 894 us
  Pallas kernels  408 us (45%)
  local copies, waits for them, and re-layouts  130 us (14%)
  matrix products  104 us (11%)
  other arithmetic  97.1 us (11%)
  waiting for transfers between devices  88 us (10%)
  starting transfers between devices  56.3 us (6%)
  between operations  10.8 us (1%)
    pallas_call x6, Pallas kernels, comm_call(): pl.pallas_call(kernel, out_shape=outs, in_specs=in_specs if in_specs is n...  408 us
    dot_general x22, matrix products, dot(): return jnp.einsum(spec, a, b, preferred_element_type=F32)  104 us
    ppermute x9, waiting for transfers between devices, line_sum(): dn = lax.ppermute(send_dn, 'seq', dns)  80.9 us
    dynamic_slice x7, local copies, waits for them, and re-layouts, take(): return lax.dynamic_index_in_dim(x, index, axis, False)  52 us
    unnamed x179, local copies, waits for them, and re-layouts  48.9 us
    convert_element_type x13, other arithmetic, plus(): return (a.astype(F32) + b.astype(F32)).astype(BF16)  28.8 us
    ppermute x9, starting transfers between devices, line_sum(): dn = lax.ppermute(send_dn, 'seq', dns)  28.2 us
    unnamed x9, other arithmetic  20.1 us
  transfers between devices with their start and end apart: 28, of which 7 were waited for; matrix products, arithmetic and copies ran while one was open for 26% of the time, Pallas kernels for 14%

profile of v2, /device:TPU:16, one launch (start us, length us, event | category | flops | bytes accessed | tf_op | source)
XLA Modules:
  0.0 893.8 jit_solution(4101687736200865210)
XLA Ops:
  6.6 154.4 %shard_map.237 = (bf16[8,256,2048]{2,1,0:T(8,128)(2,1)}, f32[4,8,512]{2,1,0:T(8,128)}, bf16[2048,256]{1,0:T(8,128)(2,1)}, bf16[2048,512]{1,0:T(8,128)(2,1)}, bf1...) custom-call(bf16[256,2048]{1,0:T(8,128)(2,1)} %fusion.22.refs_0_, ...), custom_call_target="tpu_custom_call" | custom-call | tf_op jit(solution)/shard_map/pallas_call | solution.py:81
  191.5 23.8 %shard_map.238 = (bf16[4,256,512]{2,1,0:T(8,128)(2,1)}, f32[4,8,128]{2,1,0:T(8,128)}) custom-call(bf16[256,512]{1,0:T(8,128)(2,1)} %get-tuple-element.104.x_ref, f32[8,128]{1,0:T(8,128)} %broadcast_in_dim.27.d_ref), custom_call_target="tpu_custom_call" | custom-call | tf_op jit(solution)/shard_map/pallas_call | solution.py:81
  230.5 10.5 %multiply_convert_fusion.1 = (bf16[2048,512]{1,0:T(8,128)(2,1)S(1)}, f32[2048,512]{1,0:T(8,128)}) fusion(f32[4,512,512]{2,1,0:T(8,128)} %copy-done.4, f32[2048]{0:T(1024)S(1)} %rsqrt.21, f32[2048]{0:T(1024)S(1)} %bitcast.351, bf16[2048,2048]{1,0:T(8,128)(2,1)} %bitcast.369, bf16[2048,512]{1,0:T(8,128)(2,1)} %get-tuple-element.31), kind=kOutput, calls=%fused_computation.42 | convolution fusion | flops 4303355904 | bytes 20987904 | tf_op jit(solution)/shard_map/td,dv->tv/dot_general | solution.py:857
  240.9 6.8 convolution_convert_fusion.1
  247.7 104.8 %shard_map.239 = (bf16[256,2048]{1,0:T(8,128)(2,1)}, f32[256,2048]{1,0:T(8,128)}, f32[8,2048]{1,0:T(8,128)}, bf16[8,256,2048]{2,1,0:T(8,128)(2,1)}, bf16[2048,20...) custom-call(bf16[4,2,256,2048]{3,2,1,0:T(8,128)(2,1)} %bitcast.304, bf16[256,2048]{1,0:T(8,128)(2,1)} %tok_ref.1, ...), custom_call_target="tpu_custom_call" | custom-call | tf_op jit(solution)/shard_map/pallas_call | solution.py:81
  352.6 8.4 constant_dynamic-slice_fusion.1
  367.3 8.3 constant_dynamic-slice_fusion.3
  375.6 18.2 %copy.80 = bf16[4,2,1,128,2048]{3,4,0,1,2:T(8,128)(2,1)} copy(bf16[4,2,1,128,2048]{4,3,2,1,0:T(8,128)(2,1)} %get-tuple-element.110) | data formatting | bytes 8388608 | tf_op jit(solution)/shard_map/jit(dynamic_index_in_dim)/dynamic_slice | solution.py:720
  395.9 8.7 convolution_convert_fusion.3
  404.7 7.8 multiply_reduce_fusion
  418.6 8.2 convolution_convert_fusion.4
  429.1 7.7 reshape.414
  478.6 29.4 %shard_map.240 = (bf16[4,256,512]{2,1,0:T(8,128)(2,1)}, f32[4,8,128]{2,1,0:T(8,128)}) custom-call(bf16[256,512]{1,0:T(8,128)(2,1)} %get-tuple-element.193.x_ref, f32[8,128]{1,0:T(8,128)} %broadcast_in_dim.27.d_ref), custom_call_target="tpu_custom_call" | custom-call | tf_op jit(solution)/shard_map/pallas_call | solution.py:81
  531.8 9.6 %convolution_convert_fusion.2 = bf16[2048,1024]{1,0:T(8,128)(2,1)S(1)} fusion(bf16[2048,2048]{1,0:T(8,128)(2,1)S(1)} %bitcast.375, bf16[2048,1024]{1,0:T(8,128)(2,1)S(1)} %get-tuple-element.136), kind=kOutput, calls=%fused_computation.49 | convolution fusion | flops 8592031744 | bytes 16777216 | tf_op jit(solution)/shard_map/td,tq->dq/dot_general | solution.py:857
  548.1 16.6 %convolution_convert_fusion = bf16[2048,2048]{1,0:T(8,128)(2,1)} fusion(bf16[2048,1536]{1,0:T(8,128)(2,1)S(1)} %constant_dynamic-update-slice_fusion, bf16[2048,512]{1,0:T(8,128)(2,1)S(1)} %copy-done.70, bf16[2048,512]{1,0:T(8,128)(2,1)S(1)} %copy-done.69, bf16[2048,256]{1,0:T(8,128)(2,1)} %get-tuple-element.33, bf16[2048,256]{1,0:T(8,128)(2,1)} %get-tuple-element.32), kind=kOutput, calls=%fused_computation.4 | convolution fusion | flops 12914262016 | bytes 20971520 | tf_op jit(solution)/shard_map/tq,dq->td/dot_general | solution.py:857
  577.2 42.9 %shard_map.241 = f32[256,2048]{1,0:T(8,128)} custom-call(bf16[4,2,256,2048]{3,2,1,0:T(8,128)(2,1)} %bitcast.305), custom_call_target="tpu_custom_call" | custom-call | tf_op jit(solution)/shard_map/pallas_call | solution.py:81
  644.9 52.4 %shard_map.242 = f32[8,2048]{1,0:T(8,128)} custom-call(f32[8,2048]{1,0:T(8,128)} %pad_maximum_fusion.13.x_ref), custom_call_target="tpu_custom_call" | custom-call | tf_op jit(solution)/shard_map/pallas_call | solution.py:81
  724.9 7.0 collective-permute-done.10
  742.5 9.1 %collective-permute-done.13 = bf16[4,128,1024]{2,1,0:T(8,128)(2,1)} collective-permute-done((bf16[4,128,1024]{2,1,0:T(8,128)(2,1)}, bf16[4,128,1024]{2,1,0:T(8,128)(2,1)}, u32[]{:S(2)}, u32[]{:S(2)}) %collective-permute-start.13) | collective-permute-done | bytes 1048608 | tf_op jit(solution)/shard_map/ppermute | solution.py:749
  763.9 10.2 %collective-permute-done.25 = bf16[128,4096]{0,1:T(8,128)(2,1)} collective-permute-done((bf16[128,4096]{0,1:T(8,128)(2,1)}, bf16[128,4096]{0,1:T(8,128)(2,1)}, u32[]{:S(2)}, u32[]{:S(2)}) %collective-permute-start.25) | collective-permute-done | bytes 1048608 | tf_op jit(solution)/shard_map/ppermute | solution.py:749
  783.0 13.4 %collective-permute-done.14 = bf16[4,128,1024]{2,1,0:T(8,128)(2,1)S(1)} collective-permute-done((bf16[4,128,1024]{2,1,0:T(8,128)(2,1)S(1)}, bf16[4,128,1024]{2,1,0:T(8,128)(2,1)S(1)}, u32[]{:S(2)}, u32[]{:S(2)}) %collective-permute-start.14) | collective-permute-done | bytes 1048608 | tf_op jit(solution)/shard_map/ppermute | solution.py:749
  800.0 18.9 %collective-permute-done.4 = bf16[4,128,1024]{2,1,0:T(8,128)(2,1)S(1)} collective-permute-done((bf16[4,128,1024]{2,1,0:T(8,128)(2,1)S(1)}, bf16[4,128,1024]{2,1,0:T(8,128)(2,1)S(1)}, u32[]{:S(2)}, u32[]{:S(2)}) %collective-permute-start.4) | collective-permute-done | bytes 1048608 | tf_op jit(solution)/shard_map/ppermute | solution.py:749
  826.8 14.6 %collective-permute-done.26 = bf16[128,4096]{0,1:T(8,128)(2,1)S(1)} collective-permute-done((bf16[128,4096]{0,1:T(8,128)(2,1)S(1)}, bf16[128,4096]{0,1:T(8,128)(2,1)S(1)}, u32[]{:S(2)}, u32[]{:S(2)}) %collective-permute-start.26) | collective-permute-done | bytes 1048608 | tf_op jit(solution)/shard_map/ppermute | solution.py:749
  849.1 14.7 %collective-permute-done.5 = bf16[4,128,1024]{2,1,0:T(8,128)(2,1)S(1)} collective-permute-done((bf16[4,128,1024]{2,1,0:T(8,128)(2,1)S(1)}, bf16[4,128,1024]{2,1,0:T(8,128)(2,1)S(1)}, u32[]{:S(2)}, u32[]{:S(2)}) %collective-permute-start.5) | collective-permute-done | bytes 1048608 | tf_op jit(solution)/shard_map/ppermute | solution.py:749
  (335 shorter events, 276.6 us)
Async XLA Ops:
  367.2 256.8 %collective-permute-start.20 = (bf16[4,2,128,2048]{2,3,0,1:T(8,128)(2,1)}, bf16[4,2,128,2048]{2,3,0,1:T(8,128)(2,1)}, u32[]{:S(2)}, u32[]{:S(2)}) collective-permute-start(bf16[4,2,128,2048]{2,3,0,1:T(8,128)(2,1)} %bitcast.327), channel_id=1, source_target_pairs={{0,4},{2,6},{4,0},{6,2},{8,12},{10,14},{12,8},{14,10},{16,20},{18,... | collective-permute-start | bytes 12582920 | tf_op jit(solution)/shard_map/ppermute | solution.py:716
  393.8 238.9 %collective-permute-start.18 = (bf16[4,2,128,2048]{2,3,0,1:T(8,128)(2,1)}, bf16[4,2,128,2048]{2,3,0,1:T(8,128)(2,1)}, u32[]{:S(2)}, u32[]{:S(2)}) collective-permute-start(bf16[4,2,128,2048]{2,3,0,1:T(8,128)(2,1)} %bitcast.328), channel_id=1, source_target_pairs={{0,2},{2,0},{4,6},{6,4},{8,10},{10,8},{12,14},{14,12},{16,18},{18,... | collective-permute-start | bytes 12582920 | tf_op jit(solution)/shard_map/ppermute | solution.py:716
  445.2 255.5 %collective-permute-start.9 = (bf16[4,128,1024]{2,1,0:T(8,128)(2,1)}, bf16[4,128,1024]{2,1,0:T(8,128)(2,1)}, u32[]{:S(2)}, u32[]{:S(2)}) collective-permute-start(bf16[4,128,1024]{2,1,0:T(8,128)(2,1)} %bitcast.342), channel_id=1, source_target_pairs={{0,8},{2,10},{4,12},{6,14},{1,9},{3,11},{5,13},{7,15}} | collective-permute-start | bytes 3145736 | tf_op jit(solution)/shard_map/ppermute | solution.py:748
  449.2 254.5 %collective-permute-start.12 = (bf16[4,128,1024]{2,1,0:T(8,128)(2,1)}, bf16[4,128,1024]{2,1,0:T(8,128)(2,1)}, u32[]{:S(2)}, u32[]{:S(2)}) collective-permute-start(bf16[4,128,1024]{2,1,0:T(8,128)(2,1)} %bitcast.341), channel_id=1, source_target_pairs={{24,16},{26,18},{28,20},{30,22},{25,17},{27,19},{29,21},{31,23}} | collective-permute-start | bytes 3145736 | tf_op jit(solution)/shard_map/ppermute | solution.py:749
  544.2 163.7 %collective-permute-start = (bf16[4,128,1024]{2,1,0:T(8,128)(2,1)}, bf16[4,128,1024]{2,1,0:T(8,128)(2,1)}, u32[]{:S(2)}, u32[]{:S(2)}) collective-permute-start(bf16[4,128,1024]{2,1,0:T(8,128)(2,1)} %get-tuple-element.126), channel_id=1, source_target_pairs={{0,8},{2,10},{4,12},{6,14},{1,9},{3,11},{5,13},{7,15}} | collective-permute-start | bytes 3145736 | tf_op jit(solution)/shard_map/ppermute | solution.py:748
  630.4 84.9 %collective-permute-start.21 = (bf16[4,128,2048]{1,2,0:T(8,128)(2,1)}, bf16[4,128,2048]{1,2,0:T(8,128)(2,1)}, u32[]{:S(2)}, u32[]{:S(2)}) collective-permute-start(bf16[4,128,2048]{1,2,0:T(8,128)(2,1)} %dynamic-slice_bitcast_fusion), channel_id=1, source_target_pairs={{0,2},{2,0},{4,6},{6,4},{8,10},{10,8},{12,14},{14,12},{16,18},{18,... | collective-permute-start | bytes 6291464 | tf_op jit(solution)/shard_map/ppermute | solution.py:716
  638.8 80.3 %collective-permute-start.19 = (bf16[4,128,2048]{1,2,0:T(8,128)(2,1)}, bf16[4,128,2048]{1,2,0:T(8,128)(2,1)}, u32[]{:S(2)}, u32[]{:S(2)}) collective-permute-start(bf16[4,128,2048]{1,2,0:T(8,128)(2,1)} %dynamic-slice_bitcast_fusion.1), channel_id=1, source_target_pairs={{0,4},{2,6},{4,0},{6,2},{8,12},{10,14},{12,8},{14,10},{16,20},{18,... | collective-permute-start | bytes 6291464 | tf_op jit(solution)/shard_map/ppermute | solution.py:716
  700.7 54.5 %collective-permute-start.3 = (bf16[4,128,1024]{2,1,0:T(8,128)(2,1)}, bf16[4,128,1024]{2,1,0:T(8,128)(2,1)}, u32[]{:S(2)}, u32[]{:S(2)}) collective-permute-start(bf16[4,128,1024]{2,1,0:T(8,128)(2,1)} %get-tuple-element.127), channel_id=1, source_target_pairs={{24,16},{26,18},{28,20},{30,22},{25,17},{27,19},{29,21},{31,23}} | collective-permute-start | bytes 3145736 | tf_op jit(solution)/shard_map/ppermute | solution.py:749
  703.8 28.1 %collective-permute-start.10 = (bf16[4,128,1024]{2,1,0:T(8,128)(2,1)S(1)}, bf16[4,128,1024]{2,1,0:T(8,128)(2,1)}, u32[]{:S(2)}, u32[]{:S(2)}) collective-permute-start(bf16[4,128,1024]{2,1,0:T(8,128)(2,1)S(1)} %fusion.33), channel_id=1, source_target_pairs={{0,8},{2,10},{4,12},{6,14},{8,16},{10,18},{12,20},{14,22},{1,9},{3... | collective-permute-start | bytes 3145736 | tf_op jit(solution)/shard_map/ppermute | solution.py:748
  707.9 43.8 %collective-permute-start.13 = (bf16[4,128,1024]{2,1,0:T(8,128)(2,1)}, bf16[4,128,1024]{2,1,0:T(8,128)(2,1)}, u32[]{:S(2)}, u32[]{:S(2)}) collective-permute-start(bf16[4,128,1024]{2,1,0:T(8,128)(2,1)} %fusion.31), channel_id=1, source_target_pairs={{24,16},{26,18},{28,20},{30,22},{16,8},{18,10},{20,12},{22,14},{25... | collective-permute-start | bytes 3145736 | tf_op jit(solution)/shard_map/ppermute | solution.py:749
  715.3 43.9 %collective-permute-start.1 = (bf16[4,128,1024]{2,1,0:T(8,128)(2,1)}, bf16[4,128,1024]{2,1,0:T(8,128)(2,1)}, u32[]{:S(2)}, u32[]{:S(2)}) collective-permute-start(bf16[4,128,1024]{2,1,0:T(8,128)(2,1)} %fusion.39), channel_id=1, source_target_pairs={{0,8},{2,10},{4,12},{6,14},{8,16},{10,18},{12,20},{14,22},{1,9},{3... | collective-permute-start | bytes 3145736 | tf_op jit(solution)/shard_map/ppermute | solution.py:748
  723.2 40.7 %collective-permute-start.22 = (bf16[128,4096]{0,1:T(8,128)(2,1)}, bf16[128,4096]{0,1:T(8,128)(2,1)}, u32[]{:S(2)}, u32[]{:S(2)}) collective-permute-start(bf16[128,4096]{0,1:T(8,128)(2,1)} %get-tuple-element.115), channel_id=1, source_target_pairs={{0,8},{2,10},{4,12},{6,14},{1,9},{3,11},{5,13},{7,15}} | collective-permute-start | bytes 3145736 | tf_op jit(solution)/shard_map/ppermute | solution.py:748
  731.9 42.2 %collective-permute-start.25 = (bf16[128,4096]{0,1:T(8,128)(2,1)}, bf16[128,4096]{0,1:T(8,128)(2,1)}, u32[]{:S(2)}, u32[]{:S(2)}) collective-permute-start(bf16[128,4096]{0,1:T(8,128)(2,1)} %get-tuple-element.116), channel_id=1, source_target_pairs={{24,16},{26,18},{28,20},{30,22},{25,17},{27,19},{29,21},{31,23}} | collective-permute-start | bytes 3145736 | tf_op jit(solution)/shard_map/ppermute | solution.py:749
  751.6 31.4 %collective-permute-start.11 = (bf16[4,128,1024]{2,1,0:T(8,128)(2,1)S(1)}, bf16[4,128,1024]{2,1,0:T(8,128)(2,1)S(1)}, u32[]{:S(2)}, u32[]{:S(2)}) collective-permute-start(bf16[4,128,1024]{2,1,0:T(8,128)(2,1)S(1)} %fusion.34), channel_id=1, source_target_pairs={{0,8},{2,10},{4,12},{6,14},{8,16},{10,18},{12,20},{14,22},{16,24},... | collective-permute-start | bytes 3145736 | tf_op jit(solution)/shard_map/ppermute | solution.py:748
  755.2 41.3 %collective-permute-start.14 = (bf16[4,128,1024]{2,1,0:T(8,128)(2,1)S(1)}, bf16[4,128,1024]{2,1,0:T(8,128)(2,1)S(1)}, u32[]{:S(2)}, u32[]{:S(2)}) collective-permute-start(bf16[4,128,1024]{2,1,0:T(8,128)(2,1)S(1)} %fusion.32), channel_id=1, source_target_pairs={{24,16},{26,18},{28,20},{30,22},{16,8},{18,10},{20,12},{22,14},{8,... | collective-permute-start | bytes 3145736 | tf_op jit(solution)/shard_map/ppermute | solution.py:749
  761.8 57.1 %collective-permute-start.4 = (bf16[4,128,1024]{2,1,0:T(8,128)(2,1)S(1)}, bf16[4,128,1024]{2,1,0:T(8,128)(2,1)S(1)}, u32[]{:S(2)}, u32[]{:S(2)}) collective-permute-start(bf16[4,128,1024]{2,1,0:T(8,128)(2,1)S(1)} %get-tuple-element.125), channel_id=1, source_target_pairs={{24,16},{26,18},{28,20},{30,22},{16,8},{18,10},{20,12},{22,14},{25... | collective-permute-start | bytes 3145736 | tf_op jit(solution)/shard_map/ppermute | solution.py:749
  776.2 50.7 %collective-permute-start.23 = (bf16[128,4096]{0,1:T(8,128)(2,1)S(1)}, bf16[128,4096]{0,1:T(8,128)(2,1)S(1)}, u32[]{:S(2)}, u32[]{:S(2)}) collective-permute-start(bf16[128,4096]{0,1:T(8,128)(2,1)S(1)} %get-tuple-element.113), channel_id=1, source_target_pairs={{0,8},{2,10},{4,12},{6,14},{8,16},{10,18},{12,20},{14,22},{1,9},{3... | collective-permute-start | bytes 3145736 | tf_op jit(solution)/shard_map/ppermute | solution.py:748
  777.5 63.9 %collective-permute-start.26 = (bf16[128,4096]{0,1:T(8,128)(2,1)S(1)}, bf16[128,4096]{0,1:T(8,128)(2,1)S(1)}, u32[]{:S(2)}, u32[]{:S(2)}) collective-permute-start(bf16[128,4096]{0,1:T(8,128)(2,1)S(1)} %get-tuple-element.114), channel_id=1, source_target_pairs={{24,16},{26,18},{28,20},{30,22},{16,8},{18,10},{20,12},{22,14},{25... | collective-permute-start | bytes 3145736 | tf_op jit(solution)/shard_map/ppermute | solution.py:749
  797.1 23.5 %collective-permute-start.15 = (bf16[128,1024]{1,0:T(8,128)(2,1)S(1)}, bf16[128,1024]{1,0:T(8,128)(2,1)S(1)}, u32[]{:S(2)}, u32[]{:S(2)}) collective-permute-start(bf16[128,1024]{1,0:T(8,128)(2,1)S(1)} %get-tuple-element.151), channel_id=1, source_target_pairs={{0,6},{2,4},{4,2},{6,0},{8,14},{10,12},{12,10},{14,8},{16,22},{18,... | collective-permute-start | bytes 786440 | tf_op jit(solution)/shard_map/ppermute | solution.py:716
  798.7 23.9 %collective-permute-start.16 = (bf16[128,1024]{1,0:T(8,128)(2,1)S(1)}, bf16[128,1024]{1,0:T(8,128)(2,1)S(1)}, u32[]{:S(2)}, u32[]{:S(2)}) collective-permute-start(bf16[128,1024]{1,0:T(8,128)(2,1)S(1)} %get-tuple-element.150), channel_id=1, source_target_pairs={{0,4},{2,6},{4,0},{6,2},{8,12},{10,14},{12,8},{14,10},{16,20},{18,... | collective-permute-start | bytes 786440 | tf_op jit(solution)/shard_map/ppermute | solution.py:716
  820.7 28.5 %collective-permute-start.2 = (bf16[4,128,1024]{2,1,0:T(8,128)(2,1)S(1)}, bf16[4,128,1024]{2,1,0:T(8,128)(2,1)S(1)}, u32[]{:S(2)}, u32[]{:S(2)}) collective-permute-start(bf16[4,128,1024]{2,1,0:T(8,128)(2,1)S(1)} %get-tuple-element.124), channel_id=1, source_target_pairs={{0,8},{2,10},{4,12},{6,14},{8,16},{10,18},{12,20},{14,22},{16,24},... | collective-permute-start | bytes 3145736 | tf_op jit(solution)/shard_map/ppermute | solution.py:748
  822.6 41.3 %collective-permute-start.5 = (bf16[4,128,1024]{2,1,0:T(8,128)(2,1)S(1)}, bf16[4,128,1024]{2,1,0:T(8,128)(2,1)S(1)}, u32[]{:S(2)}, u32[]{:S(2)}) collective-permute-start(bf16[4,128,1024]{2,1,0:T(8,128)(2,1)S(1)} %fusion.38), channel_id=1, source_target_pairs={{24,16},{26,18},{28,20},{30,22},{16,8},{18,10},{20,12},{22,14},{8,... | collective-permute-start | bytes 3145736 | tf_op jit(solution)/shard_map/ppermute | solution.py:749
  843.3 44.7 %collective-permute-start.24 = (bf16[128,4096]{0,1:T(8,128)(2,1)}, bf16[128,4096]{0,1:T(8,128)(2,1)}, u32[]{:S(2)}, u32[]{:S(2)}) collective-permute-start(bf16[128,4096]{0,1:T(8,128)(2,1)} %get-tuple-element.111), channel_id=1, source_target_pairs={{0,8},{2,10},{4,12},{6,14},{8,16},{10,18},{12,20},{14,22},{16,24},... | collective-permute-start | bytes 3145736 | tf_op jit(solution)/shard_map/ppermute | solution.py:748
  845.2 42.8 %collective-permute-start.27 = (bf16[128,4096]{0,1:T(8,128)(2,1)}, bf16[128,4096]{0,1:T(8,128)(2,1)}, u32[]{:S(2)}, u32[]{:S(2)}) collective-permute-start(bf16[128,4096]{0,1:T(8,128)(2,1)} %get-tuple-element.112), channel_id=1, source_target_pairs={{24,16},{26,18},{28,20},{30,22},{16,8},{18,10},{20,12},{22,14},{8,... | collective-permute-start | bytes 3145736 | tf_op jit(solution)/shard_map/ppermute | solution.py:749
  (83 other events, 736.3 us)

commit v3 on v2

--- a/solution.py
+++ b/solution.py
@@ -277,90 +277,6 @@
         cid,
         in_specs=[VM] + [ANY] * (count + 1),
     )
-
-
-def plane_reduce_kernel(x_ref, out, rx0, rx1a, rx1b, rx2a, rx2b, csend, crecv, xsend, xrecv):
-    me = Place()
-    p, f = me.p, me.f
-    greet([(me.plane(1), None), (me.plane(2), None), (me.partner(), None)])
-    q = [me.xor(m) for m in range(4)]
-    wide = x_ref.shape[-1] // 2
-    ca, cb = pl.ds(0, wide), pl.ds(wide, wide)
-    order = (3, 1, 2, 0)
-    first = []
-    for m in order:
-        c = remote(x_ref.at[q[m], 1 - f], rx0.at[q[m]], csend.at[m], crecv.at[m], me.partner())
-        c.start()
-        first.append(c)
-
-    def add(dst, cols, other, others_cols):
-        rows = dst.shape[0]
-
-        @pl.loop(0, rows, step=64)
-        def _(r):
-            at = pl.ds(pl.multiple_of(r, 64), 64)
-            dst[at, cols] = (dst[at, cols].astype(F32) + other[at, others_cols].astype(F32)).astype(BF16)
-
-    everything = pl.ds(0, 2 * wide)
-    whole = pl.ds(0, wide)
-    sends = {}
-    for c, m in zip(first, order):
-        c.wait_recv()
-        add(rx0.at[q[m]], everything, x_ref.at[q[m], f], everything)
-        if m & 1:
-            k = 0 if m == 3 else 1
-            s = remote(rx0.at[q[m], :, ca], rx1a.at[k], xsend.at[k], xrecv.at[k], me.plane(1))
-            s.start()
-            sends["a", k] = s
-        if m & 2:
-            k = 0 if m == 3 else 1
-            s = remote(rx0.at[q[m], :, cb], rx1b.at[k], xsend.at[2 + k], xrecv.at[2 + k], me.plane(2))
-            s.start()
-            sends["b", k] = s
-    sends["a", 0].wait_recv()
-    add(rx1a.at[0], whole, rx0.at[q[2]], ca)
-    s2a = remote(rx1a.at[0], rx2a, xsend.at[4], xrecv.at[4], me.plane(2))
-    s2a.start()
-    sends["b", 0].wait_recv()
-    add(rx1b.at[0], whole, rx0.at[q[1]], cb)
-    s2b = remote(rx1b.at[0], rx2b, xsend.at[5], xrecv.at[5], me.plane(1))
-    s2b.start()
-    sends["a", 1].wait_recv()
-    sends["b", 1].wait_recv()
-    s2a.wait_recv()
-    s2b.wait_recv()
-
-    @pl.loop(0, out.shape[0], step=32)
-    def _(r):
-        at = pl.ds(pl.multiple_of(r, 32), 32)
-        out[at, ca] = rx0[q[0], at, ca].astype(F32) + rx1a[1, at, :].astype(F32) + rx2a[at, :].astype(F32)
-        out[at, cb] = rx0[q[0], at, cb].astype(F32) + rx1b[1, at, :].astype(F32) + rx2b[at, :].astype(F32)
-
-    for c in first + list(sends.values()) + [s2a, s2b]:
-        c.wait_send()
-
-
-def plane_reduce(x, cid):
-    _, _, rows, cols = x.shape
-    return comm_call(
-        plane_reduce_kernel,
-        [jax.ShapeDtypeStruct((rows, cols), F32)],
-        [x],
-        [
-            pltpu.VMEM((PLANE, rows, cols), BF16),
-            pltpu.VMEM((2, rows, cols // 2), BF16),
-            pltpu.VMEM((2, rows, cols // 2), BF16),
-            pltpu.VMEM((rows, cols // 2), BF16),
-            pltpu.VMEM((rows, cols // 2), BF16),
-            DMA((4,)),
-            DMA((4,)),
-            DMA((6,)),
-            DMA((6,)),
-        ],
-        cid,
-        in_specs=[VM],
-        out_specs=[VM],
-    )[0]
 
 
 def nn(a, b):
@@ -707,6 +623,864 @@
     return state
 
 
+class LineSum:
+    def __init__(self, me, own, rx, usend, urecv, dsend, drecv, add):
+        self.me, self.own, self.rx, self.add = me, own, rx, add
+        self.sems = usend, urecv, dsend, drecv
+
+    def up(self, src, zz):
+        return remote(src, self.rx.at[zz], self.sems[0].at[zz], self.sems[1].at[zz], self.me.up())
+
+    def down(self, src, zz):
+        slot = jnp.where(zz == self.me.z - 1, LINE, zz)
+        return remote(src, self.rx.at[slot], self.sems[2].at[zz], self.sems[3].at[zz], self.me.down())
+
+    def begin(self):
+        for zz in reversed(range(1, LINE)):
+
+            @pl.when(self.me.z == 0)
+            def _():
+                self.up(self.own(zz), zz).start()
+
+            @pl.when(self.me.z == LINE - 1)
+            def _():
+                self.down(self.own(LINE - 1 - zz), LINE - 1 - zz).start()
+
+    def step(self, t):
+        z = self.me.z
+        zu, zd = LINE - 1 - t, t
+
+        @pl.when((z > 0) & (z < zu))
+        def _():
+            self.up(self.own(zu), zu).wait_recv()
+            self.add(self.rx.at[zu], self.own(zu))
+            self.up(self.rx.at[zu], zu).start()
+
+        @pl.when((z < LINE - 1) & (z > zd))
+        def _():
+            self.down(self.own(zd), zd).wait_recv()
+            self.add(self.rx.at[zd], self.own(zd))
+            self.down(self.rx.at[zd], zd).start()
+
+    def arrive(self):
+        z = self.me.z
+
+        @pl.when(z > 0)
+        def _():
+            self.up(self.own(z), z).wait_recv()
+
+        @pl.when(z < LINE - 1)
+        def _():
+            self.down(self.own(z), z).wait_recv()
+
+    def finish(self):
+        z = self.me.z
+        for zz in range(LINE):
+
+            @pl.when((z < LINE - 1) & (zz > z))
+            def _():
+                self.up(self.own(zz), zz).wait_send()
+
+            @pl.when((z > 0) & (zz < z))
+            def _():
+                self.down(self.own(zz), zz).wait_send()
+
+
+def add_rows(dst, src):
+    rows = dst.shape[0]
+    step = 32 if dst.shape[1] > 512 else 128
+
+    @pl.loop(0, rows, step=step)
+    def _(r):
+        at = rows_at(r, step)
+        dst[at, :] = (dst[at, :].astype(F32) + src[at, :].astype(F32)).astype(BF16)
+
+
+def total_rows(z, dst, own, rx):
+    rows = dst.shape[0]
+    step = 32 if dst.shape[1] > 512 else 128
+
+    @pl.loop(0, rows, step=step)
+    def _(r):
+        at = rows_at(r, step)
+        v = own[at, :].astype(F32)
+        v = v + jnp.where(z > 0, rx[z, at, :].astype(F32), 0.0)
+        v = v + jnp.where(z < LINE - 1, rx[LINE, at, :].astype(F32), 0.0)
+        dst[at, :] = v.astype(dst.dtype)
+
+
+def line_sems():
+    return [DMA((LINE,)) for _ in range(4)]
+
+
+def retention_back_kernel(
+    da_ref, wo_ref, gated_ref, gate_ref, ret_ref, q_ref, k_ref, v_ref, s_ref, cos_ref, sin_ref,
+    ccol_ref, crow_ref, scal_ref, xg_ref, fu_ref, fd_ref,
+    dh, sums, f1,
+    da, wo, gated, gr, q, k, v, st, cos, sin, dr, xt, ao, ag, rxo, rxg, fin, qo, gb, lg, got, logs, rxf, fo, pbuf, gbuf,
+    lsem, gsem, xsem, fsend, frecv, osem, fosem, ssend, srecv, lsend, lrecv, psend, precv, *line,
+):
+    me = Place()
+    z, p = me.z, me.p
+    greet(
+        [(me.plane(m), None) for m in (1, 2, 3)]
+        + [(me.at((z + t) % LINE, p, me.f), None) for t in range(1, LINE)]
+    )
+    width = da.shape[1]
+    tokens = da.shape[0]
+    keys, values = q.shape[1], v.shape[1]
+    blocks = tokens // STRETCH
+    half = keys // 2
+    pq = [me.xor(m) for m in range(4)]
+    chunk = fu_ref.shape[0] // SPANS
+
+    def f_block(h, zp, place):
+        return (fu_ref, fd_ref)[h].at[pl.ds(pl.multiple_of((zp * PLANE + place) * chunk, chunk), chunk), :]
+
+    away = ((1, 3), (2, 3))
+    kept = ((0, 2), (0, 1))
+    nbr = (1, 2)
+
+    def f_copy(h, zp, j):
+        return remote(
+            f_block(h, zp, pq[away[h][j]]), rxf.at[h, zp, j], fsend.at[h, zp, j], frecv.at[h, zp, j], me.plane(nbr[h])
+        )
+
+    loads = [
+        start(pltpu.make_async_copy(a, b, lsem.at[i]))
+        for i, (a, b) in enumerate(
+            [(da_ref, da), (gated_ref, gated), (wo_ref, wo), (q_ref, q), (k_ref, k), (v_ref, v), (s_ref, st),
+             (cos_ref, cos), (sin_ref, sin)]
+        )
+    ]
+    for zp in range(LINE):
+        for h in range(2):
+            for j in range(2):
+                f_copy(h, zp, j).start()
+
+    def f_own(u):
+        h, zp = u % 2, u // 2
+        return [
+            pltpu.make_async_copy(f_block(h, zp, pq[kept[h][j]]), fo.at[u % 2, j], fosem.at[u % 2, j])
+            for j in range(2)
+        ]
+
+    def f_out(u):
+        h, zp = u % 2, u // 2
+        return pltpu.make_async_copy(rxf.at[h, zp], f1.at[h, zp], osem.at[u])
+
+    for u in range(2):
+        for c in f_own(u):
+            c.start()
+
+    def f_unit(u):
+        h, zp = u % 2, u // 2
+        for j, c in enumerate(f_own(u)):
+            c.wait()
+            f_copy(h, zp, j).wait_recv()
+            add_rows(rxf.at[h, zp, j], fo.at[u % 2, j])
+        f_out(u).start()
+        if u + 2 < 2 * LINE:
+            for c in f_own(u + 2):
+                c.start()
+
+    def tile_rows(i):
+        return rows_at(i * 256, 256)
+
+    def gate_loads(i):
+        at = tile_rows(i)
+        slot = i % 2
+        return (
+            pltpu.make_async_copy(gate_ref.at[at, :], gr.at[slot, 0], gsem.at[slot, 0]),
+            pltpu.make_async_copy(ret_ref.at[at, :], gr.at[slot, 1], gsem.at[slot, 1]),
+        )
+
+    for c in gate_loads(0):
+        c.start()
+
+    out_sum = LineSum(me, lambda zz: ao.at[rows_at(zz * (width // LINE), width // LINE), :], rxo, *line[:4], add_rows)
+    gate_sum = LineSum(me, lambda zz: ag.at[rows_at(zz * (width // LINE), width // LINE), :], rxg, *line[4:], add_rows)
+
+    loads[0].wait()
+    loads[1].wait()
+
+    @pl.loop(0, width, step=256)
+    def _(i):
+        at = rows_at(i, 256)
+        ao[at, :] = tn(da[:, at], gated[...]).astype(BF16)
+
+    out_sum.begin()
+    for c in loads[2:]:
+        c.wait()
+
+    tiles = tokens // 256
+
+    @pl.loop(0, tiles)
+    def _(i):
+        @pl.when(i + 1 < tiles)
+        def _():
+            for c in gate_loads(i + 1):
+                c.start()
+
+        for c in gate_loads(i):
+            c.wait()
+        at = tile_rows(i)
+        slot = i % 2
+        dgated = nt(da[at, :], wo[...])
+        gate = gr[slot, 0]
+        ret = gr[slot, 1]
+        centered = ret - jnp.mean(ret, axis=1, keepdims=True)
+        scale = lax.rsqrt(jnp.mean(centered * centered, axis=1, keepdims=True) + 1e-05)
+        grouped = centered * scale
+        sig = 1.0 / (1.0 + jnp.exp(-gate))
+        silu = gate * sig
+        dh[at, 2 * keys + values :] = (dgated * grouped * (sig * (1.0 + gate * (1.0 - sig)))).astype(BF16)
+        dg = dgated * silu
+        dr[at, :] = (
+            scale * (dg - jnp.mean(dg, axis=1, keepdims=True) - grouped * jnp.mean(dg * grouped, axis=1, keepdims=True))
+        ).astype(BF16)
+
+    lg[...] = jnp.zeros_like(lg)
+
+    @pl.loop(0, blocks)
+    def _(c):
+        at = rows_at(c * STRETCH, STRETCH)
+        decayed = (q[at, :].astype(F32) * jnp.exp(ccol_ref[at, :])).astype(BF16)
+        got_q = tn(decayed, dr[at, :])
+        qo[c] = got_q
+        lg[...] += scal_ref[blocks + c, 0:1, 0:1] * got_q
+
+    gb[0] = lg[...].astype(BF16)
+
+    def state_copies(t, to, slot):
+        device = me.at(to, p, me.f)
+        return (
+            remote(gb.at[0], got.at[slot], ssend.at[t - 1], srecv.at[t - 1], device),
+            remote(scal_ref.at[2 * blocks], logs.at[slot], lsend.at[t - 1], lrecv.at[t - 1], device),
+        )
+
+    for t in range(1, LINE):
+
+        @pl.when(z - t >= 0)
+        def _():
+            for c in state_copies(t, z - t, z):
+                c.start()
+
+    def x_tile(i):
+        return pltpu.make_async_copy(xg_ref.at[:, rows_at(i * 256, 256)], xt.at[i % 2], xsem.at[i % 2])
+
+    x_tile(0).start()
+
+    @pl.loop(0, width // 256)
+    def _(i):
+        @pl.when(i + 1 < width // 256)
+        def _():
+            x_tile(i + 1).start()
+
+        x_tile(i).wait()
+        ag[rows_at(i * 256, 256), :] = tn(xt[i % 2], dh[:, 2 * keys + values :]).astype(BF16)
+
+    gate_sum.begin()
+    out_sum.step(0)
+    f_unit(0)
+    f_unit(1)
+    out_sum.step(1)
+
+    for t in range(1, LINE):
+
+        @pl.when(z + t < LINE)
+        def _():
+            for c in state_copies(t, z + t, z + t):
+                c.wait_recv()
+
+        @pl.when(z - t >= 0)
+        def _():
+            for c in state_copies(t, z - t, z):
+                c.wait_send()
+
+    lg[...] = jnp.zeros_like(lg)
+    for j in reversed(range(1, LINE)):
+
+        @pl.when(z < j)
+        def _():
+            lg[...] = lg[...] * jnp.exp(logs[j, 0:1, 0:1]) + got[j].astype(F32)
+
+    for c in reversed(range(blocks)):
+        gb[c] = lg[...].astype(BF16)
+        if c:
+            lg[...] = lg[...] * scal_ref[c, 0:1, 0:1] + qo[c]
+
+    t_size = 256
+
+    @pl.loop(0, blocks)
+    def _(c):
+        blk = rows_at(c * STRETCH, STRETCH)
+        row = crow_ref[c, 0:1, :]
+        end = crow_ref[c, 0:1, STRETCH - 1 : STRETCH]
+        for r in range(0, STRETCH, t_size):
+            at = rows_at(c * STRETCH + r, t_size)
+            col = ccol_ref[at, :]
+            t_index = lax.broadcasted_iota(jnp.int32, (t_size, STRETCH), 0) + r
+            s_index = lax.broadcasted_iota(jnp.int32, (t_size, STRETCH), 1)
+            mask = jnp.where(t_index >= s_index, jnp.exp(jnp.minimum(col - row, 0.0)), 0.0)
+            pbuf[r : r + t_size, :] = (nt(q[at, :], k[blk, :]) * mask).astype(BF16)
+            g = (nt(dr[at, :], v[blk, :]) * mask).astype(BF16)
+            gbuf[r : r + t_size, :] = g
+            dq = nt(dr[at, :], st[c]) * jnp.exp(col) + nn(g, k[blk, :])
+            a, b = dq[:, :half], dq[:, half:]
+            dh[at, :half] = (a * cos[at, :] + b * sin[at, :]).astype(BF16)
+            dh[at, half:keys] = (b * cos[at, :] - a * sin[at, :]).astype(BF16)
+        for r in range(0, STRETCH, t_size):
+            at = rows_at(c * STRETCH + r, t_size)
+            tail = jnp.exp(end - ccol_ref[at, :])
+            w = (v[at, :].astype(F32) * tail).astype(BF16)
+            dk = nt(w, gb[c]) + tn(gbuf[:, r : r + t_size], q[blk, :])
+            a, b = dk[:, :half], dk[:, half:]
+            dh[at, keys : keys + half] = (a * cos[at, :] + b * sin[at, :]).astype(BF16)
+            dh[at, keys + half : 2 * keys] = (b * cos[at, :] - a * sin[at, :]).astype(BF16)
+            dv = nn(k[at, :], gb[c]) * tail + tn(pbuf[:, r : r + t_size], dr[blk, :])
+            dh[at, 2 * keys : 2 * keys + values] = dv.astype(BF16)
+
+    plane = []
+
+    def deal(i, chain, a):
+        chain.arrive()
+        total_rows(z, fin.at[i], a.at[rows_at(z * (width // LINE), width // LINE), :], chain.rx)
+        cols = pl.ds(i * values, values)
+        for m in (1, 2, 3):
+            plane.append(
+                start(
+                    remote(
+                        fin.at[i, rows_at(pq[m] * chunk, chunk), :], sums.at[p, :, cols],
+                        psend.at[i, m], precv.at[i, m], me.plane(m),
+                    )
+                )
+            )
+        plane.append(
+            start(
+                pltpu.make_async_copy(
+                    fin.at[i, rows_at(p * chunk, chunk), :], sums.at[p, :, cols], psend.at[i, 0]
+                )
+            )
+        )
+
+    out_sum.step(2)
+    for u in range(2, 4):
+        f_unit(u)
+    gate_sum.step(0)
+    deal(0, out_sum, ao)
+    gate_sum.step(1)
+    for u in range(4, 6):
+        f_unit(u)
+    gate_sum.step(2)
+    deal(1, gate_sum, ag)
+    for u in range(6, 2 * LINE):
+        f_unit(u)
+    for c in plane:
+        c.wait()
+    out_sum.finish()
+    gate_sum.finish()
+    for u in range(2 * LINE):
+        f_out(u).wait()
+    for zp in range(LINE):
+        for h in range(2):
+            for j in range(2):
+                f_copy(h, zp, j).wait_send()
+
+
+def retention_back(da, wo, gated, gate, ret, q, k, v, states, cos, sin, ccol, crow, scal, xg, fu, fd, cid):
+    tokens, width = da.shape
+    keys, values = q.shape[1], v.shape[1]
+    chunk = width // SPANS
+    blocks = tokens // STRETCH
+    hidden = fu.shape[1]
+    deep = width // LINE
+    return comm_call(
+        retention_back_kernel,
+        [
+            jax.ShapeDtypeStruct((tokens, 2 * keys + 2 * values), BF16),
+            jax.ShapeDtypeStruct((PLANE, chunk, 2 * values), BF16),
+            jax.ShapeDtypeStruct((2, LINE, 2, chunk, hidden), BF16),
+        ],
+        [da, wo, gated, gate, ret, q, k, v, states, cos, sin, ccol, crow, scal, xg, fu, fd],
+        [
+            pltpu.VMEM((tokens, width), BF16),
+            pltpu.VMEM(wo.shape, BF16),
+            pltpu.VMEM(gated.shape, BF16),
+            pltpu.VMEM((2, 2, 256, values), F32),
+            pltpu.VMEM(q.shape, BF16),
+            pltpu.VMEM(k.shape, BF16),
+            pltpu.VMEM(v.shape, BF16),
+            pltpu.VMEM(states.shape, BF16),
+            pltpu.VMEM(cos.shape, F32),
+            pltpu.VMEM(sin.shape, F32),
+            pltpu.VMEM((tokens, values), BF16),
+            pltpu.VMEM((2, tokens, 256), BF16),
+            pltpu.VMEM((width, values), BF16),
+            pltpu.VMEM((width, values), BF16),
+            pltpu.VMEM((LINE + 1, deep, values), BF16),
+            pltpu.VMEM((LINE + 1, deep, values), BF16),
+            pltpu.VMEM((2, deep, values), BF16),
+            pltpu.VMEM((blocks, keys, values), F32),
+            pltpu.VMEM((blocks, keys, values), BF16),
+            pltpu.VMEM((keys, values), F32),
+            pltpu.VMEM((LINE, keys, values), BF16),
+            pltpu.VMEM((LINE, 8, 128), F32),
+            pltpu.VMEM((2, LINE, 2, chunk, hidden), BF16),
+            pltpu.VMEM((2, 2, chunk, hidden), BF16),
+            pltpu.VMEM((STRETCH, STRETCH), BF16),
+            pltpu.VMEM((STRETCH, STRETCH), BF16),
+            DMA((9,)),
+            DMA((2, 2)),
+            DMA((2,)),
+            DMA((2, LINE, 2)),
+            DMA((2, LINE, 2)),
+            DMA((2 * LINE,)),
+            DMA((2, 2)),
+            DMA((LINE - 1,)),
+            DMA((LINE - 1,)),
+            DMA((LINE - 1,)),
+            DMA((LINE - 1,)),
+            DMA((2, PLANE)),
+            DMA((2, PLANE)),
+        ]
+        + line_sems()
+        + line_sems(),
+        cid,
+        in_specs=[ANY] * 11 + [VM] * 3 + [ANY] * 3,
+        out_specs=[VM, ANY, ANY],
+    )
+
+
+class LineSum:
+    def __init__(self, me, own, rx, usend, urecv, dsend, drecv, add):
+        self.me, self.own, self.rx, self.add = me, own, rx, add
+        self.sems = usend, urecv, dsend, drecv
+
+    def up(self, src, zz):
+        return remote(src, self.rx.at[zz], self.sems[0].at[zz], self.sems[1].at[zz], self.me.up())
+
+    def down(self, src, zz):
+        slot = jnp.where(zz == self.me.z - 1, LINE, zz)
+        return remote(src, self.rx.at[slot], self.sems[2].at[zz], self.sems[3].at[zz], self.me.down())
+
+    def begin(self):
+        for zz in reversed(range(1, LINE)):
+
+            @pl.when(self.me.z == 0)
+            def _():
+                self.up(self.own(zz), zz).start()
+
+            @pl.when(self.me.z == LINE - 1)
+            def _():
+                self.down(self.own(LINE - 1 - zz), LINE - 1 - zz).start()
+
+    def step(self, t):
+        z = self.me.z
+        zu, zd = LINE - 1 - t, t
+
+        @pl.when((z > 0) & (z < zu))
+        def _():
+            self.up(self.own(zu), zu).wait_recv()
+            self.add(self.rx.at[zu], self.own(zu))
+            self.up(self.rx.at[zu], zu).start()
+
+        @pl.when((z < LINE - 1) & (z > zd))
+        def _():
+            self.down(self.own(zd), zd).wait_recv()
+            self.add(self.rx.at[zd], self.own(zd))
+            self.down(self.rx.at[zd], zd).start()
+
+    def arrive(self):
+        z = self.me.z
+
+        @pl.when(z > 0)
+        def _():
+            self.up(self.own(z), z).wait_recv()
+
+        @pl.when(z < LINE - 1)
+        def _():
+            self.down(self.own(z), z).wait_recv()
+
+    def finish(self):
+        z = self.me.z
+        for zz in range(LINE):
+
+            @pl.when((z < LINE - 1) & (zz > z))
+            def _():
+                self.up(self.own(zz), zz).wait_send()
+
+            @pl.when((z > 0) & (zz < z))
+            def _():
+                self.down(self.own(zz), zz).wait_send()
+
+
+def add_rows(dst, src):
+    rows = dst.shape[0]
+    step = 32 if dst.shape[1] > 512 else 128
+
+    @pl.loop(0, rows, step=step)
+    def _(r):
+        at = rows_at(r, step)
+        dst[at, :] = (dst[at, :].astype(F32) + src[at, :].astype(F32)).astype(BF16)
+
+
+def total_rows(z, dst, own, rx):
+    rows = dst.shape[0]
+    step = 32 if dst.shape[1] > 512 else 128
+
+    @pl.loop(0, rows, step=step)
+    def _(r):
+        at = rows_at(r, step)
+        v = own[at, :].astype(F32)
+        v = v + jnp.where(z > 0, rx[z, at, :].astype(F32), 0.0)
+        v = v + jnp.where(z < LINE - 1, rx[LINE, at, :].astype(F32), 0.0)
+        dst[at, :] = v.astype(dst.dtype)
+
+
+def line_sems():
+    return [DMA((LINE,)) for _ in range(4)]
+
+
+def retention_back_kernel(
+    da_ref, wo_ref, gated_ref, gate_ref, ret_ref, q_ref, k_ref, v_ref, s_ref, cos_ref, sin_ref,
+    ccol_ref, crow_ref, scal_ref, xg_ref, fu_ref, fd_ref,
+    dh, sums, f1,
+    da, wo, gated, gr, q, k, v, st, cos, sin, dr, xt, ao, ag, rxo, rxg, fin, qo, gb, lg, got, logs, rxf, fo, pbuf, gbuf,
+    lsem, gsem, xsem, fsend, frecv, osem, fosem, ssend, srecv, lsend, lrecv, psend, precv, *line,
+):
+    me = Place()
+    z, p = me.z, me.p
+    greet(
+        [(me.plane(m), None) for m in (1, 2, 3)]
+        + [(me.at((z + t) % LINE, p, me.f), None) for t in range(1, LINE)]
+    )
+    width = da.shape[1]
+    tokens = da.shape[0]
+    keys, values = q.shape[1], v.shape[1]
+    blocks = tokens // STRETCH
+    half = keys // 2
+    pq = [me.xor(m) for m in range(4)]
+    chunk = fu_ref.shape[0] // SPANS
+
+    def f_block(h, zp, place):
+        return (fu_ref, fd_ref)[h].at[pl.ds(pl.multiple_of((zp * PLANE + place) * chunk, chunk), chunk), :]
+
+    away = ((1, 3), (2, 3))
+    kept = ((0, 2), (0, 1))
+    nbr = (1, 2)
+
+    def f_copy(h, zp, j):
+        return remote(
+            f_block(h, zp, pq[away[h][j]]), rxf.at[h, zp, j], fsend.at[h, zp, j], frecv.at[h, zp, j], me.plane(nbr[h])
+        )
+
+    loads = [
+        start(pltpu.make_async_copy(a, b, lsem.at[i]))
+        for i, (a, b) in enumerate(
+            [(da_ref, da), (gated_ref, gated), (wo_ref, wo), (q_ref, q), (k_ref, k), (v_ref, v), (s_ref, st),
+             (cos_ref, cos), (sin_ref, sin)]
+        )
+    ]
+    for zp in range(LINE):
+        for h in range(2):
+            for j in range(2):
+                f_copy(h, zp, j).start()
+
+    def f_own(u):
+        h, zp = u % 2, u // 2
+        return [
+            pltpu.make_async_copy(f_block(h, zp, pq[kept[h][j]]), fo.at[u % 2, j], fosem.at[u % 2, j])
+            for j in range(2)
+        ]
+
+    def f_out(u):
+        h, zp = u % 2, u // 2
+        return pltpu.make_async_copy(rxf.at[h, zp], f1.at[h, zp], osem.at[u])
+
+    for u in range(2):
+        for c in f_own(u):
+            c.start()
+
+    def f_unit(u):
+        h, zp = u % 2, u // 2
+        for j, c in enumerate(f_own(u)):
+            c.wait()
+            f_copy(h, zp, j).wait_recv()
+            add_rows(rxf.at[h, zp, j], fo.at[u % 2, j])
+        f_out(u).start()
+        if u + 2 < 2 * LINE:
+            for c in f_own(u + 2):
+                c.start()
+
+    def tile_rows(i):
+        return rows_at(i * 256, 256)
+
+    def gate_loads(i):
+        at = tile_rows(i)
+        slot = i % 2
+        return (
+            pltpu.make_async_copy(gate_ref.at[at, :], gr.at[slot, 0], gsem.at[slot, 0]),
+            pltpu.make_async_copy(ret_ref.at[at, :], gr.at[slot, 1], gsem.at[slot, 1]),
+        )
+
+    for c in gate_loads(0):
+        c.start()
+
+    out_sum = LineSum(me, lambda zz: ao.at[rows_at(zz * (width // LINE), width // LINE), :], rxo, *line[:4], add_rows)
+    gate_sum = LineSum(me, lambda zz: ag.at[rows_at(zz * (width // LINE), width // LINE), :], rxg, *line[4:], add_rows)
+
+    loads[0].wait()
+    loads[1].wait()
+
+    @pl.loop(0, width, step=256)
+    def _(i):
+        at = rows_at(i, 256)
+        ao[at, :] = tn(da[:, at], gated[...]).astype(BF16)
+
+    out_sum.begin()
+    for c in loads[2:]:
+        c.wait()
+
+    tiles = tokens // 256
+
+    @pl.loop(0, tiles)
+    def _(i):
+        @pl.when(i + 1 < tiles)
+        def _():
+            for c in gate_loads(i + 1):
+                c.start()
+
+        for c in gate_loads(i):
+            c.wait()
+        at = tile_rows(i)
+        slot = i % 2
+        dgated = nt(da[at, :], wo[...])
+        gate = gr[slot, 0]
+        ret = gr[slot, 1]
+        centered = ret - jnp.mean(ret, axis=1, keepdims=True)
+        scale = lax.rsqrt(jnp.mean(centered * centered, axis=1, keepdims=True) + 1e-05)
+        grouped = centered * scale
+        sig = 1.0 / (1.0 + jnp.exp(-gate))
+        silu = gate * sig
+        dh[at, 2 * keys + values :] = (dgated * grouped * (sig * (1.0 + gate * (1.0 - sig)))).astype(BF16)
+        dg = dgated * silu
+        dr[at, :] = (
+            scale * (dg - jnp.mean(dg, axis=1, keepdims=True) - grouped * jnp.mean(dg * grouped, axis=1, keepdims=True))
+        ).astype(BF16)
+
+    lg[...] = jnp.zeros_like(lg)
+
+    @pl.loop(0, blocks)
+    def _(c):
+        at = rows_at(c * STRETCH, STRETCH)
+        decayed = (q[at, :].astype(F32) * jnp.exp(ccol_ref[at, :])).astype(BF16)
+        got_q = tn(decayed, dr[at, :])
+        qo[c] = got_q
+        lg[...] += scal_ref[blocks + c, 0:1, 0:1] * got_q
+
+    gb[0] = lg[...].astype(BF16)
+
+    def state_copies(t, to, slot):
+        device = me.at(to, p, me.f)
+        return (
+            remote(gb.at[0], got.at[slot], ssend.at[t - 1], srecv.at[t - 1], device),
+            remote(scal_ref.at[2 * blocks], logs.at[slot], lsend.at[t - 1], lrecv.at[t - 1], device),
+        )
+
+    for t in range(1, LINE):
+
+        @pl.when(z - t >= 0)
+        def _():
+            for c in state_copies(t, z - t, z):
+                c.start()
+
+    def x_tile(i):
+        return pltpu.make_async_copy(xg_ref.at[:, rows_at(i * 256, 256)], xt.at[i % 2], xsem.at[i % 2])
+
+    x_tile(0).start()
+
+    @pl.loop(0, width // 256)
+    def _(i):
+        @pl.when(i + 1 < width // 256)
+        def _():
+            x_tile(i + 1).start()
+
+        x_tile(i).wait()
+        ag[rows_at(i * 256, 256), :] = tn(xt[i % 2], dh[:, 2 * keys + values :]).astype(BF16)
+
+    gate_sum.begin()
+    out_sum.step(0)
+    f_unit(0)
+    f_unit(1)
+    out_sum.step(1)
+
+    for t in range(1, LINE):
+
+        @pl.when(z + t < LINE)
+        def _():
+            for c in state_copies(t, z + t, z + t):
+                c.wait_recv()
+
+        @pl.when(z - t >= 0)
+        def _():
+            for c in state_copies(t, z - t, z):
+                c.wait_send()
+
+    lg[...] = jnp.zeros_like(lg)
+    for j in reversed(range(1, LINE)):
+
+        @pl.when(z < j)
+        def _():
+            lg[...] = lg[...] * jnp.exp(logs[j, 0:1, 0:1]) + got[j].astype(F32)
+
+    for c in reversed(range(blocks)):
+        gb[c] = lg[...].astype(BF16)
+        if c:
+            lg[...] = lg[...] * scal_ref[c, 0:1, 0:1] + qo[c]
+
+    t_size = 256
+
+    @pl.loop(0, blocks)
+    def _(c):
+        blk = rows_at(c * STRETCH, STRETCH)
+        row = crow_ref[c, 0:1, :]
+        end = crow_ref[c, 0:1, STRETCH - 1 : STRETCH]
+        for r in range(0, STRETCH, t_size):
+            at = rows_at(c * STRETCH + r, t_size)
+            col = ccol_ref[at, :]
+            t_index = lax.broadcasted_iota(jnp.int32, (t_size, STRETCH), 0) + r
+            s_index = lax.broadcasted_iota(jnp.int32, (t_size, STRETCH), 1)
+            mask = jnp.where(t_index >= s_index, jnp.exp(jnp.minimum(col - row, 0.0)), 0.0)
+            pbuf[r : r + t_size, :] = (nt(q[at, :], k[blk, :]) * mask).astype(BF16)
+            g = (nt(dr[at, :], v[blk, :]) * mask).astype(BF16)
+            gbuf[r : r + t_size, :] = g
+            dq = nt(dr[at, :], st[c]) * jnp.exp(col) + nn(g, k[blk, :])
+            a, b = dq[:, :half], dq[:, half:]
+            dh[at, :half] = (a * cos[at, :] + b * sin[at, :]).astype(BF16)
+            dh[at, half:keys] = (b * cos[at, :] - a * sin[at, :]).astype(BF16)
+        for r in range(0, STRETCH, t_size):
+            at = rows_at(c * STRETCH + r, t_size)
+            tail = jnp.exp(end - ccol_ref[at, :])
+            w = (v[at, :].astype(F32) * tail).astype(BF16)
+            dk = nt(w, gb[c]) + tn(gbuf[:, r : r + t_size], q[blk, :])
+            a, b = dk[:, :half], dk[:, half:]
+            dh[at, keys : keys + half] = (a * cos[at, :] + b * sin[at, :]).astype(BF16)
+            dh[at, keys + half : 2 * keys] = (b * cos[at, :] - a * sin[at, :]).astype(BF16)
+            dv = nn(k[at, :], gb[c]) * tail + tn(pbuf[:, r : r + t_size], dr[blk, :])
+            dh[at, 2 * keys : 2 * keys + values] = dv.astype(BF16)
+
+    plane = []
+
+    def deal(i, chain, a):
+        chain.arrive()
+        total_rows(z, fin.at[i], a.at[rows_at(z * (width // LINE), width // LINE), :], chain.rx)
+        cols = pl.ds(i * values, values)
+        for m in (1, 2, 3):
+            plane.append(
+                start(
+                    remote(
+                        fin.at[i, rows_at(pq[m] * chunk, chunk), :], sums.at[p, :, cols],
+                        psend.at[i, m], precv.at[i, m], me.plane(m),
+                    )
+                )
+            )
+        plane.append(
+            start(
+                pltpu.make_async_copy(
+                    fin.at[i, rows_at(p * chunk, chunk), :], sums.at[p, :, cols], psend.at[i, 0]
+                )
+            )
+        )
+
+    out_sum.step(2)
+    for u in range(2, 4):
+        f_unit(u)
+    gate_sum.step(0)
+    deal(0, out_sum, ao)
+    gate_sum.step(1)
+    for u in range(4, 6):
+        f_unit(u)
+    gate_sum.step(2)
+    deal(1, gate_sum, ag)
+    for u in range(6, 2 * LINE):
+        f_unit(u)
+    for c in plane:
+        c.wait()
+    out_sum.finish()
+    gate_sum.finish()
+    for u in range(2 * LINE):
+        f_out(u).wait()
+    for zp in range(LINE):
+        for h in range(2):
+            for j in range(2):
+                f_copy(h, zp, j).wait_send()
+
+
+def retention_back(da, wo, gated, gate, ret, q, k, v, states, cos, sin, ccol, crow, scal, xg, fu, fd, cid):
+    tokens, width = da.shape
+    keys, values = q.shape[1], v.shape[1]
+    chunk = width // SPANS
+    blocks = tokens // STRETCH
+    hidden = fu.shape[1]
+    deep = width // LINE
+    return comm_call(
+        retention_back_kernel,
+        [
+            jax.ShapeDtypeStruct((tokens, 2 * keys + 2 * values), BF16),
+            jax.ShapeDtypeStruct((PLANE, chunk, 2 * values), BF16),
+            jax.ShapeDtypeStruct((2, LINE, 2, chunk, hidden), BF16),
+        ],
+        [da, wo, gated, gate, ret, q, k, v, states, cos, sin, ccol, crow, scal, xg, fu, fd],
+        [
+            pltpu.VMEM((tokens, width), BF16),
+            pltpu.VMEM(wo.shape, BF16),
+            pltpu.VMEM(gated.shape, BF16),
+            pltpu.VMEM((2, 2, 256, values), F32),
+            pltpu.VMEM(q.shape, BF16),
+            pltpu.VMEM(k.shape, BF16),
+            pltpu.VMEM(v.shape, BF16),
+            pltpu.VMEM(states.shape, BF16),
+            pltpu.VMEM(cos.shape, F32),
+            pltpu.VMEM(sin.shape, F32),
+            pltpu.VMEM((tokens, values), BF16),
+            pltpu.VMEM((2, tokens, 256), BF16),
+            pltpu.VMEM((width, values), BF16),
+            pltpu.VMEM((width, values), BF16),
+            pltpu.VMEM((LINE + 1, deep, values), BF16),
+            pltpu.VMEM((LINE + 1, deep, values), BF16),
+            pltpu.VMEM((2, deep, values), BF16),
+            pltpu.VMEM((blocks, keys, values), F32),
+            pltpu.VMEM((blocks, keys, values), BF16),
+            pltpu.VMEM((keys, values), F32),
+            pltpu.VMEM((LINE, keys, values), BF16),
+            pltpu.VMEM((LINE, 8, 128), F32),
+            pltpu.VMEM((2, LINE, 2, chunk, hidden), BF16),
+            pltpu.VMEM((2, 2, chunk, hidden), BF16),
+            pltpu.VMEM((STRETCH, STRETCH), BF16),
+            pltpu.VMEM((STRETCH, STRETCH), BF16),
+            DMA((9,)),
+            DMA((2, 2)),
+            DMA((2,)),
+            DMA((2, LINE, 2)),
+            DMA((2, LINE, 2)),
+            DMA((2 * LINE,)),
+            DMA((2, 2)),
+            DMA((LINE - 1,)),
+            DMA((LINE - 1,)),
+            DMA((LINE - 1,)),
+            DMA((LINE - 1,)),
+            DMA((2, PLANE)),
+            DMA((2, PLANE)),
+        ]
+        + line_sems()
+        + line_sems(),
+        cid,
+        in_specs=[ANY] * 11 + [VM] * 3 + [ANY] * 3,
+        out_specs=[VM, ANY, ANY],
+    )
+
+
 def everyone(size):
     return range(0, size, SPANS)
 
@@ -750,19 +1524,6 @@
     return take(x, z, 0).astype(F32) + up.astype(F32) + dn.astype(F32)
 
 
-def plane_sum(x, p, first):
-    here = (p // 2, p % 2)
-    if first == 1:
-        kept, sent = take(x, here[1], 2), take(x, 1 - here[1], 2)
-        x = plus(kept, swap(sent, 1))
-        kept, sent = take(x, here[0], 1), take(x, 1 - here[0], 1)
-        return plus(kept, swap(sent, 2))
-    kept, sent = take(x, here[0], 1), take(x, 1 - here[0], 1)
-    x = plus(kept, swap(sent, 2))
-    kept, sent = take(x, here[1], 1), take(x, 1 - here[1], 1)
-    return plus(kept, swap(sent, 1))
-
-
 def plane_deal(x, p):
     got = [take(x, p, 0)]
     for mask in range(1, PLANE):
@@ -810,6 +1571,283 @@
         in_specs=[VM],
         out_specs=[VM],
     )[0]
+
+
+def last_kernel(
+    dh_ref, xg_ref, wq_ref, wk_ref, wv_ref, wg_ref, f1_ref, tok_ref, gain_ref, resid_ref, second_ref,
+    grad_tokens, gains, fout, sums,
+    dh, xt, wh, share, rx0, rx1a, rx1b, rx2a, rx2b, av, aq, rxv, rxq, fin, rf2, kf, rxfa, rxfb, grx,
+    lsem, xsem, fsend, frecv, csend, crecv, xsend, xrecv, gsend, grecv, psend, precv, *line,
+):
+    me = Place()
+    z, p, f = me.z, me.p, me.f
+    rounds = [
+        [me.partner()],
+        [me.plane(m) for m in (1, 2, 3)],
+        [me.at((z + t) % LINE, p, f) for t in range(1, LINE)],
+    ]
+    greet([(d, None) for r in rounds for d in r])
+    width, keys2, values = xg_ref.shape[1], aq.shape[1], av.shape[1]
+    rows = tok_ref.shape[0]
+    pq = [me.xor(m) for m in range(4)]
+    chunk = width // SPANS
+    deep = width // LINE
+
+    def f_copy(h, zp):
+        return remote(f1_ref.at[h, zp, 1], rf2.at[h, zp], fsend.at[h, zp], frecv.at[h, zp], me.plane(2 - h))
+
+    def x_tile(i):
+        return pltpu.make_async_copy(xg_ref.at[:, rows_at(i * 256, 256)], xt.at[i % 2], xsem.at[i % 2])
+
+    load = start(pltpu.make_async_copy(dh_ref, dh, lsem.at[0]))
+    x_tile(0).start()
+    for zp in (3, 0, 2, 1):
+        for h in range(2):
+            f_copy(h, zp).start()
+    loads, at = [], 0
+    for i, w in enumerate((wq_ref, wk_ref, wv_ref, wg_ref)):
+        size = w.shape[1]
+        loads.append(start(pltpu.make_async_copy(w, wh.at[:, at : at + size], lsem.at[1 + i])))
+        at += size
+    keeps = [start(pltpu.make_async_copy(f1_ref.at[h, :, 0], kf.at[h], lsem.at[5 + h])) for h in range(2)]
+
+    def block_of(a, size):
+        return lambda zz: a.at[rows_at(zz * size, size), :]
+
+    v_sum = LineSum(me, block_of(av, deep), rxv, *line[:4], add_rows)
+    q_sum = LineSum(me, block_of(aq, deep), rxq, *line[4:8], add_rows)
+    fa_sum = LineSum(me, lambda zz: kf.at[0, zz], rxfa, *line[8:12], add_rows)
+    fb_sum = LineSum(me, lambda zz: kf.at[1, zz], rxfb, *line[12:16], add_rows)
+    load.wait()
+    tiles = width // 256
+    for out, cols, chain in ((av, pl.ds(keys2, values), v_sum), (aq, pl.ds(0, keys2), q_sum)):
+        if chain is q_sum:
+            x_tile(0).start()
+
+        @pl.loop(0, tiles)
+        def _(i):
+            @pl.when(i + 1 < tiles)
+            def _():
+                x_tile(i + 1).start()
+
+            x_tile(i).wait()
+            out[rows_at(i * 256, 256), :] = tn(xt[i % 2], dh[:, cols]).astype(BF16)
+
+        chain.begin()
+    for c in loads:
+        c.wait()
+
+    own_rows, their_rows = rows_at(f * rows, rows), rows_at((1 - f) * rows, rows)
+    wide = width // 2
+    ca, cb = pl.ds(0, wide), pl.ds(wide, wide)
+    everything, whole = pl.ds(0, width), pl.ds(0, wide)
+    first, sends = {}, {}
+
+    def share_part(m):
+        at_rows = rows_at(pq[m] * 2 * rows, 2 * rows)
+
+        @pl.loop(0, width, step=256)
+        def _(c):
+            at = rows_at(c, 256)
+            share[m, :, at] = nt(dh[at_rows, :], wh[at, :]).astype(BF16)
+
+        first[m] = start(
+            remote(share.at[m, their_rows], rx0.at[m], csend.at[m], crecv.at[m], me.partner())
+        )
+
+    def pass_on(m):
+        first[m].wait_recv()
+        add_into(rx0.at[m], everything, share.at[m, own_rows], everything)
+        k = 0 if m == 3 else 1
+        if m & 1:
+            sends["a", k] = start(
+                remote(rx0.at[m, :, ca], rx1a.at[k], xsend.at[k], xrecv.at[k], me.plane(1))
+            )
+        if m & 2:
+            sends["b", k] = start(
+                remote(rx0.at[m, :, cb], rx1b.at[k], xsend.at[2 + k], xrecv.at[2 + k], me.plane(2))
+            )
+
+    share_part(3)
+    share_part(1)
+    pass_on(3)
+    share_part(2)
+    pass_on(1)
+    share_part(0)
+    pass_on(2)
+    pass_on(0)
+    v_sum.step(0)
+    sends["a", 0].wait_recv()
+    add_into(rx1a.at[0], whole, rx0.at[2], ca)
+    s2a = start(remote(rx1a.at[0], rx2a, xsend.at[4], xrecv.at[4], me.plane(2)))
+    sends["b", 0].wait_recv()
+    add_into(rx1b.at[0], whole, rx0.at[1], cb)
+    s2b = start(remote(rx1b.at[0], rx2b, xsend.at[5], xrecv.at[5], me.plane(1)))
+    v_sum.step(1)
+    for c in keeps:
+        c.wait()
+    for zp in (3, 0, 2, 1):
+        for h in range(2):
+            f_copy(h, zp).wait_recv()
+            add_rows(kf.at[h, zp], rf2.at[h, zp])
+    fa_sum.begin()
+    fb_sum.begin()
+    v_sum.step(2)
+    q_sum.step(0)
+    sends["a", 1].wait_recv()
+    sends["b", 1].wait_recv()
+    s2a.wait_recv()
+    s2b.wait_recv()
+    gains[...] = jnp.zeros_like(gains)
+    gains[2:4, :] = second_ref[0:2, :]
+    step = 32
+
+    @pl.loop(0, rows, step=step)
+    def _(r):
+        at = rows_at(r, step)
+        left = rx0[0, at, ca].astype(F32) + rx1a[1, at, :].astype(F32) + rx2a[at, :].astype(F32)
+        right = rx0[0, at, cb].astype(F32) + rx1b[1, at, :].astype(F32) + rx2b[at, :].astype(F32)
+        dx = jnp.concatenate([left, right], axis=1)
+        v = tok_ref[at, :].astype(F32)
+        centered = v - jnp.mean(v, axis=1, keepdims=True)
+        scale = lax.rsqrt(jnp.mean(centered * centered, axis=1, keepdims=True) + 1e-05)
+        hat = centered * scale
+        gains[0:1, :] += jnp.sum(dx * hat, axis=0, keepdims=True)
+        gains[1:2, :] += jnp.sum(dx, axis=0, keepdims=True)
+        g = dx * gain_ref[...]
+        back = scale * (
+            g - jnp.mean(g, axis=1, keepdims=True) - hat * jnp.mean(g * hat, axis=1, keepdims=True)
+        )
+        grad_tokens[at, :] = (back + resid_ref[at, :]).astype(BF16)
+
+    def gain_copies(r):
+        base = (0, 1, 4)[r]
+        return [
+            remote(gains, grx.at[base + i], gsend.at[base + i], grecv.at[base + i], d)
+            for i, d in enumerate(rounds[r])
+        ]
+
+    def gain_begin(r):
+        for c in gain_copies(r):
+            c.start()
+
+    def gain_end(r):
+        for c in gain_copies(r):
+            c.wait()
+        for i in range(len(rounds[r])):
+            gains[...] += grx[(0, 1, 4)[r] + i]
+
+    plane = []
+
+    def deal(i, chain, a):
+        chain.arrive()
+        total_rows(z, fin.at[i], a.at[rows_at(z * deep, deep), :], chain.rx)
+        cols = pl.ds(i * values, values)
+        for m in (1, 2, 3):
+            plane.append(
+                start(
+                    remote(
+                        fin.at[i, rows_at(pq[m] * chunk, chunk), :], sums.at[p, :, cols],
+                        psend.at[i, m], precv.at[i, m], me.plane(m),
+                    )
+                )
+            )
+        plane.append(
+            start(
+                pltpu.make_async_copy(
+                    fin.at[i, rows_at(p * chunk, chunk), :], sums.at[p, :, cols], psend.at[i, 0]
+                )
+            )
+        )
+
+    gain_begin(0)
+    q_sum.step(1)
+    gain_end(0)
+    gain_begin(1)
+    deal(0, v_sum, av)
+    gain_end(1)
+    gain_begin(2)
+    q_sum.step(2)
+    fa_sum.step(0)
+    gain_end(2)
+    fb_sum.step(0)
+    deal(1, q_sum, aq)
+    fa_sum.step(1)
+    fb_sum.step(1)
+    fa_sum.step(2)
+    fb_sum.step(2)
+    fa_sum.arrive()
+    total_rows(z, fout.at[0], kf.at[0, z], rxfa)
+    fb_sum.arrive()
+    total_rows(z, fout.at[1], kf.at[1, z], rxfb)
+    for c in plane:
+        c.wait()
+    for chain in (v_sum, q_sum, fa_sum, fb_sum):
+        chain.finish()
+    for c in list(first.values()) + list(sends.values()) + [s2a, s2b]:
+        c.wait_send()
+    for zp in range(LINE):
+        for h in range(2):
+            f_copy(h, zp).wait_send()
+
+
+def last_sums(dh, xg, wq, wk, wv, wg, f1, tokens, gain, resid, second, cid):
+    group, width = xg.shape
+    rows = tokens.shape[0]
+    keys, values = wq.shape[1], wv.shape[1]
+    assert 2 * keys == values
+    chunk, deep = width // SPANS, width // LINE
+    hidden = f1.shape[-1]
+    return comm_call(
+        last_kernel,
+        [
+            jax.ShapeDtypeStruct((rows, width), BF16),
+            jax.ShapeDtypeStruct((8, width), F32),
+            jax.ShapeDtypeStruct((2, chunk, hidden), F32),
+            jax.ShapeDtypeStruct((PLANE, chunk, 2 * values), BF16),
+        ],
+        [dh, xg, wq, wk, wv, wg, f1, tokens, gain[None], resid, second],
+        [
+            pltpu.VMEM(dh.shape, BF16),
+            pltpu.VMEM((2, group, 256), BF16),
+            pltpu.VMEM((width, dh.shape[1]), BF16),
+            pltpu.VMEM((PLANE, 2 * rows, width), BF16),
+            pltpu.VMEM((PLANE, rows, width), BF16),
+            pltpu.VMEM((2, rows, width // 2), BF16),
+            pltpu.VMEM((2, rows, width // 2), BF16),
+            pltpu.VMEM((rows, width // 2), BF16),
+            pltpu.VMEM((rows, width // 2), BF16),
+            pltpu.VMEM((width, values), BF16),
+            pltpu.VMEM((width, 2 * keys), BF16),
+            pltpu.VMEM((LINE + 1, deep, values), BF16),
+            pltpu.VMEM((LINE + 1, deep, 2 * keys), BF16),
+            pltpu.VMEM((2, deep, values), BF16),
+            pltpu.VMEM((2, LINE, chunk, hidden), BF16),
+            pltpu.VMEM((2, LINE, chunk, hidden), BF16),
+            pltpu.VMEM((LINE + 1, chunk, hidden), BF16),
+            pltpu.VMEM((LINE + 1, chunk, hidden), BF16),
+            pltpu.VMEM((7, 8, width), F32),
+            DMA((7,)),
+            DMA((2,)),
+            DMA((2, LINE)),
+            DMA((2, LINE)),
+            DMA((4,)),
+            DMA((4,)),
+            DMA((6,)),
+            DMA((6,)),
+            DMA((7,)),
+            DMA((7,)),
+            DMA((2, PLANE)),
+            DMA((2, PLANE)),
+        ]
+        + line_sems()
+        + line_sems()
+        + line_sems()
+        + line_sems(),
+        cid,
+        in_specs=[ANY] * 7 + [VM] * 4,
+        out_specs=[VM, VM, VM, ANY],
+    )
 
 
 def layer_norm(values_in, gain_vec, bias_vec):
@@ -912,7 +1950,7 @@
     ln1_gain, ln1_bias = features_in(ln1_gain), features_in(ln1_bias)
     ln2_gain, ln2_bias = features_in(ln2_gain), features_in(ln2_bias)
     inputs32 = tokens.astype(F32)
-    xn_first, norm1_back = jax.vjp(layer_norm, inputs32, ln1_gain, ln1_bias)
+    xn_first = layer_norm(inputs32, ln1_gain, ln1_bias)
     decays = jnp.pad(decay_log.T, ((0, 8 - heads), (0, 0)))
     xg, decay_rows, key_w, value_w, query_w, gate_w, out_w = gather_in(
         xn_first.astype(BF16),
@@ -962,9 +2000,7 @@
     q_decayed = (q_blocks.astype(F32) * jnp.exp(cumulative)[:, :, None]).astype(BF16)
     retained = dot("cts,csd->ctd", weighted, v_blocks) + dot("ctk,ckd->ctd", q_decayed, prev_states)
     retained = retained.reshape(group_rows, value_width)
-    grouped, group_back = jax.vjp(group_norm, retained)
-    gated, gate_back = jax.vjp(swish_gate, gate_proj, grouped)
-    gated_low = gated.astype(BF16)
+    gated_low = swish_gate(gate_proj, group_norm(retained)).astype(BF16)
     attn_share = dot("tv,vd->td", gated_low, out_w).astype(BF16)
     block_out, grad_resid, gains_second, grad_attn, grad_up, grad_down = ffn_part(
         attn_share.reshape(PLANE, 2, row_count, width),
@@ -976,76 +2012,60 @@
         cotangent,
         2,
     )
-    split = (LINE, 2, 2, width // SPANS, w_up.shape[1])
-    ffn_sum = line_sum(
-        jnp.concatenate(
-            [plane_sum(grad_up.reshape(split), p, 1), plane_sum(grad_down.reshape(split), p, 2)], axis=-1
-        ),
-        z,
+    grad_attn = grad_attn.reshape(group_rows, width)
+    crow = jnp.broadcast_to(cumulative[:, None, :], (blocks, 8, STRETCH))
+    scalars = jnp.concatenate([jnp.exp(last), before, total[None]])
+    scalars = jnp.broadcast_to(scalars[:, None, None], (2 * blocks + 1, 8, 128))
+    grad_heads, sums_first, ffn_first = retention_back(
+        grad_attn,
+        out_w,
+        gated_low,
+        gate_proj,
+        retained,
+        q_rot,
+        k_rot,
+        value,
+        prev_states,
+        cosine,
+        sine_part,
+        cumulative.reshape(group_rows, 1),
+        crow,
+        scalars,
+        normed,
+        grad_up,
+        grad_down,
+        7,
     )
-    sum_up = narrow_out(ffn_sum[:, : w_up.shape[1]], 0)
-    sum_down = narrow_out(ffn_sum[:, w_up.shape[1] :], 0).T
-
-    grad_attn = grad_attn.reshape(group_rows, width)
-    grad_gated = dot("td,vd->tv", grad_attn, out_w)
-    grad_out_w = dot("td,tv->dv", grad_attn, gated_low).astype(BF16)
-    grad_gate, grad_grouped = gate_back(grad_gated)
-    grad_gate_low = grad_gate.astype(BF16)
-    grad_retained = group_back(grad_grouped)[0].astype(BF16)
-    grad_blocks = grad_retained.reshape(blocks, STRETCH, value_width)
-
-    query_out = dot("ctk,ctd->ckd", q_decayed, grad_blocks)
-    local_grad = jnp.sum(before[:, None, None] * query_out, axis=0)
-    outgoing = line_states(local_grad.astype(BF16), total, True, 7)
-    after = [outgoing]
-    for c in reversed(range(1, blocks)):
-        after.append(jnp.exp(last[c]) * after[-1] + query_out[c])
-    grad_kv = jnp.stack(after[::-1]).astype(BF16)
-
-    grad_weighted = dot("ctd,csd->cts", grad_blocks, v_blocks)
-    grad_scores = (grad_weighted * mask).astype(BF16)
-    grad_q = dot("ctd,ckd->ctk", grad_blocks, prev_states) * jnp.exp(cumulative)[:, :, None]
-    grad_q = grad_q + dot("cts,csk->ctk", grad_scores, k_blocks)
-    grad_k = dot("csd,ckd->csk", tail_values, grad_kv) + dot("cts,ctk->csk", grad_scores, q_blocks)
-    grad_v = dot("csk,ckd->csd", k_blocks, grad_kv) * tail_scale[:, :, None]
-    grad_v = grad_v + dot("cts,ctd->csd", weighted, grad_blocks)
-    grad_query = rotate(grad_q.reshape(group_rows, key_width), cosine, -sine_part).astype(BF16)
-    grad_keys = rotate(grad_k.reshape(group_rows, key_width), cosine, -sine_part).astype(BF16)
-    grad_values = grad_v.reshape(group_rows, value_width).astype(BF16)
-
-    grad_heads = jnp.concatenate([grad_query, grad_keys, grad_values, grad_gate_low], axis=1)
-    grad_qkv = jnp.concatenate([grad_query, grad_keys, grad_values], axis=1)
-    heads_w = jnp.concatenate([query_w, key_w, value_w, gate_w], axis=1)
-    grad_xn1_share = dot("tq,dq->td", grad_heads, heads_w).astype(BF16)
-    grad_heads_w = dot("td,tq->dq", normed, grad_qkv).astype(BF16)
-    grad_gate_w = dot("td,tq->dq", normed, grad_gate_low).astype(BF16)
-    grad_xn1 = plane_reduce(grad_xn1_share.reshape(PLANE, 2, row_count, width), 8)
-    first = jnp.concatenate([grad_gate_w, grad_out_w], axis=1)
-    sums = jnp.concatenate(
-        [
-            plane_deal(line_sum(g.reshape(LINE, PLANE, width // SPANS, -1), z).astype(BF16), p)
-            for g in (grad_heads_w, first)
-        ],
-        axis=-1,
+    grad_tokens, gains, ffn_sum, sums_last = last_sums(
+        grad_heads,
+        normed,
+        query_w,
+        key_w,
+        value_w,
+        gate_w,
+        ffn_first,
+        tokens,
+        ln1_gain,
+        grad_resid,
+        gains_second,
+        8,
     )
-    grad_inputs, grad_gain1, grad_bias1 = norm1_back(grad_xn1)
-    grad_tokens = (grad_resid + grad_inputs).astype(BF16)
-    gains = jnp.concatenate([grad_gain1[None], grad_bias1[None], gains_second[:6]])
-    gains = gains_sum(gains, 10)
+    sum_up = narrow_out(ffn_sum[0], 0)
+    sum_down = narrow_out(ffn_sum[1], 0).T
     if repeats > 1:
         gains = lax.psum(gains, "seq", axis_index_groups=peers)
     gains = features_out(gains)
     gain_one, bias_one, gain_two, bias_two = gains[0], gains[1], gains[2], gains[3]
 
-    def columns(start, size):
+    def columns(sums, start, size):
         taken = sums[:, :, start : start + size].astype(F32).swapaxes(0, 1)
         return narrow_out(taken.reshape(taken.shape[0], PLANE * size), 0)
 
-    sum_query = columns(0, key_width)
-    sum_key = columns(key_width, key_width)
-    sum_value = columns(2 * key_width, value_width)
-    sum_gate = columns(2 * key_width + value_width, value_width)
-    sum_out = columns(2 * key_width + 2 * value_width, value_width).T
+    sum_value = columns(sums_last, 0, value_width)
+    sum_query = columns(sums_last, value_width, key_width)
+    sum_key = columns(sums_last, value_width + key_width, key_width)
+    sum_out = columns(sums_first, 0, value_width).T
+    sum_gate = columns(sums_first, value_width, value_width)
     return (
         features_out(block_out),
         features_out(grad_tokens),

time: 906 us -> 736 us (0.81)
  Pallas kernels: 408 us -> 622 us
  local copies, waits for them, and re-layouts: 130 us -> 28.2 us
  waiting for transfers between devices: 88 us -> 0 us
  other arithmetic: 97.1 us -> 25.1 us
  matrix products: 104 us -> 44.4 us
  starting transfers between devices: 56.3 us -> 0 us
    pallas_call x6 -> x5, Pallas kernels: 408 us -> 622 us  [comm_call(): pl.pallas_call(kernel, out_shape=outs, in_specs=in_specs if in_specs is n...]
    ppermute x28 -> x0, waiting for transfers between devices: 88 us -> none  [the longest x9 80.9 us: line_sum(): dn = lax.ppermute(send_dn, 'seq', dns)]
    dot_general x22 -> x8, matrix products: 104 us -> 44.4 us  [dot(): return jnp.einsum(spec, a, b, preferred_element_type=F32)]
    ppermute x28 -> x0, starting transfers between devices: 56.3 us -> none  [the longest x9 28.2 us: line_sum(): dn = lax.ppermute(send_dn, 'seq', dns)]
    dynamic_slice x7 -> x0, local copies, waits for them, and re-layouts: 52 us -> none  [take(): return lax.dynamic_index_in_dim(x, index, axis, False)]
    unnamed x179 -> x65, local copies, waits for them, and re-layouts: 48.9 us -> 12.3 us
    convert_element_type x17 -> x0, other arithmetic: 36.1 us -> none  [the longest x13 28.8 us: plus(): return (a.astype(F32) + b.astype(F32)).astype(BF16)]
    unnamed x9 -> x3, other arithmetic: 20.1 us -> 0.09 us
  transfers between devices with their start and end apart: 28 -> 0, of which waited for: 7 -> 0; matrix products, arithmetic and copies ran while one was open for 26% -> 0% of each run, Pallas kernels for 14% -> 0%
where the time goes in v3:
time: 736 us; the launch traced here: 727 us
  Pallas kernels  622 us (85%)
  matrix products  44.4 us (6%)
  local copies, waits for them, and re-layouts  28.2 us (4%)
  other arithmetic  25.1 us (3%)
    pallas_call x5, Pallas kernels, comm_call(): pl.pallas_call(kernel, out_shape=outs, in_specs=in_specs if in_specs is n...  622 us
    dot_general x8, matrix products, dot(): return jnp.einsum(spec, a, b, preferred_element_type=F32)  44.4 us

profile of v3, /device:TPU:16, one launch (start us, length us, event | category | flops | bytes accessed | tf_op | source)
XLA Modules:
  0.0 727.0 jit_solution(15591444068620074325)
XLA Ops:
  0.8 1.6 convert_reduce_fusion
  2.4 1.6 fusion.2
  5.5 1.4 fusion.5.refs_0_
  6.9 154.4 %shard_map.237 = (bf16[8,256,2048]{2,1,0:T(8,128)(2,1)}, f32[4,8,512]{2,1,0:T(8,128)}, bf16[2048,256]{1,0:T(8,128)(2,1)}, bf16[2048,512]{1,0:T(8,128)(2,1)}, bf1...) custom-call(bf16[256,2048]{1,0:T(8,128)(2,1)} %fusion.5.refs_0_, ...), custom_call_target="tpu_custom_call" | custom-call | tf_op jit(solution)/shard_map/pallas_call | solution.py:81
  172.1 1.3 copy.34.ccol_ref
  173.5 10.0 %convolution_convert_fusion.1.v_ref = bf16[2048,512]{1,0:T(8,128)(2,1)} fusion(bf16[2048,2048]{1,0:T(8,128)(2,1)} %bitcast.93, bf16[2048,512]{1,0:T(8,128)(2,1)} %get-tuple-element.40.wv_ref), kind=kOutput, calls=%fused_computation.5 | convolution fusion | flops 4296015872 | bytes 12582912 | tf_op jit(solution)/shard_map/td,dv->tv/dot_general | solution.py:1895
  183.5 2.5 fusion.48
  186.0 2.5 fusion.47
  188.5 6.0 fusion.18
  196.6 2.7 fusion.6
  200.4 23.8 %shard_map.238 = (bf16[4,256,512]{2,1,0:T(8,128)(2,1)}, f32[4,8,128]{2,1,0:T(8,128)}) custom-call(bf16[256,512]{1,0:T(8,128)(2,1)} %get-tuple-element.85.x_ref, f32[8,128]{1,0:T(8,128)} %broadcast_in_dim.27.d_ref), custom_call_target="tpu_custom_call" | custom-call | tf_op jit(solution)/shard_map/pallas_call | solution.py:81
  228.2 2.0 multiply_convert_fusion.6
  230.3 2.2 add_convert_fusion.2
  234.5 1.5 pad_maximum_fusion.3
  236.1 5.8 fusion.16
  241.9 3.2 fusion.46
  248.2 10.8 %multiply_convert_fusion = (bf16[2048,512]{1,0:T(8,128)(2,1)S(1)}, f32[2048,512]{1,0:T(8,128)}) fusion(f32[2048]{0:T(1024)S(1)} %bitcast.127, f32[2048]{0:T(1024)S(1)} %bitcast.126, f32[4,512,512]{2,1,0:T(8,128)S(1)} %get-tuple-element.131, bf16[2048,2048]{1,0:T(8,128)(2,1)} %bitcast.94, bf16[2048,512]{1,0:T(8,128)(2,1)S(1)} %copy-done.11), kind=kOutput, calls=%fused_computation.1 | convolution fusion | flops 4303355904 | bytes 20987904 | tf_op jit(solution)/shard_map/td,dv->tv/dot_general | solution.py:1895
  259.0 6.9 convolution_convert_fusion
  265.9 104.9 %shard_map.239 = (bf16[256,2048]{1,0:T(8,128)(2,1)}, f32[256,2048]{1,0:T(8,128)}, f32[8,2048]{1,0:T(8,128)}, bf16[8,256,2048]{2,1,0:T(8,128)(2,1)}, bf16[2048,20...) custom-call(bf16[4,2,256,2048]{3,2,1,0:T(8,128)(2,1)} %bitcast.100, bf16[256,2048]{1,0:T(8,128)(2,1)} %tok_ref.3, ...), custom_call_target="tpu_custom_call" | custom-call | tf_op jit(solution)/shard_map/pallas_call | solution.py:81
  370.8 130.2 %shard_map.240 = (bf16[2048,1536]{1,0:T(8,128)(2,1)}, bf16[4,128,1024]{2,1,0:T(8,128)(2,1)}, bf16[2,4,2,128,2048]{4,3,2,1,0:T(8,128)(2,1)}) custom-call(bf16[2048,2048]{1,0:T(8,128)(2,1)} %bitcast.99, bf16[512,2048]{1,0:T(8,128)(2,1)} %get-tuple-element.43.wo_ref, bf16[2048,512]{1,0:T(8,128)(2,1)} %copy-done.13, f32[2048,512]{1,0:T(8,128)} %get-tuple-element.133.gate_ref, ...), custom_call_target="tpu_custom_call" | custom-call | tf_op jit(solution)/shard_map/pallas_call | solution.py:81
  501.1 209.0 %shard_map.241 = (bf16[256,2048]{1,0:T(8,128)(2,1)}, f32[8,2048]{1,0:T(8,128)}, f32[2,128,2048]{2,1,0:T(8,128)}, bf16[4,128,1024]{2,1,0:T(8,128)(2,1)}) custom-call(bf16[2048,1536]{1,0:T(8,128)(2,1)} %get-tuple-element.48.dh_ref, bf16[2048,2048]{1,0:T(8,128)(2,1)} %bitcast.96, bf16[2048,256]{1,0:T(8,128)(2,1)} %get-tuple-element.37.wq_ref, ...), custom_call_target="tpu_custom_call" | custom-call | tf_op jit(solution)/shard_map/pallas_call | solution.py:81
  710.1 1.6 fusion.42
  713.2 1.3 copy.42
  715.6 2.0 copy.41
  (103 shorter events, 30.6 us)
Async XLA Ops:
  0.6 4.8 copy-start.2
  0.7 4.8 copy-start.24
  0.7 3.4 copy-start.26
  0.7 4.8 copy-start.25
  173.5 10.0 %copy-start.1 = (bf16[8,256,2048]{2,1,0:T(8,128)(2,1)S(1)}, bf16[8,256,2048]{2,1,0:T(8,128)(2,1)}, u32[]{:S(2)}) copy-start(bf16[8,256,2048]{2,1,0:T(8,128)(2,1)} %get-tuple-element.35) | copy-start | bytes 25165828
  173.5 10.0 %copy-start.16 = (bf16[2048,256]{1,0:T(8,128)(2,1)S(1)}, bf16[2048,256]{1,0:T(8,128)(2,1)}, u32[]{:S(2)}) copy-start(bf16[2048,256]{1,0:T(8,128)(2,1)} %get-tuple-element.38.wk_ref) | copy-start | bytes 3145732
  183.5 2.5 copy-start.17
  194.5 1.0 copy-start.3
  224.2 6.0 copy-start.15
  230.3 4.3 copy-start.4
  234.5 1.5 copy-start.22
  234.5 1.6 copy-start.23
  236.1 5.8 copy-start.6
  236.1 5.8 copy-start.8
  236.1 5.8 copy-start.10
  245.1 2.1 copy-start
  245.1 3.1 copy-start.11
  248.2 10.8 %copy-start.12 = (bf16[512,2048]{1,0:T(8,128)(2,1)S(1)}, bf16[512,2048]{1,0:T(8,128)(2,1)}, u32[]{:S(2)}) copy-start(bf16[512,2048]{1,0:T(8,128)(2,1)} %get-tuple-element.43.wo_ref) | copy-start | bytes 6291460
  259.0 6.9 copy-start.13
  712.8 1.7 copy-start.19
  714.6 4.2 copy-start.14
  720.0 1.3 copy-start.18
  722.9 1.7 copy-start.20
  723.3 2.3 copy-start.21
  (3 other events, 2.4 us)

commit v4 on v3

--- a/solution.py
+++ b/solution.py
@@ -91,192 +91,6 @@
 
 
 DMA = pltpu.SemaphoreType.DMA
-
-
-def gather_kernel(widths, rows, *refs):
-    count = len(widths)
-    xn_ref, dec_ref = refs[:2]
-    shards_in = refs[2 : 2 + count]
-    xg, decg = refs[2 + count : 4 + count]
-    full = refs[4 + count : 4 + 2 * count]
-    hold = refs[4 + 2 * count : 4 + 3 * count]
-    lsem, psend, precv, usend, dsend, zrecv, xsend, xrecv, csend, crecv, tsend, trecv = refs[4 + 3 * count :]
-    me = Place()
-    z, p, f = me.z, me.p, me.f
-    spot = z * PLANE + p
-    chunk = shards_in[0].shape[0]
-    deep = chunk * PLANE
-    greet(
-        [(me.plane(m), None) for m in (1, 2, 3)]
-        + [(me.partner(), None), (me.up(), z < LINE - 1), (me.down(), z > 0)]
-    )
-
-    def part(i, q):
-        w = widths[i]
-        if rows[i]:
-            return shards_in[i].at[pl.ds(pl.multiple_of(q * w, w), w), :]
-        return shards_in[i].at[:, pl.ds(pl.multiple_of(q * w, w), w)]
-
-    def slot(i, ss):
-        at = pl.ds(pl.multiple_of(ss * chunk, chunk), chunk)
-        return full[i].at[:, at] if rows[i] else full[i].at[at, :]
-
-    def block(i, zz):
-        at = pl.ds(pl.multiple_of(zz * deep, deep), deep)
-        return full[i].at[:, at] if rows[i] else full[i].at[at, :]
-
-    local, plane, held = [], [], []
-    for i in range(count):
-        load = pltpu.make_async_copy(part(i, p), hold[i], lsem.at[i])
-        load.start()
-        held.append(load)
-        local.append(pltpu.make_async_copy(hold[i], slot(i, spot), lsem.at[i]))
-        sends = []
-        for m in (1, 2, 3):
-            c = remote(part(i, me.xor(m)), slot(i, spot), psend.at[i, m], precv.at[i, m], me.plane(m))
-            c.start()
-            sends.append(c)
-        plane.append(sends)
-    tiny = []
-    for m in (1, 2, 3):
-        c = remote(dec_ref, decg.at[p], tsend.at[m], trecv.at[m], me.plane(m))
-        c.start()
-        tiny.append(c)
-    dec_own = pltpu.make_async_copy(dec_ref, decg.at[p], lsem.at[count])
-    dec_own.start()
-
-    seat = p * 2 + f
-    x_own = pltpu.make_async_copy(xn_ref, xg.at[seat], lsem.at[count + 1])
-    x_own.start()
-    half = xn_ref.shape[0] // 2
-    x1 = remote(xn_ref, xg.at[seat], xsend.at[0], xrecv.at[0], me.plane(1))
-    x2 = remote(xn_ref, xg.at[seat], xsend.at[1], xrecv.at[1], me.plane(2))
-    xc = remote(xn_ref, xg.at[seat], csend.at[0], crecv.at[0], me.partner())
-    x1.start()
-    x2.start()
-    xc.start()
-
-    def up_copy(i, zz):
-        return remote(block(i, zz), block(i, zz), usend.at[i, zz], zrecv.at[i, zz], me.up())
-
-    def down_copy(i, zz):
-        return remote(block(i, zz), block(i, zz), dsend.at[i, zz], zrecv.at[i, zz], me.down())
-
-    for i in range(count):
-        held[i].wait()
-        local[i].start()
-    for i in range(count):
-        local[i].wait()
-        for c in plane[i]:
-            c.wait_recv()
-
-        @pl.when(z < LINE - 1)
-        def _():
-            up_copy(i, z).start()
-
-        @pl.when(z > 0)
-        def _():
-            down_copy(i, z).start()
-
-    seat1, seat2, seat3 = (me.xor(m) * 2 + f for m in (1, 2, 3))
-    low, high = pl.ds(0, half), pl.ds(half, half)
-    x1.wait_recv()
-    g1 = remote(xg.at[seat1, low], xg.at[seat1, low], xsend.at[2], xrecv.at[2], me.plane(2))
-    g1.start()
-    c1 = remote(xg.at[seat1], xg.at[seat1], csend.at[1], crecv.at[1], me.partner())
-    c1.start()
-    x2.wait_recv()
-    g2 = remote(xg.at[seat2, high], xg.at[seat2, high], xsend.at[3], xrecv.at[3], me.plane(1))
-    g2.start()
-    c2 = remote(xg.at[seat2], xg.at[seat2], csend.at[2], crecv.at[2], me.partner())
-    c2.start()
-    g1.wait_recv()
-    g2.wait_recv()
-    c3 = remote(xg.at[seat3], xg.at[seat3], csend.at[3], crecv.at[3], me.partner())
-    c3.start()
-
-    for t in range(1, LINE):
-        for i in range(count):
-
-            @pl.when(z - t >= 0)
-            def _():
-                up_copy(i, z - t).wait_recv()
-
-                @pl.when(z < LINE - 1)
-                def _():
-                    up_copy(i, z - t).start()
-
-            @pl.when(z + t < LINE)
-            def _():
-                down_copy(i, z + t).wait_recv()
-
-                @pl.when(z > 0)
-                def _():
-                    down_copy(i, z + t).start()
-
-    for c in (xc, c1, c2, c3):
-        c.wait()
-    for c in (x1, x2, g1, g2):
-        c.wait_send()
-    for c in tiny:
-        c.wait()
-    dec_own.wait()
-    x_own.wait()
-    for i in range(count):
-        for c in plane[i]:
-            c.wait_send()
-        for zz in range(LINE):
-
-            @pl.when((z < LINE - 1) & (zz <= z))
-            def _():
-                up_copy(i, zz).wait_send()
-
-            @pl.when((z > 0) & (zz >= z))
-            def _():
-                down_copy(i, zz).wait_send()
-
-
-def gather_in(xn, dec, shards_in, rows, cid):
-    count = len(shards_in)
-    chunk = shards_in[0].shape[0]
-    widths, outs = [], []
-    for w, r in zip(shards_in, rows):
-        if r:
-            widths.append(w.shape[0] // PLANE)
-            outs.append(jax.ShapeDtypeStruct((w.shape[0] // PLANE, chunk * SPANS), BF16))
-        else:
-            widths.append(w.shape[1] // PLANE)
-            outs.append(jax.ShapeDtypeStruct((chunk * SPANS, w.shape[1] // PLANE), BF16))
-    outs = [
-        jax.ShapeDtypeStruct((2 * PLANE,) + xn.shape, BF16),
-        jax.ShapeDtypeStruct((PLANE,) + dec.shape, F32),
-    ] + outs
-    parts = [
-        (w.shape[0] // PLANE, chunk) if r else (chunk, w.shape[1] // PLANE)
-        for w, r in zip(shards_in, rows)
-    ]
-    scratch = [pltpu.VMEM(shape, BF16) for shape in parts] + [
-        DMA((count + 2,)),
-        DMA((count, PLANE)),
-        DMA((count, PLANE)),
-        DMA((count, LINE)),
-        DMA((count, LINE)),
-        DMA((count, LINE)),
-        DMA((4,)),
-        DMA((4,)),
-        DMA((4,)),
-        DMA((4,)),
-        DMA((PLANE,)),
-        DMA((PLANE,)),
-    ]
-    return comm_call(
-        functools.partial(gather_kernel, widths, rows),
-        outs,
-        [xn, dec] + shards_in,
-        scratch,
-        cid,
-        in_specs=[VM] + [ANY] * (count + 1),
-    )
 
 
 def nn(a, b):
@@ -558,69 +372,411 @@
     )
 
 
-def line_states_kernel(backward, x_ref, d_ref, out, dout, lsem, xsend, xrecv, dsend, drecv):
+def attention_kernel(
+    widths, by_rows,
+    tok_ref, gain_ref, bias_ref, dec_ref, cbase, sbase, coff, soff, *refs,
+):
+    count = len(widths)
+    shards_in, refs = refs[:count], refs[count:]
+    (xg, q_out, k_out, v_out, gate_out, ret_out, gated_out, states_out, share_out, cos_out, sin_out, ccol, crow, scal), refs = (
+        refs[:14], refs[14:],
+    )
+    full, refs = refs[:count], refs[count:]
+    hold, refs = refs[:count], refs[count:]
+    wl, refs = refs[:count], refs[count:]
+    (xn, xv, q, k, v, gate, ret, gated, share, cos, sin, kv, st, sloc, sgot, decg, pbuf,
+     lsem, psend, precv, usend, dsend, zrecv, xsend, xrecv, csend, crecv, tsend, trecv, ssend, srecv, osem, wsem) = refs
     me = Place()
-    z = me.z
-    others = [(z + t) % LINE for t in range(1, LINE)]
-    greet([(me.at(o, me.p, me.f), None) for o in others])
-    own = pltpu.make_async_copy(x_ref, out.at[z], lsem.at[0])
-    own.start()
-    down = pltpu.make_async_copy(d_ref, dout.at[z], lsem.at[1])
-    down.start()
-
-    def pair(step, to, slot):
-        sem = step - 1
-        device = me.at(to, me.p, me.f)
-        return (
-            remote(x_ref, out.at[slot], xsend.at[sem], xrecv.at[sem], device),
-            remote(d_ref, dout.at[slot], dsend.at[sem], drecv.at[sem], device),
+    z, p, f = me.z, me.p, me.f
+    spot = z * PLANE + p
+    chunk = hold[0].shape[0]
+    deep = chunk * PLANE
+    tokens, width = xv.shape
+    rows = tok_ref.shape[0]
+    keys, values = q.shape[1], v.shape[1]
+    half = keys // 2
+    blocks = tokens // STRETCH
+    greet(
+        [(me.plane(m), None) for m in (1, 2, 3)]
+        + [(me.partner(), None), (me.up(), z < LINE - 1), (me.down(), z > 0)]
+    )
+
+    def part(i, at):
+        w = widths[i]
+        if by_rows[i]:
+            return shards_in[i].at[pl.ds(pl.multiple_of(at * w, w), w), :]
+        return shards_in[i].at[:, pl.ds(pl.multiple_of(at * w, w), w)]
+
+    def slot(i, ss):
+        at = pl.ds(pl.multiple_of(ss * chunk, chunk), chunk)
+        return full[i].at[:, at] if by_rows[i] else full[i].at[at, :]
+
+    def block(i, zz):
+        at = pl.ds(pl.multiple_of(zz * deep, deep), deep)
+        return full[i].at[:, at] if by_rows[i] else full[i].at[at, :]
+
+    local, plane, held = [], [], []
+    for i in range(count):
+        held.append(start(pltpu.make_async_copy(part(i, p), hold[i], lsem.at[i])))
+        local.append(pltpu.make_async_copy(hold[i], slot(i, spot), lsem.at[i]))
+        plane.append(
+            [
+                start(remote(part(i, me.xor(m)), slot(i, spot), psend.at[i, m], precv.at[i, m], me.plane(m)))
+                for m in (1, 2, 3)
+            ]
         )
-
-    sign = -1 if backward else 1
-    for t in range(1, LINE):
-        to, source = z + sign * t, z - sign * t
-
-        @pl.when((to >= 0) & (to < LINE))
+    tiny = [start(remote(dec_ref, decg.at[p], tsend.at[m], trecv.at[m], me.plane(m))) for m in (1, 2, 3)]
+    tiny_own = start(pltpu.make_async_copy(dec_ref, decg.at[p], tsend.at[0]))
+    step = 32
+
+    @pl.loop(0, rows, step=step)
+    def _(r):
+        at = rows_at(r, step)
+        t = tok_ref[at, :].astype(F32)
+        centered = t - jnp.mean(t, axis=1, keepdims=True)
+        scale = lax.rsqrt(jnp.mean(centered * centered, axis=1, keepdims=True) + 1e-05)
+        xn[at, :] = (centered * scale * gain_ref[...] + bias_ref[...]).astype(BF16)
+
+    def seat(m, h=None):
+        base = (me.xor(m) * 2 + f) * rows
+        if h is None:
+            return xv.at[rows_at(base, rows)]
+        return xv.at[pl.ds(pl.multiple_of(base + h * (rows // 2), rows // 2), rows // 2)]
+
+    x_own = start(pltpu.make_async_copy(xn, seat(0), lsem.at[count]))
+    x1 = start(remote(xn, seat(0), xsend.at[0], xrecv.at[0], me.plane(1)))
+    x2 = start(remote(xn, seat(0), xsend.at[1], xrecv.at[1], me.plane(2)))
+    xc = start(remote(xn, seat(0), csend.at[0], crecv.at[0], me.partner()))
+    for i in range(count):
+        held[i].wait()
+        local[i].start()
+
+    def up_copy(i, zz):
+        return remote(block(i, zz), block(i, zz), usend.at[i, zz], zrecv.at[i, zz], me.up())
+
+    def down_copy(i, zz):
+        return remote(block(i, zz), block(i, zz), dsend.at[i, zz], zrecv.at[i, zz], me.down())
+
+    def own(i):
+        local[i].wait()
+        for c in plane[i]:
+            c.wait_recv()
+
+        @pl.when(z < LINE - 1)
         def _():
-            for c in pair(t, to, z):
-                c.start()
-
-    for t in range(1, LINE):
-        to, source = z + sign * t, z - sign * t
-
-        @pl.when((source >= 0) & (source < LINE))
+            up_copy(i, z).start()
+
+        @pl.when(z > 0)
         def _():
-            for c in pair(t, source, source):
-                c.wait_recv()
-
-        @pl.when((to >= 0) & (to < LINE))
+            down_copy(i, z).start()
+
+    def forward(i, t):
+        @pl.when(z - t >= 0)
         def _():
-            for c in pair(t, to, z):
-                c.wait_send()
-
-    own.wait()
-    down.wait()
-
-
-def line_states(x, total, backward, cid):
-    sent = jnp.broadcast_to(total, (8, 128))
-    got, logs = comm_call(
-        functools.partial(line_states_kernel, backward),
-        [
-            jax.ShapeDtypeStruct((LINE,) + x.shape, x.dtype),
-            jax.ShapeDtypeStruct((LINE, 8, 128), F32),
-        ],
-        [x, sent],
-        [DMA((2,)), DMA((3,)), DMA((3,)), DMA((3,)), DMA((3,))],
+            up_copy(i, z - t).wait_recv()
+
+            @pl.when(z < LINE - 1)
+            def _():
+                up_copy(i, z - t).start()
+
+        @pl.when(z + t < LINE)
+        def _():
+            down_copy(i, z + t).wait_recv()
+
+            @pl.when(z > 0)
+            def _():
+                down_copy(i, z + t).start()
+
+    def fetch(i):
+        forward(i, LINE - 1)
+        return start(pltpu.make_async_copy(full[i], wl[i], wsem.at[i]))
+
+    K, V, Q, G, O = range(count)
+    own(K)
+    own(V)
+    forward(K, 1)
+    forward(K, 2)
+    own(Q)
+
+    for c in tiny:
+        c.wait()
+    tiny_own.wait()
+    heads = lax.broadcasted_iota(jnp.int32, decg.shape[1:], 0)
+    lines = [jnp.sum(jnp.where(heads == p, decg[j], 0.0), axis=0, keepdims=True) for j in range(blocks)]
+    lines = jnp.concatenate(lines + [jnp.zeros_like(lines[0])] * (8 - blocks), axis=0)
+    i0 = lax.broadcasted_iota(jnp.int32, (STRETCH, STRETCH), 0)
+    i1 = lax.broadcasted_iota(jnp.int32, (STRETCH, STRETCH), 1)
+    row_sums = jnp.dot(
+        lines, jnp.where(i0 <= i1, 1.0, 0.0), preferred_element_type=F32, precision=lax.Precision.HIGHEST
+    )
+    col_sums = lax.dot_general(
+        jnp.where(i1 <= i0, 1.0, 0.0), lines, (((1,), (1,)), ((), ())),
+        preferred_element_type=F32, precision=lax.Precision.HIGHEST,
+    )
+    total = jnp.zeros((1, 1), F32)
+    for c in range(blocks):
+        end = row_sums[c : c + 1, STRETCH - 1 : STRETCH]
+        crow[c] = jnp.broadcast_to(row_sums[c : c + 1, :], (8, STRETCH))
+        ccol[c * STRETCH : (c + 1) * STRETCH, :] = col_sums[:, c : c + 1]
+        scal[c] = jnp.broadcast_to(jnp.exp(end), (8, 128))
+        scal[blocks + c] = jnp.broadcast_to(jnp.exp(total), (8, 128))
+        total = total + end
+    scal[2 * blocks] = jnp.broadcast_to(total, (8, 128))
+
+    fine = coff.shape[0]
+
+    @pl.loop(0, tokens // fine)
+    def _(a):
+        at = rows_at(a * fine, fine)
+        ca, sa = cbase[a, 0:1, :], sbase[a, 0:1, :]
+        cos[at, :] = ca * coff[...] - sa * soff[...]
+        sin[at, :] = sa * coff[...] + ca * soff[...]
+
+    forward(V, 1)
+    x1.wait_recv()
+    g1 = start(remote(seat(1, 0), seat(1, 0), xsend.at[2], xrecv.at[2], me.plane(2)))
+    c1 = start(remote(seat(1), seat(1), csend.at[1], crecv.at[1], me.partner()))
+    x2.wait_recv()
+    g2 = start(remote(seat(2, 1), seat(2, 1), xsend.at[3], xrecv.at[3], me.plane(1)))
+    c2 = start(remote(seat(2), seat(2), csend.at[2], crecv.at[2], me.partner()))
+    forward(V, 2)
+    forward(Q, 1)
+    own(G)
+    forward(Q, 2)
+    own(O)
+    load_k = fetch(K)
+    g1.wait_recv()
+    g2.wait_recv()
+    c3 = start(remote(seat(3), seat(3), csend.at[3], crecv.at[3], me.partner()))
+    x_own.wait()
+    for c in (xc, c1, c2, c3):
+        c.wait_recv()
+    outs = []
+
+    def put(src, dst):
+        outs.append(start(pltpu.make_async_copy(src, dst, osem.at[len(outs)])))
+
+    put(xv, xg)
+    put(cos, cos_out)
+    put(sin, sin_out)
+    load_k.wait()
+
+    def turned(at, w, dst):
+        y = nn(xv[at, :], w[...])
+        a, b = y[:, :half], y[:, half:]
+        dst[at, :half] = (a * cos[at, :] - b * sin[at, :]).astype(BF16)
+        dst[at, half:] = (b * cos[at, :] + a * sin[at, :]).astype(BF16)
+
+    @pl.loop(0, blocks)
+    def _(c):
+        turned(rows_at(c * STRETCH, STRETCH), wl[K], k)
+
+    fetch(V).wait()
+
+    @pl.loop(0, blocks)
+    def _(c):
+        at = rows_at(c * STRETCH, STRETCH)
+        val = nn(xv[at, :], wl[V][...]).astype(BF16)
+        v[at, :] = val
+        end = crow[c, 0:1, STRETCH - 1 : STRETCH]
+        kv[c] = tn(k[at, :], (val.astype(F32) * jnp.exp(end - ccol[at, :])).astype(BF16))
+
+    put(k, k_out)
+    put(v, v_out)
+    sloc[...] = kv[0]
+    kv[0] = jnp.zeros_like(sloc)
+    for c in range(1, blocks):
+        nxt = sloc[...] * scal[c, 0:1, 0:1] + kv[c]
+        kv[c] = sloc[...]
+        sloc[...] = nxt
+
+    def state_copy(zz):
+        return remote(st.at[0], sgot, ssend.at[zz], srecv.at[zz], me.up())
+
+    def send_state():
+        st[0] = sloc[...].astype(BF16)
+        state_copy(0).start()
+
+    @pl.when(z == 0)
+    def _():
+        send_state()
+
+    def pass_state(zz):
+        @pl.when(z == zz)
+        def _():
+            state_copy(0).wait_recv()
+            if zz < LINE - 1:
+                sloc[...] = sloc[...] + sgot[...].astype(F32) * jnp.exp(scal[2 * blocks, 0:1, 0:1])
+                send_state()
+
+    pass_state(1)
+    forward(G, 1)
+    forward(O, 1)
+    fetch(Q).wait()
+    t_size = 256
+
+    @pl.loop(0, blocks)
+    def _(c):
+        blk = rows_at(c * STRETCH, STRETCH)
+        turned(blk, wl[Q], q)
+        row = crow[c, 0:1, :]
+        for r in range(0, STRETCH, t_size):
+            at = rows_at(c * STRETCH + r, t_size)
+            col = ccol[at, :]
+            t_index = lax.broadcasted_iota(jnp.int32, (t_size, STRETCH), 0) + r
+            s_index = lax.broadcasted_iota(jnp.int32, (t_size, STRETCH), 1)
+            mask = jnp.where(t_index >= s_index, jnp.exp(jnp.minimum(col - row, 0.0)), 0.0)
+            scores = (nt(q[at, :], k[blk, :]) * mask).astype(BF16)
+            ret[at, :] = nn(scores, v[blk, :])
+
+    put(q, q_out)
+    pass_state(2)
+    forward(G, 2)
+    forward(O, 2)
+    pass_state(3)
+
+    @pl.when((z > 0) & (z < LINE - 1))
+    def _():
+        state_copy(0).wait_send()
+
+    @pl.when(z == 0)
+    def _():
+        state_copy(0).wait_send()
+        sgot[...] = jnp.zeros_like(sgot)
+
+    for c in range(blocks):
+        st[c] = (kv[c] + sgot[...].astype(F32) * scal[blocks + c, 0:1, 0:1]).astype(BF16)
+
+    @pl.loop(0, blocks)
+    def _(c):
+        at = rows_at(c * STRETCH, STRETCH)
+        decayed = (q[at, :].astype(F32) * jnp.exp(ccol[at, :])).astype(BF16)
+        ret[at, :] += nn(decayed, st[c])
+
+    put(ret, ret_out)
+    put(st, states_out)
+    fetch(G).wait()
+
+    @pl.loop(0, tokens, step=256)
+    def _(r):
+        at = rows_at(r, 256)
+        g = nn(xv[at, :], wl[G][...])
+        gate[at, :] = g
+        t = ret[at, :]
+        centered = t - jnp.mean(t, axis=1, keepdims=True)
+        scale = lax.rsqrt(jnp.mean(centered * centered, axis=1, keepdims=True) + 1e-05)
+        gated[at, :] = (g / (1.0 + jnp.exp(-g)) * centered * scale).astype(BF16)
+
+    put(gate, gate_out)
+    put(gated, gated_out)
+    fetch(O).wait()
+    for c in range(blocks):
+        at = pl.ds(c * STRETCH, STRETCH)
+
+        @pl.loop(0, width, step=512)
+        def _(d):
+            cols = rows_at(d, 512)
+            share[at, cols] = nn(gated[at, :], wl[O][:, cols]).astype(BF16)
+
+        put(share.at[at], share_out.at[at])
+
+    for c in (xc, c1, c2, c3, x1, x2, g1, g2):
+        c.wait_send()
+    for i in range(count):
+        for c in plane[i]:
+            c.wait_send()
+        for zz in range(LINE):
+
+            @pl.when((z < LINE - 1) & (zz <= z))
+            def _():
+                up_copy(i, zz).wait_send()
+
+            @pl.when((z > 0) & (zz >= z))
+            def _():
+                down_copy(i, zz).wait_send()
+
+    for c in outs:
+        c.wait()
+
+
+def attention(tokens, gain, bias, decays, tables, shards_in, by_rows, cid):
+    rows, width = tokens.shape
+    count = len(shards_in)
+    chunk = shards_in[0].shape[0]
+    group = 2 * PLANE * rows
+    blocks = group // STRETCH
+    parts = [
+        (w.shape[0] // PLANE, chunk) if r else (chunk, w.shape[1] // PLANE) for w, r in zip(shards_in, by_rows)
+    ]
+    widths = [s[0] if r else s[1] for s, r in zip(parts, by_rows)]
+    wholes = [(s[0], width) if r else (width, s[1]) for s, r in zip(parts, by_rows)]
+    values, keys = widths[1], widths[0]
+    half = keys // 2
+    sd = jax.ShapeDtypeStruct
+    outs = [
+        sd((group, width), BF16),
+        sd((group, keys), BF16),
+        sd((group, keys), BF16),
+        sd((group, values), BF16),
+        sd((group, values), F32),
+        sd((group, values), F32),
+        sd((group, values), BF16),
+        sd((blocks, keys, values), BF16),
+        sd((group, width), BF16),
+        sd((group, half), F32),
+        sd((group, half), F32),
+        sd((group, 1), F32),
+        sd((blocks, 8, STRETCH), F32),
+        sd((2 * blocks + 1, 8, 128), F32),
+    ] + [sd(s, BF16) for s in wholes]
+    scratch = (
+        [pltpu.VMEM(s, BF16) for s in parts]
+        + [pltpu.VMEM(s, BF16) for s in wholes]
+        + [
+            pltpu.VMEM((rows, width), BF16),
+            pltpu.VMEM((group, width), BF16),
+            pltpu.VMEM((group, keys), BF16),
+            pltpu.VMEM((group, keys), BF16),
+            pltpu.VMEM((group, values), BF16),
+            pltpu.VMEM((group, values), F32),
+            pltpu.VMEM((group, values), F32),
+            pltpu.VMEM((group, values), BF16),
+            pltpu.VMEM((group, width), BF16),
+            pltpu.VMEM((group, half), F32),
+            pltpu.VMEM((group, half), F32),
+            pltpu.VMEM((blocks, keys, values), F32),
+            pltpu.VMEM((blocks, keys, values), BF16),
+            pltpu.VMEM((keys, values), F32),
+            pltpu.VMEM((keys, values), BF16),
+            pltpu.VMEM((PLANE,) + decays.shape, F32),
+            pltpu.VMEM((8, 128), BF16),
+            DMA((count + 1,)),
+            DMA((count, PLANE)),
+            DMA((count, PLANE)),
+            DMA((count, LINE)),
+            DMA((count, LINE)),
+            DMA((count, LINE)),
+            DMA((4,)),
+            DMA((4,)),
+            DMA((4,)),
+            DMA((4,)),
+            DMA((PLANE,)),
+            DMA((PLANE,)),
+            DMA((1,)),
+            DMA((1,)),
+            DMA((16,)),
+            DMA((count,)),
+        ]
+    )
+    return comm_call(
+        functools.partial(attention_kernel, widths, by_rows),
+        outs,
+        [tokens, gain[None], bias[None], decays] + list(tables) + list(shards_in),
+        scratch,
         cid,
-        in_specs=[VM, VM],
-    )
-    z = (lax.axis_index("seq") % SPANS) // PLANE
-    state = jnp.zeros(x.shape, F32)
-    for j in reversed(range(LINE)) if backward else range(LINE):
-        used = j > z if backward else j < z
-        state = jnp.where(used, jnp.exp(logs[j, 0, 0]) * state + got[j].astype(F32), state)
-    return state
+        in_specs=[VM] * 8 + [ANY] * count,
+        out_specs=[ANY] * 11 + [VM] * 3 + [ANY] * count,
+    )
 
 
 class LineSum:
@@ -635,8 +791,8 @@
         slot = jnp.where(zz == self.me.z - 1, LINE, zz)
         return remote(src, self.rx.at[slot], self.sems[2].at[zz], self.sems[3].at[zz], self.me.down())
 
-    def begin(self):
-        for zz in reversed(range(1, LINE)):
+    def begin(self, order=(3, 2, 1)):
+        for zz in order:
 
             @pl.when(self.me.z == 0)
             def _():
@@ -646,21 +802,33 @@
             def _():
                 self.down(self.own(LINE - 1 - zz), LINE - 1 - zz).start()
 
-    def step(self, t):
-        z = self.me.z
-        zu, zd = LINE - 1 - t, t
-
-        @pl.when((z > 0) & (z < zu))
+    def pass_up(self, zz):
+        self.up(self.own(zz), zz).wait_recv()
+        self.add(self.rx.at[zz], self.own(zz))
+        self.up(self.rx.at[zz], zz).start()
+
+    def pass_down(self, zz):
+        self.down(self.own(zz), zz).wait_recv()
+        self.add(self.rx.at[zz], self.own(zz))
+        self.down(self.rx.at[zz], zz).start()
+
+    def near(self, k):
+        @pl.when(self.me.z == 1)
         def _():
-            self.up(self.own(zu), zu).wait_recv()
-            self.add(self.rx.at[zu], self.own(zu))
-            self.up(self.rx.at[zu], zu).start()
-
-        @pl.when((z < LINE - 1) & (z > zd))
+            self.pass_up(LINE - 1 - k)
+
+        @pl.when(self.me.z == 2)
         def _():
-            self.down(self.own(zd), zd).wait_recv()
-            self.add(self.rx.at[zd], self.own(zd))
-            self.down(self.rx.at[zd], zd).start()
+            self.pass_down(k)
+
+    def far(self):
+        @pl.when(self.me.z == 1)
+        def _():
+            self.pass_down(0)
+
+        @pl.when(self.me.z == 2)
+        def _():
+            self.pass_up(LINE - 1)
 
     def arrive(self):
         z = self.me.z
@@ -809,7 +977,7 @@
         at = rows_at(i, 256)
         ao[at, :] = tn(da[:, at], gated[...]).astype(BF16)
 
-    out_sum.begin()
+    out_sum.begin((3, 2))
     for c in loads[2:]:
         c.wait()
 
@@ -866,6 +1034,8 @@
             for c in state_copies(t, z - t, z):
                 c.start()
 
+    out_sum.begin((1,))
+    out_sum.near(0)
     def x_tile(i):
         return pltpu.make_async_copy(xg_ref.at[:, rows_at(i * 256, 256)], xt.at[i % 2], xsem.at[i % 2])
 
@@ -881,10 +1051,10 @@
         ag[rows_at(i * 256, 256), :] = tn(xt[i % 2], dh[:, 2 * keys + values :]).astype(BF16)
 
     gate_sum.begin()
-    out_sum.step(0)
+    out_sum.near(1)
+    out_sum.far()
     f_unit(0)
     f_unit(1)
-    out_sum.step(1)
 
     for t in range(1, LINE):
 
@@ -964,15 +1134,14 @@
             )
         )
 
-    out_sum.step(2)
+    gate_sum.near(0)
+    gate_sum.near(1)
     for u in range(2, 4):
         f_unit(u)
-    gate_sum.step(0)
+    gate_sum.far()
     deal(0, out_sum, ao)
-    gate_sum.step(1)
     for u in range(4, 6):
         f_unit(u)
-    gate_sum.step(2)
     deal(1, gate_sum, ag)
     for u in range(6, 2 * LINE):
         f_unit(u)
@@ -1052,527 +1221,6 @@
     )
 
 
-class LineSum:
-    def __init__(self, me, own, rx, usend, urecv, dsend, drecv, add):
-        self.me, self.own, self.rx, self.add = me, own, rx, add
-        self.sems = usend, urecv, dsend, drecv
-
-    def up(self, src, zz):
-        return remote(src, self.rx.at[zz], self.sems[0].at[zz], self.sems[1].at[zz], self.me.up())
-
-    def down(self, src, zz):
-        slot = jnp.where(zz == self.me.z - 1, LINE, zz)
-        return remote(src, self.rx.at[slot], self.sems[2].at[zz], self.sems[3].at[zz], self.me.down())
-
-    def begin(self):
-        for zz in reversed(range(1, LINE)):
-
-            @pl.when(self.me.z == 0)
-            def _():
-                self.up(self.own(zz), zz).start()
-
-            @pl.when(self.me.z == LINE - 1)
-            def _():
-                self.down(self.own(LINE - 1 - zz), LINE - 1 - zz).start()
-
-    def step(self, t):
-        z = self.me.z
-        zu, zd = LINE - 1 - t, t
-
-        @pl.when((z > 0) & (z < zu))
-        def _():
-            self.up(self.own(zu), zu).wait_recv()
-            self.add(self.rx.at[zu], self.own(zu))
-            self.up(self.rx.at[zu], zu).start()
-
-        @pl.when((z < LINE - 1) & (z > zd))
-        def _():
-            self.down(self.own(zd), zd).wait_recv()
-            self.add(self.rx.at[zd], self.own(zd))
-            self.down(self.rx.at[zd], zd).start()
-
-    def arrive(self):
-        z = self.me.z
-
-        @pl.when(z > 0)
-        def _():
-            self.up(self.own(z), z).wait_recv()
-
-        @pl.when(z < LINE - 1)
-        def _():
-            self.down(self.own(z), z).wait_recv()
-
-    def finish(self):
-        z = self.me.z
-        for zz in range(LINE):
-
-            @pl.when((z < LINE - 1) & (zz > z))
-            def _():
-                self.up(self.own(zz), zz).wait_send()
-
-            @pl.when((z > 0) & (zz < z))
-            def _():
-                self.down(self.own(zz), zz).wait_send()
-
-
-def add_rows(dst, src):
-    rows = dst.shape[0]
-    step = 32 if dst.shape[1] > 512 else 128
-
-    @pl.loop(0, rows, step=step)
-    def _(r):
-        at = rows_at(r, step)
-        dst[at, :] = (dst[at, :].astype(F32) + src[at, :].astype(F32)).astype(BF16)
-
-
-def total_rows(z, dst, own, rx):
-    rows = dst.shape[0]
-    step = 32 if dst.shape[1] > 512 else 128
-
-    @pl.loop(0, rows, step=step)
-    def _(r):
-        at = rows_at(r, step)
-        v = own[at, :].astype(F32)
-        v = v + jnp.where(z > 0, rx[z, at, :].astype(F32), 0.0)
-        v = v + jnp.where(z < LINE - 1, rx[LINE, at, :].astype(F32), 0.0)
-        dst[at, :] = v.astype(dst.dtype)
-
-
-def line_sems():
-    return [DMA((LINE,)) for _ in range(4)]
-
-
-def retention_back_kernel(
-    da_ref, wo_ref, gated_ref, gate_ref, ret_ref, q_ref, k_ref, v_ref, s_ref, cos_ref, sin_ref,
-    ccol_ref, crow_ref, scal_ref, xg_ref, fu_ref, fd_ref,
-    dh, sums, f1,
-    da, wo, gated, gr, q, k, v, st, cos, sin, dr, xt, ao, ag, rxo, rxg, fin, qo, gb, lg, got, logs, rxf, fo, pbuf, gbuf,
-    lsem, gsem, xsem, fsend, frecv, osem, fosem, ssend, srecv, lsend, lrecv, psend, precv, *line,
-):
-    me = Place()
-    z, p = me.z, me.p
-    greet(
-        [(me.plane(m), None) for m in (1, 2, 3)]
-        + [(me.at((z + t) % LINE, p, me.f), None) for t in range(1, LINE)]
-    )
-    width = da.shape[1]
-    tokens = da.shape[0]
-    keys, values = q.shape[1], v.shape[1]
-    blocks = tokens // STRETCH
-    half = keys // 2
-    pq = [me.xor(m) for m in range(4)]
-    chunk = fu_ref.shape[0] // SPANS
-
-    def f_block(h, zp, place):
-        return (fu_ref, fd_ref)[h].at[pl.ds(pl.multiple_of((zp * PLANE + place) * chunk, chunk), chunk), :]
-
-    away = ((1, 3), (2, 3))
-    kept = ((0, 2), (0, 1))
-    nbr = (1, 2)
-
-    def f_copy(h, zp, j):
-        return remote(
-            f_block(h, zp, pq[away[h][j]]), rxf.at[h, zp, j], fsend.at[h, zp, j], frecv.at[h, zp, j], me.plane(nbr[h])
-        )
-
-    loads = [
-        start(pltpu.make_async_copy(a, b, lsem.at[i]))
-        for i, (a, b) in enumerate(
-            [(da_ref, da), (gated_ref, gated), (wo_ref, wo), (q_ref, q), (k_ref, k), (v_ref, v), (s_ref, st),
-             (cos_ref, cos), (sin_ref, sin)]
-        )
-    ]
-    for zp in range(LINE):
-        for h in range(2):
-            for j in range(2):
-                f_copy(h, zp, j).start()
-
-    def f_own(u):
-        h, zp = u % 2, u // 2
-        return [
-            pltpu.make_async_copy(f_block(h, zp, pq[kept[h][j]]), fo.at[u % 2, j], fosem.at[u % 2, j])
-            for j in range(2)
-        ]
-
-    def f_out(u):
-        h, zp = u % 2, u // 2
-        return pltpu.make_async_copy(rxf.at[h, zp], f1.at[h, zp], osem.at[u])
-
-    for u in range(2):
-        for c in f_own(u):
-            c.start()
-
-    def f_unit(u):
-        h, zp = u % 2, u // 2
-        for j, c in enumerate(f_own(u)):
-            c.wait()
-            f_copy(h, zp, j).wait_recv()
-            add_rows(rxf.at[h, zp, j], fo.at[u % 2, j])
-        f_out(u).start()
-        if u + 2 < 2 * LINE:
-            for c in f_own(u + 2):
-                c.start()
-
-    def tile_rows(i):
-        return rows_at(i * 256, 256)
-
-    def gate_loads(i):
-        at = tile_rows(i)
-        slot = i % 2
-        return (
-            pltpu.make_async_copy(gate_ref.at[at, :], gr.at[slot, 0], gsem.at[slot, 0]),
-            pltpu.make_async_copy(ret_ref.at[at, :], gr.at[slot, 1], gsem.at[slot, 1]),
-        )
-
-    for c in gate_loads(0):
-        c.start()
-
-    out_sum = LineSum(me, lambda zz: ao.at[rows_at(zz * (width // LINE), width // LINE), :], rxo, *line[:4], add_rows)
-    gate_sum = LineSum(me, lambda zz: ag.at[rows_at(zz * (width // LINE), width // LINE), :], rxg, *line[4:], add_rows)
-
-    loads[0].wait()
-    loads[1].wait()
-
-    @pl.loop(0, width, step=256)
-    def _(i):
-        at = rows_at(i, 256)
-        ao[at, :] = tn(da[:, at], gated[...]).astype(BF16)
-
-    out_sum.begin()
-    for c in loads[2:]:
-        c.wait()
-
-    tiles = tokens // 256
-
-    @pl.loop(0, tiles)
-    def _(i):
-        @pl.when(i + 1 < tiles)
-        def _():
-            for c in gate_loads(i + 1):
-                c.start()
-
-        for c in gate_loads(i):
-            c.wait()
-        at = tile_rows(i)
-        slot = i % 2
-        dgated = nt(da[at, :], wo[...])
-        gate = gr[slot, 0]
-        ret = gr[slot, 1]
-        centered = ret - jnp.mean(ret, axis=1, keepdims=True)
-        scale = lax.rsqrt(jnp.mean(centered * centered, axis=1, keepdims=True) + 1e-05)
-        grouped = centered * scale
-        sig = 1.0 / (1.0 + jnp.exp(-gate))
-        silu = gate * sig
-        dh[at, 2 * keys + values :] = (dgated * grouped * (sig * (1.0 + gate * (1.0 - sig)))).astype(BF16)
-        dg = dgated * silu
-        dr[at, :] = (
-            scale * (dg - jnp.mean(dg, axis=1, keepdims=True) - grouped * jnp.mean(dg * grouped, axis=1, keepdims=True))
-        ).astype(BF16)
-
-    lg[...] = jnp.zeros_like(lg)
-
-    @pl.loop(0, blocks)
-    def _(c):
-        at = rows_at(c * STRETCH, STRETCH)
-        decayed = (q[at, :].astype(F32) * jnp.exp(ccol_ref[at, :])).astype(BF16)
-        got_q = tn(decayed, dr[at, :])
-        qo[c] = got_q
-        lg[...] += scal_ref[blocks + c, 0:1, 0:1] * got_q
-
-    gb[0] = lg[...].astype(BF16)
-
-    def state_copies(t, to, slot):
-        device = me.at(to, p, me.f)
-        return (
-            remote(gb.at[0], got.at[slot], ssend.at[t - 1], srecv.at[t - 1], device),
-            remote(scal_ref.at[2 * blocks], logs.at[slot], lsend.at[t - 1], lrecv.at[t - 1], device),
-        )
-
-    for t in range(1, LINE):
-
-        @pl.when(z - t >= 0)
-        def _():
-            for c in state_copies(t, z - t, z):
-                c.start()
-
-    def x_tile(i):
-        return pltpu.make_async_copy(xg_ref.at[:, rows_at(i * 256, 256)], xt.at[i % 2], xsem.at[i % 2])
-
-    x_tile(0).start()
-
-    @pl.loop(0, width // 256)
-    def _(i):
-        @pl.when(i + 1 < width // 256)
-        def _():
-            x_tile(i + 1).start()
-
-        x_tile(i).wait()
-        ag[rows_at(i * 256, 256), :] = tn(xt[i % 2], dh[:, 2 * keys + values :]).astype(BF16)
-
-    gate_sum.begin()
-    out_sum.step(0)
-    f_unit(0)
-    f_unit(1)
-    out_sum.step(1)
-
-    for t in range(1, LINE):
-
-        @pl.when(z + t < LINE)
-        def _():
-            for c in state_copies(t, z + t, z + t):
-                c.wait_recv()
-
-        @pl.when(z - t >= 0)
-        def _():
-            for c in state_copies(t, z - t, z):
-                c.wait_send()
-
-    lg[...] = jnp.zeros_like(lg)
-    for j in reversed(range(1, LINE)):
-
-        @pl.when(z < j)
-        def _():
-            lg[...] = lg[...] * jnp.exp(logs[j, 0:1, 0:1]) + got[j].astype(F32)
-
-    for c in reversed(range(blocks)):
-        gb[c] = lg[...].astype(BF16)
-        if c:
-            lg[...] = lg[...] * scal_ref[c, 0:1, 0:1] + qo[c]
-
-    t_size = 256
-
-    @pl.loop(0, blocks)
-    def _(c):
-        blk = rows_at(c * STRETCH, STRETCH)
-        row = crow_ref[c, 0:1, :]
-        end = crow_ref[c, 0:1, STRETCH - 1 : STRETCH]
-        for r in range(0, STRETCH, t_size):
-            at = rows_at(c * STRETCH + r, t_size)
-            col = ccol_ref[at, :]
-            t_index = lax.broadcasted_iota(jnp.int32, (t_size, STRETCH), 0) + r
-            s_index = lax.broadcasted_iota(jnp.int32, (t_size, STRETCH), 1)
-            mask = jnp.where(t_index >= s_index, jnp.exp(jnp.minimum(col - row, 0.0)), 0.0)
-            pbuf[r : r + t_size, :] = (nt(q[at, :], k[blk, :]) * mask).astype(BF16)
-            g = (nt(dr[at, :], v[blk, :]) * mask).astype(BF16)
-            gbuf[r : r + t_size, :] = g
-            dq = nt(dr[at, :], st[c]) * jnp.exp(col) + nn(g, k[blk, :])
-            a, b = dq[:, :half], dq[:, half:]
-            dh[at, :half] = (a * cos[at, :] + b * sin[at, :]).astype(BF16)
-            dh[at, half:keys] = (b * cos[at, :] - a * sin[at, :]).astype(BF16)
-        for r in range(0, STRETCH, t_size):
-            at = rows_at(c * STRETCH + r, t_size)
-            tail = jnp.exp(end - ccol_ref[at, :])
-            w = (v[at, :].astype(F32) * tail).astype(BF16)
-            dk = nt(w, gb[c]) + tn(gbuf[:, r : r + t_size], q[blk, :])
-            a, b = dk[:, :half], dk[:, half:]
-            dh[at, keys : keys + half] = (a * cos[at, :] + b * sin[at, :]).astype(BF16)
-            dh[at, keys + half : 2 * keys] = (b * cos[at, :] - a * sin[at, :]).astype(BF16)
-            dv = nn(k[at, :], gb[c]) * tail + tn(pbuf[:, r : r + t_size], dr[blk, :])
-            dh[at, 2 * keys : 2 * keys + values] = dv.astype(BF16)
-
-    plane = []
-
-    def deal(i, chain, a):
-        chain.arrive()
-        total_rows(z, fin.at[i], a.at[rows_at(z * (width // LINE), width // LINE), :], chain.rx)
-        cols = pl.ds(i * values, values)
-        for m in (1, 2, 3):
-            plane.append(
-                start(
-                    remote(
-                        fin.at[i, rows_at(pq[m] * chunk, chunk), :], sums.at[p, :, cols],
-                        psend.at[i, m], precv.at[i, m], me.plane(m),
-                    )
-                )
-            )
-        plane.append(
-            start(
-                pltpu.make_async_copy(
-                    fin.at[i, rows_at(p * chunk, chunk), :], sums.at[p, :, cols], psend.at[i, 0]
-                )
-            )
-        )
-
-    out_sum.step(2)
-    for u in range(2, 4):
-        f_unit(u)
-    gate_sum.step(0)
-    deal(0, out_sum, ao)
-    gate_sum.step(1)
-    for u in range(4, 6):
-        f_unit(u)
-    gate_sum.step(2)
-    deal(1, gate_sum, ag)
-    for u in range(6, 2 * LINE):
-        f_unit(u)
-    for c in plane:
-        c.wait()
-    out_sum.finish()
-    gate_sum.finish()
-    for u in range(2 * LINE):
-        f_out(u).wait()
-    for zp in range(LINE):
-        for h in range(2):
-            for j in range(2):
-                f_copy(h, zp, j).wait_send()
-
-
-def retention_back(da, wo, gated, gate, ret, q, k, v, states, cos, sin, ccol, crow, scal, xg, fu, fd, cid):
-    tokens, width = da.shape
-    keys, values = q.shape[1], v.shape[1]
-    chunk = width // SPANS
-    blocks = tokens // STRETCH
-    hidden = fu.shape[1]
-    deep = width // LINE
-    return comm_call(
-        retention_back_kernel,
-        [
-            jax.ShapeDtypeStruct((tokens, 2 * keys + 2 * values), BF16),
-            jax.ShapeDtypeStruct((PLANE, chunk, 2 * values), BF16),
-            jax.ShapeDtypeStruct((2, LINE, 2, chunk, hidden), BF16),
-        ],
-        [da, wo, gated, gate, ret, q, k, v, states, cos, sin, ccol, crow, scal, xg, fu, fd],
-        [
-            pltpu.VMEM((tokens, width), BF16),
-            pltpu.VMEM(wo.shape, BF16),
-            pltpu.VMEM(gated.shape, BF16),
-            pltpu.VMEM((2, 2, 256, values), F32),
-            pltpu.VMEM(q.shape, BF16),
-            pltpu.VMEM(k.shape, BF16),
-            pltpu.VMEM(v.shape, BF16),
-            pltpu.VMEM(states.shape, BF16),
-            pltpu.VMEM(cos.shape, F32),
-            pltpu.VMEM(sin.shape, F32),
-            pltpu.VMEM((tokens, values), BF16),
-            pltpu.VMEM((2, tokens, 256), BF16),
-            pltpu.VMEM((width, values), BF16),
-            pltpu.VMEM((width, values), BF16),
-            pltpu.VMEM((LINE + 1, deep, values), BF16),
-            pltpu.VMEM((LINE + 1, deep, values), BF16),
-            pltpu.VMEM((2, deep, values), BF16),
-            pltpu.VMEM((blocks, keys, values), F32),
-            pltpu.VMEM((blocks, keys, values), BF16),
-            pltpu.VMEM((keys, values), F32),
-            pltpu.VMEM((LINE, keys, values), BF16),
-            pltpu.VMEM((LINE, 8, 128), F32),
-            pltpu.VMEM((2, LINE, 2, chunk, hidden), BF16),
-            pltpu.VMEM((2, 2, chunk, hidden), BF16),
-            pltpu.VMEM((STRETCH, STRETCH), BF16),
-            pltpu.VMEM((STRETCH, STRETCH), BF16),
-            DMA((9,)),
-            DMA((2, 2)),
-            DMA((2,)),
-            DMA((2, LINE, 2)),
-            DMA((2, LINE, 2)),
-            DMA((2 * LINE,)),
-            DMA((2, 2)),
-            DMA((LINE - 1,)),
-            DMA((LINE - 1,)),
-            DMA((LINE - 1,)),
-            DMA((LINE - 1,)),
-            DMA((2, PLANE)),
-            DMA((2, PLANE)),
-        ]
-        + line_sems()
-        + line_sems(),
-        cid,
-        in_specs=[ANY] * 11 + [VM] * 3 + [ANY] * 3,
-        out_specs=[VM, ANY, ANY],
-    )
-
-
-def everyone(size):
-    return range(0, size, SPANS)
-
-
-def swap(x, mask):
-    n = lax.axis_size("seq")
-    return lax.ppermute(x, "seq", [(s, s ^ mask) for s in range(n)])
-
-
-def take(x, index, axis):
-    return lax.dynamic_index_in_dim(x, index, axis, False)
-
-
-def plus(a, b):
-    return (a.astype(F32) + b.astype(F32)).astype(BF16)
-
-
-def line_sum(x, z):
-    n = lax.axis_size("seq")
-    up = dn = None
-    for t in range(1, LINE):
-        up_at = jnp.clip(LINE - t + z, 0, LINE - 1)
-        dn_at = jnp.clip(z + t - LINE, 0, LINE - 1)
-        ups = [
-            (b + k * PLANE + p, b + (k + 1) * PLANE + p)
-            for b in everyone(n)
-            for k in range(t)
-            for p in range(PLANE)
-        ]
-        dns = [
-            (b + (LINE - 1 - k) * PLANE + p, b + (LINE - 2 - k) * PLANE + p)
-            for b in everyone(n)
-            for k in range(t)
-            for p in range(PLANE)
-        ]
-        send_up, send_dn = take(x, up_at, 0), take(x, dn_at, 0)
-        if t > 1:
-            send_up, send_dn = plus(send_up, up), plus(send_dn, dn)
-        up = lax.ppermute(send_up, "seq", ups)
-        dn = lax.ppermute(send_dn, "seq", dns)
-    return take(x, z, 0).astype(F32) + up.astype(F32) + dn.astype(F32)
-
-
-def plane_deal(x, p):
-    got = [take(x, p, 0)]
-    for mask in range(1, PLANE):
-        got.append(swap(take(x, p ^ mask, 0), mask))
-    return jnp.stack([sum_of_choice(got, p, q) for q in range(PLANE)])
-
-
-def sum_of_choice(got, p, q):
-    out = got[0]
-    for mask in range(1, PLANE):
-        out = jnp.where((p ^ q) == mask, got[mask], out)
-    return out
-
-
-def gains_kernel(x_ref, out, rx, send, recv):
-    me = Place()
-    rounds = [
-        [me.partner()],
-        [me.plane(m) for m in (1, 2, 3)],
-        [me.at((me.z + t) % LINE, me.p, me.f) for t in (1, 2, 3)],
-    ]
-    greet([(d, None) for r in rounds for d in r])
-    out[...] = x_ref[...]
-    k = 0
-    for peers in rounds:
-        copies = []
-        for d in peers:
-            c = remote(out, rx.at[k], send.at[k], recv.at[k], d)
-            c.start()
-            copies.append(c)
-            k += 1
-        for c in copies:
-            c.wait()
-        for j in range(k - len(peers), k):
-            out[...] += rx[j]
-
-
-def gains_sum(x, cid):
-    return comm_call(
-        gains_kernel,
-        [jax.ShapeDtypeStruct(x.shape, F32)],
-        [x],
-        [pltpu.VMEM((7,) + x.shape, F32), DMA((7,)), DMA((7,))],
-        cid,
-        in_specs=[VM],
-        out_specs=[VM],
-    )[0]
-
-
 def last_kernel(
     dh_ref, xg_ref, wq_ref, wk_ref, wv_ref, wg_ref, f1_ref, tok_ref, gain_ref, resid_ref, second_ref,
     grad_tokens, gains, fout, sums,
@@ -1671,29 +1319,32 @@
     share_part(3)
     share_part(1)
     pass_on(3)
+    v_sum.near(0)
     share_part(2)
     pass_on(1)
     share_part(0)
+    v_sum.near(1)
     pass_on(2)
     pass_on(0)
-    v_sum.step(0)
+    v_sum.far()
+    for c in keeps:
+        c.wait()
+    for zp in (3, 0, 2, 1):
+        for h in range(2):
+            f_copy(h, zp).wait_recv()
+            add_rows(kf.at[h, zp], rf2.at[h, zp])
+    for zz in (3, 2, 1):
+        fa_sum.begin((zz,))
+        fb_sum.begin((zz,))
+    q_sum.near(0)
     sends["a", 0].wait_recv()
     add_into(rx1a.at[0], whole, rx0.at[2], ca)
     s2a = start(remote(rx1a.at[0], rx2a, xsend.at[4], xrecv.at[4], me.plane(2)))
     sends["b", 0].wait_recv()
     add_into(rx1b.at[0], whole, rx0.at[1], cb)
     s2b = start(remote(rx1b.at[0], rx2b, xsend.at[5], xrecv.at[5], me.plane(1)))
-    v_sum.step(1)
-    for c in keeps:
-        c.wait()
-    for zp in (3, 0, 2, 1):
-        for h in range(2):
-            f_copy(h, zp).wait_recv()
-            add_rows(kf.at[h, zp], rf2.at[h, zp])
-    fa_sum.begin()
-    fb_sum.begin()
-    v_sum.step(2)
-    q_sum.step(0)
+    q_sum.near(1)
+    q_sum.far()
     sends["a", 1].wait_recv()
     sends["b", 1].wait_recv()
     s2a.wait_recv()
@@ -1761,25 +1412,23 @@
         )
 
     gain_begin(0)
-    q_sum.step(1)
+    deal(0, v_sum, av)
     gain_end(0)
     gain_begin(1)
-    deal(0, v_sum, av)
+    deal(1, q_sum, aq)
     gain_end(1)
     gain_begin(2)
-    q_sum.step(2)
-    fa_sum.step(0)
-    gain_end(2)
-    fb_sum.step(0)
-    deal(1, q_sum, aq)
-    fa_sum.step(1)
-    fb_sum.step(1)
-    fa_sum.step(2)
-    fb_sum.step(2)
+    fa_sum.near(0)
+    fb_sum.near(0)
+    fa_sum.near(1)
+    fa_sum.far()
+    fb_sum.near(1)
+    fb_sum.far()
     fa_sum.arrive()
     total_rows(z, fout.at[0], kf.at[0, z], rxfa)
     fb_sum.arrive()
     total_rows(z, fout.at[1], kf.at[1, z], rxfb)
+    gain_end(2)
     for c in plane:
         c.wait()
     for chain in (v_sum, q_sum, fa_sum, fb_sum):
@@ -1850,49 +1499,17 @@
     )
 
 
-def layer_norm(values_in, gain_vec, bias_vec):
-    average = jnp.mean(values_in, axis=-1, keepdims=True)
-    centered = values_in - average
-    variance = jnp.mean(centered * centered, axis=-1, keepdims=True)
-    return centered * lax.rsqrt(variance + 1e-05) * gain_vec + bias_vec
-
-
-def group_norm(values_in):
-    average = jnp.mean(values_in, axis=-1, keepdims=True)
-    centered = values_in - average
-    variance = jnp.mean(centered * centered, axis=-1, keepdims=True)
-    return centered * lax.rsqrt(variance + 1e-05)
-
-
-def exact_gelu(values_in):
-    return jax.nn.gelu(values_in, approximate=False)
-
-
-def swish_gate(gate_proj, grouped):
-    return jax.nn.silu(gate_proj) * grouped
-
-
-def angles_of(positions, half_width):
+def angle_tables(first, count, fine, half_width):
     frequency = 10000.0 ** (-jnp.linspace(0.0, 1.0, half_width, dtype=F32))
-    angles = positions.astype(F32)[:, None] * frequency[None, :]
-    return jnp.cos(angles), jnp.sin(angles)
-
-
-def rotate(values_in, cosine, sine_part):
-    half_width = values_in.shape[-1] // 2
-    first_half = values_in[..., :half_width]
-    second_half = values_in[..., half_width:]
-    return jnp.concatenate(
-        [
-            first_half * cosine - second_half * sine_part,
-            second_half * cosine + first_half * sine_part,
-        ],
-        axis=-1,
-    )
-
-
-def dot(spec, a, b):
-    return jnp.einsum(spec, a, b, preferred_element_type=F32)
+    coarse = ((first + fine * jnp.arange(count)) % SEQUENCE_LENGTH).astype(F32)[:, None] * frequency[None, :]
+    near = jnp.arange(fine).astype(F32)[:, None] * frequency[None, :]
+    wide = (count, 8, half_width)
+    return [
+        jnp.broadcast_to(jnp.cos(coarse)[:, None], wide),
+        jnp.broadcast_to(jnp.sin(coarse)[:, None], wide),
+        jnp.cos(near),
+        jnp.sin(near),
+    ]
 
 
 def shards(
@@ -1949,12 +1566,17 @@
     w_up = features_in(w_up.T).T if repeats > 1 else w_up
     ln1_gain, ln1_bias = features_in(ln1_gain), features_in(ln1_bias)
     ln2_gain, ln2_bias = features_in(ln2_gain), features_in(ln2_bias)
-    inputs32 = tokens.astype(F32)
-    xn_first = layer_norm(inputs32, ln1_gain, ln1_bias)
     decays = jnp.pad(decay_log.T, ((0, 8 - heads), (0, 0)))
-    xg, decay_rows, key_w, value_w, query_w, gate_w, out_w = gather_in(
-        xn_first.astype(BF16),
+    fine = 64
+    (
+        normed, q_rot, k_rot, value, gate_proj, retained, gated_low, prev_states, attn_share,
+        cosine, sine_part, ccol, crow, scalars, key_w, value_w, query_w, gate_w, out_w,
+    ) = attention(
+        tokens,
+        ln1_gain,
+        ln1_bias,
         decays,
+        angle_tables(z * group_rows, group_rows // fine, fine, w_key.shape[1] // heads // 2),
         [
             wide_in(w_key, 0),
             wide_in(w_value, 0),
@@ -1965,43 +1587,7 @@
         (False, False, False, False, True),
         0,
     )
-    normed = xg.reshape(group_rows, width)
     key_width, value_width = key_w.shape[1], value_w.shape[1]
-    log_decay = lax.dynamic_index_in_dim(decay_rows, p, 1, False).reshape(blocks, STRETCH)
-    cumulative = jnp.cumsum(log_decay, axis=1)
-    last = cumulative[:, -1]
-    total = jnp.sum(last)
-
-    positions = (z * group_rows + jnp.arange(group_rows)) % SEQUENCE_LENGTH
-    cosine, sine_part = angles_of(positions, key_width // 2)
-    q_rot = rotate(dot("td,dq->tq", normed, query_w), cosine, sine_part).astype(BF16)
-    k_rot = rotate(dot("td,dq->tq", normed, key_w), cosine, sine_part).astype(BF16)
-    value = dot("td,dv->tv", normed, value_w).astype(BF16)
-    gate_proj = dot("td,dv->tv", normed, gate_w)
-
-    q_blocks = q_rot.reshape(blocks, STRETCH, key_width)
-    k_blocks = k_rot.reshape(blocks, STRETCH, key_width)
-    v_blocks = value.reshape(blocks, STRETCH, value_width)
-    tail_scale = jnp.exp(last[:, None] - cumulative)
-    tail_values = (v_blocks.astype(F32) * tail_scale[:, :, None]).astype(BF16)
-    key_values = dot("csk,csd->ckd", k_blocks, tail_values)
-    local = [jnp.zeros((key_width, value_width), F32)]
-    for c in range(blocks):
-        local.append(jnp.exp(last[c]) * local[-1] + key_values[c])
-    incoming = line_states(local[-1].astype(BF16), total, False, 1)
-    before = jnp.exp(jnp.cumsum(last) - last)
-    prev_states = jnp.stack([local[c] + before[c] * incoming for c in range(blocks)]).astype(BF16)
-
-    gaps = cumulative[:, :, None] - cumulative[:, None, :]
-    indices = jnp.arange(STRETCH)
-    lower = indices[:, None] >= indices[None, :]
-    mask = jnp.where(lower[None], jnp.exp(jnp.minimum(gaps, 0.0)), 0.0)
-    weighted = (dot("ctk,csk->cts", q_blocks, k_blocks) * mask).astype(BF16)
-    q_decayed = (q_blocks.astype(F32) * jnp.exp(cumulative)[:, :, None]).astype(BF16)
-    retained = dot("cts,csd->ctd", weighted, v_blocks) + dot("ctk,ckd->ctd", q_decayed, prev_states)
-    retained = retained.reshape(group_rows, value_width)
-    gated_low = swish_gate(gate_proj, group_norm(retained)).astype(BF16)
-    attn_share = dot("tv,vd->td", gated_low, out_w).astype(BF16)
     block_out, grad_resid, gains_second, grad_attn, grad_up, grad_down = ffn_part(
         attn_share.reshape(PLANE, 2, row_count, width),
         tokens,
@@ -2013,9 +1599,6 @@
         2,
     )
     grad_attn = grad_attn.reshape(group_rows, width)
-    crow = jnp.broadcast_to(cumulative[:, None, :], (blocks, 8, STRETCH))
-    scalars = jnp.concatenate([jnp.exp(last), before, total[None]])
-    scalars = jnp.broadcast_to(scalars[:, None, None], (2 * blocks + 1, 8, 128))
     grad_heads, sums_first, ffn_first = retention_back(
         grad_attn,
         out_w,
@@ -2028,7 +1611,7 @@
         prev_states,
         cosine,
         sine_part,
-        cumulative.reshape(group_rows, 1),
+        ccol,
         crow,
         scalars,
         normed,

time: 736 us -> 567 us (0.77)
  Pallas kernels: 622 us -> 541 us
  matrix products: 44.4 us -> 0 us
  other arithmetic: 25.1 us -> 4.92 us
  local copies, waits for them, and re-layouts: 28.2 us -> 17.5 us
    pallas_call x5 -> x4, Pallas kernels: 622 us -> 541 us  [comm_call(): pl.pallas_call(kernel, out_shape=outs, in_specs=in_specs if in_specs is n...]
    dot_general x8 -> x0, matrix products: 44.4 us -> none  [dot(): return jnp.einsum(spec, a, b, preferred_element_type=F32)]
    another operation x8 -> x0, other arithmetic: 13 us -> none
where the time goes in v4:
time: 567 us; the launch traced here: 564 us
  Pallas kernels  541 us (95%)
  local copies, waits for them, and re-layouts  17.5 us (3%)
    pallas_call x4, Pallas kernels, comm_call(): pl.pallas_call(kernel, out_shape=outs, in_specs=in_specs if in_specs is n...  541 us

profile of v4, /device:TPU:16, one launch (start us, length us, event | category | flops | bytes accessed | tf_op | source)
XLA Modules:
  0.0 564.1 jit_solution(16918509325394659045)
XLA Ops:
  0.8 1.3 pad.4.dec_ref
  2.2 0.8 multiply_sine_fusion
  3.1 0.7 broadcast_in_dim.17.sbase
  3.7 0.7 broadcast_in_dim.16.cbase
  4.4 154.4 %shard_map.237 = (bf16[2048,2048]{1,0:T(8,128)(2,1)}, bf16[2048,256]{1,0:T(8,128)(2,1)}, bf16[2048,256]{1,0:T(8,128)(2,1)}, bf16[2048,512]{1,0:T(8,128)(2,1)}, f...) custom-call(bf16[256,2048]{1,0:T(8,128)(2,1)} %tok_ref.5, ...), custom_call_target="tpu_custom_call" | custom-call | tf_op jit(solution)/shard_map/pallas_call | solution.py:81
  158.9 105.0 %shard_map.238 = (bf16[256,2048]{1,0:T(8,128)(2,1)}, f32[256,2048]{1,0:T(8,128)}, f32[8,2048]{1,0:T(8,128)}, bf16[8,256,2048]{2,1,0:T(8,128)(2,1)}, bf16[2048,20...) custom-call(bf16[4,2,256,2048]{3,2,1,0:T(8,128)(2,1)} %bitcast.34, bf16[256,2048]{1,0:T(8,128)(2,1)} %tok_ref.5, ...), custom_call_target="tpu_custom_call" | custom-call | tf_op jit(solution)/shard_map/pallas_call | solution.py:81
  263.8 120.8 %shard_map.239 = (bf16[2048,1536]{1,0:T(8,128)(2,1)}, bf16[4,128,1024]{2,1,0:T(8,128)(2,1)}, bf16[2,4,2,128,2048]{4,3,2,1,0:T(8,128)(2,1)}) custom-call(bf16[2048,2048]{1,0:T(8,128)(2,1)} %bitcast.35, bf16[512,2048]{1,0:T(8,128)(2,1)} %get-tuple-element.48.wo_ref, bf16[2048,512]{1,0:T(8,128)(2,1)} %get-tuple-element.49.gated_ref, ...), custom_call_target="tpu_custom_call" | custom-call | tf_op jit(solution)/shard_map/pallas_call | solution.py:81
  384.7 160.6 %shard_map.240 = (bf16[256,2048]{1,0:T(8,128)(2,1)}, f32[8,2048]{1,0:T(8,128)}, f32[2,128,2048]{2,1,0:T(8,128)}, bf16[4,128,1024]{2,1,0:T(8,128)(2,1)}) custom-call(bf16[2048,1536]{1,0:T(8,128)(2,1)} %get-tuple-element.64.dh_ref, bf16[2048,2048]{1,0:T(8,128)(2,1)} %get-tuple-element.61.xg_ref, bf16[2048,256]{1,0:T(8,128)(2,1)} %get-tuple-element.65.wq_ref, ...), custom_call_target="tpu_custom_call" | custom-call | tf_op jit(solution)/shard_map/pallas_call | solution.py:81
  545.3 1.6 fusion.3
  546.9 1.2 convert_bitcast_fusion.2
  548.1 0.3 copy.30
  548.4 1.3 copy.35
  549.8 1.1 convert_bitcast_fusion.3
  550.9 1.0 copy.29
  551.9 2.0 copy.34
  554.1 1.0 copy.33
  555.1 1.2 slice_bitcast_fusion
  556.3 1.3 copy.37
  557.6 1.6 convert_bitcast_fusion
  559.2 1.3 copy.32
  560.5 0.3 copy.31
  560.8 1.3 copy.36
  562.1 1.0 copy.40
  563.1 1.0 copy.41
  (12 shorter events, 0.4 us)
Async XLA Ops:
  548.4 6.7 %copy-start = (f32[2,128,2048]{2,1,0:T(8,128)S(1)}, f32[2,128,2048]{2,1,0:T(8,128)}, u32[]{:S(2)}) copy-start(f32[2,128,2048]{2,1,0:T(8,128)} %get-tuple-element.76) | copy-start | bytes 6291460
  557.6 4.5 copy-start.1
  560.8 2.3 copy-start.2

commit v5 on v4

--- a/solution.py
+++ b/solution.py
@@ -122,10 +122,10 @@
 
 
 def ffn_kernel(
-    x_ref, tok_ref, gain_ref, bias_ref, wu_ref, wd_ref, cot_ref,
+    gated_ref, wo_ref, tok_ref, gain_ref, bias_ref, wu_ref, wd_ref, cot_ref,
     block_out, resid_grad, gains, da, fu, fd,
-    wu, wd, rx0, rx1a, rx1b, rx2a, rx2b, resid, xn, act, dact, du, part, prx, dab, stage,
-    lsem, csend, crecv, xsend, xrecv, psend, precv, gsend, grecv, ssem,
+    share, wu, wd, rx0, rx1a, rx1b, rx2a, rx2b, resid, xn, act, dact, du, cot, dab, stage, tmp,
+    lsem, gload, csend, crecv, xsend, xrecv, psend, precv, gsend, grecv, ksend, krecv, ssem,
 ):
     me = Place()
     p, f = me.p, me.f
@@ -134,211 +134,305 @@
     hidden = wu.shape[1]
     q = [me.xor(m) for m in range(4)]
     wide = width // 2
+    hr = rows // 2
+    span = 2 * rows
     ca, cb = pl.ds(0, wide), pl.ds(wide, wide)
     everything, whole = pl.ds(0, width), pl.ds(0, wide)
-    load_d = start(pltpu.make_async_copy(wd_ref, wd, lsem.at[0]))
-    load_u = start(pltpu.make_async_copy(wu_ref, wu, lsem.at[1]))
+    own_half = [pl.ds(h * hr, hr) for h in range(2)]
+    mine = [rows_at(h * rows + f * hr, hr) for h in range(2)]
+    theirs = [rows_at(h * rows + (1 - f) * hr, hr) for h in range(2)]
+    both = [pl.ds(h * rows, rows) for h in range(2)]
+
     order = (3, 1, 2, 0)
-    first = [
-        start(remote(x_ref.at[q[m], 1 - f], rx0.at[q[m]], csend.at[m], crecv.at[m], me.partner()))
+    part_width = gated_ref.shape[1]
+    load_o = start(pltpu.make_async_copy(wo_ref, act, lsem.at[0]))
+    load_g = {
+        m: start(
+            pltpu.make_async_copy(
+                gated_ref.at[rows_at(q[m] * span, span), :],
+                xn.at[:, m * part_width : (m + 1) * part_width],
+                gload.at[m],
+            )
+        )
         for m in order
+    }
+    load_d = start(pltpu.make_async_copy(wd_ref, wd, lsem.at[1]))
+    load_c = [
+        start(
+            pltpu.make_async_copy(
+                cot_ref.at[pl.ds(c * rows + h * hr, hr), :], cot.at[pl.ds(h * rows + c * hr, hr), :], lsem.at[3 + 2 * h + c]
+            )
+        )
+        for h in range(2)
+        for c in range(2)
     ]
-    sends = {}
-    for c, m in zip(first, order):
-        c.wait_recv()
-        add_into(rx0.at[q[m]], everything, x_ref.at[q[m], f], everything)
+    load_u = start(pltpu.make_async_copy(wu_ref, wu, lsem.at[2]))
+    load_o.wait()
+    first, sends = {}, {}
+
+    def to_partner(m, h):
+        first[m, h] = start(
+            remote(
+                share.at[m, rows_at((1 - f) * rows + h * hr, hr)], rx0.at[m, own_half[h]],
+                csend.at[m, h], crecv.at[m, h], me.partner(),
+            )
+        )
+
+    for m in order:
+        load_g[m].wait()
+
+        @pl.loop(0, width, step=512)
+        def _(c):
+            at = rows_at(c, 512)
+            share[m, :, at] = nn(xn[:, m * part_width : (m + 1) * part_width], act[:, at]).astype(BF16)
+
+        to_partner(m, 0)
+    for m in order:
+        to_partner(m, 1)
+
+    def pass_on(m, h):
+        first[m, h].wait_recv()
+        at = own_half[h]
+        add_into(rx0.at[m, at], everything, share.at[m, rows_at(f * rows + h * hr, hr)], everything)
         k = 0 if m == 3 else 1
         if m & 1:
-            sends["a", k] = start(
-                remote(rx0.at[q[m], :, ca], rx1a.at[k], xsend.at[k], xrecv.at[k], me.plane(1))
+            sends["a", k, h] = start(
+                remote(rx0.at[m, at, ca], rx1a.at[k, at], xsend.at[k, h], xrecv.at[k, h], me.plane(1))
             )
         if m & 2:
-            sends["b", k] = start(
-                remote(rx0.at[q[m], :, cb], rx1b.at[k], xsend.at[2 + k], xrecv.at[2 + k], me.plane(2))
+            sends["b", k, h] = start(
+                remote(rx0.at[m, at, cb], rx1b.at[k, at], xsend.at[2 + k, h], xrecv.at[2 + k, h], me.plane(2))
             )
 
+    def second(h):
+        at = own_half[h]
+        sends["a", 0, h].wait_recv()
+        add_into(rx1a.at[0, at], whole, rx0.at[2, at], ca)
+        sends["a", 2, h] = start(
+            remote(rx1a.at[0, at], rx2a.at[at], xsend.at[4, h], xrecv.at[4, h], me.plane(2))
+        )
+        sends["b", 0, h].wait_recv()
+        add_into(rx1b.at[0, at], whole, rx0.at[1, at], cb)
+        sends["b", 2, h] = start(
+            remote(rx1b.at[0, at], rx2b.at[at], xsend.at[5, h], xrecv.at[5, h], me.plane(1))
+        )
+
+    for m in order:
+        pass_on(m, 0)
+
     load_d.wait()
+    for c in load_c:
+        c.wait()
 
     @pl.loop(0, hidden, step=256)
     def _(c):
         at = rows_at(c, 256)
-        dact[:, at] = nt(cot_ref[...], wd[at, :])
-
-    sends["a", 0].wait_recv()
-    add_into(rx1a.at[0], whole, rx0.at[q[2]], ca)
-    s2a = start(remote(rx1a.at[0], rx2a, xsend.at[4], xrecv.at[4], me.plane(2)))
-    sends["b", 0].wait_recv()
-    add_into(rx1b.at[0], whole, rx0.at[q[1]], cb)
-    s2b = start(remote(rx1b.at[0], rx2b, xsend.at[5], xrecv.at[5], me.plane(1)))
-    sends["a", 1].wait_recv()
-    sends["b", 1].wait_recv()
+        dact[:, at] = nt(cot[...], wd[at, :])
+
+    second(0)
+    for m in order:
+        pass_on(m, 1)
     load_u.wait()
-    s2a.wait_recv()
-    s2b.wait_recv()
-
-    mine = f * rows
-    theirs = (1 - f) * rows
     step = 32
+
+    def norm(h):
+        for key in (("a", 1, h), ("b", 1, h), ("a", 2, h), ("b", 2, h)):
+            sends[key].wait_recv()
+
+        @pl.loop(0, hr, step=step)
+        def _(r):
+            at = pl.ds(pl.multiple_of(h * hr + r, step), step)
+            left = rx0[0, at, ca].astype(F32) + rx1a[1, at, :].astype(F32) + rx2a[at, :].astype(F32)
+            right = rx0[0, at, cb].astype(F32) + rx1b[1, at, :].astype(F32) + rx2b[at, :].astype(F32)
+            v = tok_ref[at, :].astype(F32) + jnp.concatenate([left, right], axis=1)
+            resid[at, :] = v
+            centered = v - jnp.mean(v, axis=1, keepdims=True)
+            scale = lax.rsqrt(jnp.mean(centered * centered, axis=1, keepdims=True) + 1e-05)
+            xn[pl.ds(pl.multiple_of(h * rows + f * hr + r, step), step), :] = (
+                centered * scale * gain_ref[...] + bias_ref[...]
+            ).astype(BF16)
+
+        return start(remote(xn.at[mine[h]], xn.at[mine[h]], psend.at[0, h], precv.at[0, h], me.partner()))
+
+    def hidden_part(h):
+        @pl.loop(0, hidden, step=512)
+        def _(c):
+            at = rows_at(c, 512)
+            u = nn(xn[both[h], :], wu[:, at])
+            e = 0.5 * (1.0 + lax.erf(u * 0.7071067811865476))
+            act[both[h], at] = (u * e).astype(BF16)
+            slope = e + u * jnp.exp(-0.5 * u * u) * 0.3989422804014327
+            du[both[h], at] = (dact[both[h], at] * slope).astype(BF16)
+
+    def back_part(h):
+        @pl.loop(0, width, step=512)
+        def _(c):
+            at = rows_at(c, 512)
+            tmp[:rows, :] = nt(du[both[h], :], wu[at, :])
+            resid_grad[own_half[h], at] = tmp[rows_at(f * hr, hr), :]
+            share[0, own_half[h], at] = tmp[rows_at((1 - f) * hr, hr), :].astype(BF16)
+
+        return start(
+            remote(share.at[0, own_half[h]], share.at[1, own_half[h]], psend.at[1, h], precv.at[1, h], me.partner())
+        )
+
+    def norm_back(h):
+        @pl.loop(0, hr, step=step)
+        def _(r):
+            at = pl.ds(pl.multiple_of(h * hr + r, step), step)
+            dx = resid_grad[at, :] + share[1, at, :].astype(F32)
+            v = resid[at, :]
+            centered = v - jnp.mean(v, axis=1, keepdims=True)
+            scale = lax.rsqrt(jnp.mean(centered * centered, axis=1, keepdims=True) + 1e-05)
+            hat = centered * scale
+            gains[0:1, :] += jnp.sum(dx * hat, axis=0, keepdims=True)
+            gains[1:2, :] += jnp.sum(dx, axis=0, keepdims=True)
+            g = dx * gain_ref[...]
+            back = scale * (
+                g - jnp.mean(g, axis=1, keepdims=True) - hat * jnp.mean(g * hat, axis=1, keepdims=True)
+            )
+            back = back + cot[pl.ds(pl.multiple_of(h * rows + f * hr + r, step), step), :].astype(F32)
+            resid_grad[at, :] = back
+            dab[at, :] = back.astype(BF16)
+
+    quarter = hr // 2
+
+    def seat(m, h, k=None):
+        base = (q[m] * 2 + f) * rows + h * hr
+        if k is None:
+            return da.at[pl.ds(pl.multiple_of(base, hr), hr), :]
+        return da.at[pl.ds(pl.multiple_of(base + k * quarter, quarter), quarter), :]
+
+    spread = {}
+
+    def spread_begin(h):
+        spread["own", h] = start(pltpu.make_async_copy(dab.at[own_half[h]], seat(0, h), gload.at[h]))
+        for i in range(2):
+            for to, k in ((1, i), (2, 1 - i)):
+                sem = (to - 1) * 2 + i
+                spread[to, i, h] = start(
+                    remote(
+                        dab.at[pl.ds(h * hr + k * quarter, quarter)], seat(0, h, k),
+                        gsend.at[sem, h], grecv.at[sem, h], me.plane(to),
+                    )
+                )
+        spread["core", 0, h] = start(
+            remote(dab.at[own_half[h]], seat(0, h), ksend.at[0, h], krecv.at[0, h], me.partner())
+        )
+
+    def spread_on(h):
+        spread[1, 0, h].wait_recv()
+        spread["g1", h] = start(
+            remote(seat(1, h, 0), seat(1, h, 0), gsend.at[4, h], grecv.at[4, h], me.plane(2))
+        )
+        spread[2, 0, h].wait_recv()
+        spread["g2", h] = start(
+            remote(seat(2, h, 1), seat(2, h, 1), gsend.at[5, h], grecv.at[5, h], me.plane(1))
+        )
+
+    def spread_end(h):
+        for m in (1, 2):
+            spread[m, 1, h].wait_recv()
+            spread["core", m, h] = start(
+                remote(seat(m, h), seat(m, h), ksend.at[m, h], krecv.at[m, h], me.partner())
+            )
+        spread["g1", h].wait_recv()
+        spread["g2", h].wait_recv()
+        spread["core", 3, h] = start(
+            remote(seat(3, h), seat(3, h), ksend.at[3, h], krecv.at[3, h], me.partner())
+        )
+
+    gains[...] = jnp.zeros_like(gains)
+    for c in first.values():
+        c.wait_send()
+    swaps = [norm(0)]
+    swaps[0].wait_recv()
+    hidden_part(0)
+    second(1)
+    swaps.append(back_part(0))
+    swaps[1].wait_recv()
+    norm_back(0)
+    spread_begin(0)
+    swaps.append(norm(1))
+    swaps[2].wait_recv()
+    hidden_part(1)
+    spread_on(0)
+    swaps.append(back_part(1))
+    swaps[3].wait_recv()
+    norm_back(1)
+    spread_begin(1)
+
+    @pl.loop(0, width, step=512)
+    def _(c):
+        at = rows_at(c, 512)
+        tmp[...] = nn(act[...], wd[:, at])
+        for h in range(2):
+            resid[own_half[h], at] = resid[own_half[h], at] + tmp[mine[h], :]
+            share[2, own_half[h], at] = tmp[theirs[h], :].astype(BF16)
+
+    swaps.append(
+        start(remote(share.at[2, pl.ds(0, rows)], share.at[3, pl.ds(0, rows)], psend.at[2, 0], precv.at[2, 0], me.partner()))
+    )
+    spread_on(1)
+
+    def weights_part(left, right, out):
+        def spill(slot, i):
+            return pltpu.make_async_copy(stage.at[slot], out.at[rows_at(i * 256, 256), :], ssem.at[slot])
+
+        @pl.loop(0, width // 256)
+        def _(i):
+            slot = i % 2
+
+            @pl.when(i >= 2)
+            def _():
+                spill(slot, i - 2).wait()
+
+            stage[slot] = tn(left[:, rows_at(i * 256, 256)], right[...]).astype(BF16)
+            spill(slot, i).start()
+
+        for k in (2, 1):
+            i = width // 256 - k
+            spill(i % 2, i).wait()
+
+    weights_part(xn, du, fu)
+    spread_end(0)
+    swaps[4].wait_recv()
 
     @pl.loop(0, rows, step=step)
     def _(r):
         at = rows_at(r, step)
-        left = rx0[q[0], at, ca].astype(F32) + rx1a[1, at, :].astype(F32) + rx2a[at, :].astype(F32)
-        right = rx0[q[0], at, cb].astype(F32) + rx1b[1, at, :].astype(F32) + rx2b[at, :].astype(F32)
-        v = tok_ref[at, :].astype(F32) + jnp.concatenate([left, right], axis=1)
-        resid[at, :] = v
-        average = jnp.mean(v, axis=1, keepdims=True)
-        centered = v - average
-        scale = lax.rsqrt(jnp.mean(centered * centered, axis=1, keepdims=True) + 1e-05)
-        xn[pl.ds(pl.multiple_of(mine + r, step), step), :] = (
-            centered * scale * gain_ref[...] + bias_ref[...]
-        ).astype(BF16)
-
-    own_rows = rows_at(mine, rows)
-    their_rows = rows_at(theirs, rows)
-    swap_x = start(remote(xn.at[own_rows], xn.at[own_rows], psend.at[0], precv.at[0], me.partner()))
-
-    def hidden_part(at_rows):
-        @pl.loop(0, hidden, step=512)
-        def _(c):
-            at = rows_at(c, 512)
-            u = nn(xn[at_rows, :], wu[:, at])
-            e = 0.5 * (1.0 + lax.erf(u * 0.7071067811865476))
-            act[at_rows, at] = (u * e).astype(BF16)
-            slope = e + u * jnp.exp(-0.5 * u * u) * 0.3989422804014327
-            du[at_rows, at] = (dact[at_rows, at] * slope).astype(BF16)
-
-    hidden_part(own_rows)
-    swap_x.wait_recv()
-    hidden_part(their_rows)
-
-    @pl.loop(0, width, step=256)
-    def _(c):
-        at = rows_at(c, 256)
-        part[0, :, at] = nt(du[their_rows, :], wu[at, :]).astype(BF16)
-
-    swap_d = start(remote(part.at[0], prx.at[0], psend.at[1], precv.at[1], me.partner()))
-    @pl.loop(0, width, step=256)
-    def _(c):
-        at = rows_at(c, 256)
-        resid_grad[:, at] = nt(du[own_rows, :], wu[at, :])
-
-    swap_d.wait_recv()
-    gains[...] = jnp.zeros_like(gains)
-
-    @pl.loop(0, rows, step=step)
-    def _(r):
-        at = rows_at(r, step)
-        dx = resid_grad[at, :] + prx[0, at, :].astype(F32)
-        v = resid[at, :]
-        average = jnp.mean(v, axis=1, keepdims=True)
-        centered = v - average
-        scale = lax.rsqrt(jnp.mean(centered * centered, axis=1, keepdims=True) + 1e-05)
-        hat = centered * scale
-        gains[0:1, :] += jnp.sum(dx * hat, axis=0, keepdims=True)
-        gains[1:2, :] += jnp.sum(dx, axis=0, keepdims=True)
-        g = dx * gain_ref[...]
-        back = scale * (
-            g - jnp.mean(g, axis=1, keepdims=True) - hat * jnp.mean(g * hat, axis=1, keepdims=True)
-        )
-        back = back + cot_ref[pl.ds(pl.multiple_of(mine + r, step), step), :].astype(F32)
-        resid_grad[at, :] = back
-        dab[at, :] = back.astype(BF16)
-
-    half = rows // 2
-    low, high = pl.ds(0, half), pl.ds(half, half)
-    seat, seat1, seat2, seat3 = (me.xor(m) * 2 + f for m in (0, 1, 2, 3))
-    own = start(pltpu.make_async_copy(dab, da.at[seat], lsem.at[2]))
-    x1, x2 = [], []
-    for k, (h1, h2) in enumerate(((low, high), (high, low))):
-        x1.append(start(remote(dab.at[h1], da.at[seat, h1], gsend.at[k], grecv.at[k], me.plane(1))))
-        x2.append(
-            start(remote(dab.at[h2], da.at[seat, h2], gsend.at[2 + k], grecv.at[2 + k], me.plane(2)))
-        )
-    to_core = [start(remote(dab, da.at[seat], gsend.at[6], grecv.at[6], me.partner()))]
-
-    @pl.loop(0, width, step=256)
-    def _(c):
-        at = rows_at(c, 256)
-        part[1, :, at] = nn(act[their_rows, :], wd[:, at]).astype(BF16)
-
-    swap_o = start(remote(part.at[1], prx.at[1], psend.at[2], precv.at[2], me.partner()))
-    @pl.loop(0, width, step=256)
-    def _(c):
-        at = rows_at(c, 256)
-        resid[:, at] = resid[:, at] + nn(act[own_rows, :], wd[:, at])
-
-    swap_o.wait_recv()
-
-    @pl.loop(0, rows, step=step)
-    def _(r):
-        at = rows_at(r, step)
-        block_out[at, :] = (resid[at, :] + prx[1, at, :].astype(F32)).astype(BF16)
-
-    x1[0].wait_recv()
-    g1 = start(remote(da.at[seat1, low], da.at[seat1, low], gsend.at[4], grecv.at[4], me.plane(2)))
-    x2[0].wait_recv()
-    g2 = start(remote(da.at[seat2, high], da.at[seat2, high], gsend.at[5], grecv.at[5], me.plane(1)))
-
-    def weights_part(left, right, out, base):
-        def spill(slot, i):
-            return pltpu.make_async_copy(stage.at[slot], out.at[rows_at(i * 256, 256), :], ssem.at[slot])
-
-        @pl.loop(0, width // 256)
-        def _(i):
-            slot = i % 2
-
-            @pl.when(i >= 2)
-            def _():
-                spill(slot, i - 2).wait()
-
-            @pl.loop(0, hidden, step=512)
-            def _(c):
-                at = rows_at(c, 512)
-                stage[slot, :, at] = tn(left[:, rows_at(i * 256, 256)], right[:, at]).astype(BF16)
-
-            spill(slot, i).start()
-
-        for k in (2, 1):
-            i = width // 256 - k
-            spill(i % 2, i).wait()
-
-    weights_part(xn, du, fu, 0)
-    x1[1].wait_recv()
-    to_core.append(start(remote(da.at[seat1], da.at[seat1], gsend.at[7], grecv.at[7], me.partner())))
-    x2[1].wait_recv()
-    to_core.append(start(remote(da.at[seat2], da.at[seat2], gsend.at[8], grecv.at[8], me.partner())))
-    weights_part(cot_ref, act, fd, 0)
-    g1.wait_recv()
-    to_core.append(
-        start(remote(da.at[seat3, low], da.at[seat3, low], gsend.at[9], grecv.at[9], me.partner()))
-    )
-    g2.wait_recv()
-    to_core.append(
-        start(remote(da.at[seat3, high], da.at[seat3, high], gsend.at[10], grecv.at[10], me.partner()))
-    )
-    for c in to_core:
-        c.wait()
-    for c in x1 + x2 + [g1, g2, swap_x, swap_d, swap_o, s2a, s2b] + first + list(sends.values()):
+        block_out[at, :] = (resid[at, :] + share[3, at, :].astype(F32)).astype(BF16)
+
+    weights_part(cot, act, fd)
+    spread_end(1)
+    for h in range(2):
+        spread["own", h].wait()
+        for m in range(4):
+            spread["core", m, h].wait()
+        for key in ((1, 0, h), (1, 1, h), (2, 0, h), (2, 1, h), ("g1", h), ("g2", h)):
+            spread[key].wait_send()
+    for c in swaps + list(sends.values()):
         c.wait_send()
-    own.wait()
-
-
-def ffn_part(share, tokens, gain, bias, w_up, w_down, cotangent, cid):
-    _, _, rows, width = share.shape
+
+
+def ffn_part(gated, w_out, tokens, gain, bias, w_up, w_down, cotangent, cid):
+    rows, width = tokens.shape
+    assert PLANE * gated.shape[1] == width and w_out.shape == (2 * rows, w_up.shape[1])
     span, hidden = 2 * rows, w_up.shape[1]
+    sd = jax.ShapeDtypeStruct
     return comm_call(
         ffn_kernel,
         [
-            jax.ShapeDtypeStruct((rows, width), BF16),
-            jax.ShapeDtypeStruct((rows, width), F32),
-            jax.ShapeDtypeStruct((8, width), F32),
-            jax.ShapeDtypeStruct((2 * PLANE, rows, width), BF16),
-            jax.ShapeDtypeStruct((width, hidden), BF16),
-            jax.ShapeDtypeStruct((width, hidden), BF16),
+            sd((rows, width), BF16),
+            sd((rows, width), F32),
+            sd((8, width), F32),
+            sd((2 * PLANE * rows, width), BF16),
+            sd((width, hidden), BF16),
+            sd((width, hidden), BF16),
         ],
-        [share, tokens, gain[None], bias[None], w_up, w_down, cotangent],
+        [gated, w_out, tokens, gain[None], bias[None], w_up, w_down, cotangent],
         [
+            pltpu.VMEM((PLANE, span, width), BF16),
             pltpu.VMEM(w_up.shape, BF16),
             pltpu.VMEM(w_down.shape, BF16),
             pltpu.VMEM((PLANE, rows, width), BF16),
@@ -351,23 +445,26 @@
             pltpu.VMEM((span, hidden), BF16),
             pltpu.VMEM((span, hidden), F32),
             pltpu.VMEM((span, hidden), BF16),
-            pltpu.VMEM((2, rows, width), BF16),
-            pltpu.VMEM((2, rows, width), BF16),
+            pltpu.VMEM((span, width), BF16),
             pltpu.VMEM((rows, width), BF16),
             pltpu.VMEM((2, 256, hidden), BF16),
-            DMA((3,)),
-            DMA((4,)),
-            DMA((4,)),
-            DMA((6,)),
-            DMA((6,)),
-            DMA((3,)),
-            DMA((3,)),
-            DMA((11,)),
-            DMA((11,)),
+            pltpu.VMEM((span, 512), F32),
+            DMA((7,)),
+            DMA((PLANE,)),
+            DMA((PLANE, 2)),
+            DMA((PLANE, 2)),
+            DMA((6, 2)),
+            DMA((6, 2)),
+            DMA((3, 2)),
+            DMA((3, 2)),
+            DMA((6, 2)),
+            DMA((6, 2)),
+            DMA((4, 2)),
+            DMA((4, 2)),
             DMA((2,)),
         ],
         cid,
-        in_specs=[VM, VM, VM, VM, ANY, ANY, VM],
+        in_specs=[ANY, ANY, VM, VM, VM, ANY, ANY, ANY],
         out_specs=[VM, VM, VM, ANY, ANY, ANY],
     )
 
@@ -378,13 +475,13 @@
 ):
     count = len(widths)
     shards_in, refs = refs[:count], refs[count:]
-    (xg, q_out, k_out, v_out, gate_out, ret_out, gated_out, states_out, share_out, cos_out, sin_out, ccol, crow, scal), refs = (
-        refs[:14], refs[14:],
+    (xg, q_out, k_out, v_out, gate_out, ret_out, gated_out, states_out, cos_out, sin_out, ccol, crow, scal), refs = (
+        refs[:13], refs[13:],
     )
     full, refs = refs[:count], refs[count:]
     hold, refs = refs[:count], refs[count:]
-    wl, refs = refs[:count], refs[count:]
-    (xn, xv, q, k, v, gate, ret, gated, share, cos, sin, kv, st, sloc, sgot, decg, pbuf,
+    wl, refs = refs[: count - 1], refs[count - 1 :]
+    (xn, xv, q, k, v, gate, ret, gated, cos, sin, kv, st, sloc, sgot, decg,
      lsem, psend, precv, usend, dsend, zrecv, xsend, xrecv, csend, crecv, tsend, trecv, ssend, srecv, osem, wsem) = refs
     me = Place()
     z, p, f = me.z, me.p, me.f
@@ -669,17 +766,7 @@
 
     put(gate, gate_out)
     put(gated, gated_out)
-    fetch(O).wait()
-    for c in range(blocks):
-        at = pl.ds(c * STRETCH, STRETCH)
-
-        @pl.loop(0, width, step=512)
-        def _(d):
-            cols = rows_at(d, 512)
-            share[at, cols] = nn(gated[at, :], wl[O][:, cols]).astype(BF16)
-
-        put(share.at[at], share_out.at[at])
-
+    forward(O, LINE - 1)
     for c in (xc, c1, c2, c3, x1, x2, g1, g2):
         c.wait_send()
     for i in range(count):
@@ -722,7 +809,6 @@
         sd((group, values), F32),
         sd((group, values), BF16),
         sd((blocks, keys, values), BF16),
-        sd((group, width), BF16),
         sd((group, half), F32),
         sd((group, half), F32),
         sd((group, 1), F32),
@@ -731,7 +817,7 @@
     ] + [sd(s, BF16) for s in wholes]
     scratch = (
         [pltpu.VMEM(s, BF16) for s in parts]
-        + [pltpu.VMEM(s, BF16) for s in wholes]
+        + [pltpu.VMEM(s, BF16) for s in wholes[:-1]]
         + [
             pltpu.VMEM((rows, width), BF16),
             pltpu.VMEM((group, width), BF16),
@@ -741,7 +827,6 @@
             pltpu.VMEM((group, values), F32),
             pltpu.VMEM((group, values), F32),
             pltpu.VMEM((group, values), BF16),
-            pltpu.VMEM((group, width), BF16),
             pltpu.VMEM((group, half), F32),
             pltpu.VMEM((group, half), F32),
             pltpu.VMEM((blocks, keys, values), F32),
@@ -749,7 +834,6 @@
             pltpu.VMEM((keys, values), F32),
             pltpu.VMEM((keys, values), BF16),
             pltpu.VMEM((PLANE,) + decays.shape, F32),
-            pltpu.VMEM((8, 128), BF16),
             DMA((count + 1,)),
             DMA((count, PLANE)),
             DMA((count, PLANE)),
@@ -775,7 +859,7 @@
         scratch,
         cid,
         in_specs=[VM] * 8 + [ANY] * count,
-        out_specs=[ANY] * 11 + [VM] * 3 + [ANY] * count,
+        out_specs=[ANY] * 10 + [VM] * 3 + [ANY] * count,
     )
 
 
@@ -791,16 +875,17 @@
         slot = jnp.where(zz == self.me.z - 1, LINE, zz)
         return remote(src, self.rx.at[slot], self.sems[2].at[zz], self.sems[3].at[zz], self.me.down())
 
-    def begin(self, order=(3, 2, 1)):
+    def begin(self, order=(3, 2, 1), src=None):
+        src = src or self.own
         for zz in order:
 
             @pl.when(self.me.z == 0)
             def _():
-                self.up(self.own(zz), zz).start()
+                self.up(src(zz), zz).start()
 
             @pl.when(self.me.z == LINE - 1)
             def _():
-                self.down(self.own(LINE - 1 - zz), LINE - 1 - zz).start()
+                self.down(src(LINE - 1 - zz), LINE - 1 - zz).start()
 
     def pass_up(self, zz):
         self.up(self.own(zz), zz).wait_recv()
@@ -884,15 +969,15 @@
 def retention_back_kernel(
     da_ref, wo_ref, gated_ref, gate_ref, ret_ref, q_ref, k_ref, v_ref, s_ref, cos_ref, sin_ref,
     ccol_ref, crow_ref, scal_ref, xg_ref, fu_ref, fd_ref,
-    dh, sums, f1,
-    da, wo, gated, gr, q, k, v, st, cos, sin, dr, xt, ao, ag, rxo, rxg, fin, qo, gb, lg, got, logs, rxf, fo, pbuf, gbuf,
-    lsem, gsem, xsem, fsend, frecv, osem, fosem, ssend, srecv, lsend, lrecv, psend, precv, *line,
+    dh, sums, f1, av_out, aq_out,
+    da, wo, gated, gr, q, k, v, st, cos, sin, dr, xt, ao, ag, rxo, rxg, fin, qo, gb, lg, got, rxf, fo, pbuf, gbuf,
+    lsem, gsem, xsem, fsend, frecv, osem, fosem, ssend, srecv, psend, precv, *line,
 ):
     me = Place()
     z, p = me.z, me.p
     greet(
         [(me.plane(m), None) for m in (1, 2, 3)]
-        + [(me.at((z + t) % LINE, p, me.f), None) for t in range(1, LINE)]
+        + [(me.up(), z < LINE - 1), (me.down(), z > 0)]
     )
     width = da.shape[1]
     tokens = da.shape[0]
@@ -1018,22 +1103,21 @@
         qo[c] = got_q
         lg[...] += scal_ref[blocks + c, 0:1, 0:1] * got_q
 
-    gb[0] = lg[...].astype(BF16)
-
-    def state_copies(t, to, slot):
-        device = me.at(to, p, me.f)
-        return (
-            remote(gb.at[0], got.at[slot], ssend.at[t - 1], srecv.at[t - 1], device),
-            remote(scal_ref.at[2 * blocks], logs.at[slot], lsend.at[t - 1], lrecv.at[t - 1], device),
-        )
-
-    for t in range(1, LINE):
-
-        @pl.when(z - t >= 0)
+    state_copy = remote(gb.at[0], got, ssend.at[0], srecv.at[0], me.down())
+
+    def pass_state(zz):
+        @pl.when(z == zz)
         def _():
-            for c in state_copies(t, z - t, z):
-                c.start()
-
+            if zz < LINE - 1:
+                state_copy.wait_recv()
+            if zz > 0:
+                add = lg[...]
+                if zz < LINE - 1:
+                    add = add + got[...].astype(F32) * jnp.exp(scal_ref[2 * blocks, 0:1, 0:1])
+                gb[0] = add.astype(BF16)
+                state_copy.start()
+
+    pass_state(LINE - 1)
     out_sum.begin((1,))
     out_sum.near(0)
     def x_tile(i):
@@ -1052,28 +1136,25 @@
 
     gate_sum.begin()
     out_sum.near(1)
-    out_sum.far()
+    pass_state(2)
     f_unit(0)
     f_unit(1)
-
-    for t in range(1, LINE):
-
-        @pl.when(z + t < LINE)
-        def _():
-            for c in state_copies(t, z + t, z + t):
-                c.wait_recv()
-
-        @pl.when(z - t >= 0)
-        def _():
-            for c in state_copies(t, z - t, z):
-                c.wait_send()
-
-    lg[...] = jnp.zeros_like(lg)
-    for j in reversed(range(1, LINE)):
-
-        @pl.when(z < j)
-        def _():
-            lg[...] = lg[...] * jnp.exp(logs[j, 0:1, 0:1]) + got[j].astype(F32)
+    out_sum.far()
+
+    pass_state(1)
+    pass_state(0)
+
+    @pl.when(z > 0)
+    def _():
+        state_copy.wait_send()
+
+    @pl.when(z < LINE - 1)
+    def _():
+        lg[...] = got[...].astype(F32)
+
+    @pl.when(z == LINE - 1)
+    def _():
+        lg[...] = jnp.zeros_like(lg)
 
     for c in reversed(range(blocks)):
         gb[c] = lg[...].astype(BF16)
@@ -1135,17 +1216,33 @@
         )
 
     gate_sum.near(0)
-    gate_sum.near(1)
     for u in range(2, 4):
         f_unit(u)
+    deal(0, out_sum, ao)
+    x_tile(0).start()
+    wide = 2 * keys + values
+
+    @pl.loop(0, width // 256)
+    def _(i):
+        @pl.when(i + 1 < width // 256)
+        def _():
+            x_tile(i + 1).start()
+
+        x_tile(i).wait()
+        da[rows_at(i * 256, 256), :wide] = tn(xt[i % 2], dh[:, :wide]).astype(BF16)
+
+    to_last = [
+        start(pltpu.make_async_copy(da.at[:, : 2 * keys], aq_out, lsem.at[0])),
+        start(pltpu.make_async_copy(da.at[:, 2 * keys : wide], av_out, lsem.at[1])),
+    ]
+    gate_sum.near(1)
     gate_sum.far()
-    deal(0, out_sum, ao)
     for u in range(4, 6):
         f_unit(u)
     deal(1, gate_sum, ag)
     for u in range(6, 2 * LINE):
         f_unit(u)
-    for c in plane:
+    for c in plane + to_last:
         c.wait()
     out_sum.finish()
     gate_sum.finish()
@@ -1170,6 +1267,8 @@
             jax.ShapeDtypeStruct((tokens, 2 * keys + 2 * values), BF16),
             jax.ShapeDtypeStruct((PLANE, chunk, 2 * values), BF16),
             jax.ShapeDtypeStruct((2, LINE, 2, chunk, hidden), BF16),
+            jax.ShapeDtypeStruct((width, values), BF16),
+            jax.ShapeDtypeStruct((width, 2 * keys), BF16),
         ],
         [da, wo, gated, gate, ret, q, k, v, states, cos, sin, ccol, crow, scal, xg, fu, fd],
         [
@@ -1193,8 +1292,7 @@
             pltpu.VMEM((blocks, keys, values), F32),
             pltpu.VMEM((blocks, keys, values), BF16),
             pltpu.VMEM((keys, values), F32),
-            pltpu.VMEM((LINE, keys, values), BF16),
-            pltpu.VMEM((LINE, 8, 128), F32),
+            pltpu.VMEM((keys, values), BF16),
             pltpu.VMEM((2, LINE, 2, chunk, hidden), BF16),
             pltpu.VMEM((2, 2, chunk, hidden), BF16),
             pltpu.VMEM((STRETCH, STRETCH), BF16),
@@ -1206,10 +1304,8 @@
             DMA((2, LINE, 2)),
             DMA((2 * LINE,)),
             DMA((2, 2)),
-            DMA((LINE - 1,)),
-            DMA((LINE - 1,)),
-            DMA((LINE - 1,)),
-            DMA((LINE - 1,)),
+            DMA((1,)),
+            DMA((1,)),
             DMA((2, PLANE)),
             DMA((2, PLANE)),
         ]
@@ -1217,15 +1313,15 @@
         + line_sems(),
         cid,
         in_specs=[ANY] * 11 + [VM] * 3 + [ANY] * 3,
-        out_specs=[VM, ANY, ANY],
+        out_specs=[VM, ANY, ANY, ANY, ANY],
     )
 
 
 def last_kernel(
-    dh_ref, xg_ref, wq_ref, wk_ref, wv_ref, wg_ref, f1_ref, tok_ref, gain_ref, resid_ref, second_ref,
+    dh_ref, av_ref, aq_ref, wq_ref, wk_ref, wv_ref, wg_ref, f1_ref, tok_ref, gain_ref, resid_ref, second_ref,
     grad_tokens, gains, fout, sums,
-    dh, xt, wh, share, rx0, rx1a, rx1b, rx2a, rx2b, av, aq, rxv, rxq, fin, rf2, kf, rxfa, rxfb, grx,
-    lsem, xsem, fsend, frecv, csend, crecv, xsend, xrecv, gsend, grecv, psend, precv, *line,
+    dh, wh, share, rx0, rx1a, rx1b, rx2a, rx2b, av, aq, rxv, rxq, fin, rf2, kf, rxfa, rxfb, grx,
+    lsem, fsend, frecv, csend, crecv, xsend, xrecv, gsend, grecv, psend, precv, *line,
 ):
     me = Place()
     z, p, f = me.z, me.p, me.f
@@ -1235,7 +1331,7 @@
         [me.at((z + t) % LINE, p, f) for t in range(1, LINE)],
     ]
     greet([(d, None) for r in rounds for d in r])
-    width, keys2, values = xg_ref.shape[1], aq.shape[1], av.shape[1]
+    width, keys2, values = av.shape[0], aq.shape[1], av.shape[1]
     rows = tok_ref.shape[0]
     pq = [me.xor(m) for m in range(4)]
     chunk = width // SPANS
@@ -1244,14 +1340,23 @@
     def f_copy(h, zp):
         return remote(f1_ref.at[h, zp, 1], rf2.at[h, zp], fsend.at[h, zp], frecv.at[h, zp], me.plane(2 - h))
 
-    def x_tile(i):
-        return pltpu.make_async_copy(xg_ref.at[:, rows_at(i * 256, 256)], xt.at[i % 2], xsem.at[i % 2])
-
-    load = start(pltpu.make_async_copy(dh_ref, dh, lsem.at[0]))
-    x_tile(0).start()
+    def block_of(a, size):
+        return lambda zz: a.at[rows_at(zz * size, size), :]
+
+    v_sum = LineSum(me, block_of(av, deep), rxv, *line[:4], add_rows)
+    q_sum = LineSum(me, block_of(aq, deep), rxq, *line[4:8], add_rows)
+    fa_sum = LineSum(me, lambda zz: kf.at[0, zz], rxfa, *line[8:12], add_rows)
+    fb_sum = LineSum(me, lambda zz: kf.at[1, zz], rxfb, *line[12:16], add_rows)
+    v_sum.begin(src=block_of(av_ref, deep))
+    q_sum.begin(src=block_of(aq_ref, deep))
     for zp in (3, 0, 2, 1):
         for h in range(2):
             f_copy(h, zp).start()
+    load = start(pltpu.make_async_copy(dh_ref, dh, lsem.at[0]))
+    owns = [
+        start(pltpu.make_async_copy(av_ref, av, lsem.at[7])),
+        start(pltpu.make_async_copy(aq_ref, aq, lsem.at[8])),
+    ]
     loads, at = [], 0
     for i, w in enumerate((wq_ref, wk_ref, wv_ref, wg_ref)):
         size = w.shape[1]
@@ -1259,30 +1364,8 @@
         at += size
     keeps = [start(pltpu.make_async_copy(f1_ref.at[h, :, 0], kf.at[h], lsem.at[5 + h])) for h in range(2)]
 
-    def block_of(a, size):
-        return lambda zz: a.at[rows_at(zz * size, size), :]
-
-    v_sum = LineSum(me, block_of(av, deep), rxv, *line[:4], add_rows)
-    q_sum = LineSum(me, block_of(aq, deep), rxq, *line[4:8], add_rows)
-    fa_sum = LineSum(me, lambda zz: kf.at[0, zz], rxfa, *line[8:12], add_rows)
-    fb_sum = LineSum(me, lambda zz: kf.at[1, zz], rxfb, *line[12:16], add_rows)
     load.wait()
-    tiles = width // 256
-    for out, cols, chain in ((av, pl.ds(keys2, values), v_sum), (aq, pl.ds(0, keys2), q_sum)):
-        if chain is q_sum:
-            x_tile(0).start()
-
-        @pl.loop(0, tiles)
-        def _(i):
-            @pl.when(i + 1 < tiles)
-            def _():
-                x_tile(i + 1).start()
-
-            x_tile(i).wait()
-            out[rows_at(i * 256, 256), :] = tn(xt[i % 2], dh[:, cols]).astype(BF16)
-
-        chain.begin()
-    for c in loads:
+    for c in loads + owns:
         c.wait()
 
     own_rows, their_rows = rows_at(f * rows, rows), rows_at((1 - f) * rows, rows)
@@ -1440,8 +1523,8 @@
             f_copy(h, zp).wait_send()
 
 
-def last_sums(dh, xg, wq, wk, wv, wg, f1, tokens, gain, resid, second, cid):
-    group, width = xg.shape
+def last_sums(dh, av, aq, wq, wk, wv, wg, f1, tokens, gain, resid, second, cid):
+    width = av.shape[0]
     rows = tokens.shape[0]
     keys, values = wq.shape[1], wv.shape[1]
     assert 2 * keys == values
@@ -1455,10 +1538,9 @@
             jax.ShapeDtypeStruct((2, chunk, hidden), F32),
             jax.ShapeDtypeStruct((PLANE, chunk, 2 * values), BF16),
         ],
-        [dh, xg, wq, wk, wv, wg, f1, tokens, gain[None], resid, second],
+        [dh, av, aq, wq, wk, wv, wg, f1, tokens, gain[None], resid, second],
         [
             pltpu.VMEM(dh.shape, BF16),
-            pltpu.VMEM((2, group, 256), BF16),
             pltpu.VMEM((width, dh.shape[1]), BF16),
             pltpu.VMEM((PLANE, 2 * rows, width), BF16),
             pltpu.VMEM((PLANE, rows, width), BF16),
@@ -1476,8 +1558,7 @@
             pltpu.VMEM((LINE + 1, chunk, hidden), BF16),
             pltpu.VMEM((LINE + 1, chunk, hidden), BF16),
             pltpu.VMEM((7, 8, width), F32),
-            DMA((7,)),
-            DMA((2,)),
+            DMA((9,)),
             DMA((2, LINE)),
             DMA((2, LINE)),
             DMA((4,)),
@@ -1494,9 +1575,59 @@
         + line_sems()
         + line_sems(),
         cid,
-        in_specs=[ANY] * 7 + [VM] * 4,
+        in_specs=[ANY] * 8 + [VM] * 4,
         out_specs=[VM, VM, VM, ANY],
     )
+
+
+def outputs_kernel(last, first, ffn, low_out, low_grad, q, k, v, gate, out, up, down, block_out, grad_tokens):
+    values = v.shape[1]
+    keys = q.shape[1]
+    v[...] = last[0, :, :values].astype(F32)
+    q[...] = last[0, :, values : values + keys].astype(F32)
+    k[...] = last[0, :, values + keys :].astype(F32)
+    out[...] = first[0, :, :values].astype(F32).T
+    gate[...] = first[0, :, values:].astype(F32)
+    up[...] = ffn[0]
+    down[...] = ffn[1].T
+    block_out[...] = low_out[...]
+    grad_tokens[...] = low_grad[...]
+
+
+def outputs(last, first, ffn, low_out, low_grad, keys):
+    heads, chunk, both = last.shape
+    values, hidden = both // 2, ffn.shape[-1]
+    rows, width = low_out.shape
+    piece, slab = hidden // heads, rows // heads
+    sd = jax.ShapeDtypeStruct
+    by_column = [pl.BlockSpec((chunk, size), lambda i: (0, i)) for size in (keys, keys, values, values)]
+    by_row = pl.BlockSpec((values, chunk), lambda i: (i, 0))
+    low = pl.BlockSpec((slab, width), lambda i: (i, 0))
+    sums = pl.BlockSpec((1, chunk, both), lambda i: (i, 0, 0))
+    return pl.pallas_call(
+        outputs_kernel,
+        grid=(heads,),
+        in_specs=[sums, sums, pl.BlockSpec((2, chunk, piece), lambda i: (0, 0, i)), low, low],
+        out_specs=by_column
+        + [
+            by_row,
+            pl.BlockSpec((chunk, piece), lambda i: (0, i)),
+            pl.BlockSpec((piece, chunk), lambda i: (i, 0)),
+            low,
+            low,
+        ],
+        out_shape=[
+            sd((chunk, heads * keys), F32),
+            sd((chunk, heads * keys), F32),
+            sd((chunk, heads * values), F32),
+            sd((chunk, heads * values), F32),
+            sd((heads * values, chunk), F32),
+            sd((chunk, hidden), F32),
+            sd((hidden, chunk), F32),
+            sd((rows, width), BF16),
+            sd((rows, width), BF16),
+        ],
+    )(last, first, ffn, low_out, low_grad)
 
 
 def angle_tables(first, count, fine, half_width):
@@ -1569,7 +1700,7 @@
     decays = jnp.pad(decay_log.T, ((0, 8 - heads), (0, 0)))
     fine = 64
     (
-        normed, q_rot, k_rot, value, gate_proj, retained, gated_low, prev_states, attn_share,
+        normed, q_rot, k_rot, value, gate_proj, retained, gated_low, prev_states,
         cosine, sine_part, ccol, crow, scalars, key_w, value_w, query_w, gate_w, out_w,
     ) = attention(
         tokens,
@@ -1587,9 +1718,9 @@
         (False, False, False, False, True),
         0,
     )
-    key_width, value_width = key_w.shape[1], value_w.shape[1]
     block_out, grad_resid, gains_second, grad_attn, grad_up, grad_down = ffn_part(
-        attn_share.reshape(PLANE, 2, row_count, width),
+        gated_low,
+        out_w,
         tokens,
         ln2_gain,
         ln2_bias,
@@ -1598,8 +1729,7 @@
         cotangent,
         2,
     )
-    grad_attn = grad_attn.reshape(group_rows, width)
-    grad_heads, sums_first, ffn_first = retention_back(
+    grad_heads, sums_first, ffn_first, grad_value_w, grad_qk_w = retention_back(
         grad_attn,
         out_w,
         gated_low,
@@ -1621,7 +1751,8 @@
     )
     grad_tokens, gains, ffn_sum, sums_last = last_sums(
         grad_heads,
-        normed,
+        grad_value_w,
+        grad_qk_w,
         query_w,
         key_w,
         value_w,
@@ -1633,22 +1764,17 @@
         gains_second,
         8,
     )
-    sum_up = narrow_out(ffn_sum[0], 0)
-    sum_down = narrow_out(ffn_sum[1], 0).T
     if repeats > 1:
         gains = lax.psum(gains, "seq", axis_index_groups=peers)
     gains = features_out(gains)
     gain_one, bias_one, gain_two, bias_two = gains[0], gains[1], gains[2], gains[3]
 
-    def columns(sums, start, size):
-        taken = sums[:, :, start : start + size].astype(F32).swapaxes(0, 1)
-        return narrow_out(taken.reshape(taken.shape[0], PLANE * size), 0)
-
-    sum_value = columns(sums_last, 0, value_width)
-    sum_query = columns(sums_last, value_width, key_width)
-    sum_key = columns(sums_last, value_width + key_width, key_width)
-    sum_out = columns(sums_first, 0, value_width).T
-    sum_gate = columns(sums_first, value_width, value_width)
+    *sums, block_out, grad_tokens = outputs(
+        sums_last, sums_first, ffn_sum, block_out, grad_tokens, key_w.shape[1]
+    )
+    sum_query, sum_key, sum_value, sum_gate, sum_out, sum_up, sum_down = (
+        narrow_out(g, axis) for g, axis in zip(sums, (0, 0, 0, 0, 1, 0, 1))
+    )
     return (
         features_out(block_out),
         features_out(grad_tokens),

time: 567 us -> 522 us (0.921)
  Pallas kernels: 541 us -> 515 us
  local copies, waits for them, and re-layouts: 17.5 us -> 4.26 us
    pallas_call x4, Pallas kernels: 541 us -> 508 us  [comm_call(): pl.pallas_call(kernel, out_shape=outs, in_specs=in_specs if in_specs is n...]
    unnamed x13 -> x0, local copies, waits for them, and re-layouts: 8.91 us -> none
    pallas_call x0 -> x1, Pallas kernels: none -> 6.28 us  [outputs(): pl.pallas_call(outputs_kernel, grid=(heads,), in_specs=[sums, sums, pl.Bl...]
where the time goes in v5:
time: 522 us; the launch traced here: 521 us
  Pallas kernels  515 us (99%)
    pallas_call x4, Pallas kernels, comm_call(): pl.pallas_call(kernel, out_shape=outs, in_specs=in_specs if in_specs is n...  508 us

profile of v5, /device:TPU:16, one launch (start us, length us, event | category | flops | bytes accessed | tf_op | source)
XLA Modules:
  0.0 520.7 jit_solution(2630177189448505600)
XLA Ops:
  0.7 0.1 fusion.2
  0.8 1.3 pad.4.dec_ref
  2.1 0.1 multiply_sine_fusion.1
  2.2 0.8 multiply_sine_fusion
  3.1 0.7 broadcast_in_dim.17.sbase
  3.7 0.7 broadcast_in_dim.16.cbase
  4.4 151.5 %shard_map.237 = (bf16[2048,2048]{1,0:T(8,128)(2,1)}, bf16[2048,256]{1,0:T(8,128)(2,1)}, bf16[2048,256]{1,0:T(8,128)(2,1)}, bf16[2048,512]{1,0:T(8,128)(2,1)}, f...) custom-call(bf16[256,2048]{1,0:T(8,128)(2,1)} %tok_ref.5, ...), custom_call_target="tpu_custom_call" | custom-call | tf_op jit(solution)/shard_map/pallas_call | solution.py:81
  155.9 93.9 %shard_map.238 = (bf16[256,2048]{1,0:T(8,128)(2,1)}, f32[256,2048]{1,0:T(8,128)}, f32[8,2048]{1,0:T(8,128)}, bf16[2048,2048]{1,0:T(8,128)(2,1)}, bf16[2048,2048]{1,0:T(8,128)(2,1)}, /*index=5*/bf16[2048,2048]{1,0:T(8,128)(2,1)}) custom-call(bf16[2048,512]{1,0:T(8,128)(2,1)} %get-tuple-element.55.gated_ref, bf16[512,2048]{1,0:T(8,128)(2,1)} %get-tuple-element.56.wo_ref, ...), custom_call_target="tpu_custom_call" | custom-call | tf_op jit(solution)/shard_map/pallas_call | solution.py:81
  249.8 112.6 %shard_map.239 = (bf16[2048,1536]{1,0:T(8,128)(2,1)}, bf16[4,128,1024]{2,1,0:T(8,128)(2,1)}, bf16[2,4,2,128,2048]{4,3,2,1,0:T(8,128)(2,1)}, bf16[2048,512]{1,0:T(8,128)(2,1)}, bf16[2048,512]{1,0:T(8,128)(2,1)}) custom-call(bf16[2048,2048]{1,0:T(8,128)(2,1)} %get-tuple-element.57.da_ref, bf16[512,2048]{1,0:T(8,128)(2,1)} %get-tuple-element.56.wo_ref, ...), custom_call_target="tpu_custom_call" | custom-call | tf_op jit(solution)/shard_map/pallas_call | solution.py:81
  362.4 150.2 %shard_map.240 = (bf16[256,2048]{1,0:T(8,128)(2,1)}, f32[8,2048]{1,0:T(8,128)}, f32[2,128,2048]{2,1,0:T(8,128)}, bf16[4,128,1024]{2,1,0:T(8,128)(2,1)}) custom-call(bf16[2048,1536]{1,0:T(8,128)(2,1)} %get-tuple-element.72.dh_ref, bf16[2048,512]{1,0:T(8,128)(2,1)} %get-tuple-element.73.av_ref, bf16[2048,512]{1,0:T(8,128)(2,1)} %get-tuple-element.74.aq_ref, ...), custom_call_target="tpu_custom_call" | custom-call | tf_op jit(solution)/shard_map/pallas_call | solution.py:81
  512.7 1.6 fusion.3
  514.3 6.3 %shard_map.241 = (f32[128,1024]{1,0:T(8,128)}, f32[128,1024]{1,0:T(8,128)}, f32[128,2048]{1,0:T(8,128)}, f32[128,2048]{1,0:T(8,128)}, f32[2048,128]{1,0:T(8,128)...) custom-call(bf16[4,128,1024]{2,1,0:T(8,128)(2,1)} %get-tuple-element.82.las, ...), custom_call_target="tpu_custom_call" | custom-call | tf_op jit(solution)/shard_map/pallas_call | solution.py:1607
  (3 shorter events, 0.0 us)

commit v6 on v5

--- a/solution.py
+++ b/solution.py
@@ -13,7 +13,7 @@
 LINE = 4
 SPANS = PLANE * LINE
 MESH = pl.DeviceIdType.MESH
-VMEM_LIMIT = 60 * 1024 * 1024
+VMEM_LIMIT = 63 * 1024 * 1024
 ANY = pl.BlockSpec(memory_space=pl.ANY)
 VM = pl.BlockSpec(memory_space=pltpu.VMEM)
 BF16 = jnp.bfloat16
@@ -123,8 +123,8 @@
 
 def ffn_kernel(
     gated_ref, wo_ref, tok_ref, gain_ref, bias_ref, wu_ref, wd_ref, cot_ref,
-    block_out, resid_grad, gains, da, fu, fd,
-    share, wu, wd, rx0, rx1a, rx1b, rx2a, rx2b, resid, xn, act, dact, du, cot, dab, stage, tmp,
+    block_out, resid_out, gains, da, fu, fd,
+    tok, resid_grad, share, wu, wd, rx0, rx1a, rx1b, rx2a, rx2b, resid, xn, act, dact, du, cot, dab, stage, tmp,
     lsem, gload, csend, crecv, xsend, xrecv, psend, precv, gsend, grecv, ksend, krecv, ssem,
 ):
     me = Place()
@@ -146,6 +146,7 @@
     order = (3, 1, 2, 0)
     part_width = gated_ref.shape[1]
     load_o = start(pltpu.make_async_copy(wo_ref, act, lsem.at[0]))
+    load_t = pltpu.make_async_copy(tok_ref, tok, lsem.at[7])
     load_g = {
         m: start(
             pltpu.make_async_copy(
@@ -156,6 +157,7 @@
         )
         for m in order
     }
+    load_t.start()
     load_d = start(pltpu.make_async_copy(wd_ref, wd, lsem.at[1]))
     load_c = [
         start(
@@ -244,7 +246,7 @@
             at = pl.ds(pl.multiple_of(h * hr + r, step), step)
             left = rx0[0, at, ca].astype(F32) + rx1a[1, at, :].astype(F32) + rx2a[at, :].astype(F32)
             right = rx0[0, at, cb].astype(F32) + rx1b[1, at, :].astype(F32) + rx2b[at, :].astype(F32)
-            v = tok_ref[at, :].astype(F32) + jnp.concatenate([left, right], axis=1)
+            v = tok[at, :].astype(F32) + jnp.concatenate([left, right], axis=1)
             resid[at, :] = v
             centered = v - jnp.mean(v, axis=1, keepdims=True)
             scale = lax.rsqrt(jnp.mean(centered * centered, axis=1, keepdims=True) + 1e-05)
@@ -268,7 +270,7 @@
         @pl.loop(0, width, step=512)
         def _(c):
             at = rows_at(c, 512)
-            tmp[:rows, :] = nt(du[both[h], :], wu[at, :])
+            tmp[...] = nt(du[both[h], :], wu[at, :])
             resid_grad[own_half[h], at] = tmp[rows_at(f * hr, hr), :]
             share[0, own_half[h], at] = tmp[rows_at((1 - f) * hr, hr), :].astype(BF16)
 
@@ -295,6 +297,18 @@
             resid_grad[at, :] = back
             dab[at, :] = back.astype(BF16)
 
+    def out_part(h):
+        @pl.loop(0, width, step=512)
+        def _(c):
+            at = rows_at(c, 512)
+            tmp[...] = nn(act[both[h], :], wd[:, at])
+            dact[pl.ds(h * rows, hr), at] = tmp[rows_at(f * hr, hr), :]
+            share[2, own_half[h], at] = tmp[rows_at((1 - f) * hr, hr), :].astype(BF16)
+
+        return start(
+            remote(share.at[2, own_half[h]], share.at[3, own_half[h]], psend.at[2, h], precv.at[2, h], me.partner())
+        )
+
     quarter = hr // 2
 
     def seat(m, h, k=None):
@@ -345,11 +359,13 @@
     gains[...] = jnp.zeros_like(gains)
     for c in first.values():
         c.wait_send()
+    load_t.wait()
     swaps = [norm(0)]
     swaps[0].wait_recv()
     hidden_part(0)
     second(1)
     swaps.append(back_part(0))
+    out_swaps = [out_part(0)]
     swaps[1].wait_recv()
     norm_back(0)
     spread_begin(0)
@@ -358,22 +374,11 @@
     hidden_part(1)
     spread_on(0)
     swaps.append(back_part(1))
+    out_swaps.append(out_part(1))
     swaps[3].wait_recv()
     norm_back(1)
     spread_begin(1)
-
-    @pl.loop(0, width, step=512)
-    def _(c):
-        at = rows_at(c, 512)
-        tmp[...] = nn(act[...], wd[:, at])
-        for h in range(2):
-            resid[own_half[h], at] = resid[own_half[h], at] + tmp[mine[h], :]
-            share[2, own_half[h], at] = tmp[theirs[h], :].astype(BF16)
-
-    swaps.append(
-        start(remote(share.at[2, pl.ds(0, rows)], share.at[3, pl.ds(0, rows)], psend.at[2, 0], precv.at[2, 0], me.partner()))
-    )
-    spread_on(1)
+    resid_copy = start(pltpu.make_async_copy(resid_grad, resid_out, lsem.at[0]))
 
     def weights_part(left, right, out):
         def spill(slot, i):
@@ -381,37 +386,43 @@
 
         @pl.loop(0, width // 256)
         def _(i):
-            slot = i % 2
-
-            @pl.when(i >= 2)
+            slot = i % 3
+
+            @pl.when(i >= 3)
             def _():
-                spill(slot, i - 2).wait()
+                spill(slot, i - 3).wait()
 
             stage[slot] = tn(left[:, rows_at(i * 256, 256)], right[...]).astype(BF16)
             spill(slot, i).start()
 
-        for k in (2, 1):
+        for k in (3, 2, 1):
             i = width // 256 - k
-            spill(i % 2, i).wait()
-
+            spill(i % 3, i).wait()
+
+    weights_part(cot, act, fd)
+    spread_on(1)
+    spread_end(0)
+    for h in range(2):
+        out_swaps[h].wait_recv()
+
+        @pl.loop(0, hr, step=step)
+        def _(r):
+            at = pl.ds(pl.multiple_of(h * hr + r, step), step)
+            own = dact[pl.ds(pl.multiple_of(h * rows + r, step), step), :]
+            tok[at, :] = (resid[at, :] + own + share[3, at, :].astype(F32)).astype(BF16)
+
+    out_copy = start(pltpu.make_async_copy(tok, block_out, lsem.at[1]))
     weights_part(xn, du, fu)
-    spread_end(0)
-    swaps[4].wait_recv()
-
-    @pl.loop(0, rows, step=step)
-    def _(r):
-        at = rows_at(r, step)
-        block_out[at, :] = (resid[at, :] + share[3, at, :].astype(F32)).astype(BF16)
-
-    weights_part(cot, act, fd)
     spread_end(1)
+    resid_copy.wait()
+    out_copy.wait()
     for h in range(2):
         spread["own", h].wait()
         for m in range(4):
             spread["core", m, h].wait()
         for key in ((1, 0, h), (1, 1, h), (2, 0, h), (2, 1, h), ("g1", h), ("g2", h)):
             spread[key].wait_send()
-    for c in swaps + list(sends.values()):
+    for c in swaps + out_swaps + list(sends.values()):
         c.wait_send()
 
 
@@ -432,6 +443,8 @@
         ],
         [gated, w_out, tokens, gain[None], bias[None], w_up, w_down, cotangent],
         [
+            pltpu.VMEM((rows, width), BF16),
+            pltpu.VMEM((rows, width), F32),
             pltpu.VMEM((PLANE, span, width), BF16),
             pltpu.VMEM(w_up.shape, BF16),
             pltpu.VMEM(w_down.shape, BF16),
@@ -447,9 +460,9 @@
             pltpu.VMEM((span, hidden), BF16),
             pltpu.VMEM((span, width), BF16),
             pltpu.VMEM((rows, width), BF16),
-            pltpu.VMEM((2, 256, hidden), BF16),
-            pltpu.VMEM((span, 512), F32),
-            DMA((7,)),
+            pltpu.VMEM((3, 256, hidden), BF16),
+            pltpu.VMEM((rows, 512), F32),
+            DMA((8,)),
             DMA((PLANE,)),
             DMA((PLANE, 2)),
             DMA((PLANE, 2)),
@@ -461,11 +474,11 @@
             DMA((6, 2)),
             DMA((4, 2)),
             DMA((4, 2)),
-            DMA((2,)),
+            DMA((3,)),
         ],
         cid,
-        in_specs=[ANY, ANY, VM, VM, VM, ANY, ANY, ANY],
-        out_specs=[VM, VM, VM, ANY, ANY, ANY],
+        in_specs=[ANY, ANY, ANY, VM, VM, ANY, ANY, ANY],
+        out_specs=[ANY, ANY, VM, ANY, ANY, ANY],
     )
 
 
@@ -969,8 +982,8 @@
 def retention_back_kernel(
     da_ref, wo_ref, gated_ref, gate_ref, ret_ref, q_ref, k_ref, v_ref, s_ref, cos_ref, sin_ref,
     ccol_ref, crow_ref, scal_ref, xg_ref, fu_ref, fd_ref,
-    dh, sums, f1, av_out, aq_out,
-    da, wo, gated, gr, q, k, v, st, cos, sin, dr, xt, ao, ag, rxo, rxg, fin, qo, gb, lg, got, rxf, fo, pbuf, gbuf,
+    dh_out, sums, f1, av_out, aq_out,
+    dh, da, wo, gated, gr, q, k, v, st, cos, sin, dr, xt, ao, ag, rxo, rxg, fin, qo, gb, lg, got, rxf, fo, pbuf, gbuf,
     lsem, gsem, xsem, fsend, frecv, osem, fosem, ssend, srecv, psend, precv, *line,
 ):
     me = Place()
@@ -990,13 +1003,15 @@
     def f_block(h, zp, place):
         return (fu_ref, fd_ref)[h].at[pl.ds(pl.multiple_of((zp * PLANE + place) * chunk, chunk), chunk), :]
 
+    early = (3, 0, 2)
+    units = 2 * len(early)
     away = ((1, 3), (2, 3))
     kept = ((0, 2), (0, 1))
     nbr = (1, 2)
 
     def f_copy(h, zp, j):
         return remote(
-            f_block(h, zp, pq[away[h][j]]), rxf.at[h, zp, j], fsend.at[h, zp, j], frecv.at[h, zp, j], me.plane(nbr[h])
+            f_block(h, zp, pq[away[h][j]]), rxf.at[h, early.index(zp), j], fsend.at[h, zp, j], frecv.at[h, zp, j], me.plane(nbr[h])
         )
 
     loads = [
@@ -1006,34 +1021,34 @@
              (cos_ref, cos), (sin_ref, sin)]
         )
     ]
-    for zp in range(LINE):
+    for zp in early:
         for h in range(2):
             for j in range(2):
                 f_copy(h, zp, j).start()
 
     def f_own(u):
-        h, zp = u % 2, u // 2
+        h, zp = u % 2, early[u // 2]
         return [
             pltpu.make_async_copy(f_block(h, zp, pq[kept[h][j]]), fo.at[u % 2, j], fosem.at[u % 2, j])
             for j in range(2)
         ]
 
     def f_out(u):
-        h, zp = u % 2, u // 2
-        return pltpu.make_async_copy(rxf.at[h, zp], f1.at[h, zp], osem.at[u])
+        h, zp = u % 2, early[u // 2]
+        return pltpu.make_async_copy(rxf.at[h, u // 2], f1.at[h, zp], osem.at[u])
 
     for u in range(2):
         for c in f_own(u):
             c.start()
 
     def f_unit(u):
-        h, zp = u % 2, u // 2
+        h, zp = u % 2, early[u // 2]
         for j, c in enumerate(f_own(u)):
             c.wait()
             f_copy(h, zp, j).wait_recv()
-            add_rows(rxf.at[h, zp, j], fo.at[u % 2, j])
+            add_rows(rxf.at[h, u // 2, j], fo.at[u % 2, j])
         f_out(u).start()
-        if u + 2 < 2 * LINE:
+        if u + 2 < units:
             for c in f_own(u + 2):
                 c.start()
 
@@ -1042,13 +1057,13 @@
 
     def gate_loads(i):
         at = tile_rows(i)
-        slot = i % 2
+        slot = i % 3
         return (
             pltpu.make_async_copy(gate_ref.at[at, :], gr.at[slot, 0], gsem.at[slot, 0]),
             pltpu.make_async_copy(ret_ref.at[at, :], gr.at[slot, 1], gsem.at[slot, 1]),
         )
 
-    for c in gate_loads(0):
+    for c in gate_loads(0) + gate_loads(1):
         c.start()
 
     out_sum = LineSum(me, lambda zz: ao.at[rows_at(zz * (width // LINE), width // LINE), :], rxo, *line[:4], add_rows)
@@ -1057,12 +1072,15 @@
     loads[0].wait()
     loads[1].wait()
 
-    @pl.loop(0, width, step=256)
-    def _(i):
-        at = rows_at(i, 256)
-        ao[at, :] = tn(da[:, at], gated[...]).astype(BF16)
-
-    out_sum.begin((3, 2))
+    for ends, turn in (((3, 0), 3), ((2, 1), 2)):
+        for zz in ends:
+
+            @pl.loop(0, width // LINE, step=256)
+            def _(i):
+                at = rows_at(zz * (width // LINE) + i, 256)
+                ao[at, :] = tn(da[:, at], gated[...]).astype(BF16)
+
+        out_sum.begin((turn,))
     for c in loads[2:]:
         c.wait()
 
@@ -1070,15 +1088,15 @@
 
     @pl.loop(0, tiles)
     def _(i):
-        @pl.when(i + 1 < tiles)
+        @pl.when(i + 2 < tiles)
         def _():
-            for c in gate_loads(i + 1):
+            for c in gate_loads(i + 2):
                 c.start()
 
         for c in gate_loads(i):
             c.wait()
         at = tile_rows(i)
-        slot = i % 2
+        slot = i % 3
         dgated = nt(da[at, :], wo[...])
         gate = gr[slot, 0]
         ret = gr[slot, 1]
@@ -1121,18 +1139,19 @@
     out_sum.begin((1,))
     out_sum.near(0)
     def x_tile(i):
-        return pltpu.make_async_copy(xg_ref.at[:, rows_at(i * 256, 256)], xt.at[i % 2], xsem.at[i % 2])
+        return pltpu.make_async_copy(xg_ref.at[:, rows_at(i * 256, 256)], xt.at[i % 3], xsem.at[i % 3])
 
     x_tile(0).start()
+    x_tile(1).start()
 
     @pl.loop(0, width // 256)
     def _(i):
-        @pl.when(i + 1 < width // 256)
+        @pl.when(i + 2 < width // 256)
         def _():
-            x_tile(i + 1).start()
+            x_tile(i + 2).start()
 
         x_tile(i).wait()
-        ag[rows_at(i * 256, 256), :] = tn(xt[i % 2], dh[:, 2 * keys + values :]).astype(BF16)
+        ag[rows_at(i * 256, 256), :] = tn(xt[i % 3], dh[:, 2 * keys + values :]).astype(BF16)
 
     gate_sum.begin()
     out_sum.near(1)
@@ -1192,6 +1211,7 @@
             dv = nn(k[at, :], gb[c]) * tail + tn(pbuf[:, r : r + t_size], dr[blk, :])
             dh[at, 2 * keys : 2 * keys + values] = dv.astype(BF16)
 
+    dh_copy = start(pltpu.make_async_copy(dh, dh_out, lsem.at[2]))
     plane = []
 
     def deal(i, chain, a):
@@ -1220,16 +1240,17 @@
         f_unit(u)
     deal(0, out_sum, ao)
     x_tile(0).start()
+    x_tile(1).start()
     wide = 2 * keys + values
 
     @pl.loop(0, width // 256)
     def _(i):
-        @pl.when(i + 1 < width // 256)
+        @pl.when(i + 2 < width // 256)
         def _():
-            x_tile(i + 1).start()
+            x_tile(i + 2).start()
 
         x_tile(i).wait()
-        da[rows_at(i * 256, 256), :wide] = tn(xt[i % 2], dh[:, :wide]).astype(BF16)
+        da[rows_at(i * 256, 256), :wide] = tn(xt[i % 3], dh[:, :wide]).astype(BF16)
 
     to_last = [
         start(pltpu.make_async_copy(da.at[:, : 2 * keys], aq_out, lsem.at[0])),
@@ -1240,15 +1261,13 @@
     for u in range(4, 6):
         f_unit(u)
     deal(1, gate_sum, ag)
-    for u in range(6, 2 * LINE):
-        f_unit(u)
-    for c in plane + to_last:
+    for c in plane + to_last + [dh_copy]:
         c.wait()
     out_sum.finish()
     gate_sum.finish()
-    for u in range(2 * LINE):
+    for u in range(units):
         f_out(u).wait()
-    for zp in range(LINE):
+    for zp in early:
         for h in range(2):
             for j in range(2):
                 f_copy(h, zp, j).wait_send()
@@ -1272,10 +1291,11 @@
         ],
         [da, wo, gated, gate, ret, q, k, v, states, cos, sin, ccol, crow, scal, xg, fu, fd],
         [
+            pltpu.VMEM((tokens, 2 * keys + 2 * values), BF16),
             pltpu.VMEM((tokens, width), BF16),
             pltpu.VMEM(wo.shape, BF16),
             pltpu.VMEM(gated.shape, BF16),
-            pltpu.VMEM((2, 2, 256, values), F32),
+            pltpu.VMEM((3, 2, 256, values), F32),
             pltpu.VMEM(q.shape, BF16),
             pltpu.VMEM(k.shape, BF16),
             pltpu.VMEM(v.shape, BF16),
@@ -1283,7 +1303,7 @@
             pltpu.VMEM(cos.shape, F32),
             pltpu.VMEM(sin.shape, F32),
             pltpu.VMEM((tokens, values), BF16),
-            pltpu.VMEM((2, tokens, 256), BF16),
+            pltpu.VMEM((3, tokens, 256), BF16),
             pltpu.VMEM((width, values), BF16),
             pltpu.VMEM((width, values), BF16),
             pltpu.VMEM((LINE + 1, deep, values), BF16),
@@ -1293,13 +1313,13 @@
             pltpu.VMEM((blocks, keys, values), BF16),
             pltpu.VMEM((keys, values), F32),
             pltpu.VMEM((keys, values), BF16),
-            pltpu.VMEM((2, LINE, 2, chunk, hidden), BF16),
+            pltpu.VMEM((2, LINE - 1, 2, chunk, hidden), BF16),
             pltpu.VMEM((2, 2, chunk, hidden), BF16),
             pltpu.VMEM((STRETCH, STRETCH), BF16),
             pltpu.VMEM((STRETCH, STRETCH), BF16),
             DMA((9,)),
-            DMA((2, 2)),
-            DMA((2,)),
+            DMA((3, 2)),
+            DMA((3,)),
             DMA((2, LINE, 2)),
             DMA((2, LINE, 2)),
             DMA((2 * LINE,)),
@@ -1313,15 +1333,15 @@
         + line_sems(),
         cid,
         in_specs=[ANY] * 11 + [VM] * 3 + [ANY] * 3,
-        out_specs=[VM, ANY, ANY, ANY, ANY],
+        out_specs=[ANY] * 5,
     )
 
 
 def last_kernel(
-    dh_ref, av_ref, aq_ref, wq_ref, wk_ref, wv_ref, wg_ref, f1_ref, tok_ref, gain_ref, resid_ref, second_ref,
-    grad_tokens, gains, fout, sums,
-    dh, wh, share, rx0, rx1a, rx1b, rx2a, rx2b, av, aq, rxv, rxq, fin, rf2, kf, rxfa, rxfb, grx,
-    lsem, fsend, frecv, csend, crecv, xsend, xrecv, gsend, grecv, psend, precv, *line,
+    dh_ref, av_ref, aq_ref, wq_ref, wk_ref, wv_ref, wg_ref, f1_ref, fu_ref, fd_ref, tok_ref, gain_ref, resid_ref, second_ref,
+    grad_out, gains, fout, sums,
+    tok, resid, rxl, flow, dh, wh, share, rx0, rx1a, rx1b, rx2a, rx2b, av, aq, rxv, rxq, fin, rf2, kf, rxfa, rxfb, grx,
+    lsem, ksem, lsend, lrecv, fsend, frecv, csend, crecv, xsend, xrecv, gsend, grecv, psend, precv, *line,
 ):
     me = Place()
     z, p, f = me.z, me.p, me.f
@@ -1337,8 +1357,18 @@
     chunk = width // SPANS
     deep = width // LINE
 
+    late = 1
+
     def f_copy(h, zp):
-        return remote(f1_ref.at[h, zp, 1], rf2.at[h, zp], fsend.at[h, zp], frecv.at[h, zp], me.plane(2 - h))
+        src = flow.at[h] if zp == late else f1_ref.at[h, zp, 1]
+        return remote(src, rf2.at[h, zp], fsend.at[h, zp], frecv.at[h, zp], me.plane(2 - h))
+
+    def f_block(h, place):
+        return (fu_ref, fd_ref)[h].at[rows_at((late * PLANE + place) * chunk, chunk), :]
+
+    def late_copy(h, j):
+        place = pq[((1, 3), (2, 3))[h][j]]
+        return remote(f_block(h, place), rxl.at[h, j], lsend.at[h, j], lrecv.at[h, j], me.plane(1 + h))
 
     def block_of(a, size):
         return lambda zz: a.at[rows_at(zz * size, size), :]
@@ -1349,7 +1379,10 @@
     fb_sum = LineSum(me, lambda zz: kf.at[1, zz], rxfb, *line[12:16], add_rows)
     v_sum.begin(src=block_of(av_ref, deep))
     q_sum.begin(src=block_of(aq_ref, deep))
-    for zp in (3, 0, 2, 1):
+    for j in (1, 0):
+        for h in range(2):
+            late_copy(h, j).start()
+    for zp in (3, 0, 2):
         for h in range(2):
             f_copy(h, zp).start()
     load = start(pltpu.make_async_copy(dh_ref, dh, lsem.at[0]))
@@ -1362,7 +1395,17 @@
         size = w.shape[1]
         loads.append(start(pltpu.make_async_copy(w, wh.at[:, at : at + size], lsem.at[1 + i])))
         at += size
-    keeps = [start(pltpu.make_async_copy(f1_ref.at[h, :, 0], kf.at[h], lsem.at[5 + h])) for h in range(2)]
+    keeps = []
+    for h in range(2):
+        for i, zp in enumerate((3, 0, 2)):
+            keeps.append(start(pltpu.make_async_copy(f1_ref.at[h, zp, 0], kf.at[h, zp], ksem.at[h, i])))
+        for j, dst in ((0, kf.at[h, late]), (1, flow.at[h])):
+            place = pq[((0, 2), (0, 1))[h][j]]
+            keeps.append(start(pltpu.make_async_copy(f_block(h, place), dst, ksem.at[h, 3 + j])))
+    rest = [
+        start(pltpu.make_async_copy(tok_ref, tok, lsem.at[5])),
+        start(pltpu.make_async_copy(resid_ref, resid, lsem.at[6])),
+    ]
 
     load.wait()
     for c in loads + owns:
@@ -1398,78 +1441,6 @@
             sends["b", k] = start(
                 remote(rx0.at[m, :, cb], rx1b.at[k], xsend.at[2 + k], xrecv.at[2 + k], me.plane(2))
             )
-
-    share_part(3)
-    share_part(1)
-    pass_on(3)
-    v_sum.near(0)
-    share_part(2)
-    pass_on(1)
-    share_part(0)
-    v_sum.near(1)
-    pass_on(2)
-    pass_on(0)
-    v_sum.far()
-    for c in keeps:
-        c.wait()
-    for zp in (3, 0, 2, 1):
-        for h in range(2):
-            f_copy(h, zp).wait_recv()
-            add_rows(kf.at[h, zp], rf2.at[h, zp])
-    for zz in (3, 2, 1):
-        fa_sum.begin((zz,))
-        fb_sum.begin((zz,))
-    q_sum.near(0)
-    sends["a", 0].wait_recv()
-    add_into(rx1a.at[0], whole, rx0.at[2], ca)
-    s2a = start(remote(rx1a.at[0], rx2a, xsend.at[4], xrecv.at[4], me.plane(2)))
-    sends["b", 0].wait_recv()
-    add_into(rx1b.at[0], whole, rx0.at[1], cb)
-    s2b = start(remote(rx1b.at[0], rx2b, xsend.at[5], xrecv.at[5], me.plane(1)))
-    q_sum.near(1)
-    q_sum.far()
-    sends["a", 1].wait_recv()
-    sends["b", 1].wait_recv()
-    s2a.wait_recv()
-    s2b.wait_recv()
-    gains[...] = jnp.zeros_like(gains)
-    gains[2:4, :] = second_ref[0:2, :]
-    step = 32
-
-    @pl.loop(0, rows, step=step)
-    def _(r):
-        at = rows_at(r, step)
-        left = rx0[0, at, ca].astype(F32) + rx1a[1, at, :].astype(F32) + rx2a[at, :].astype(F32)
-        right = rx0[0, at, cb].astype(F32) + rx1b[1, at, :].astype(F32) + rx2b[at, :].astype(F32)
-        dx = jnp.concatenate([left, right], axis=1)
-        v = tok_ref[at, :].astype(F32)
-        centered = v - jnp.mean(v, axis=1, keepdims=True)
-        scale = lax.rsqrt(jnp.mean(centered * centered, axis=1, keepdims=True) + 1e-05)
-        hat = centered * scale
-        gains[0:1, :] += jnp.sum(dx * hat, axis=0, keepdims=True)
-        gains[1:2, :] += jnp.sum(dx, axis=0, keepdims=True)
-        g = dx * gain_ref[...]
-        back = scale * (
-            g - jnp.mean(g, axis=1, keepdims=True) - hat * jnp.mean(g * hat, axis=1, keepdims=True)
-        )
-        grad_tokens[at, :] = (back + resid_ref[at, :]).astype(BF16)
-
-    def gain_copies(r):
-        base = (0, 1, 4)[r]
-        return [
-            remote(gains, grx.at[base + i], gsend.at[base + i], grecv.at[base + i], d)
-            for i, d in enumerate(rounds[r])
-        ]
-
-    def gain_begin(r):
-        for c in gain_copies(r):
-            c.start()
-
-    def gain_end(r):
-        for c in gain_copies(r):
-            c.wait()
-        for i in range(len(rounds[r])):
-            gains[...] += grx[(0, 1, 4)[r] + i]
 
     plane = []
 
@@ -1494,26 +1465,112 @@
             )
         )
 
+    share_part(3)
+    share_part(1)
+    v_sum.near(0)
+    share_part(2)
+    for c in keeps:
+        c.wait()
+    for h in range(2):
+        late_copy(h, 1).wait_recv()
+        add_rows(flow.at[h], rxl.at[h, 1])
+        f_copy(h, late).start()
+    pass_on(3)
+    pass_on(1)
+    share_part(0)
+    v_sum.near(1)
+    pass_on(2)
+    pass_on(0)
+    for h in range(2):
+        late_copy(h, 0).wait_recv()
+        add_rows(kf.at[h, late], rxl.at[h, 0])
+    v_sum.far()
+    q_sum.near(0)
+    for zp in (3, 0, 2, 1):
+        for h in range(2):
+            f_copy(h, zp).wait_recv()
+            add_rows(kf.at[h, zp], rf2.at[h, zp])
+    for zz in (3, 2, 1):
+        fa_sum.begin((zz,))
+        fb_sum.begin((zz,))
+    q_sum.near(1)
+    q_sum.far()
+    deal(0, v_sum, av)
+    sends["a", 0].wait_recv()
+    add_into(rx1a.at[0], whole, rx0.at[2], ca)
+    s2a = start(remote(rx1a.at[0], rx2a, xsend.at[4], xrecv.at[4], me.plane(2)))
+    sends["b", 0].wait_recv()
+    add_into(rx1b.at[0], whole, rx0.at[1], cb)
+    s2b = start(remote(rx1b.at[0], rx2b, xsend.at[5], xrecv.at[5], me.plane(1)))
+    fa_sum.near(0)
+    sends["a", 1].wait_recv()
+    sends["b", 1].wait_recv()
+    deal(1, q_sum, aq)
+    fb_sum.near(0)
+    s2a.wait_recv()
+    s2b.wait_recv()
+    for c in rest:
+        c.wait()
+    gains[...] = jnp.zeros_like(gains)
+    gains[2:4, :] = second_ref[0:2, :]
+    step = 32
+
+    @pl.loop(0, rows, step=step)
+    def _(r):
+        at = rows_at(r, step)
+        left = rx0[0, at, ca].astype(F32) + rx1a[1, at, :].astype(F32) + rx2a[at, :].astype(F32)
+        right = rx0[0, at, cb].astype(F32) + rx1b[1, at, :].astype(F32) + rx2b[at, :].astype(F32)
+        dx = jnp.concatenate([left, right], axis=1)
+        v = tok[at, :].astype(F32)
+        centered = v - jnp.mean(v, axis=1, keepdims=True)
+        scale = lax.rsqrt(jnp.mean(centered * centered, axis=1, keepdims=True) + 1e-05)
+        hat = centered * scale
+        gains[0:1, :] += jnp.sum(dx * hat, axis=0, keepdims=True)
+        gains[1:2, :] += jnp.sum(dx, axis=0, keepdims=True)
+        g = dx * gain_ref[...]
+        back = scale * (
+            g - jnp.mean(g, axis=1, keepdims=True) - hat * jnp.mean(g * hat, axis=1, keepdims=True)
+        )
+        tok[at, :] = (back + resid[at, :]).astype(BF16)
+
+    out_copy = start(pltpu.make_async_copy(tok, grad_out, lsem.at[0]))
+
+    def gain_copies(r):
+        base = (0, 1, 4)[r]
+        return [
+            remote(gains, grx.at[base + i], gsend.at[base + i], grecv.at[base + i], d)
+            for i, d in enumerate(rounds[r])
+        ]
+
+    def gain_begin(r):
+        for c in gain_copies(r):
+            c.start()
+
+    def gain_end(r):
+        for c in gain_copies(r):
+            c.wait()
+        for i in range(len(rounds[r])):
+            gains[...] += grx[(0, 1, 4)[r] + i]
+
     gain_begin(0)
-    deal(0, v_sum, av)
+    fa_sum.near(1)
+    fa_sum.far()
     gain_end(0)
     gain_begin(1)
-    deal(1, q_sum, aq)
+    fb_sum.near(1)
     gain_end(1)
     gain_begin(2)
-    fa_sum.near(0)
-    fb_sum.near(0)
-    fa_sum.near(1)
-    fa_sum.far()
-    fb_sum.near(1)
     fb_sum.far()
     fa_sum.arrive()
     total_rows(z, fout.at[0], kf.at[0, z], rxfa)
     fb_sum.arrive()
     total_rows(z, fout.at[1], kf.at[1, z], rxfb)
     gain_end(2)
-    for c in plane:
+    for c in plane + [out_copy]:
         c.wait()
+    for h in range(2):
+        for j in range(2):
+            late_copy(h, j).wait_send()
     for chain in (v_sum, q_sum, fa_sum, fb_sum):
         chain.finish()
     for c in list(first.values()) + list(sends.values()) + [s2a, s2b]:
@@ -1523,7 +1580,7 @@
             f_copy(h, zp).wait_send()
 
 
-def last_sums(dh, av, aq, wq, wk, wv, wg, f1, tokens, gain, resid, second, cid):
+def last_sums(dh, av, aq, wq, wk, wv, wg, f1, fu, fd, tokens, gain, resid, second, cid):
     width = av.shape[0]
     rows = tokens.shape[0]
     keys, values = wq.shape[1], wv.shape[1]
@@ -1538,8 +1595,12 @@
             jax.ShapeDtypeStruct((2, chunk, hidden), F32),
             jax.ShapeDtypeStruct((PLANE, chunk, 2 * values), BF16),
         ],
-        [dh, av, aq, wq, wk, wv, wg, f1, tokens, gain[None], resid, second],
+        [dh, av, aq, wq, wk, wv, wg, f1, fu, fd, tokens, gain[None], resid, second],
         [
+            pltpu.VMEM((rows, width), BF16),
+            pltpu.VMEM((rows, width), F32),
+            pltpu.VMEM((2, 2, chunk, hidden), BF16),
+            pltpu.VMEM((2, chunk, hidden), BF16),
             pltpu.VMEM(dh.shape, BF16),
             pltpu.VMEM((width, dh.shape[1]), BF16),
             pltpu.VMEM((PLANE, 2 * rows, width), BF16),
@@ -1559,6 +1620,9 @@
             pltpu.VMEM((LINE + 1, chunk, hidden), BF16),
             pltpu.VMEM((7, 8, width), F32),
             DMA((9,)),
+            DMA((2, 5)),
+            DMA((2, 2)),
+            DMA((2, 2)),
             DMA((2, LINE)),
             DMA((2, LINE)),
             DMA((4,)),
@@ -1575,8 +1639,8 @@
         + line_sems()
         + line_sems(),
         cid,
-        in_specs=[ANY] * 8 + [VM] * 4,
-        out_specs=[VM, VM, VM, ANY],
+        in_specs=[ANY] * 11 + [VM, ANY, VM],
+        out_specs=[ANY, VM, VM, ANY],
     )
 
 
@@ -1758,6 +1822,8 @@
         value_w,
         gate_w,
         ffn_first,
+        grad_up,
+        grad_down,
         tokens,
         ln1_gain,
         grad_resid,

time: 522 us -> 498 us (0.954)
  Pallas kernels: 515 us -> 490 us
    pallas_call x4, Pallas kernels: 508 us -> 483 us  [comm_call(): pl.pallas_call(kernel, out_shape=outs, in_specs=in_specs if in_specs is n...]
where the time goes in v6:
time: 498 us; the launch traced here: 496 us
  Pallas kernels  490 us (98%)
    pallas_call x4, Pallas kernels, comm_call(): pl.pallas_call(kernel, out_shape=outs, in_specs=in_specs if in_specs is n...  483 us

profile of v6, /device:TPU:16, one launch (start us, length us, event | category | flops | bytes accessed | tf_op | source)
XLA Modules:
  0.0 496.0 jit_solution(9182395946795078811)
XLA Ops:
  0.7 0.1 fusion.2
  0.8 1.3 pad.4.dec_ref
  2.1 0.1 multiply_sine_fusion.1
  2.2 0.8 multiply_sine_fusion
  3.1 0.7 broadcast_in_dim.17.sbase
  3.7 0.7 broadcast_in_dim.16.cbase
  4.4 151.5 %shard_map.237 = (bf16[2048,2048]{1,0:T(8,128)(2,1)}, bf16[2048,256]{1,0:T(8,128)(2,1)}, bf16[2048,256]{1,0:T(8,128)(2,1)}, bf16[2048,512]{1,0:T(8,128)(2,1)}, f...) custom-call(bf16[256,2048]{1,0:T(8,128)(2,1)} %tok_ref.5, ...), custom_call_target="tpu_custom_call" | custom-call | tf_op jit(solution)/shard_map/pallas_call | solution.py:81
  155.9 85.4 %shard_map.238 = (bf16[256,2048]{1,0:T(8,128)(2,1)}, f32[256,2048]{1,0:T(8,128)}, f32[8,2048]{1,0:T(8,128)}, bf16[2048,2048]{1,0:T(8,128)(2,1)}, bf16[2048,2048]{1,0:T(8,128)(2,1)}, /*index=5*/bf16[2048,2048]{1,0:T(8,128)(2,1)}) custom-call(bf16[2048,512]{1,0:T(8,128)(2,1)} %get-tuple-element.55.gated_ref, bf16[512,2048]{1,0:T(8,128)(2,1)} %get-tuple-element.56.wo_ref, ...), custom_call_target="tpu_custom_call" | custom-call | tf_op jit(solution)/shard_map/pallas_call | solution.py:81
  241.3 100.4 %shard_map.239 = (bf16[2048,1536]{1,0:T(8,128)(2,1)}, bf16[4,128,1024]{2,1,0:T(8,128)(2,1)}, bf16[2,4,2,128,2048]{4,3,2,1,0:T(8,128)(2,1)}, bf16[2048,512]{1,0:T(8,128)(2,1)}, bf16[2048,512]{1,0:T(8,128)(2,1)}) custom-call(bf16[2048,2048]{1,0:T(8,128)(2,1)} %get-tuple-element.57.da_ref, bf16[512,2048]{1,0:T(8,128)(2,1)} %get-tuple-element.56.wo_ref, ...), custom_call_target="tpu_custom_call" | custom-call | tf_op jit(solution)/shard_map/pallas_call | solution.py:81
  341.8 146.1 %shard_map.240 = (bf16[256,2048]{1,0:T(8,128)(2,1)}, f32[8,2048]{1,0:T(8,128)}, f32[2,128,2048]{2,1,0:T(8,128)}, bf16[4,128,1024]{2,1,0:T(8,128)(2,1)}) custom-call(bf16[2048,1536]{1,0:T(8,128)(2,1)} %get-tuple-element.72.dh_ref, bf16[2048,512]{1,0:T(8,128)(2,1)} %get-tuple-element.73.av_ref, bf16[2048,512]{1,0:T(8,128)(2,1)} %get-tuple-element.74.aq_ref, ...), custom_call_target="tpu_custom_call" | custom-call | tf_op jit(solution)/shard_map/pallas_call | solution.py:81
  487.9 1.6 fusion.3
  489.5 6.3 %shard_map.241 = (f32[128,1024]{1,0:T(8,128)}, f32[128,1024]{1,0:T(8,128)}, f32[128,2048]{1,0:T(8,128)}, f32[128,2048]{1,0:T(8,128)}, f32[2048,128]{1,0:T(8,128)...) custom-call(bf16[4,128,1024]{2,1,0:T(8,128)(2,1)} %get-tuple-element.82.las, ...), custom_call_target="tpu_custom_call" | custom-call | tf_op jit(solution)/shard_map/pallas_call | solution.py:1671
  (3 shorter events, 0.0 us)

commit v7 on v6

--- a/solution.py
+++ b/solution.py
@@ -2,6 +2,7 @@
 
 import jax
 import jax.numpy as jnp
+import numpy as np
 from jax import lax
 from jax.experimental import pallas as pl
 from jax.experimental.pallas import tpu as pltpu
@@ -488,13 +489,13 @@
 ):
     count = len(widths)
     shards_in, refs = refs[:count], refs[count:]
-    (xg, q_out, k_out, v_out, gate_out, ret_out, gated_out, states_out, cos_out, sin_out, ccol, crow, scal), refs = (
+    (xg, q_out, k_out, v_out, gate_out, ret_out, gated_out, states_out, cos_out, sin_out, ccol_out, crow_out, scal_out), refs = (
         refs[:13], refs[13:],
     )
     full, refs = refs[:count], refs[count:]
     hold, refs = refs[:count], refs[count:]
     wl, refs = refs[: count - 1], refs[count - 1 :]
-    (xn, xv, q, k, v, gate, ret, gated, cos, sin, kv, st, sloc, sgot, decg,
+    (tok, ccol, crow, scal, xn, xv, q, k, v, gate, ret, gated, cos, sin, kv, st, sloc, sgot, decg,
      lsem, psend, precv, usend, dsend, zrecv, xsend, xrecv, csend, crecv, tsend, trecv, ssend, srecv, osem, wsem) = refs
     me = Place()
     z, p, f = me.z, me.p, me.f
@@ -525,6 +526,29 @@
         at = pl.ds(pl.multiple_of(zz * deep, deep), deep)
         return full[i].at[:, at] if by_rows[i] else full[i].at[at, :]
 
+    def up_copy(i, zz):
+        return remote(block(i, zz), block(i, zz), usend.at[i, zz], zrecv.at[i, zz], me.up())
+
+    def down_copy(i, zz):
+        return remote(block(i, zz), block(i, zz), dsend.at[i, zz], zrecv.at[i, zz], me.down())
+
+    def part_copies(i, src, at):
+        return (
+            remote(src, slot(i, at), usend.at[i, z], zrecv.at[i, z], me.up()),
+            remote(src, slot(i, at), dsend.at[i, z], zrecv.at[i, z], me.down()),
+        )
+
+    def to_line(copies):
+        @pl.when(z < LINE - 1)
+        def _():
+            copies[0].start()
+
+        @pl.when(z > 0)
+        def _():
+            copies[1].start()
+
+    ahead = 2
+    load_t = start(pltpu.make_async_copy(tok_ref, tok, lsem.at[count + 1]))
     local, plane, held = [], [], []
     for i in range(count):
         held.append(start(pltpu.make_async_copy(part(i, p), hold[i], lsem.at[i])))
@@ -535,14 +559,17 @@
                 for m in (1, 2, 3)
             ]
         )
+    for i in range(ahead):
+        to_line(part_copies(i, part(i, p), spot))
     tiny = [start(remote(dec_ref, decg.at[p], tsend.at[m], trecv.at[m], me.plane(m))) for m in (1, 2, 3)]
     tiny_own = start(pltpu.make_async_copy(dec_ref, decg.at[p], tsend.at[0]))
     step = 32
+    load_t.wait()
 
     @pl.loop(0, rows, step=step)
     def _(r):
         at = rows_at(r, step)
-        t = tok_ref[at, :].astype(F32)
+        t = tok[at, :].astype(F32)
         centered = t - jnp.mean(t, axis=1, keepdims=True)
         scale = lax.rsqrt(jnp.mean(centered * centered, axis=1, keepdims=True) + 1e-05)
         xn[at, :] = (centered * scale * gain_ref[...] + bias_ref[...]).astype(BF16)
@@ -561,24 +588,16 @@
         held[i].wait()
         local[i].start()
 
-    def up_copy(i, zz):
-        return remote(block(i, zz), block(i, zz), usend.at[i, zz], zrecv.at[i, zz], me.up())
-
-    def down_copy(i, zz):
-        return remote(block(i, zz), block(i, zz), dsend.at[i, zz], zrecv.at[i, zz], me.down())
-
     def own(i):
         local[i].wait()
         for c in plane[i]:
             c.wait_recv()
-
-        @pl.when(z < LINE - 1)
-        def _():
-            up_copy(i, z).start()
-
-        @pl.when(z > 0)
-        def _():
-            down_copy(i, z).start()
+        if i < ahead:
+            for m in (1, 2, 3):
+                at = z * PLANE + me.xor(m)
+                to_line(part_copies(i, slot(i, at), at))
+        else:
+            to_line((up_copy(i, z), down_copy(i, z)))
 
     def forward(i, t):
         @pl.when(z - t >= 0)
@@ -638,7 +657,8 @@
     @pl.loop(0, tokens // fine)
     def _(a):
         at = rows_at(a * fine, fine)
-        ca, sa = cbase[a, 0:1, :], sbase[a, 0:1, :]
+        place = pl.ds(z * (tokens // fine) + a, 1)
+        ca, sa = cbase[place, :], sbase[place, :]
         cos[at, :] = ca * coff[...] - sa * soff[...]
         sin[at, :] = sa * coff[...] + ca * soff[...]
 
@@ -667,6 +687,9 @@
         outs.append(start(pltpu.make_async_copy(src, dst, osem.at[len(outs)])))
 
     put(xv, xg)
+    put(ccol, ccol_out)
+    put(crow, crow_out)
+    put(scal, scal_out)
     put(cos, cos_out)
     put(sin, sin_out)
     load_k.wait()
@@ -833,6 +856,10 @@
         + [pltpu.VMEM(s, BF16) for s in wholes[:-1]]
         + [
             pltpu.VMEM((rows, width), BF16),
+            pltpu.VMEM((group, 1), F32),
+            pltpu.VMEM((blocks, 8, STRETCH), F32),
+            pltpu.VMEM((2 * blocks + 1, 8, 128), F32),
+            pltpu.VMEM((rows, width), BF16),
             pltpu.VMEM((group, width), BF16),
             pltpu.VMEM((group, keys), BF16),
             pltpu.VMEM((group, keys), BF16),
@@ -847,7 +874,7 @@
             pltpu.VMEM((keys, values), F32),
             pltpu.VMEM((keys, values), BF16),
             pltpu.VMEM((PLANE,) + decays.shape, F32),
-            DMA((count + 1,)),
+            DMA((count + 2,)),
             DMA((count, PLANE)),
             DMA((count, PLANE)),
             DMA((count, LINE)),
@@ -871,8 +898,8 @@
         [tokens, gain[None], bias[None], decays] + list(tables) + list(shards_in),
         scratch,
         cid,
-        in_specs=[VM] * 8 + [ANY] * count,
-        out_specs=[ANY] * 10 + [VM] * 3 + [ANY] * count,
+        in_specs=[ANY] + [VM] * 7 + [ANY] * count,
+        out_specs=[ANY] * (13 + count),
     )
 
 
@@ -981,9 +1008,9 @@
 
 def retention_back_kernel(
     da_ref, wo_ref, gated_ref, gate_ref, ret_ref, q_ref, k_ref, v_ref, s_ref, cos_ref, sin_ref,
-    ccol_ref, crow_ref, scal_ref, xg_ref, fu_ref, fd_ref,
-    dh_out, sums, f1, av_out, aq_out,
-    dh, da, wo, gated, gr, q, k, v, st, cos, sin, dr, xt, ao, ag, rxo, rxg, fin, qo, gb, lg, got, rxf, fo, pbuf, gbuf,
+    ccol_in, crow_in, scal_in, xg_ref, fu_ref, fd_ref,
+    dh_out, sums, gate_fin, f1, av_out, aq_out,
+    ccol_ref, crow_ref, scal_ref, dh, da, wo, gated, gr, q, k, v, st, cos, sin, dr, xt, ao, ag, rxo, rxg, fin, qo, gb, lg, got, rxf, fo, pbuf, gbuf,
     lsem, gsem, xsem, fsend, frecv, osem, fosem, ssend, srecv, psend, precv, *line,
 ):
     me = Place()
@@ -1014,13 +1041,23 @@
             f_block(h, zp, pq[away[h][j]]), rxf.at[h, early.index(zp), j], fsend.at[h, zp, j], frecv.at[h, zp, j], me.plane(nbr[h])
         )
 
+    deep = width // LINE
+    ends_first = [jnp.where(z < LINE // 2, LINE - 1 - i, i) for i in range(LINE)]
+
+    def slab(i):
+        at = rows_at(ends_first[i] * deep, deep)
+        return pltpu.make_async_copy(da_ref.at[:, at], da.at[:, at], lsem.at[12 + i])
+
+    slab(0).start()
     loads = [
         start(pltpu.make_async_copy(a, b, lsem.at[i]))
         for i, (a, b) in enumerate(
-            [(da_ref, da), (gated_ref, gated), (wo_ref, wo), (q_ref, q), (k_ref, k), (v_ref, v), (s_ref, st),
-             (cos_ref, cos), (sin_ref, sin)]
+            [(gated_ref, gated), (wo_ref, wo), (q_ref, q), (k_ref, k), (v_ref, v), (s_ref, st),
+             (cos_ref, cos), (sin_ref, sin), (ccol_in, ccol_ref), (crow_in, crow_ref), (scal_in, scal_ref)]
         )
     ]
+    for i in range(1, LINE):
+        slab(i).start()
     for zp in early:
         for h in range(2):
             for j in range(2):
@@ -1070,18 +1107,17 @@
     gate_sum = LineSum(me, lambda zz: ag.at[rows_at(zz * (width // LINE), width // LINE), :], rxg, *line[4:], add_rows)
 
     loads[0].wait()
-    loads[1].wait()
-
-    for ends, turn in (((3, 0), 3), ((2, 1), 2)):
-        for zz in ends:
-
-            @pl.loop(0, width // LINE, step=256)
-            def _(i):
-                at = rows_at(zz * (width // LINE) + i, 256)
-                ao[at, :] = tn(da[:, at], gated[...]).astype(BF16)
-
-        out_sum.begin((turn,))
-    for c in loads[2:]:
+    for turn in range(LINE):
+        slab(turn).wait()
+
+        @pl.loop(0, deep, step=256)
+        def _(i):
+            at = rows_at(ends_first[turn] * deep + i, 256)
+            ao[at, :] = tn(da[:, at], gated[...]).astype(BF16)
+
+        if turn < 2:
+            out_sum.begin((LINE - 1 - turn,))
+    for c in loads[1:]:
         c.wait()
 
     tiles = tokens // 256
@@ -1260,7 +1296,9 @@
     gate_sum.far()
     for u in range(4, 6):
         f_unit(u)
-    deal(1, gate_sum, ag)
+    gate_sum.arrive()
+    total_rows(z, fin.at[1], ag.at[rows_at(z * deep, deep), :], rxg)
+    to_last.append(start(pltpu.make_async_copy(fin.at[1], gate_fin, lsem.at[3])))
     for c in plane + to_last + [dh_copy]:
         c.wait()
     out_sum.finish()
@@ -1284,13 +1322,17 @@
         retention_back_kernel,
         [
             jax.ShapeDtypeStruct((tokens, 2 * keys + 2 * values), BF16),
-            jax.ShapeDtypeStruct((PLANE, chunk, 2 * values), BF16),
+            jax.ShapeDtypeStruct((PLANE, chunk, values), BF16),
+            jax.ShapeDtypeStruct((deep, values), BF16),
             jax.ShapeDtypeStruct((2, LINE, 2, chunk, hidden), BF16),
             jax.ShapeDtypeStruct((width, values), BF16),
             jax.ShapeDtypeStruct((width, 2 * keys), BF16),
         ],
         [da, wo, gated, gate, ret, q, k, v, states, cos, sin, ccol, crow, scal, xg, fu, fd],
         [
+            pltpu.VMEM(ccol.shape, F32),
+            pltpu.VMEM(crow.shape, F32),
+            pltpu.VMEM(scal.shape, F32),
             pltpu.VMEM((tokens, 2 * keys + 2 * values), BF16),
             pltpu.VMEM((tokens, width), BF16),
             pltpu.VMEM(wo.shape, BF16),
@@ -1317,7 +1359,7 @@
             pltpu.VMEM((2, 2, chunk, hidden), BF16),
             pltpu.VMEM((STRETCH, STRETCH), BF16),
             pltpu.VMEM((STRETCH, STRETCH), BF16),
-            DMA((9,)),
+            DMA((12 + LINE,)),
             DMA((3, 2)),
             DMA((3,)),
             DMA((2, LINE, 2)),
@@ -1332,13 +1374,13 @@
         + line_sems()
         + line_sems(),
         cid,
-        in_specs=[ANY] * 11 + [VM] * 3 + [ANY] * 3,
-        out_specs=[ANY] * 5,
+        in_specs=[ANY] * 17,
+        out_specs=[ANY] * 6,
     )
 
 
 def last_kernel(
-    dh_ref, av_ref, aq_ref, wq_ref, wk_ref, wv_ref, wg_ref, f1_ref, fu_ref, fd_ref, tok_ref, gain_ref, resid_ref, second_ref,
+    dh_ref, av_ref, aq_ref, wq_ref, wk_ref, wv_ref, wg_ref, f1_ref, fu_ref, fd_ref, gate_ref, tok_ref, gain_ref, resid_ref, second_ref,
     grad_out, gains, fout, sums,
     tok, resid, rxl, flow, dh, wh, share, rx0, rx1a, rx1b, rx2a, rx2b, av, aq, rxv, rxq, fin, rf2, kf, rxfa, rxfb, grx,
     lsem, ksem, lsend, lrecv, fsend, frecv, csend, crecv, xsend, xrecv, gsend, grecv, psend, precv, *line,
@@ -1408,8 +1450,36 @@
     ]
 
     load.wait()
-    for c in loads + owns:
+    plane = []
+
+    def deal(i, chain, a):
+        chain.arrive()
+        total_rows(z, fin.at[i], a.at[rows_at(z * deep, deep), :], chain.rx)
+        spread(i, fin.at[i])
+
+    def spread(i, src):
+        cols = pl.ds(i * values, values)
+        for m in (1, 2, 3):
+            plane.append(
+                start(
+                    remote(
+                        src.at[rows_at(pq[m] * chunk, chunk), :], sums.at[p, :, cols],
+                        psend.at[i, m], precv.at[i, m], me.plane(m),
+                    )
+                )
+            )
+        plane.append(
+            start(
+                pltpu.make_async_copy(
+                    src.at[rows_at(p * chunk, chunk), :], sums.at[p, :, cols], psend.at[i, 0]
+                )
+            )
+        )
+
+    gate_load = start(pltpu.make_async_copy(gate_ref, fin.at[2], lsem.at[9]))
+    for c in loads + owns + [gate_load]:
         c.wait()
+    spread(2, fin.at[2])
 
     own_rows, their_rows = rows_at(f * rows, rows), rows_at((1 - f) * rows, rows)
     wide = width // 2
@@ -1441,29 +1511,6 @@
             sends["b", k] = start(
                 remote(rx0.at[m, :, cb], rx1b.at[k], xsend.at[2 + k], xrecv.at[2 + k], me.plane(2))
             )
-
-    plane = []
-
-    def deal(i, chain, a):
-        chain.arrive()
-        total_rows(z, fin.at[i], a.at[rows_at(z * deep, deep), :], chain.rx)
-        cols = pl.ds(i * values, values)
-        for m in (1, 2, 3):
-            plane.append(
-                start(
-                    remote(
-                        fin.at[i, rows_at(pq[m] * chunk, chunk), :], sums.at[p, :, cols],
-                        psend.at[i, m], precv.at[i, m], me.plane(m),
-                    )
-                )
-            )
-        plane.append(
-            start(
-                pltpu.make_async_copy(
-                    fin.at[i, rows_at(p * chunk, chunk), :], sums.at[p, :, cols], psend.at[i, 0]
-                )
-            )
-        )
 
     share_part(3)
     share_part(1)
@@ -1486,13 +1533,14 @@
         add_rows(kf.at[h, late], rxl.at[h, 0])
     v_sum.far()
     q_sum.near(0)
-    for zp in (3, 0, 2, 1):
-        for h in range(2):
-            f_copy(h, zp).wait_recv()
-            add_rows(kf.at[h, zp], rf2.at[h, zp])
-    for zz in (3, 2, 1):
-        fa_sum.begin((zz,))
-        fb_sum.begin((zz,))
+    for ends, turns in (((3, 0), (3,)), ((2, 1), (2, 1))):
+        for zp in ends:
+            for h in range(2):
+                f_copy(h, zp).wait_recv()
+                add_rows(kf.at[h, zp], rf2.at[h, zp])
+        for zz in turns:
+            fa_sum.begin((zz,))
+            fb_sum.begin((zz,))
     q_sum.near(1)
     q_sum.far()
     deal(0, v_sum, av)
@@ -1580,7 +1628,7 @@
             f_copy(h, zp).wait_send()
 
 
-def last_sums(dh, av, aq, wq, wk, wv, wg, f1, fu, fd, tokens, gain, resid, second, cid):
+def last_sums(dh, av, aq, wq, wk, wv, wg, f1, fu, fd, gate_fin, tokens, gain, resid, second, cid):
     width = av.shape[0]
     rows = tokens.shape[0]
     keys, values = wq.shape[1], wv.shape[1]
@@ -1592,10 +1640,10 @@
         [
             jax.ShapeDtypeStruct((rows, width), BF16),
             jax.ShapeDtypeStruct((8, width), F32),
-            jax.ShapeDtypeStruct((2, chunk, hidden), F32),
-            jax.ShapeDtypeStruct((PLANE, chunk, 2 * values), BF16),
+            jax.ShapeDtypeStruct((2, chunk, hidden), BF16),
+            jax.ShapeDtypeStruct((PLANE, chunk, 3 * values), BF16),
         ],
-        [dh, av, aq, wq, wk, wv, wg, f1, fu, fd, tokens, gain[None], resid, second],
+        [dh, av, aq, wq, wk, wv, wg, f1, fu, fd, gate_fin, tokens, gain[None], resid, second],
         [
             pltpu.VMEM((rows, width), BF16),
             pltpu.VMEM((rows, width), F32),
@@ -1613,13 +1661,13 @@
             pltpu.VMEM((width, 2 * keys), BF16),
             pltpu.VMEM((LINE + 1, deep, values), BF16),
             pltpu.VMEM((LINE + 1, deep, 2 * keys), BF16),
-            pltpu.VMEM((2, deep, values), BF16),
+            pltpu.VMEM((3, deep, values), BF16),
             pltpu.VMEM((2, LINE, chunk, hidden), BF16),
             pltpu.VMEM((2, LINE, chunk, hidden), BF16),
             pltpu.VMEM((LINE + 1, chunk, hidden), BF16),
             pltpu.VMEM((LINE + 1, chunk, hidden), BF16),
             pltpu.VMEM((7, 8, width), F32),
-            DMA((9,)),
+            DMA((10,)),
             DMA((2, 5)),
             DMA((2, 2)),
             DMA((2, 2)),
@@ -1631,47 +1679,57 @@
             DMA((6,)),
             DMA((7,)),
             DMA((7,)),
-            DMA((2, PLANE)),
-            DMA((2, PLANE)),
+            DMA((3, PLANE)),
+            DMA((3, PLANE)),
         ]
         + line_sems()
         + line_sems()
         + line_sems()
         + line_sems(),
         cid,
-        in_specs=[ANY] * 11 + [VM, ANY, VM],
+        in_specs=[ANY] * 12 + [VM, ANY, VM],
         out_specs=[ANY, VM, VM, ANY],
     )
 
 
-def outputs_kernel(last, first, ffn, low_out, low_grad, q, k, v, gate, out, up, down, block_out, grad_tokens):
+def outputs_kernel(
+    last, first, ffn, low_out, low_grad, gains, q, k, v, gate, out, up, down, block_out, grad_tokens, *vectors
+):
     values = v.shape[1]
     keys = q.shape[1]
     v[...] = last[0, :, :values].astype(F32)
     q[...] = last[0, :, values : values + keys].astype(F32)
-    k[...] = last[0, :, values + keys :].astype(F32)
-    out[...] = first[0, :, :values].astype(F32).T
-    gate[...] = first[0, :, values:].astype(F32)
-    up[...] = ffn[0]
-    down[...] = ffn[1].T
+    k[...] = last[0, :, values + keys : 2 * values].astype(F32)
+    gate[...] = last[0, :, 2 * values :].astype(F32)
+    out[...] = first[0].astype(F32).T
+    up[...] = ffn[0].astype(F32)
+    down[...] = ffn[1].astype(F32).T
     block_out[...] = low_out[...]
     grad_tokens[...] = low_grad[...]
-
-
-def outputs(last, first, ffn, low_out, low_grad, keys):
-    heads, chunk, both = last.shape
-    values, hidden = both // 2, ffn.shape[-1]
+    for i, g in enumerate(vectors):
+        g[...] = gains[i, :]
+
+
+def outputs(last, first, ffn, low_out, low_grad, gains, keys):
+    heads, chunk, values = first.shape
+    hidden = ffn.shape[-1]
     rows, width = low_out.shape
     piece, slab = hidden // heads, rows // heads
     sd = jax.ShapeDtypeStruct
     by_column = [pl.BlockSpec((chunk, size), lambda i: (0, i)) for size in (keys, keys, values, values)]
     by_row = pl.BlockSpec((values, chunk), lambda i: (i, 0))
     low = pl.BlockSpec((slab, width), lambda i: (i, 0))
-    sums = pl.BlockSpec((1, chunk, both), lambda i: (i, 0, 0))
+    sums = [pl.BlockSpec((1, chunk, a.shape[-1]), lambda i: (i, 0, 0)) for a in (last, first)]
     return pl.pallas_call(
         outputs_kernel,
         grid=(heads,),
-        in_specs=[sums, sums, pl.BlockSpec((2, chunk, piece), lambda i: (0, 0, i)), low, low],
+        in_specs=[
+            *sums,
+            pl.BlockSpec((2, chunk, piece), lambda i: (0, 0, i)),
+            low,
+            low,
+            pl.BlockSpec(gains.shape, lambda i: (0, 0)),
+        ],
         out_specs=by_column
         + [
             by_row,
@@ -1679,7 +1737,8 @@
             pl.BlockSpec((piece, chunk), lambda i: (i, 0)),
             low,
             low,
-        ],
+        ]
+        + [pl.BlockSpec((width,), lambda i: (0,))] * 4,
         out_shape=[
             sd((chunk, heads * keys), F32),
             sd((chunk, heads * keys), F32),
@@ -1690,21 +1749,16 @@
             sd((hidden, chunk), F32),
             sd((rows, width), BF16),
             sd((rows, width), BF16),
-        ],
-    )(last, first, ffn, low_out, low_grad)
-
-
-def angle_tables(first, count, fine, half_width):
-    frequency = 10000.0 ** (-jnp.linspace(0.0, 1.0, half_width, dtype=F32))
-    coarse = ((first + fine * jnp.arange(count)) % SEQUENCE_LENGTH).astype(F32)[:, None] * frequency[None, :]
-    near = jnp.arange(fine).astype(F32)[:, None] * frequency[None, :]
-    wide = (count, 8, half_width)
-    return [
-        jnp.broadcast_to(jnp.cos(coarse)[:, None], wide),
-        jnp.broadcast_to(jnp.sin(coarse)[:, None], wide),
-        jnp.cos(near),
-        jnp.sin(near),
-    ]
+        ]
+        + [sd((width,), F32)] * 4,
+    )(last, first, ffn, low_out, low_grad, gains)
+
+
+def angle_tables(fine, half_width):
+    frequency = 10000.0 ** (-np.linspace(0.0, 1.0, half_width))
+    coarse = fine * np.arange(SEQUENCE_LENGTH // fine)[:, None] * frequency[None, :]
+    near = np.arange(fine)[:, None] * frequency[None, :]
+    return [np.asarray(f(a), np.float32) for a in (coarse, near) for f in (np.cos, np.sin)]
 
 
 def shards(
@@ -1761,8 +1815,7 @@
     w_up = features_in(w_up.T).T if repeats > 1 else w_up
     ln1_gain, ln1_bias = features_in(ln1_gain), features_in(ln1_bias)
     ln2_gain, ln2_bias = features_in(ln2_gain), features_in(ln2_bias)
-    decays = jnp.pad(decay_log.T, ((0, 8 - heads), (0, 0)))
-    fine = 64
+    decays = decay_log.T
     (
         normed, q_rot, k_rot, value, gate_proj, retained, gated_low, prev_states,
         cosine, sine_part, ccol, crow, scalars, key_w, value_w, query_w, gate_w, out_w,
@@ -1771,7 +1824,7 @@
         ln1_gain,
         ln1_bias,
         decays,
-        angle_tables(z * group_rows, group_rows // fine, fine, w_key.shape[1] // heads // 2),
+        angle_tables(64, w_key.shape[1] // heads // 2),
         [
             wide_in(w_key, 0),
             wide_in(w_value, 0),
@@ -1793,7 +1846,7 @@
         cotangent,
         2,
     )
-    grad_heads, sums_first, ffn_first, grad_value_w, grad_qk_w = retention_back(
+    grad_heads, sums_first, gate_sum, ffn_first, grad_value_w, grad_qk_w = retention_back(
         grad_attn,
         out_w,
         gated_low,
@@ -1824,6 +1877,7 @@
         ffn_first,
         grad_up,
         grad_down,
+        gate_sum,
         tokens,
         ln1_gain,
         grad_resid,
@@ -1832,12 +1886,11 @@
     )
     if repeats > 1:
         gains = lax.psum(gains, "seq", axis_index_groups=peers)
-    gains = features_out(gains)
-    gain_one, bias_one, gain_two, bias_two = gains[0], gains[1], gains[2], gains[3]
-
-    *sums, block_out, grad_tokens = outputs(
-        sums_last, sums_first, ffn_sum, block_out, grad_tokens, key_w.shape[1]
+
+    *sums, block_out, grad_tokens, gain_one, bias_one, gain_two, bias_two = outputs(
+        sums_last, sums_first, ffn_sum, block_out, grad_tokens, gains, key_w.shape[1]
     )
+    gain_one, bias_one, gain_two, bias_two = map(features_out, (gain_one, bias_one, gain_two, bias_two))
     sum_query, sum_key, sum_value, sum_gate, sum_out, sum_up, sum_down = (
         narrow_out(g, axis) for g, axis in zip(sums, (0, 0, 0, 0, 1, 0, 1))
     )

time: 498 us -> 490 us (0.984)
  Pallas kernels: 490 us -> 484 us
    pallas_call x4, Pallas kernels: 483 us -> 478 us  [comm_call(): pl.pallas_call(kernel, out_shape=outs, in_specs=in_specs if in_specs is n...]
where the time goes in v7:
time: 490 us; the launch traced here: 485 us
  Pallas kernels  484 us (99%)
    pallas_call x4, Pallas kernels, comm_call(): pl.pallas_call(kernel, out_shape=outs, in_specs=in_specs if in_specs is n...  478 us

profile of v7, /device:TPU:16, one launch (start us, length us, event | category | flops | bytes accessed | tf_op | source)
XLA Modules:
  0.0 485.2 jit_solution(16698851332129296638)
XLA Ops:
  0.6 147.3 %shard_map.273 = (bf16[2048,2048]{1,0:T(8,128)(2,1)}, bf16[2048,256]{1,0:T(8,128)(2,1)}, bf16[2048,256]{1,0:T(8,128)(2,1)}, bf16[2048,512]{1,0:T(8,128)(2,1)}, f...) custom-call(bf16[256,2048]{1,0:T(8,128)(2,1)} %tok_ref.5, ...), custom_call_target="tpu_custom_call" | custom-call | tf_op jit(solution)/shard_map/pallas_call | solution.py:82
  147.9 86.2 %shard_map.274 = (bf16[256,2048]{1,0:T(8,128)(2,1)}, f32[256,2048]{1,0:T(8,128)}, f32[8,2048]{1,0:T(8,128)}, bf16[2048,2048]{1,0:T(8,128)(2,1)}, bf16[2048,2048]{1,0:T(8,128)(2,1)}, /*index=5*/bf16[2048,2048]{1,0:T(8,128)(2,1)}) custom-call(bf16[2048,512]{1,0:T(8,128)(2,1)} %get-tuple-element.60.gated_ref, bf16[512,2048]{1,0:T(8,128)(2,1)} %get-tuple-element.61.wo_ref, ...), custom_call_target="tpu_custom_call" | custom-call | tf_op jit(solution)/shard_map/pallas_call | solution.py:82
  234.1 97.1 %shard_map.275 = (bf16[2048,1536]{1,0:T(8,128)(2,1)}, bf16[4,128,512]{2,1,0:T(8,128)(2,1)}, bf16[512,512]{1,0:T(8,128)(2,1)}, bf16[2,4,2,128,2048]{4,3,2,1,0:T(8...) custom-call(bf16[2048,2048]{1,0:T(8,128)(2,1)} %get-tuple-element.62.da_ref, ...), custom_call_target="tpu_custom_call" | custom-call | tf_op jit(solution)/shard_map/pallas_call | solution.py:82
  331.2 147.7 %shard_map.276 = (bf16[256,2048]{1,0:T(8,128)(2,1)}, f32[8,2048]{1,0:T(8,128)}, bf16[2,128,2048]{2,1,0:T(8,128)(2,1)}, bf16[4,128,1536]{2,1,0:T(8,128)(2,1)}) custom-call(bf16[2048,1536]{1,0:T(8,128)(2,1)} %get-tuple-element.77.dh_ref, bf16[2048,512]{1,0:T(8,128)(2,1)} %get-tuple-element.78.av_ref, bf16[2048,512]{1,0:T(8,128)(2,1)} %get-tuple-element.79.aq_ref, ...), custom_call_target="tpu_custom_call" | custom-call | tf_op jit(solution)/shard_map/pallas_call | solution.py:82
  478.9 6.2 %shard_map.277 = (f32[128,1024]{1,0:T(8,128)}, f32[128,1024]{1,0:T(8,128)}, f32[128,2048]{1,0:T(8,128)}, f32[128,2048]{1,0:T(8,128)}, f32[2048,128]{1,0:T(8,128)...) custom-call(bf16[4,128,1536]{2,1,0:T(8,128)(2,1)} %get-tuple-element, ...), custom_call_target="tpu_custom_call" | custom-call | tf_op jit(solution)/shard_map/pallas_call | solution.py:1723

commit v8 on v7

--- a/solution.py
+++ b/solution.py
@@ -56,6 +56,14 @@
 
 
 def greet(peers):
+    meet(call(peers))
+
+
+def meet(count):
+    pl.semaphore_wait(pltpu.get_barrier_semaphore(), count)
+
+
+def call(peers):
     bar = pltpu.get_barrier_semaphore()
     count = 0
     for device, cond in peers:
@@ -69,7 +77,7 @@
                 pl.semaphore_signal(bar, inc=1, device_id=device, device_id_type=MESH)
 
             count = count + cond.astype(jnp.int32)
-    pl.semaphore_wait(bar, count)
+    return count
 
 
 def remote(src, dst, send, recv, device):
@@ -126,11 +134,11 @@
     gated_ref, wo_ref, tok_ref, gain_ref, bias_ref, wu_ref, wd_ref, cot_ref,
     block_out, resid_out, gains, da, fu, fd,
     tok, resid_grad, share, wu, wd, rx0, rx1a, rx1b, rx2a, rx2b, resid, xn, act, dact, du, cot, dab, stage, tmp,
-    lsem, gload, csend, crecv, xsend, xrecv, psend, precv, gsend, grecv, ksend, krecv, ssem,
+    lsem, gload, csend, crecv, xsend, xrecv, psend, precv, gsend, grecv, ksend, krecv, ssem, osem,
 ):
     me = Place()
     p, f = me.p, me.f
-    greet([(me.plane(1), None), (me.plane(2), None), (me.partner(), None)])
+    greeted = call([(me.plane(1), None), (me.plane(2), None), (me.partner(), None)])
     rows, width = tok_ref.shape
     hidden = wu.shape[1]
     q = [me.xor(m) for m in range(4)]
@@ -146,7 +154,12 @@
 
     order = (3, 1, 2, 0)
     part_width = gated_ref.shape[1]
-    load_o = start(pltpu.make_async_copy(wo_ref, act, lsem.at[0]))
+    def out_slab(i):
+        at = rows_at(i * 512, 512)
+        return pltpu.make_async_copy(wo_ref.at[:, at], act.at[:, at], osem.at[i])
+
+    slabs = width // 512
+    out_slab(0).start()
     load_t = pltpu.make_async_copy(tok_ref, tok, lsem.at[7])
     load_g = {
         m: start(
@@ -158,6 +171,8 @@
         )
         for m in order
     }
+    for i in range(1, slabs):
+        out_slab(i).start()
     load_t.start()
     load_d = start(pltpu.make_async_copy(wd_ref, wd, lsem.at[1]))
     load_c = [
@@ -170,7 +185,6 @@
         for c in range(2)
     ]
     load_u = start(pltpu.make_async_copy(wu_ref, wu, lsem.at[2]))
-    load_o.wait()
     first, sends = {}, {}
 
     def to_partner(m, h):
@@ -184,11 +198,15 @@
     for m in order:
         load_g[m].wait()
 
-        @pl.loop(0, width, step=512)
-        def _(c):
-            at = rows_at(c, 512)
+        @pl.loop(0, slabs)
+        def _(i):
+            if m == order[0]:
+                out_slab(i).wait()
+            at = rows_at(i * 512, 512)
             share[m, :, at] = nn(xn[:, m * part_width : (m + 1) * part_width], act[:, at]).astype(BF16)
 
+        if m == order[0]:
+            meet(greeted)
         to_partner(m, 0)
     for m in order:
         to_partner(m, 1)
@@ -476,6 +494,7 @@
             DMA((4, 2)),
             DMA((4, 2)),
             DMA((3,)),
+            DMA((width // 512,)),
         ],
         cid,
         in_specs=[ANY, ANY, ANY, VM, VM, ANY, ANY, ANY],
@@ -1015,7 +1034,7 @@
 ):
     me = Place()
     z, p = me.z, me.p
-    greet(
+    greeted = call(
         [(me.plane(m), None) for m in (1, 2, 3)]
         + [(me.up(), z < LINE - 1), (me.down(), z > 0)]
     )
@@ -1030,15 +1049,17 @@
     def f_block(h, zp, place):
         return (fu_ref, fd_ref)[h].at[pl.ds(pl.multiple_of((zp * PLANE + place) * chunk, chunk), chunk), :]
 
-    early = (3, 0, 2)
-    units = 2 * len(early)
+    units = [(h, zp, (0, 1)) for zp in (3, 0, 2) for h in range(2)] + [(h, 1, (1,)) for h in range(2)]
+
+    def f_slot(h, zp, j):
+        return rxf.at[h, 2 * (3, 0, 2, 1).index(zp) + (j if zp != 1 else 0)]
     away = ((1, 3), (2, 3))
     kept = ((0, 2), (0, 1))
     nbr = (1, 2)
 
     def f_copy(h, zp, j):
         return remote(
-            f_block(h, zp, pq[away[h][j]]), rxf.at[h, early.index(zp), j], fsend.at[h, zp, j], frecv.at[h, zp, j], me.plane(nbr[h])
+            f_block(h, zp, pq[away[h][j]]), f_slot(h, zp, j), fsend.at[h, zp, j], frecv.at[h, zp, j], me.plane(nbr[h])
         )
 
     deep = width // LINE
@@ -1058,34 +1079,31 @@
     ]
     for i in range(1, LINE):
         slab(i).start()
-    for zp in early:
-        for h in range(2):
-            for j in range(2):
-                f_copy(h, zp, j).start()
 
     def f_own(u):
-        h, zp = u % 2, early[u // 2]
+        h, zp, js = units[u]
         return [
             pltpu.make_async_copy(f_block(h, zp, pq[kept[h][j]]), fo.at[u % 2, j], fosem.at[u % 2, j])
-            for j in range(2)
+            for j in js
         ]
 
     def f_out(u):
-        h, zp = u % 2, early[u // 2]
-        return pltpu.make_async_copy(rxf.at[h, u // 2], f1.at[h, zp], osem.at[u])
+        h, zp, js = units[u]
+        return [pltpu.make_async_copy(f_slot(h, zp, j), f1.at[h, zp, j], osem.at[u, j]) for j in js]
 
     for u in range(2):
         for c in f_own(u):
             c.start()
 
     def f_unit(u):
-        h, zp = u % 2, early[u // 2]
-        for j, c in enumerate(f_own(u)):
+        h, zp, js = units[u]
+        for j, c in zip(js, f_own(u)):
             c.wait()
             f_copy(h, zp, j).wait_recv()
-            add_rows(rxf.at[h, u // 2, j], fo.at[u % 2, j])
-        f_out(u).start()
-        if u + 2 < units:
+            add_rows(f_slot(h, zp, j), fo.at[u % 2, j])
+        for c in f_out(u):
+            c.start()
+        if u + 2 < len(units):
             for c in f_own(u + 2):
                 c.start()
 
@@ -1115,8 +1133,14 @@
             at = rows_at(ends_first[turn] * deep + i, 256)
             ao[at, :] = tn(da[:, at], gated[...]).astype(BF16)
 
+        if turn == 0:
+            meet(greeted)
         if turn < 2:
             out_sum.begin((LINE - 1 - turn,))
+        if turn == 0:
+            for h, zp, js in units:
+                for j in js:
+                    f_copy(h, zp, j).start()
     for c in loads[1:]:
         c.wait()
 
@@ -1275,6 +1299,8 @@
     for u in range(2, 4):
         f_unit(u)
     deal(0, out_sum, ao)
+    gate_sum.near(1)
+    gate_sum.far()
     x_tile(0).start()
     x_tile(1).start()
     wide = 2 * keys + values
@@ -1292,9 +1318,7 @@
         start(pltpu.make_async_copy(da.at[:, : 2 * keys], aq_out, lsem.at[0])),
         start(pltpu.make_async_copy(da.at[:, 2 * keys : wide], av_out, lsem.at[1])),
     ]
-    gate_sum.near(1)
-    gate_sum.far()
-    for u in range(4, 6):
+    for u in range(4, len(units)):
         f_unit(u)
     gate_sum.arrive()
     total_rows(z, fin.at[1], ag.at[rows_at(z * deep, deep), :], rxg)
@@ -1303,12 +1327,11 @@
         c.wait()
     out_sum.finish()
     gate_sum.finish()
-    for u in range(units):
-        f_out(u).wait()
-    for zp in early:
-        for h in range(2):
-            for j in range(2):
-                f_copy(h, zp, j).wait_send()
+    for u, (h, zp, js) in enumerate(units):
+        for c in f_out(u):
+            c.wait()
+        for j in js:
+            f_copy(h, zp, j).wait_send()
 
 
 def retention_back(da, wo, gated, gate, ret, q, k, v, states, cos, sin, ccol, crow, scal, xg, fu, fd, cid):
@@ -1355,7 +1378,7 @@
             pltpu.VMEM((blocks, keys, values), BF16),
             pltpu.VMEM((keys, values), F32),
             pltpu.VMEM((keys, values), BF16),
-            pltpu.VMEM((2, LINE - 1, 2, chunk, hidden), BF16),
+            pltpu.VMEM((2, 2 * LINE - 1, chunk, hidden), BF16),
             pltpu.VMEM((2, 2, chunk, hidden), BF16),
             pltpu.VMEM((STRETCH, STRETCH), BF16),
             pltpu.VMEM((STRETCH, STRETCH), BF16),
@@ -1364,7 +1387,7 @@
             DMA((3,)),
             DMA((2, LINE, 2)),
             DMA((2, LINE, 2)),
-            DMA((2 * LINE,)),
+            DMA((2 * LINE, 2)),
             DMA((2, 2)),
             DMA((1,)),
             DMA((1,)),
@@ -1382,15 +1405,15 @@
 def last_kernel(
     dh_ref, av_ref, aq_ref, wq_ref, wk_ref, wv_ref, wg_ref, f1_ref, fu_ref, fd_ref, gate_ref, tok_ref, gain_ref, resid_ref, second_ref,
     grad_out, gains, fout, sums,
-    tok, resid, rxl, flow, dh, wh, share, rx0, rx1a, rx1b, rx2a, rx2b, av, aq, rxv, rxq, fin, rf2, kf, rxfa, rxfb, grx,
+    tok, resid, rxl, dh, wh, share, rx0, rx1a, rx1b, rx2a, rx2b, av, aq, rxv, rxq, fin, rf2, kf, rxfa, rxfb, grx,
     lsem, ksem, lsend, lrecv, fsend, frecv, csend, crecv, xsend, xrecv, gsend, grecv, psend, precv, *line,
 ):
     me = Place()
     z, p, f = me.z, me.p, me.f
     rounds = [
+        [me.at((z + t) % LINE, p, f) for t in range(1, LINE)],
         [me.partner()],
         [me.plane(m) for m in (1, 2, 3)],
-        [me.at((z + t) % LINE, p, f) for t in range(1, LINE)],
     ]
     greet([(d, None) for r in rounds for d in r])
     width, keys2, values = av.shape[0], aq.shape[1], av.shape[1]
@@ -1402,15 +1425,13 @@
     late = 1
 
     def f_copy(h, zp):
-        src = flow.at[h] if zp == late else f1_ref.at[h, zp, 1]
-        return remote(src, rf2.at[h, zp], fsend.at[h, zp], frecv.at[h, zp], me.plane(2 - h))
+        return remote(f1_ref.at[h, zp, 1], rf2.at[h, zp], fsend.at[h, zp], frecv.at[h, zp], me.plane(2 - h))
 
     def f_block(h, place):
         return (fu_ref, fd_ref)[h].at[rows_at((late * PLANE + place) * chunk, chunk), :]
 
-    def late_copy(h, j):
-        place = pq[((1, 3), (2, 3))[h][j]]
-        return remote(f_block(h, place), rxl.at[h, j], lsend.at[h, j], lrecv.at[h, j], me.plane(1 + h))
+    def late_copy(h):
+        return remote(f_block(h, pq[1 + h]), rxl.at[h], lsend.at[h], lrecv.at[h], me.plane(1 + h))
 
     def block_of(a, size):
         return lambda zz: a.at[rows_at(zz * size, size), :]
@@ -1421,12 +1442,11 @@
     fb_sum = LineSum(me, lambda zz: kf.at[1, zz], rxfb, *line[12:16], add_rows)
     v_sum.begin(src=block_of(av_ref, deep))
     q_sum.begin(src=block_of(aq_ref, deep))
-    for j in (1, 0):
-        for h in range(2):
-            late_copy(h, j).start()
-    for zp in (3, 0, 2):
+    for zp in (3, 0, 2, 1):
         for h in range(2):
             f_copy(h, zp).start()
+    for h in range(2):
+        late_copy(h).start()
     load = start(pltpu.make_async_copy(dh_ref, dh, lsem.at[0]))
     owns = [
         start(pltpu.make_async_copy(av_ref, av, lsem.at[7])),
@@ -1441,9 +1461,7 @@
     for h in range(2):
         for i, zp in enumerate((3, 0, 2)):
             keeps.append(start(pltpu.make_async_copy(f1_ref.at[h, zp, 0], kf.at[h, zp], ksem.at[h, i])))
-        for j, dst in ((0, kf.at[h, late]), (1, flow.at[h])):
-            place = pq[((0, 2), (0, 1))[h][j]]
-            keeps.append(start(pltpu.make_async_copy(f_block(h, place), dst, ksem.at[h, 3 + j])))
+        keeps.append(start(pltpu.make_async_copy(f_block(h, p), kf.at[h, late], ksem.at[h, 3])))
     rest = [
         start(pltpu.make_async_copy(tok_ref, tok, lsem.at[5])),
         start(pltpu.make_async_copy(resid_ref, resid, lsem.at[6])),
@@ -1479,7 +1497,6 @@
     gate_load = start(pltpu.make_async_copy(gate_ref, fin.at[2], lsem.at[9]))
     for c in loads + owns + [gate_load]:
         c.wait()
-    spread(2, fin.at[2])
 
     own_rows, their_rows = rows_at(f * rows, rows), rows_at((1 - f) * rows, rows)
     wide = width // 2
@@ -1514,42 +1531,39 @@
 
     share_part(3)
     share_part(1)
+    pass_on(3)
     v_sum.near(0)
     share_part(2)
+    pass_on(1)
+    share_part(0)
+    pass_on(2)
+    v_sum.near(1)
+    pass_on(0)
     for c in keeps:
         c.wait()
-    for h in range(2):
-        late_copy(h, 1).wait_recv()
-        add_rows(flow.at[h], rxl.at[h, 1])
-        f_copy(h, late).start()
-    pass_on(3)
-    pass_on(1)
-    share_part(0)
-    v_sum.near(1)
-    pass_on(2)
-    pass_on(0)
-    for h in range(2):
-        late_copy(h, 0).wait_recv()
-        add_rows(kf.at[h, late], rxl.at[h, 0])
     v_sum.far()
     q_sum.near(0)
-    for ends, turns in (((3, 0), (3,)), ((2, 1), (2, 1))):
+    for ends, turns in (((3, 0), (3,)), ((2, 1), (2,))):
         for zp in ends:
             for h in range(2):
                 f_copy(h, zp).wait_recv()
                 add_rows(kf.at[h, zp], rf2.at[h, zp])
+                if zp == late:
+                    late_copy(h).wait_recv()
+                    add_rows(kf.at[h, zp], rxl.at[h])
         for zz in turns:
             fa_sum.begin((zz,))
             fb_sum.begin((zz,))
     q_sum.near(1)
     q_sum.far()
-    deal(0, v_sum, av)
     sends["a", 0].wait_recv()
     add_into(rx1a.at[0], whole, rx0.at[2], ca)
     s2a = start(remote(rx1a.at[0], rx2a, xsend.at[4], xrecv.at[4], me.plane(2)))
     sends["b", 0].wait_recv()
     add_into(rx1b.at[0], whole, rx0.at[1], cb)
     s2b = start(remote(rx1b.at[0], rx2b, xsend.at[5], xrecv.at[5], me.plane(1)))
+    spread(2, fin.at[2])
+    deal(0, v_sum, av)
     fa_sum.near(0)
     sends["a", 1].wait_recv()
     sends["b", 1].wait_recv()
@@ -1584,7 +1598,7 @@
     out_copy = start(pltpu.make_async_copy(tok, grad_out, lsem.at[0]))
 
     def gain_copies(r):
-        base = (0, 1, 4)[r]
+        base = (0, 3, 4)[r]
         return [
             remote(gains, grx.at[base + i], gsend.at[base + i], grecv.at[base + i], d)
             for i, d in enumerate(rounds[r])
@@ -1598,9 +1612,11 @@
         for c in gain_copies(r):
             c.wait()
         for i in range(len(rounds[r])):
-            gains[...] += grx[(0, 1, 4)[r] + i]
+            gains[...] += grx[(0, 3, 4)[r] + i]
 
     gain_begin(0)
+    fa_sum.begin((1,))
+    fb_sum.begin((1,))
     fa_sum.near(1)
     fa_sum.far()
     gain_end(0)
@@ -1609,16 +1625,15 @@
     gain_end(1)
     gain_begin(2)
     fb_sum.far()
+    gain_end(2)
     fa_sum.arrive()
     total_rows(z, fout.at[0], kf.at[0, z], rxfa)
     fb_sum.arrive()
     total_rows(z, fout.at[1], kf.at[1, z], rxfb)
-    gain_end(2)
     for c in plane + [out_copy]:
         c.wait()
     for h in range(2):
-        for j in range(2):
-            late_copy(h, j).wait_send()
+        late_copy(h).wait_send()
     for chain in (v_sum, q_sum, fa_sum, fb_sum):
         chain.finish()
     for c in list(first.values()) + list(sends.values()) + [s2a, s2b]:
@@ -1647,7 +1662,6 @@
         [
             pltpu.VMEM((rows, width), BF16),
             pltpu.VMEM((rows, width), F32),
-            pltpu.VMEM((2, 2, chunk, hidden), BF16),
             pltpu.VMEM((2, chunk, hidden), BF16),
             pltpu.VMEM(dh.shape, BF16),
             pltpu.VMEM((width, dh.shape[1]), BF16),
@@ -1668,9 +1682,9 @@
             pltpu.VMEM((LINE + 1, chunk, hidden), BF16),
             pltpu.VMEM((7, 8, width), F32),
             DMA((10,)),
-            DMA((2, 5)),
-            DMA((2, 2)),
-            DMA((2, 2)),
+            DMA((2, 4)),
+            DMA((2,)),
+            DMA((2,)),
             DMA((2, LINE)),
             DMA((2, LINE)),
             DMA((4,)),

time: 490 us -> 480 us (0.980)
  Pallas kernels: 484 us -> 478 us
    pallas_call x4, Pallas kernels: 478 us -> 471 us  [comm_call(): pl.pallas_call(kernel, out_shape=outs, in_specs=in_specs if in_specs is n...]
where the time goes in v8:
time: 480 us; the launch traced here: 479 us
  Pallas kernels  478 us (100%)
    pallas_call x4, Pallas kernels, comm_call(): pl.pallas_call(kernel, out_shape=outs, in_specs=in_specs if in_specs is n...  471 us

profile of v8, /device:TPU:16, one launch (start us, length us, event | category | flops | bytes accessed | tf_op | source)
XLA Modules:
  0.0 478.5 jit_solution(13681676101881958801)
XLA Ops:
  0.6 147.3 %shard_map.273 = (bf16[2048,2048]{1,0:T(8,128)(2,1)}, bf16[2048,256]{1,0:T(8,128)(2,1)}, bf16[2048,256]{1,0:T(8,128)(2,1)}, bf16[2048,512]{1,0:T(8,128)(2,1)}, f...) custom-call(bf16[256,2048]{1,0:T(8,128)(2,1)} %tok_ref.5, ...), custom_call_target="tpu_custom_call" | custom-call | tf_op jit(solution)/shard_map/pallas_call | solution.py:90
  147.9 84.6 %shard_map.274 = (bf16[256,2048]{1,0:T(8,128)(2,1)}, f32[256,2048]{1,0:T(8,128)}, f32[8,2048]{1,0:T(8,128)}, bf16[2048,2048]{1,0:T(8,128)(2,1)}, bf16[2048,2048]{1,0:T(8,128)(2,1)}, /*index=5*/bf16[2048,2048]{1,0:T(8,128)(2,1)}) custom-call(bf16[2048,512]{1,0:T(8,128)(2,1)} %get-tuple-element.60.gated_ref, bf16[512,2048]{1,0:T(8,128)(2,1)} %get-tuple-element.61.wo_ref, ...), custom_call_target="tpu_custom_call" | custom-call | tf_op jit(solution)/shard_map/pallas_call | solution.py:90
  232.5 95.6 %shard_map.275 = (bf16[2048,1536]{1,0:T(8,128)(2,1)}, bf16[4,128,512]{2,1,0:T(8,128)(2,1)}, bf16[512,512]{1,0:T(8,128)(2,1)}, bf16[2,4,2,128,2048]{4,3,2,1,0:T(8...) custom-call(bf16[2048,2048]{1,0:T(8,128)(2,1)} %get-tuple-element.62.da_ref, ...), custom_call_target="tpu_custom_call" | custom-call | tf_op jit(solution)/shard_map/pallas_call | solution.py:90
  328.1 144.1 %shard_map.276 = (bf16[256,2048]{1,0:T(8,128)(2,1)}, f32[8,2048]{1,0:T(8,128)}, bf16[2,128,2048]{2,1,0:T(8,128)(2,1)}, bf16[4,128,1536]{2,1,0:T(8,128)(2,1)}) custom-call(bf16[2048,1536]{1,0:T(8,128)(2,1)} %get-tuple-element.77.dh_ref, bf16[2048,512]{1,0:T(8,128)(2,1)} %get-tuple-element.78.av_ref, bf16[2048,512]{1,0:T(8,128)(2,1)} %get-tuple-element.79.aq_ref, ...), custom_call_target="tpu_custom_call" | custom-call | tf_op jit(solution)/shard_map/pallas_call | solution.py:90
  472.2 6.2 %shard_map.277 = (f32[128,1024]{1,0:T(8,128)}, f32[128,1024]{1,0:T(8,128)}, f32[128,2048]{1,0:T(8,128)}, f32[128,2048]{1,0:T(8,128)}, f32[2048,128]{1,0:T(8,128)...) custom-call(bf16[4,128,1536]{2,1,0:T(8,128)(2,1)} %get-tuple-element, ...), custom_call_target="tpu_custom_call" | custom-call | tf_op jit(solution)/shard_map/pallas_call | solution.py:1737

commit v9 on v8

--- a/solution.py
+++ b/solution.py
@@ -567,6 +567,8 @@
             copies[1].start()
 
     ahead = 2
+    for i in range(ahead):
+        to_line(part_copies(i, part(i, p), spot))
     load_t = start(pltpu.make_async_copy(tok_ref, tok, lsem.at[count + 1]))
     local, plane, held = [], [], []
     for i in range(count):
@@ -578,8 +580,6 @@
                 for m in (1, 2, 3)
             ]
         )
-    for i in range(ahead):
-        to_line(part_copies(i, part(i, p), spot))
     tiny = [start(remote(dec_ref, decg.at[p], tsend.at[m], trecv.at[m], me.plane(m))) for m in (1, 2, 3)]
     tiny_own = start(pltpu.make_async_copy(dec_ref, decg.at[p], tsend.at[0]))
     step = 32
@@ -1829,7 +1829,7 @@
     w_up = features_in(w_up.T).T if repeats > 1 else w_up
     ln1_gain, ln1_bias = features_in(ln1_gain), features_in(ln1_bias)
     ln2_gain, ln2_bias = features_in(ln2_gain), features_in(ln2_bias)
-    decays = decay_log.T
+    decays = jnp.pad(decay_log.T, ((0, 8 - heads), (0, 0)))
     (
         normed, q_rot, k_rot, value, gate_proj, retained, gated_low, prev_states,
         cosine, sine_part, ccol, crow, scalars, key_w, value_w, query_w, gate_w, out_w,

time: 480 us -> 481 us (level)
  no operation moved by 1% of the time
where the time goes in v9:
time: 481 us; the launch traced here: 480 us
  Pallas kernels  477 us (99%)
    pallas_call x4, Pallas kernels, comm_call(): pl.pallas_call(kernel, out_shape=outs, in_specs=in_specs if in_specs is n...  471 us

profile of v9, /device:TPU:16, one launch (start us, length us, event | category | flops | bytes accessed | tf_op | source)
XLA Modules:
  0.0 479.5 jit_solution(8760787859441076089)
XLA Ops:
  0.6 1.3 pad.4.dec_ref
  2.0 147.2 %shard_map.273 = (bf16[2048,2048]{1,0:T(8,128)(2,1)}, bf16[2048,256]{1,0:T(8,128)(2,1)}, bf16[2048,256]{1,0:T(8,128)(2,1)}, bf16[2048,512]{1,0:T(8,128)(2,1)}, f...) custom-call(bf16[256,2048]{1,0:T(8,128)(2,1)} %tok_ref.5, ...), custom_call_target="tpu_custom_call" | custom-call | tf_op jit(solution)/shard_map/pallas_call | solution.py:90
  149.2 84.3 %shard_map.274 = (bf16[256,2048]{1,0:T(8,128)(2,1)}, f32[256,2048]{1,0:T(8,128)}, f32[8,2048]{1,0:T(8,128)}, bf16[2048,2048]{1,0:T(8,128)(2,1)}, bf16[2048,2048]{1,0:T(8,128)(2,1)}, /*index=5*/bf16[2048,2048]{1,0:T(8,128)(2,1)}) custom-call(bf16[2048,512]{1,0:T(8,128)(2,1)} %get-tuple-element.60.gated_ref, bf16[512,2048]{1,0:T(8,128)(2,1)} %get-tuple-element.61.wo_ref, ...), custom_call_target="tpu_custom_call" | custom-call | tf_op jit(solution)/shard_map/pallas_call | solution.py:90
  233.5 95.6 %shard_map.275 = (bf16[2048,1536]{1,0:T(8,128)(2,1)}, bf16[4,128,512]{2,1,0:T(8,128)(2,1)}, bf16[512,512]{1,0:T(8,128)(2,1)}, bf16[2,4,2,128,2048]{4,3,2,1,0:T(8...) custom-call(bf16[2048,2048]{1,0:T(8,128)(2,1)} %get-tuple-element.62.da_ref, ...), custom_call_target="tpu_custom_call" | custom-call | tf_op jit(solution)/shard_map/pallas_call | solution.py:90
  329.1 144.1 %shard_map.276 = (bf16[256,2048]{1,0:T(8,128)(2,1)}, f32[8,2048]{1,0:T(8,128)}, bf16[2,128,2048]{2,1,0:T(8,128)(2,1)}, bf16[4,128,1536]{2,1,0:T(8,128)(2,1)}) custom-call(bf16[2048,1536]{1,0:T(8,128)(2,1)} %get-tuple-element.77.dh_ref, bf16[2048,512]{1,0:T(8,128)(2,1)} %get-tuple-element.78.av_ref, bf16[2048,512]{1,0:T(8,128)(2,1)} %get-tuple-element.79.aq_ref, ...), custom_call_target="tpu_custom_call" | custom-call | tf_op jit(solution)/shard_map/pallas_call | solution.py:90
  473.2 6.2 %shard_map.277 = (f32[128,1024]{1,0:T(8,128)}, f32[128,1024]{1,0:T(8,128)}, f32[128,2048]{1,0:T(8,128)}, f32[128,2048]{1,0:T(8,128)}, f32[2048,128]{1,0:T(8,128)...) custom-call(bf16[4,128,1536]{2,1,0:T(8,128)(2,1)} %get-tuple-element, ...), custom_call_target="tpu_custom_call" | custom-call | tf_op jit(solution)/shard_map/pallas_call | solution.py:1737

commit v10 on v9

--- a/solution.py
+++ b/solution.py
@@ -195,7 +195,7 @@
             )
         )
 
-    for m in order:
+    def make(m):
         load_g[m].wait()
 
         @pl.loop(0, slabs)
@@ -208,8 +208,6 @@
         if m == order[0]:
             meet(greeted)
         to_partner(m, 0)
-    for m in order:
-        to_partner(m, 1)
 
     def pass_on(m, h):
         first[m, h].wait_recv()
@@ -238,16 +236,24 @@
             remote(rx1b.at[0, at], rx2b.at[at], xsend.at[5, h], xrecv.at[5, h], me.plane(1))
         )
 
+    make(3)
+    make(1)
+    pass_on(3, 0)
+    make(2)
+    pass_on(1, 0)
+    make(0)
+    pass_on(2, 0)
+    pass_on(0, 0)
     for m in order:
-        pass_on(m, 0)
+        to_partner(m, 1)
 
     load_d.wait()
     for c in load_c:
         c.wait()
 
-    @pl.loop(0, hidden, step=256)
+    @pl.loop(0, hidden, step=512)
     def _(c):
-        at = rows_at(c, 256)
+        at = rows_at(c, 512)
         dact[:, at] = nt(cot[...], wd[at, :])
 
     second(0)

time: 481 us -> 480 us (level)
  no operation moved by 1% of the time
where the time goes in v10:
time: 480 us; the launch traced here: 478 us
  Pallas kernels  476 us (99%)
    pallas_call x4, Pallas kernels, comm_call(): pl.pallas_call(kernel, out_shape=outs, in_specs=in_specs if in_specs is n...  470 us

profile of v10, /device:TPU:16, one launch (start us, length us, event | category | flops | bytes accessed | tf_op | source)
XLA Modules:
  0.0 478.3 jit_solution(15972176615952775251)
XLA Ops:
  0.6 1.3 pad.4.dec_ref
  2.0 147.2 %shard_map.273 = (bf16[2048,2048]{1,0:T(8,128)(2,1)}, bf16[2048,256]{1,0:T(8,128)(2,1)}, bf16[2048,256]{1,0:T(8,128)(2,1)}, bf16[2048,512]{1,0:T(8,128)(2,1)}, f...) custom-call(bf16[256,2048]{1,0:T(8,128)(2,1)} %tok_ref.5, ...), custom_call_target="tpu_custom_call" | custom-call | tf_op jit(solution)/shard_map/pallas_call | solution.py:90
  149.2 82.0 %shard_map.274 = (bf16[256,2048]{1,0:T(8,128)(2,1)}, f32[256,2048]{1,0:T(8,128)}, f32[8,2048]{1,0:T(8,128)}, bf16[2048,2048]{1,0:T(8,128)(2,1)}, bf16[2048,2048]{1,0:T(8,128)(2,1)}, /*index=5*/bf16[2048,2048]{1,0:T(8,128)(2,1)}) custom-call(bf16[2048,512]{1,0:T(8,128)(2,1)} %get-tuple-element.60.gated_ref, bf16[512,2048]{1,0:T(8,128)(2,1)} %get-tuple-element.61.wo_ref, ...), custom_call_target="tpu_custom_call" | custom-call | tf_op jit(solution)/shard_map/pallas_call | solution.py:90
  231.2 95.6 %shard_map.275 = (bf16[2048,1536]{1,0:T(8,128)(2,1)}, bf16[4,128,512]{2,1,0:T(8,128)(2,1)}, bf16[512,512]{1,0:T(8,128)(2,1)}, bf16[2,4,2,128,2048]{4,3,2,1,0:T(8...) custom-call(bf16[2048,2048]{1,0:T(8,128)(2,1)} %get-tuple-element.62.da_ref, ...), custom_call_target="tpu_custom_call" | custom-call | tf_op jit(solution)/shard_map/pallas_call | solution.py:90
  326.8 145.1 %shard_map.276 = (bf16[256,2048]{1,0:T(8,128)(2,1)}, f32[8,2048]{1,0:T(8,128)}, bf16[2,128,2048]{2,1,0:T(8,128)(2,1)}, bf16[4,128,1536]{2,1,0:T(8,128)(2,1)}) custom-call(bf16[2048,1536]{1,0:T(8,128)(2,1)} %get-tuple-element.77.dh_ref, bf16[2048,512]{1,0:T(8,128)(2,1)} %get-tuple-element.78.av_ref, bf16[2048,512]{1,0:T(8,128)(2,1)} %get-tuple-element.79.aq_ref, ...), custom_call_target="tpu_custom_call" | custom-call | tf_op jit(solution)/shard_map/pallas_call | solution.py:90
  472.0 6.2 %shard_map.277 = (f32[128,1024]{1,0:T(8,128)}, f32[128,1024]{1,0:T(8,128)}, f32[128,2048]{1,0:T(8,128)}, f32[128,2048]{1,0:T(8,128)}, f32[2048,128]{1,0:T(8,128)...) custom-call(bf16[4,128,1536]{2,1,0:T(8,128)(2,1)} %get-tuple-element, ...), custom_call_target="tpu_custom_call" | custom-call | tf_op jit(solution)/shard_map/pallas_call | solution.py:1743

commit v11 on v10

--- a/solution.py
+++ b/solution.py
@@ -572,7 +572,7 @@
         def _():
             copies[1].start()
 
-    ahead = 2
+    ahead = count
     for i in range(ahead):
         to_line(part_copies(i, part(i, p), spot))
     load_t = start(pltpu.make_async_copy(tok_ref, tok, lsem.at[count + 1]))

time: 480 us -> 478 us (level)
  no operation moved by 1% of the time
where the time goes in v11:
time: 478 us; the launch traced here: 477 us
  Pallas kernels  475 us (99%)
    pallas_call x4, Pallas kernels, comm_call(): pl.pallas_call(kernel, out_shape=outs, in_specs=in_specs if in_specs is n...  468 us

profile of v11, /device:TPU:16, one launch (start us, length us, event | category | flops | bytes accessed | tf_op | source)
XLA Modules:
  0.0 476.7 jit_solution(17299011798567861542)
XLA Ops:
  0.6 1.3 pad.4.dec_ref
  2.0 146.1 %shard_map.273 = (bf16[2048,2048]{1,0:T(8,128)(2,1)}, bf16[2048,256]{1,0:T(8,128)(2,1)}, bf16[2048,256]{1,0:T(8,128)(2,1)}, bf16[2048,512]{1,0:T(8,128)(2,1)}, f...) custom-call(bf16[256,2048]{1,0:T(8,128)(2,1)} %tok_ref.5, ...), custom_call_target="tpu_custom_call" | custom-call | tf_op jit(solution)/shard_map/pallas_call | solution.py:90
  148.0 81.1 %shard_map.274 = (bf16[256,2048]{1,0:T(8,128)(2,1)}, f32[256,2048]{1,0:T(8,128)}, f32[8,2048]{1,0:T(8,128)}, bf16[2048,2048]{1,0:T(8,128)(2,1)}, bf16[2048,2048]{1,0:T(8,128)(2,1)}, /*index=5*/bf16[2048,2048]{1,0:T(8,128)(2,1)}) custom-call(bf16[2048,512]{1,0:T(8,128)(2,1)} %get-tuple-element.60.gated_ref, bf16[512,2048]{1,0:T(8,128)(2,1)} %get-tuple-element.61.wo_ref, ...), custom_call_target="tpu_custom_call" | custom-call | tf_op jit(solution)/shard_map/pallas_call | solution.py:90
  229.1 95.6 %shard_map.275 = (bf16[2048,1536]{1,0:T(8,128)(2,1)}, bf16[4,128,512]{2,1,0:T(8,128)(2,1)}, bf16[512,512]{1,0:T(8,128)(2,1)}, bf16[2,4,2,128,2048]{4,3,2,1,0:T(8...) custom-call(bf16[2048,2048]{1,0:T(8,128)(2,1)} %get-tuple-element.62.da_ref, ...), custom_call_target="tpu_custom_call" | custom-call | tf_op jit(solution)/shard_map/pallas_call | solution.py:90
  324.7 145.7 %shard_map.276 = (bf16[256,2048]{1,0:T(8,128)(2,1)}, f32[8,2048]{1,0:T(8,128)}, bf16[2,128,2048]{2,1,0:T(8,128)(2,1)}, bf16[4,128,1536]{2,1,0:T(8,128)(2,1)}) custom-call(bf16[2048,1536]{1,0:T(8,128)(2,1)} %get-tuple-element.77.dh_ref, bf16[2048,512]{1,0:T(8,128)(2,1)} %get-tuple-element.78.av_ref, bf16[2048,512]{1,0:T(8,128)(2,1)} %get-tuple-element.79.aq_ref, ...), custom_call_target="tpu_custom_call" | custom-call | tf_op jit(solution)/shard_map/pallas_call | solution.py:90
  470.4 6.2 %shard_map.277 = (f32[128,1024]{1,0:T(8,128)}, f32[128,1024]{1,0:T(8,128)}, f32[128,2048]{1,0:T(8,128)}, f32[128,2048]{1,0:T(8,128)}, f32[2048,128]{1,0:T(8,128)...) custom-call(bf16[4,128,1536]{2,1,0:T(8,128)(2,1)} %get-tuple-element, ...), custom_call_target="tpu_custom_call" | custom-call | tf_op jit(solution)/shard_map/pallas_call | solution.py:1743
